TPU v7x, 32 devices: a whole 2x2x4 slice. The times are simulated.
32 devices in a mesh: seq: 8 (over z, x), mp: 4 (over y, core).
Axes of the slice: x: 2, y: 2, z: 4, core: 2. Of those that a mesh axis runs over, the one named last changes fastest.
Arguments:
- tokens: bfloat16 [2048, 2048], P('seq'), may hold values from -6 to 6
- gate_weight: bfloat16 [2048, 64, 64], P('seq', 'mp'), may hold values from -0.125 to 0.125
- input_weight: bfloat16 [2048, 64, 64], P('seq', 'mp'), may hold values from -0.125 to 0.125
- group_weight: bfloat16 [2048, 4, 2, 128], P('seq', 'mp'), may hold values from -0.125 to 0.125
- step_weight: bfloat16 [2048, 64], P('seq', 'mp'), may hold values from -0.0625 to 0.0625
- step_bias: float32 [64], P('mp'), may hold values from -3.91 to -1.5
- bucket_table: float32 [4, 64], P(None, 'mp'), may hold values from -1.2 to 2.5
- bucket_ids: int32 [2048], P('seq'), may hold values from 0 to 3, as said below
- decay_rate: float32 [64], P('mp'), may hold values from 0.00072753906 to 2.001
- conv_input: float32 [4, 64, 64], P(None, 'mp'), may hold values from -3 to 3
- conv_input_bias: float32 [64, 64], P('mp'), may hold values from -2 to 2
- conv_group: float32 [4, 4, 2, 128], P(None, 'mp'), may hold values from -3 to 3
- conv_group_bias: float32 [4, 2, 128], P('mp'), may hold values from -2 to 2
- skip_gain: float32 [64], P('mp'), may hold values from 0.5 to 1.5
- norm_gain: float32 [64, 64], P('mp'), may hold values from 0.1 to 1.9
- out_weight: bfloat16 [64, 64, 2048], P('mp'), may hold values from -0.09375 to 0.09375
Outputs:
- layer_out: bfloat16 [2048, 2048], P(('seq', 'mp'))
Inputs may be any that keep to these rules, and one draw needn't show every extreme that they name: `bucket_ids`: exactly 3 tokens of the sequence have a bucket other than 0.
All inputs are finite; a program needn't handle non-finite values.
Results may differ from a plain program's by a relative error of at most 0.02.
Values may be sent and summed in bfloat16 or wider, within the bound.
No kernel may reach another device: no remote copies, remote signals or barrier semaphores. Data moves between devices by JAX's collectives and lax.ppermute only.
A program may use at most 128 MiB of HBM per device.

v0:
```python
import jax
import jax.numpy as jnp
from jax import lax
from jax.sharding import PartitionSpec as P

SPAN = 256
PLACE_BINS = 4


norm_epsilon = 1e-05
highest = lax.Precision.HIGHEST


def causal_conv(raw_rows, rim_rows, tap_weights, tap_bias):
    extended = jnp.concatenate([rim_rows, raw_rows], axis=0).astype(jnp.float32)
    row_count = raw_rows.shape[0]
    tap_count = tap_weights.shape[0]
    running = (
        tap_bias[None, :]
        + tap_weights[tap_count - 1][None, :] * extended[tap_count - 1 : tap_count - 1 + row_count]
    )
    for tap_index in range(tap_count - 1):
        running = (
            running + tap_weights[tap_index][None, :] * extended[tap_index : tap_index + row_count]
        )
    return jax.nn.silu(running).astype(jnp.bfloat16)


def ssd_block(carried_state, block_inputs, decay_neg):
    block_values, block_b, block_c, block_steps = block_inputs
    step_rates = block_steps.astype(jnp.float32) * decay_neg[None, :]
    cumulative = jnp.cumsum(step_rates, axis=0)
    scores = jnp.einsum("tn,sn->ts", block_c, block_b, preferred_element_type=jnp.float32)
    by_head = jnp.transpose(cumulative)
    spread = by_head[:, :, None] - by_head[:, None, :]
    block_rows = block_values.shape[0]
    causal = (jnp.arange(block_rows)[:, None] >= jnp.arange(block_rows)[None, :])[None]
    decays = jnp.where(causal, jnp.exp(jnp.where(causal, spread, 0.0)), 0.0)
    mixing = scores[None] * decays
    driven = block_steps.astype(jnp.float32)[:, :, None] * block_values.astype(jnp.float32)
    within = jnp.einsum("rts,srp->trp", mixing, driven, precision=highest)
    readout = jnp.einsum(
        "tn,rpn->trp", block_c.astype(jnp.float32), carried_state, precision=highest
    )
    outputs = within + jnp.exp(cumulative)[:, :, None] * readout
    remaining = jnp.exp(cumulative[-1][None, :] - cumulative)
    injected = jnp.einsum(
        "srp,sn->rpn",
        driven * remaining[:, :, None],
        block_b.astype(jnp.float32),
        precision=highest,
    )
    next_state = jnp.exp(cumulative[-1])[:, None, None] * carried_state + injected
    return (next_state, outputs)


def ssd_group(start_state, group_values, group_b, group_c, group_steps, decay_neg):
    row_total = group_values.shape[0]
    block_count = row_total // SPAN

    def advance(carried_state, block_inputs):
        return ssd_block(carried_state, block_inputs, decay_neg)

    blocked = (
        group_values.reshape((block_count, SPAN) + group_values.shape[1:]),
        group_b.reshape(block_count, SPAN, -1),
        group_c.reshape(block_count, SPAN, -1),
        group_steps.reshape(block_count, SPAN, -1),
    )
    final_state, outputs = lax.scan(advance, start_state, blocked)
    return (final_state, outputs.reshape((row_total,) + outputs.shape[2:]))


def on_device(
    tokens,
    gate_weight,
    input_weight,
    group_weight,
    step_weight,
    step_bias,
    bucket_table,
    bucket_ids,
    decay_rate,
    conv_input,
    conv_input_bias,
    conv_group,
    conv_group_bias,
    skip_gain,
    norm_gain,
    out_weight,
):
    tok_rows = tokens.shape[0]
    heads_here = step_bias.shape[0]
    groups_here = group_weight.shape[1]
    per_group = heads_here // groups_here
    head_size = gate_weight.shape[2]
    state_size = group_weight.shape[3]
    tap_count = conv_input.shape[0]
    channel_width = heads_here * head_size
    group_width = groups_here * 2 * state_size
    pieces = (
        lax.all_gather(gate_weight, "seq", axis=0, tiled=True),
        lax.all_gather(input_weight, "seq", axis=0, tiled=True),
        lax.all_gather(group_weight, "seq", axis=0, tiled=True),
        lax.all_gather(step_weight, "seq", axis=0, tiled=True),
    )
    rows_here = pieces[0].shape[0]
    gate_sum, input_sum, group_sum, step_sum = tuple(
        (
            jnp.dot(tokens, piece.reshape(rows_here, -1), preferred_element_type=jnp.float32)
            for piece in pieces
        )
    )
    gate_act = gate_sum.astype(jnp.bfloat16)
    input_raw = input_sum.astype(jnp.bfloat16)
    group_raw = group_sum.astype(jnp.bfloat16)
    onehot = (bucket_ids[:, None] == jnp.arange(PLACE_BINS, dtype=jnp.int32)[None, :]).astype(
        jnp.float32
    )
    offsets = jnp.dot(onehot, bucket_table, precision=highest)
    steps_tok = jax.nn.softplus(step_sum + step_bias[None, :] + offsets).astype(jnp.bfloat16)
    decay_neg = -decay_rate
    seq_count = lax.axis_size("seq")
    piece_width = channel_width // seq_count
    sub_width = min(piece_width, head_size)
    sub_count = piece_width // sub_width
    subs_per_head = head_size // sub_width
    steps_sub = jnp.repeat(steps_tok, subs_per_head, axis=1)
    wide_groups = jnp.broadcast_to(
        group_raw[:, None, :], (tok_rows, seq_count, group_width)
    ).reshape(tok_rows, seq_count * group_width)
    head_inputs, head_steps, head_groups = (
        lax.all_to_all(input_raw, "seq", split_axis=1, concat_axis=0, tiled=True),
        lax.all_to_all(steps_sub, "seq", split_axis=1, concat_axis=0, tiled=True),
        lax.all_to_all(wide_groups, "seq", split_axis=1, concat_axis=0, tiled=True),
    )
    seq_total = head_inputs.shape[0]
    first_channel = lax.axis_index("seq") * piece_width
    input_taps = lax.dynamic_slice_in_dim(
        conv_input.reshape(tap_count, -1), first_channel, piece_width, 1
    )
    input_shift = lax.dynamic_slice_in_dim(
        conv_input_bias.reshape(-1), first_channel, piece_width, 0
    )
    conv_values = causal_conv(
        head_inputs, jnp.zeros((tap_count - 1, piece_width), jnp.bfloat16), input_taps, input_shift
    )
    conv_groups = causal_conv(
        head_groups,
        jnp.zeros((tap_count - 1, group_width), jnp.bfloat16),
        conv_group.reshape(tap_count, -1),
        conv_group_bias.reshape(-1),
    )
    conv_groups = conv_groups.reshape(seq_total, groups_here, 2, state_size)
    sub_heads = (first_channel + jnp.arange(sub_count, dtype=jnp.int32) * sub_width) // head_size
    sub_groups = sub_heads // per_group
    sub_decay = jnp.take(decay_neg, sub_heads)[:, None]
    sub_skip = jnp.take(skip_gain, sub_heads)
    values_sub = jnp.moveaxis(conv_values.reshape(seq_total, sub_count, 1, sub_width), 1, 0)
    steps_heads = jnp.moveaxis(head_steps, 1, 0)[:, :, None]

    def run_sub(member):
        chosen = lax.dynamic_index_in_dim(conv_groups, member[3], 1, False)
        start_state = jnp.zeros((1, sub_width, state_size), jnp.float32)
        return ssd_group(start_state, member[0], chosen[:, 0], chosen[:, 1], member[1], member[2])[
            1
        ]

    scanned = jnp.moveaxis(
        lax.map(run_sub, (values_sub, steps_heads, sub_decay, sub_groups)), 0, 1
    ).reshape(seq_total, sub_count, sub_width)
    head_out = (
        scanned
        + sub_skip[None, :, None]
        * conv_values.reshape(seq_total, sub_count, sub_width).astype(jnp.float32)
    ).astype(jnp.bfloat16)
    ssd_out = lax.all_to_all(
        head_out.reshape(seq_total, piece_width), "seq", split_axis=0, concat_axis=1, tiled=True
    )
    gated_out = ssd_out.astype(jnp.float32) * jax.nn.silu(gate_act.astype(jnp.float32))
    grouped = gated_out.reshape(tok_rows, groups_here, -1)
    mean_square = jnp.mean(grouped * grouped, axis=2)
    scales = lax.rsqrt(mean_square + norm_epsilon)
    normed = (
        (grouped * scales[:, :, None]).reshape(tok_rows, -1) * norm_gain.reshape(-1)[None, :]
    ).astype(jnp.bfloat16)
    flat_out = out_weight.reshape(-1, out_weight.shape[2])
    layer_out = lax.psum_scatter(
        jnp.dot(normed, flat_out, preferred_element_type=jnp.float32).astype(jnp.bfloat16),
        "mp",
        scatter_dimension=0,
        tiled=True,
    )
    return layer_out


def solution(mesh):
    placed = (
        P("seq", None),
        P("seq", "mp", None),
        P("seq", "mp", None),
        P("seq", "mp", None, None),
        P("seq", "mp"),
        P("mp"),
        P(None, "mp"),
        P("seq"),
        P("mp"),
        P(None, "mp", None),
        P("mp", None),
        P(None, "mp", None, None),
        P("mp", None, None),
        P("mp"),
        P("mp", None),
        P("mp", None, None),
    )
    return jax.shard_map(
        on_device, mesh=mesh, in_specs=placed, out_specs=P(("seq", "mp"), None), check_vma=False
    )
```

profile of v0, /device:TPU:0, one launch (start us, length us, event | category | flops | bytes accessed | tf_op | source)
XLA Modules:
  0.0 394.6 jit_solution(5507819699891726263)
XLA Ops:
  8.0 44.4 %all-gather.6.cloned.1.call-done = bf16[2048,1,2,128]{3,2,1,0:T(2,128)(2,1)} async-done(((bf16[256,1,2,128]{3,2,1,0:T(2,128)(2,1)}), bf16[2048,1,2,128]{3,2,1,0:T(2,128)(2,1)}) %all-gather.6.cloned.1.call-update) | async-done | bytes 1048592 | tf_op jit(solution)/shard_map/all_gather | solution.py:104
  52.4 1.7 convolution_convert_fusion.3
  54.2 1.1 broadcast_in_dim.24
  55.3 3.7 all-to-all-start.1
  59.9 62.5 %all_gather.14 = bf16[2048,16]{0,1:T(8,128)(2,1)S(1)} all-gather(bf16[256,16]{0,1:T(8,128)(2,1)S(1)} %copy-done.3), channel_id=1, replica_groups=mesh['seq'=8,'mp'=4] {'seq'}, dimensions={0}, use_global_device_ids=true | all-gather | bytes 73728 | tf_op jit(solution)/shard_map/all_gather | solution.py:105
  125.5 20.1 %all-gather.4.cloned.1.call-done = bf16[2048,16,64]{0,2,1:T(8,128)(2,1)} async-done(((bf16[256,16,64]{0,2,1:T(8,128)(2,1)}), bf16[2048,16,64]{0,2,1:T(8,128)(2,1)}) %all-gather.4.cloned.1.call-update) | async-done | bytes 4194320 | tf_op jit(solution)/shard_map/all_gather | solution.py:103
  145.7 3.5 fusion.33
  150.0 4.3 %all-to-all-start = ((bf16[256,8,128]{2,0,1:T(8,128)(2,1)}), bf16[256,8,128]{2,0,1:T(8,128)(2,1)}, u32[]{:S(2)}, u32[]{:S(2)}) async-start(bf16[256,8,128]{2,0,1:T(8,128)(2,1)} %bitcast.141), calls=%async_computation | async-start | bytes 1048576 | tf_op jit(solution)/shard_map/all_to_all | solution.py:133
  154.7 2.2 multiply_convert_fusion
  156.9 1.3 copy.36
  158.2 23.8 %all-to-all-done = bf16[256,8,128]{2,0,1:T(8,128)(2,1)} async-done(((bf16[256,8,128]{2,0,1:T(8,128)(2,1)}), bf16[256,8,128]{2,0,1:T(8,128)(2,1)}, u32[]{:S(2)}, u32[]{:S(2)}) %all-to-all-start) | async-done | bytes 524320 | tf_op jit(solution)/shard_map/all_to_all | solution.py:133
  182.0 4.2 %all-to-all-start.2 = ((bf16[256,8,2]{0,2,1:T(2,128)(2,1)}), bf16[256,8,2]{0,2,1:T(2,128)(2,1)S(1)}, u32[]{:S(2)}, u32[]{:S(2)}) async-start(bf16[256,8,2]{0,2,1:T(2,128)(2,1)} %all_to_all.57), calls=%async_computation.2 | async-start | bytes 16384 | tf_op jit(solution)/shard_map/all_to_all | solution.py:134
  186.2 1.1 pad_convert_fusion.1
  189.1 3.6 all-to-all-done.2
  192.7 145.4 %while.28 = (s32[]{:T(128)}, f32[2,2048,1,64]{1,3,0,2:T(8,128)}, bf16[2,2048,1,64]{1,3,2,0:T(8,128)(2,1)}, bf16[2048,1,2,128]{3,0,2,1:T(8,128)(2,1)}, bf16[2,204...) while((s32[]{:T(128)}, f32[2,2048,1,64]{1,3,0,2:T(8,128)}, ...), condition=%wide.region_5.7_spmd, body=%wide.region_0.0_spmd.sunk | while | flops 117932808 | bytes 7761885 | solution.py:170
  194.4 2.1 fusion.74
  196.5 63.9 %while.29 = (s32[]{:T(128)}, f32[1,64,128]{2,1,0:T(8,128)S(1)}, f32[8,256,1,64]{1,3,2,0:T(8,128)}, bf16[8,256,1]{1,2,0:T(2,128)(2,1)S(1)}, f32[1]{0:T(128)}, /*i...) while((s32[]{:T(128)}, f32[1,64,128]{2,1,0:T(8,128)S(1)}, ...), condition=%wide.region_4.5_spmd.clone, body=%wide.region_1.4_spmd.clone.sunk | while | flops 117932808 | bytes 1461500 | solution.py:70
  199.5 1.1 fusion.86
  203.2 1.2 fusion.84
  207.5 1.1 fusion.86
  211.2 1.2 fusion.84
  215.5 1.1 fusion.86
  219.2 1.2 fusion.84
  223.5 1.1 fusion.86
  227.2 1.2 fusion.84
  231.5 1.1 fusion.86
  235.2 1.2 fusion.84
  239.5 1.1 fusion.86
  243.2 1.2 fusion.84
  247.5 1.1 fusion.86
  251.2 1.2 fusion.84
  255.4 1.1 fusion.86
  259.2 1.2 fusion.84
  260.4 1.4 copy.63
  261.8 1.8 copy.64
  263.5 1.9 constant_dynamic-update-slice_fusion.2
  267.1 2.1 fusion.74
  269.2 63.9 %while.29 = (s32[]{:T(128)}, f32[1,64,128]{2,1,0:T(8,128)S(1)}, f32[8,256,1,64]{1,3,2,0:T(8,128)}, bf16[8,256,1]{1,2,0:T(2,128)(2,1)S(1)}, f32[1]{0:T(128)}, /*i...) while((s32[]{:T(128)}, f32[1,64,128]{2,1,0:T(8,128)S(1)}, ...), condition=%wide.region_4.5_spmd.clone, body=%wide.region_1.4_spmd.clone.sunk | while | flops 117932808 | bytes 1461500 | solution.py:70
  272.2 1.1 fusion.86
  276.0 1.2 fusion.84
  280.2 1.1 fusion.86
  283.9 1.2 fusion.84
  288.2 1.1 fusion.86
  291.9 1.2 fusion.84
  296.2 1.1 fusion.86
  299.9 1.2 fusion.84
  304.2 1.1 fusion.86
  307.9 1.2 fusion.84
  312.2 1.1 fusion.86
  315.9 1.2 fusion.84
  320.2 1.1 fusion.86
  323.9 1.2 fusion.84
  328.2 1.1 fusion.86
  331.9 1.2 fusion.84
  333.1 1.4 copy.63
  334.5 1.8 copy.64
  336.3 1.9 constant_dynamic-update-slice_fusion.2
  338.2 1.5 copy.39
  339.7 1.6 add_convert_fusion
  341.3 3.5 all-to-all-start.3
  345.1 13.3 %all-to-all-done.3 = bf16[8,256,128]{2,1,0:T(8,128)(2,1)S(1)} async-done(((bf16[8,256,128]{2,1,0:T(8,128)(2,1)}), bf16[8,256,128]{2,1,0:T(8,128)(2,1)S(1)}, u32[]{:S(2)}, u32[]{:S(2)}) %all-to-all-start.3) | async-done | bytes 524320 | tf_op jit(solution)/shard_map/all_to_all | solution.py:177
  358.4 3.9 multiply_reduce_fusion
  362.3 2.4 convolution_convert_fusion
  364.7 23.4 %reduce-scatter.2.cloned.1.call-done = bf16[64,2048]{1,0:T(8,128)(2,1)} async-done(((bf16[256,2048]{1,0:T(8,128)(2,1)}), bf16[64,2048]{1,0:T(8,128)(2,1)}) %reduce-scatter.2.cloned.1.call-update) | async-done | bytes 262160 | tf_op jit(solution)/shard_map/reduce_scatter | solution.py:188
  (315 shorter events, 80.9 us)
Async XLA Ops:
  6.5 45.8 %copy-start = (bf16[256,2048]{1,0:T(8,128)(2,1)S(1)}, bf16[256,2048]{1,0:T(8,128)(2,1)}, u32[]{:S(2)}) copy-start(bf16[256,2048]{1,0:T(8,128)(2,1)} %param.22) | copy-start | bytes 3145732
  6.5 45.8 %all-gather.6.cloned.1.call-start = ((), (), s32[]{:S(2)}) async-start(), calls=%async_computation.6 | async-start | bytes 1179648 | tf_op jit(solution)/shard_map/all_gather | solution.py:104
  7.3 138.4 %all-gather.4.cloned.1.call-start = ((), (), s32[]{:S(2)}) async-start(), calls=%async_computation.5 | async-start | bytes 4718592 | tf_op jit(solution)/shard_map/all_gather | solution.py:103
  54.0 5.7 %copy-start.2 = (f32[4,16,64]{2,1,0:T(8,128)S(1)}, f32[4,16,64]{2,1,0:T(8,128)}, u32[]{:S(2)}) copy-start(f32[4,16,64]{2,1,0:T(8,128)} %param.31) | copy-start | bytes 49156
  54.0 5.8 %copy-start.4 = (f32[16,64]{1,0:T(8,128)S(1)}, f32[16,64]{1,0:T(8,128)}, u32[]{:S(2)}) copy-start(f32[16,64]{1,0:T(8,128)} %param.32) | copy-start | bytes 12292
  54.1 5.9 %copy-start.12 = (f32[16]{0:T(128)S(1)}, f32[16]{0:T(128)}, u32[]{:S(2)}) copy-start(f32[16]{0:T(128)} %param.30) | copy-start | bytes 196
  54.1 5.8 %copy-start.3 = (bf16[256,16]{0,1:T(8,128)(2,1)S(1)}, bf16[256,16]{0,1:T(8,128)(2,1)}, u32[]{:S(2)}) copy-start(bf16[256,16]{0,1:T(8,128)(2,1)} %param.26) | copy-start | bytes 24580
  54.1 68.4 %copy-start.8 = (f32[16]{0:T(128)S(1)}, f32[16]{0:T(128)}, u32[]{:S(2)}) copy-start(f32[16]{0:T(128)} %param.27) | copy-start | bytes 196
  55.3 67.6 %copy-start.10 = (f32[4,16]{1,0:T(4,128)S(1)}, f32[4,16]{1,0:T(4,128)}, u32[]{:S(2)}) copy-start(f32[4,16]{1,0:T(4,128)} %param.28) | copy-start | bytes 772
  55.3 67.6 %copy-start.11 = (s32[256]{0:T(256)S(1)}, s32[256]{0:T(256)}, u32[]{:S(2)}) copy-start(s32[256]{0:T(256)} %param.29) | copy-start | bytes 3076
  55.3 69.2 %copy-start.1 = (f32[16]{0:T(128)S(1)}, f32[16]{0:T(128)}, u32[]{:S(2)}) copy-start(f32[16]{0:T(128)} %param.35) | copy-start | bytes 196
  55.3 70.1 %copy-start.6 = (f32[4,1,2,128]{3,2,1,0:T(2,128)S(1)}, f32[4,1,2,128]{3,2,1,0:T(2,128)}, u32[]{:S(2)}) copy-start(f32[4,1,2,128]{3,2,1,0:T(2,128)} %param.33) | copy-start | bytes 12292
  55.3 70.1 %all-to-all-start.1 = ((bf16[256,8,256]{0,2,1:T(8,128)(2,1)}), bf16[256,8,256]{0,2,1:T(8,128)(2,1)S(1)}, u32[]{:S(2)}, u32[]{:S(2)}) async-start(bf16[256,8,256]{0,2,1:T(8,128)(2,1)} %broadcast_in_dim.24), calls=%async_computation.1 | async-start | bytes 2097152 | tf_op jit(solution)/shard_map/all_to_all | solution.py:135
  59.0 286.1 %all-gather.8.cloned.1.call-start = ((), (), s32[]{:S(2)}) async-start(), calls=%async_computation.7 | async-start | bytes 4718592 | tf_op jit(solution)/shard_map/all_gather | solution.py:102
  150.0 4.7 %copy-start.7 = (f32[1,2,128]{2,1,0:T(2,128)S(1)}, f32[1,2,128]{2,1,0:T(2,128)}, u32[]{:S(2)}) copy-start(f32[1,2,128]{2,1,0:T(2,128)} %param.34) | copy-start | bytes 3076
  150.0 31.9 %all-to-all-start = ((bf16[256,8,128]{2,0,1:T(8,128)(2,1)}), bf16[256,8,128]{2,0,1:T(8,128)(2,1)}, u32[]{:S(2)}, u32[]{:S(2)}) async-start(bf16[256,8,128]{2,0,1:T(8,128)(2,1)} %bitcast.141), calls=%async_computation | async-start | bytes 1048576 | tf_op jit(solution)/shard_map/all_to_all | solution.py:133
  182.0 10.7 %all-to-all-start.2 = ((bf16[256,8,2]{0,2,1:T(2,128)(2,1)}), bf16[256,8,2]{0,2,1:T(2,128)(2,1)S(1)}, u32[]{:S(2)}, u32[]{:S(2)}) async-start(bf16[256,8,2]{0,2,1:T(2,128)(2,1)} %all_to_all.57), calls=%async_computation.2 | async-start | bytes 16384 | tf_op jit(solution)/shard_map/all_to_all | solution.py:134
  339.7 5.3 %copy-start.5 = (f32[16,64]{1,0:T(8,128)S(1)}, f32[16,64]{1,0:T(8,128)}, u32[]{:S(2)}) copy-start(f32[16,64]{1,0:T(8,128)} %param.36) | copy-start | bytes 12292
  341.3 17.1 %all-to-all-start.3 = ((bf16[8,256,128]{2,1,0:T(8,128)(2,1)}), bf16[8,256,128]{2,1,0:T(8,128)(2,1)S(1)}, u32[]{:S(2)}, u32[]{:S(2)}) async-start(bf16[8,256,128]{2,1,0:T(8,128)(2,1)} %bitcast.215), calls=%async_computation.3 | async-start | bytes 1048576 | tf_op jit(solution)/shard_map/all_to_all | solution.py:177
  344.8 43.3 %reduce-scatter.2.cloned.1.call-start = ((), (), s32[]{:S(2)}) async-start(), calls=%async_computation.8 | async-start | bytes 1310720 | tf_op jit(solution)/shard_map/reduce_scatter | solution.py:188
  358.4 3.9 copy-start.9
Sparse Core Ops, SparseCore 0:
  9.5 42.8 all-gather.5
  54.4 91.2 all-gather.3
  147.7 84.0 all-gather.7
  364.8 23.2 reduce-scatter.1
where the time goes:
time: 397 us; the launch traced here: 395 us
  waiting for transfers between devices  131 us (33%)
  matrix products  68.8 us (17%)
  blocking collectives  62.5 us (16%)
  local copies, waits for them, and re-layouts  53.5 us (13%)
  other arithmetic  27.4 us (7%)
  loops' own time  22.3 us (6%)
  starting transfers between devices  16 us (4%)
  between operations  13.4 us (3%)
    all_gather x1, blocking collectives, on_device(): lax.all_gather(step_weight, 'seq', axis=0, tiled=True)  62.5 us
    all_gather x1, waiting for transfers between devices, on_device(): lax.all_gather(group_weight, 'seq', axis=0, tiled=True)  44.4 us
    all_to_all x1, waiting for transfers between devices, on_device(): lax.all_to_all(input_raw, 'seq', split_axis=1, concat_axis=0, tiled=True)  23.8 us
    reduce_scatter x1, waiting for transfers between devices, on_device(): lax.psum_scatter(jnp.dot(normed, flat_out, preferred_element_type=jnp.flo...  23.4 us
    another operation x2, loops' own time, ssd_group(): final_state, outputs = lax.scan(advance, start_state, blocked)  22.3 us
    all_gather x1, waiting for transfers between devices, on_device(): lax.all_gather(input_weight, 'seq', axis=0, tiled=True)  20.1 us
    slice x32, local copies, waits for them, and re-layouts, ssd_block(): cumulative[-1]  19.9 us
    dot_general x16, matrix products, ssd_block(): jnp.einsum('srp,sn->rpn', driven * remaining[:, :, None], block_b.astype(...  19.5 us
  transfers between devices with their start and end apart: 8, of which 6 were waited for; matrix products, arithmetic and copies ran while one was open for 36% of the time, Pallas kernels for 0%

commit v1 on v0

--- a/solution.py
+++ b/solution.py
@@ -1,6 +1,10 @@
+import functools
+
 import jax
 import jax.numpy as jnp
 from jax import lax
+from jax.experimental import pallas as pl
+from jax.experimental.pallas import tpu as pltpu
 from jax.sharding import PartitionSpec as P
 
 SPAN = 256
@@ -71,7 +75,7 @@
     return (final_state, outputs.reshape((row_total,) + outputs.shape[2:]))
 
 
-def on_device(
+def weights_travel(
     tokens,
     gate_weight,
     input_weight,
@@ -194,6 +198,376 @@
     return layer_out
 
 
+bf16 = jnp.bfloat16
+f32 = jnp.float32
+ROW_PAD = 16
+
+
+def matmul(left, right, dims=((1,), (0,))):
+    return lax.dot_general(left, right, (dims, ((), ())), preferred_element_type=f32)
+
+
+def softplus(value):
+    return jnp.maximum(value, 0.0) + jnp.log1p(jnp.exp(-jnp.abs(value)))
+
+
+def silu(value):
+    return value / (1.0 + jnp.exp(-value))
+
+
+def project_kernel(place, first, second, weight, raw_in, step_in, raw, step):
+    del place, raw_in, step_in
+    raw_width = raw.shape[1]
+
+    def emit(tok):
+        total = matmul(tok, weight[...])
+        raw[...] = total[:, :raw_width].astype(bf16)
+        step[...] = total[:, raw_width:]
+
+    @pl.when(pl.program_id(0) == 0)
+    def _():
+        emit(first[...])
+
+    @pl.when(pl.program_id(0) == 1)
+    def _():
+        emit(second[...])
+
+
+def project(place, first, second, weight, raw, step):
+    rows, depth = first.shape
+    whole = lambda i, place: (0, 0)
+    spot = lambda i, place: (place[i], 0)
+    width = raw.shape[1]
+    extra = step.shape[1]
+    return pl.pallas_call(
+        project_kernel,
+        grid_spec=pltpu.PrefetchScalarGridSpec(
+            num_scalar_prefetch=1,
+            grid=(2,),
+            in_specs=[
+                pl.BlockSpec((rows, depth), whole),
+                pl.BlockSpec((rows, depth), whole),
+                pl.BlockSpec(weight.shape, whole),
+                pl.BlockSpec(memory_space=pl.ANY),
+                pl.BlockSpec(memory_space=pl.ANY),
+            ],
+            out_specs=[pl.BlockSpec((rows, width), spot), pl.BlockSpec((rows, extra), spot)],
+        ),
+        out_shape=[
+            jax.ShapeDtypeStruct(raw.shape, raw.dtype),
+            jax.ShapeDtypeStruct(step.shape, step.dtype),
+        ],
+        input_output_aliases={4: 0, 5: 1},
+        compiler_params=pltpu.CompilerParams(vmem_limit_bytes=32 * 1024 * 1024),
+        cost_estimate=pl.CostEstimate(
+            flops=4 * rows * depth * (width + extra),
+            bytes_accessed=4 * rows * depth + 2 * weight.size,
+            transcendentals=0,
+        ),
+        name="project",
+    )(place, first, second, weight, raw, step)
+
+
+def scan_kernel(
+    head_size, raw, step, ids, table, bias, decay, skip, x_taps, x_shift, g_taps, g_shift,
+    out, state, x_ext, g_ext,
+):
+    rows, channels = step.shape
+    states = state.shape[1]
+    heads = channels // head_size
+    tap_count = x_taps.shape[0]
+    rim = x_ext.shape[0] - rows
+
+    @pl.when(pl.program_id(0) == 0)
+    def _():
+        state[...] = jnp.zeros_like(state)
+        x_ext[:rim] = jnp.zeros((rim, channels), f32)
+        g_ext[:rim] = jnp.zeros((rim, g_ext.shape[1]), f32)
+
+    @pl.when(pl.program_id(0) > 0)
+    def _():
+        x_ext[:rim] = x_ext[rows:]
+        g_ext[:rim] = g_ext[rows:]
+
+    x_ext[rim:] = raw[:, :channels].astype(f32)
+    g_ext[rim:] = raw[:, 2 * channels :].astype(f32)
+
+    def conv(ext, taps, shift):
+        first = rim - tap_count + 1
+        running = shift[...]
+        for tap in range(tap_count):
+            running = running + taps[tap : tap + 1] * ext[first + tap : first + tap + rows]
+        return silu(running).astype(bf16)
+
+    values = conv(x_ext, x_taps, x_shift).astype(f32)
+    groups = conv(g_ext, g_taps, g_shift)
+    b_rows, c_rows = groups[:, :states], groups[:, states:]
+
+    bucket = lax.broadcasted_iota(jnp.int32, (table.shape[0], rows), 0).astype(f32)
+    onehot = (bucket == ids[0]).astype(f32)
+    offsets = lax.dot_general(
+        onehot, table[...], (((0,), (0,)), ((), ())),
+        precision=highest, preferred_element_type=f32,
+    )
+    sizes = softplus(step[...] + bias[...] + offsets).astype(bf16).astype(f32)
+    rates = -decay[...] * sizes
+    row_at = lax.broadcasted_iota(jnp.int32, (rows, rows), 0)
+    col_at = lax.broadcasted_iota(jnp.int32, (rows, rows), 1)
+    causal = row_at >= col_at
+    lower = jnp.where(causal, 1.0, 0.0).astype(bf16)
+    coarse = rates.astype(bf16)
+    left = rates - coarse.astype(f32)
+    middle = left.astype(bf16)
+    fine = (left - middle.astype(f32)).astype(bf16)
+    cumulative = matmul(lower, coarse) + (matmul(lower, middle) + matmul(lower, fine))
+    across = jnp.transpose(cumulative)
+
+    scores = matmul(c_rows, b_rows, ((1,), (1,)))
+    driven = sizes * values
+    driven_low = driven.astype(bf16)
+    lane = lax.broadcasted_iota(jnp.int32, (rows, channels), 1)
+    within = jnp.zeros((rows, channels), f32)
+    for head in range(heads):
+        at = head * head_size
+        spread = cumulative[:, at : at + 1] - across[at : at + 1, :]
+        decays = jnp.exp(jnp.where(causal, spread, -1e30))
+        part = matmul((scores * decays).astype(bf16), driven_low)
+        within = jnp.where(lane >= at, part, within)
+    readout = matmul(c_rows, state[...].astype(bf16), ((1,), (1,)))
+    scanned = within + jnp.exp(cumulative) * readout + skip[...] * values
+    scanned = scanned.astype(bf16).astype(f32)
+    out[...] = (scanned * silu(raw[:, channels : 2 * channels].astype(f32))).astype(bf16)
+    last = cumulative[rows - 1 : rows, :]
+    remaining = jnp.exp(last - cumulative)
+    injected = matmul((driven * remaining).astype(bf16), b_rows, ((0,), (0,)))
+    state[...] = jnp.exp(across[:, rows - 1 : rows]) * state[...] + injected
+
+
+def scan(head_size, state_size, raw, step, ids, table, *params):
+    total, channels = step.shape
+    rows = ids.shape[2]
+    width = raw.shape[1]
+    rim = 8
+    block = lambda i: (i, 0)
+    whole = lambda i: (0, 0)
+    return pl.pallas_call(
+        functools.partial(scan_kernel, head_size),
+        grid=(total // rows,),
+        in_specs=[
+            pl.BlockSpec((rows, width), block),
+            pl.BlockSpec((rows, channels), block),
+            pl.BlockSpec((1, 1, rows), lambda i: (i, 0, 0)),
+            pl.BlockSpec(table.shape, whole),
+        ]
+        + [pl.BlockSpec(param.shape, whole) for param in params],
+        out_specs=pl.BlockSpec((rows, channels), block),
+        out_shape=jax.ShapeDtypeStruct((total, channels), bf16),
+        scratch_shapes=[
+            pltpu.VMEM((channels, state_size), f32),
+            pltpu.VMEM((rim + rows, channels), f32),
+            pltpu.VMEM((rim + rows, 2 * state_size), f32),
+        ],
+        compiler_params=pltpu.CompilerParams(vmem_limit_bytes=32 * 1024 * 1024),
+        cost_estimate=pl.CostEstimate(
+            flops=2 * total * rows * (state_size + 2 * channels),
+            bytes_accessed=4 * total * width,
+            transcendentals=4 * total * rows,
+        ),
+        name="scan",
+    )(raw, step, ids, table, *params)
+
+
+def close_kernel(gated, gain, weight, out):
+    pieces, _, width = gated.shape
+    square = jnp.zeros(gated.shape[1:], f32)
+    total = jnp.zeros(out.shape, f32)
+    parts = []
+    for piece in range(pieces):
+        part = gated[piece].astype(f32)
+        square = square + part * part
+        parts.append((part * gain[:, piece * width : (piece + 1) * width]).astype(bf16))
+    total = matmul(jnp.concatenate(parts, axis=1), weight[...])
+    mean = jnp.sum(square, axis=1, keepdims=True) * (1.0 / (pieces * width))
+    out[...] = (total * lax.rsqrt(mean + norm_epsilon)).astype(bf16)
+
+
+def close(gated, gain, weight):
+    pieces, rows, width = gated.shape
+    columns = 512
+    return pl.pallas_call(
+        close_kernel,
+        grid=(weight.shape[1] // columns,),
+        in_specs=[
+            pl.BlockSpec(gated.shape, lambda i: (0, 0, 0)),
+            pl.BlockSpec(gain.shape, lambda i: (0, 0)),
+            pl.BlockSpec((weight.shape[0], columns), lambda i: (0, i)),
+        ],
+        out_specs=pl.BlockSpec((rows, columns), lambda i: (0, i)),
+        out_shape=jax.ShapeDtypeStruct((rows, weight.shape[1]), bf16),
+        compiler_params=pltpu.CompilerParams(vmem_limit_bytes=32 * 1024 * 1024),
+        cost_estimate=pl.CostEstimate(
+            flops=2 * rows * weight.size, bytes_accessed=2 * weight.size, transcendentals=0
+        ),
+        name="close",
+    )(gated, gain, weight)
+
+
+def tokens_travel(
+    tokens,
+    gate_weight,
+    input_weight,
+    group_weight,
+    step_weight,
+    step_bias,
+    bucket_table,
+    bucket_ids,
+    decay_rate,
+    conv_input,
+    conv_input_bias,
+    conv_group,
+    conv_group_bias,
+    skip_gain,
+    norm_gain,
+    out_weight,
+):
+    rows, depth = tokens.shape
+    slab = gate_weight.shape[0]
+    heads_here = step_bias.shape[0]
+    head_size = gate_weight.shape[2]
+    state_size = group_weight.shape[3]
+    tap_count = conv_input.shape[0]
+    ring = lax.axis_size("seq")
+    seats = lax.axis_size("mp")
+    me = lax.axis_index("seq")
+    seat = lax.axis_index("mp")
+    core = seat % 2
+    channels = heads_here * head_size // ring
+    heads = channels // head_size
+    half = rows // 2
+    order = list(range(0, ring, 2)) + list(range(ring - 1, 0, -2))
+    onward = [(order[i], order[(i + 1) % ring]) for i in range(ring)]
+    backward = [(b, a) for a, b in onward]
+    swap_core = [(i, i ^ 1) for i in range(seats)]
+    position = [order.index(i) for i in range(ring)]
+    place_of = jnp.asarray(position, jnp.int32)[me]
+    source = lambda distance: jnp.asarray(order, jnp.int32)[(place_of + ring - distance) % ring]
+
+    pair = jnp.stack(
+        [input_weight.reshape(slab, ring, channels), gate_weight.reshape(slab, ring, channels)],
+        axis=2,
+    ).reshape(slab, ring, 2 * channels)
+    pair = lax.all_to_all(pair, "seq", split_axis=1, concat_axis=0, tiled=True)
+    pair = pair.reshape(ring * slab, 2 * channels)
+
+    lanes = 2 * state_size
+    step_rows = step_weight.size // lanes
+    id_rows = rows // lanes
+    pad_rows = -(step_rows + id_rows) % ROW_PAD
+    shared = jnp.concatenate(
+        [
+            group_weight.reshape(slab, lanes),
+            step_weight.reshape(step_rows, lanes),
+            bucket_ids.astype(bf16).reshape(id_rows, lanes),
+            jnp.zeros((pad_rows, lanes), bf16),
+        ],
+        axis=0,
+    )
+    mine = lax.dynamic_slice_in_dim(tokens, core * half, half, 0)
+    other = lax.dynamic_slice_in_dim(tokens, (1 - core) * half, half, 0)
+
+    gathered = jnp.zeros((ring,) + shared.shape, bf16)
+    gathered = lax.dynamic_update_slice_in_dim(gathered, shared[None], me, 0)
+    ahead = behind = shared
+    for distance in range(1, ring // 2 + 1):
+        ahead = lax.ppermute(ahead, "seq", onward)
+        gathered = lax.dynamic_update_slice_in_dim(gathered, ahead[None], source(distance), 0)
+        if distance < ring - distance:
+            behind = lax.ppermute(behind, "seq", backward)
+            gathered = lax.dynamic_update_slice_in_dim(
+                gathered, behind[None], source(ring - distance), 0
+            )
+    group_all = gathered[:, :slab].reshape(ring * slab, lanes)
+    step_all = gathered[:, slab : slab + step_rows].reshape(ring * slab, heads_here)
+    step_mine = lax.dynamic_slice_in_dim(step_all, me * heads, heads, 1)
+    step_wide = jnp.repeat(step_mine, head_size, axis=1)
+    ids = gathered[:, slab + step_rows : slab + step_rows + id_rows].reshape(ring, 1, rows)
+    weight = jnp.concatenate([pair, group_all, step_wide], axis=1)
+
+    raw = jnp.zeros((ring * rows, 2 * channels + lanes), bf16)
+    step = jnp.zeros((ring * rows, channels), f32)
+
+    def put(block, near, far, raw, step):
+        place = jnp.stack([2 * block + core, 2 * block + 1 - core]).astype(jnp.int32)
+        return project(place, near, far, weight, raw, step)
+
+    raw, step = put(me, mine, other, raw, step)
+    ahead = behind = mine
+    for distance in range(1, ring // 2 + 1):
+        ahead = lax.ppermute(ahead, "seq", onward)
+        far = lax.ppermute(ahead, "mp", swap_core)
+        raw, step = put(source(distance), ahead, far, raw, step)
+        if distance < ring - distance:
+            behind = lax.ppermute(behind, "seq", backward)
+            far = lax.ppermute(behind, "mp", swap_core)
+            raw, step = put(source(ring - distance), behind, far, raw, step)
+
+    def wide(per_head):
+        own = lax.dynamic_slice_in_dim(per_head, me * heads, heads, per_head.ndim - 1)
+        return jnp.repeat(own, head_size, axis=-1).reshape(-1, channels)
+
+    def own(per_channel):
+        flat = per_channel.reshape(-1, heads_here * head_size)
+        return lax.dynamic_slice_in_dim(flat, me * channels, channels, 1)
+
+    table = jnp.pad(wide(bucket_table), ((0, 8 - bucket_table.shape[0]), (0, 0)))
+    gated = scan(
+        head_size,
+        state_size,
+        raw,
+        step,
+        ids.astype(f32),
+        table,
+        wide(step_bias),
+        wide(decay_rate),
+        wide(skip_gain),
+        own(conv_input),
+        own(conv_input_bias),
+        conv_group.reshape(tap_count, lanes),
+        conv_group_bias.reshape(1, lanes),
+    )
+    gated = lax.all_to_all(
+        gated.reshape(ring, rows, channels), "seq", split_axis=0, concat_axis=0, tiled=True
+    )
+    partial = close(
+        gated, norm_gain.reshape(1, -1), out_weight.reshape(-1, out_weight.shape[2])
+    )
+    swap_chip = [(i, (i + 2) % seats) for i in range(seats)]
+    quarters = partial.reshape(seats // 2, 2, rows // seats, -1)
+    keep = lax.dynamic_index_in_dim(quarters, core, 1, False)
+    give = lax.dynamic_index_in_dim(quarters, 1 - core, 1, False)
+    both = (keep.astype(f32) + lax.ppermute(give, "mp", swap_core).astype(f32)).astype(bf16)
+    chip = seat // 2
+    keep = lax.dynamic_index_in_dim(both, chip, 0, False)
+    give = lax.dynamic_index_in_dim(both, 1 - chip, 0, False)
+    return (keep.astype(f32) + lax.ppermute(give, "mp", swap_chip).astype(f32)).astype(bf16)
+
+
+def on_device(*arrays):
+    tokens, gate_weight, group_weight = arrays[0], arrays[1], arrays[3]
+    ring = lax.axis_size("seq")
+    channels = gate_weight.shape[1] * gate_weight.shape[2] // ring
+    weights = 2 * gate_weight.size + group_weight.size + arrays[4].size
+    fits = (
+        tokens.size <= weights
+        and channels % 128 == 0
+        and channels % gate_weight.shape[2] == 0
+        and group_weight.shape[1] == 1
+        and lax.axis_size("mp") == 4
+        and ring % 2 == 0
+    )
+    return (tokens_travel if fits else weights_travel)(*arrays)
+
+
 def solution(mesh):
     placed = (
         P("seq", None),

time: 397 us -> 172 us (0.43)
  waiting for transfers between devices: 131 us -> 40.5 us
  matrix products: 68.8 us -> 0 us
  blocking collectives: 62.5 us -> 0 us
  Pallas kernels: 0 us -> 35.9 us
  local copies, waits for them, and re-layouts: 53.5 us -> 29.6 us
  loops' own time: 22.3 us -> 0 us
  other arithmetic: 27.4 us -> 7.49 us
  starting transfers between devices: 16 us -> 34.8 us
  between operations: 13.4 us -> 21.9 us
    dot_general x70 -> x0, matrix products: 68.8 us -> none  [the longest x16 19.5 us: ssd_block(): jnp.einsum('srp,sn->rpn', driven * remaining[:, :, None], block_b.astype(...]
    all_gather x3 -> x0, waiting for transfers between devices: 64.5 us -> none  [the longest x1 44.4 us: on_device(): lax.all_gather(group_weight, 'seq', axis=0, tiled=True)]
    all_gather x1 -> x0, blocking collectives: 62.5 us -> none  [on_device(): lax.all_gather(step_weight, 'seq', axis=0, tiled=True)]
    pallas_call x0 -> x10, Pallas kernels: none -> 35.9 us  [the longest x8 21.9 us: project(): pl.pallas_call(project_kernel, grid_spec=pltpu.PrefetchScalarGridSpec(num...]
    all_to_all x4 -> x2, waiting for transfers between devices: 40.7 us -> 15 us  [the longest x1 15 us: tokens_travel(): lax.all_to_all(gated.reshape(ring, rows, channels), 'seq', split_axis=0,...]
    ppermute x0 -> x23, waiting for transfers between devices: none -> 25.5 us  [the longest x8 16.8 us: tokens_travel(): ahead = lax.ppermute(ahead, 'seq', onward)]
    slice x50 -> x2, local copies, waits for them, and re-layouts: 27.1 us -> 3.11 us  [the longest x1 2.27 us: tokens_travel(): group_all = gathered[:, :slab].reshape(ring * slab, lanes)]
    reduce_scatter x1 -> x0, waiting for transfers between devices: 23.4 us -> none  [on_device(): lax.psum_scatter(jnp.dot(normed, flat_out, preferred_element_type=jnp.flo...]
  transfers between devices with their start and end apart: 8 -> 25, of which waited for: 6 -> 8; matrix products, arithmetic and copies ran while one was open for 36% -> 18% of each run, Pallas kernels for 0% -> 11%
where the time goes in v1:
time: 172 us; the launch traced here: 170 us
  waiting for transfers between devices  40.5 us (24%)
  Pallas kernels  35.9 us (21%)
  starting transfers between devices  34.8 us (20%)
  local copies, waits for them, and re-layouts  29.6 us (17%)
  between operations  21.9 us (13%)
  other arithmetic  7.49 us (4%)
    pallas_call x8, Pallas kernels, project(): pl.pallas_call(project_kernel, grid_spec=pltpu.PrefetchScalarGridSpec(num...  21.9 us
    ppermute x8, starting transfers between devices, tokens_travel(): ahead = lax.ppermute(ahead, 'seq', onward)  17 us
    ppermute x8, waiting for transfers between devices, tokens_travel(): ahead = lax.ppermute(ahead, 'seq', onward)  16.8 us
    all_to_all x1, waiting for transfers between devices, tokens_travel(): lax.all_to_all(gated.reshape(ring, rows, channels), 'seq', split_axis=0,...  15 us
    pallas_call x1, Pallas kernels, scan(): pl.pallas_call(functools.partial(scan_kernel, head_size), grid=(total //...  11.7 us
    ppermute x1, waiting for transfers between devices, tokens_travel(): lax.ppermute(give, 'mp', swap_chip).astype(f32)  6.83 us
    all_to_all x1, starting transfers between devices, tokens_travel(): pair = lax.all_to_all(pair, 'seq', split_axis=1, concat_axis=0, tiled=True)  6.38 us
    all_to_all x1, starting transfers between devices, tokens_travel(): lax.all_to_all(gated.reshape(ring, rows, channels), 'seq', split_axis=0,...  5.98 us
  transfers between devices with their start and end apart: 25, of which 8 were waited for; matrix products, arithmetic and copies ran while one was open for 18% of the time, Pallas kernels for 11%

profile of v1, /device:TPU:0, one launch (start us, length us, event | category | flops | bytes accessed | tf_op | source)
XLA Modules:
  0.0 170.2 jit_solution(9967269165755266739)
XLA Ops:
  0.0 0.9 copy.61
  0.9 0.8 copy.52
  1.9 0.7 convert_element_type.32
  2.7 0.8 maximum_maximum_fusion
  3.4 3.0 %collective-permute-start.5 = (bf16[288,256]{1,0:T(8,128)(2,1)}, bf16[288,256]{1,0:T(8,128)(2,1)}, u32[]{:S(2)}, u32[]{:S(2)}) collective-permute-start(bf16[288,256]{1,0:T(8,128)(2,1)} %maximum_maximum_fusion), channel_id=1, source_target_pairs={{0,8},{8,16},{16,24},{24,28},{28,20},{20,12},{12,4},{4,0},{1,9},{9... | collective-permute-start | bytes 442376 | tf_op jit(solution)/shard_map/ppermute | solution.py:482
  6.5 1.3 constant_dynamic-slice_fusion.3
  7.7 2.1 %collective-permute-start = (bf16[128,2048]{1,0:T(8,128)(2,1)S(1)}, bf16[128,2048]{1,0:T(8,128)(2,1)S(1)}, u32[]{:S(2)}, u32[]{:S(2)}) collective-permute-start(bf16[128,2048]{1,0:T(8,128)(2,1)S(1)} %get-tuple-element.38.first), channel_id=1, source_target_pairs={{0,8},{8,16},{16,24},{24,28},{28,20},{20,12},{12,4},{4,0},{1,9},{9... | collective-permute-start | bytes 1572872 | tf_op jit(solution)/shard_map/ppermute | solution.py:506
  9.8 1.1 pad_maximum_fusion.1
  10.9 2.5 %copy.51 = bf16[256,8,2,128]{3,2,0,1:T(2,128)(2,1)S(1)} copy(bf16[256,8,2,128]{0,3,1,2:T(8,128)(2,1)} %pad_maximum_fusion.1) | data formatting | bytes 2097152 | tf_op jit(solution)/shard_map/stack | solution.py:455
  13.4 1.5 reshape.84
  14.9 6.4 %all-to-all-start = ((bf16[256,8,256]{2,0,1:T(8,128)(2,1)}), bf16[256,8,256]{2,0,1:T(8,128)(2,1)}, u32[]{:S(2)}, u32[]{:S(2)}) async-start(bf16[256,8,256]{2,0,1:T(8,128)(2,1)} %reshape.84), calls=%async_computation | async-start | bytes 2097152 | tf_op jit(solution)/shard_map/all_to_all | solution.py:459
  21.3 0.7 dynamic_slice.86
  26.5 0.7 fusion.2
  32.2 1.1 broadcast_in_dim.51
  33.3 0.8 bitcast_dynamic-update-slice_fusion.7
  47.9 2.0 %collective-permute-start.7 = (bf16[288,256]{1,0:T(8,128)(2,1)}, bf16[288,256]{1,0:T(8,128)(2,1)S(1)}, u32[]{:S(2)}, u32[]{:S(2)}) collective-permute-start(bf16[288,256]{1,0:T(8,128)(2,1)} %collective-permute-done.5), channel_id=1, source_target_pairs={{0,8},{8,16},{16,24},{24,28},{28,20},{20,12},{12,4},{4,0},{1,9},{9... | collective-permute-start | bytes 442376 | tf_op jit(solution)/shard_map/ppermute | solution.py:482
  50.0 1.9 %collective-permute-start.1 = (bf16[128,2048]{1,0:T(8,128)(2,1)S(1)}, bf16[128,2048]{1,0:T(8,128)(2,1)S(1)}, u32[]{:S(2)}, u32[]{:S(2)}) collective-permute-start(bf16[128,2048]{1,0:T(8,128)(2,1)S(1)} %collective-permute-done.first), channel_id=1, source_target_pairs={{0,8},{8,16},{16,24},{24,28},{28,20},{20,12},{12,4},{4,0},{1,9},{9... | collective-permute-start | bytes 1572872 | tf_op jit(solution)/shard_map/ppermute | solution.py:506
  51.9 1.6 bitcast_dynamic-update-slice_fusion.6
  53.5 0.7 bitcast_dynamic-update-slice_fusion.5
  54.2 0.7 collective-permute-done.7
  54.9 2.0 %collective-permute-start.9 = (bf16[288,256]{1,0:T(8,128)(2,1)S(1)}, bf16[288,256]{1,0:T(8,128)(2,1)S(1)}, u32[]{:S(2)}, u32[]{:S(2)}) collective-permute-start(bf16[288,256]{1,0:T(8,128)(2,1)S(1)} %collective-permute-done.7), channel_id=1, source_target_pairs={{0,8},{8,16},{16,24},{24,28},{28,20},{20,12},{12,4},{4,0},{1,9},{9... | collective-permute-start | bytes 442376 | tf_op jit(solution)/shard_map/ppermute | solution.py:482
  56.9 0.7 bitcast_dynamic-update-slice_fusion.4
  57.6 2.0 %collective-permute-start.13 = (bf16[128,2048]{1,0:T(8,128)(2,1)S(1)}, bf16[128,2048]{1,0:T(8,128)(2,1)}, u32[]{:S(2)}, u32[]{:S(2)}) collective-permute-start(bf16[128,2048]{1,0:T(8,128)(2,1)S(1)} %collective-permute-done.12.first), channel_id=1, source_target_pairs={{8,0},{16,8},{24,16},{28,24},{20,28},{12,20},{4,12},{0,4},{9,1},{1... | collective-permute-start | bytes 1572872 | tf_op jit(solution)/shard_map/ppermute | solution.py:510
  59.6 6.5 %collective-permute-done.1.first = bf16[128,2048]{1,0:T(8,128)(2,1)S(1)} collective-permute-done((bf16[128,2048]{1,0:T(8,128)(2,1)S(1)}, bf16[128,2048]{1,0:T(8,128)(2,1)S(1)}, u32[]{:S(2)}, u32[]{:S(2)}) %collective-permute-start.1) | collective-permute-done | bytes 524320 | tf_op jit(solution)/shard_map/ppermute | solution.py:506
  66.1 2.0 %collective-permute-start.2 = (bf16[128,2048]{1,0:T(8,128)(2,1)S(1)}, bf16[128,2048]{1,0:T(8,128)(2,1)S(1)}, u32[]{:S(2)}, u32[]{:S(2)}) collective-permute-start(bf16[128,2048]{1,0:T(8,128)(2,1)S(1)} %collective-permute-done.1.first), channel_id=1, source_target_pairs={{0,8},{8,16},{16,24},{24,28},{28,20},{20,12},{12,4},{4,0},{1,9},{9... | collective-permute-start | bytes 1572872 | tf_op jit(solution)/shard_map/ppermute | solution.py:506
  68.1 0.7 bitcast_dynamic-update-slice_fusion.3
  68.8 0.5 collective-permute-done.9
  69.3 2.0 %collective-permute-start.11 = (bf16[288,256]{1,0:T(8,128)(2,1)S(1)}, bf16[288,256]{1,0:T(8,128)(2,1)S(1)}, u32[]{:S(2)}, u32[]{:S(2)}) collective-permute-start(bf16[288,256]{1,0:T(8,128)(2,1)S(1)} %collective-permute-done.9), channel_id=1, source_target_pairs={{0,8},{8,16},{16,24},{24,28},{28,20},{20,12},{12,4},{4,0},{1,9},{9... | collective-permute-start | bytes 442376 | tf_op jit(solution)/shard_map/ppermute | solution.py:482
  71.3 0.7 bitcast_dynamic-update-slice_fusion.2
  72.0 0.7 bitcast_dynamic-update-slice_fusion.1
  72.6 0.5 collective-permute-start.19
  73.2 7.8 %collective-permute-done.2.first = bf16[128,2048]{1,0:T(8,128)(2,1)S(1)} collective-permute-done((bf16[128,2048]{1,0:T(8,128)(2,1)S(1)}, bf16[128,2048]{1,0:T(8,128)(2,1)S(1)}, u32[]{:S(2)}, u32[]{:S(2)}) %collective-permute-start.2) | collective-permute-done | bytes 524320 | tf_op jit(solution)/shard_map/ppermute | solution.py:506
  81.0 2.0 %collective-permute-start.3 = (bf16[128,2048]{1,0:T(8,128)(2,1)S(1)}, bf16[128,2048]{1,0:T(8,128)(2,1)}, u32[]{:S(2)}, u32[]{:S(2)}) collective-permute-start(bf16[128,2048]{1,0:T(8,128)(2,1)S(1)} %collective-permute-done.2.first), channel_id=1, source_target_pairs={{0,8},{8,16},{16,24},{24,28},{28,20},{20,12},{12,4},{4,0},{1,9},{9... | collective-permute-start | bytes 1572872 | tf_op jit(solution)/shard_map/ppermute | solution.py:506
  83.0 1.2 collective-permute-done.11
  84.2 0.7 bitcast_dynamic-update-slice_fusion
  84.8 0.8 slice.13
  85.7 1.2 reshape.90
  86.9 2.1 %constant_dynamic-slice_fusion.4 = bf16[2048,2]{1,0:T(8,128)(2,1)} fusion(bf16[2048,16]{1,0:T(8,128)(2,1)} %reshape.90, s32[]{:T(128)S(6)} %select_n.161), kind=kLoop, calls=%fused_computation.23 | loop fusion | bytes 16388 | tf_op jit(solution)/shard_map/dynamic_slice | solution.py:491
  89.0 0.8 slice_convert_fusion.ids
  89.7 2.3 %slice.12 = bf16[8,256,256]{2,1,0:T(8,128)(2,1)} slice(bf16[8,288,256]{2,1,0:T(8,128)(2,1)} %bitcast_dynamic-update-slice_fusion), slice={[0:8], [0:256], [0:256]} | slice | bytes 2097152 | tf_op jit(solution)/shard_map/slice | solution.py:489
  92.0 1.2 copy.53
  93.3 0.9 broadcast_in_dim.61
  94.2 2.0 %copy.54 = bf16[2048,128]{1,0:T(8,128)(2,1)} copy(bf16[2048,128]{0,1:T(8,128)(2,1)} %bitcast.96) | data formatting | bytes 1048576 | tf_op jit(solution)/shard_map/reshape | solution.py:492
  96.2 0.5 collective-permute-start.17
  96.8 0.4 collective-permute-start.15
  97.3 1.9 %pad_maximum_fusion.weight = bf16[2048,640]{1,0:T(8,128)(2,1)S(1)} fusion(bf16[2048,128]{1,0:T(8,128)(2,1)} %copy.54, bf16[2048,256]{1,0:T(8,128)(2,1)} %bitcast.95, bf16[2048,256]{1,0:T(8,128)(2,1)} %bitcast.8), kind=kLoop, calls=%fused_computation | loop fusion | flops 7864320 | bytes 5242880 | tf_op jit(solution)/shard_map/concatenate | solution.py:494
  99.3 0.1 broadcast_in_dim.62.raw_in
  99.5 1.8 %project.8 = (bf16[2048,512]{1,0:T(8,128)(2,1)S(1)}, f32[2048,128]{1,0:T(8,128)S(1)}) custom-call(s32[2]{0:T(128)S(1)} %pad_add_fusion.7.place, bf16[128,2048]{1,0:T(8,128)(2,1)S(1)} %get-tuple-element.38.first, bf16[128,2048]{1,0:T(8,128)(2,1)S(1)} %get-tuple-element.37.second, ...), custom_call_target="tpu_custom_call", output_to_operand_aliasing={{0}: (4, {}), {1}: (5, {})} | custom-call | flops 671088640 | bytes 3670016 | tf_op jit(solution)/shard_map/project/pallas_call | solution.py:242
  101.3 2.8 %project.9 = (bf16[2048,512]{1,0:T(8,128)(2,1)S(1)}, f32[2048,128]{1,0:T(8,128)S(1)}) custom-call(s32[2]{0:T(128)S(1)} %pad_add_fusion.6.place, bf16[128,2048]{1,0:T(8,128)(2,1)S(1)} %collective-permute-done.first, bf16[128,2048]{1,0:T(8,128)(2,1)} %collective-permute-done.20.second, ...), custom_call_target="tpu_custom_call", output_to_operand_aliasing={{0}: (4, {}), {1}: (5, {})} | custom-call | flops 671088640 | bytes 3670016 | tf_op jit(solution)/shard_map/project/pallas_call | solution.py:242
  104.1 2.8 %project.10 = (bf16[2048,512]{1,0:T(8,128)(2,1)S(1)}, f32[2048,128]{1,0:T(8,128)S(1)}) custom-call(s32[2]{0:T(128)S(1)} %pad_add_fusion.5.place, bf16[128,2048]{1,0:T(8,128)(2,1)S(1)} %collective-permute-done.12.first, bf16[128,2048]{1,0:T(8,128)(2,1)} %collective-permute-done.19.second, ...), custom_call_target="tpu_custom_call", output_to_operand_aliasing={{0}: (4, {}), {1}: (5, {})} | custom-call | flops 671088640 | bytes 3670016 | tf_op jit(solution)/shard_map/project/pallas_call | solution.py:242
  106.9 2.8 %project.11 = (bf16[2048,512]{1,0:T(8,128)(2,1)S(1)}, f32[2048,128]{1,0:T(8,128)S(1)}) custom-call(s32[2]{0:T(128)S(1)} %pad_add_fusion.4.place, bf16[128,2048]{1,0:T(8,128)(2,1)S(1)} %collective-permute-done.1.first, bf16[128,2048]{1,0:T(8,128)(2,1)} %collective-permute-done.18.second, ...), custom_call_target="tpu_custom_call", output_to_operand_aliasing={{0}: (4, {}), {1}: (5, {})} | custom-call | flops 671088640 | bytes 3670016 | tf_op jit(solution)/shard_map/project/pallas_call | solution.py:242
  109.8 3.0 %project.12 = (bf16[2048,512]{1,0:T(8,128)(2,1)S(1)}, f32[2048,128]{1,0:T(8,128)S(1)}) custom-call(s32[2]{0:T(128)S(1)} %pad_add_fusion.3.place, bf16[128,2048]{1,0:T(8,128)(2,1)} %collective-permute-done.13.first, bf16[128,2048]{1,0:T(8,128)(2,1)} %collective-permute-done.17.second, ...), custom_call_target="tpu_custom_call", output_to_operand_aliasing={{0}: (4, {}), {1}: (5, {})} | custom-call | flops 671088640 | bytes 3670016 | tf_op jit(solution)/shard_map/project/pallas_call | solution.py:242
  112.7 2.8 %project.13 = (bf16[2048,512]{1,0:T(8,128)(2,1)S(1)}, f32[2048,128]{1,0:T(8,128)S(1)}) custom-call(s32[2]{0:T(128)S(1)} %pad_add_fusion.2.place, bf16[128,2048]{1,0:T(8,128)(2,1)S(1)} %collective-permute-done.2.first, bf16[128,2048]{1,0:T(8,128)(2,1)} %collective-permute-done.16.second, ...), custom_call_target="tpu_custom_call", output_to_operand_aliasing={{0}: (4, {}), {1}: (5, {})} | custom-call | flops 671088640 | bytes 3670016 | tf_op jit(solution)/shard_map/project/pallas_call | solution.py:242
  115.6 3.0 %project.14 = (bf16[2048,512]{1,0:T(8,128)(2,1)S(1)}, f32[2048,128]{1,0:T(8,128)S(1)}) custom-call(s32[2]{0:T(128)S(1)} %pad_add_fusion.1.place, bf16[128,2048]{1,0:T(8,128)(2,1)} %collective-permute-done.14.first, bf16[128,2048]{1,0:T(8,128)(2,1)} %collective-permute-done.15.second, ...), custom_call_target="tpu_custom_call", output_to_operand_aliasing={{0}: (4, {}), {1}: (5, {})} | custom-call | flops 671088640 | bytes 3670016 | tf_op jit(solution)/shard_map/project/pallas_call | solution.py:242
  118.6 3.0 %project.15 = (bf16[2048,512]{1,0:T(8,128)(2,1)S(1)}, f32[2048,128]{1,0:T(8,128)S(1)}) custom-call(s32[2]{0:T(128)S(1)} %pad_add_fusion.place, bf16[128,2048]{1,0:T(8,128)(2,1)} %collective-permute-done.3.first, bf16[128,2048]{1,0:T(8,128)(2,1)} %collective-permute-done.4.second, ...), custom_call_target="tpu_custom_call", output_to_operand_aliasing={{0}: (4, {}), {1}: (5, {})} | custom-call | flops 671088640 | bytes 3670016 | tf_op jit(solution)/shard_map/project/pallas_call | solution.py:242
  121.6 11.7 %scan.1 = bf16[2048,128]{1,0:T(8,128)(2,1)} custom-call(bf16[2048,512]{1,0:T(8,128)(2,1)S(1)} %get-tuple-element.35.raw, f32[2048,128]{1,0:T(8,128)S(1)} %get-tuple-element.36.step, f32[8,1,256]{2,1,0:T(1,128)S(1)} %slice_convert_fusion.ids, f32[8,128]{1,0:T(8,128)S(1)} %pad.4.table, f32[1,128]{1,0:T(1,128)S(1)} %reshape_reshape.9.bias, ...), custom_call_target="tpu_custom_call" | custom-call | flops 402653184 | bytes 4194304 | tf_op jit(solution)/shard_map/scan/pallas_call | solution.py:353
  133.3 6.0 %all-to-all-start.1 = ((bf16[8,256,128]{2,1,0:T(8,128)(2,1)}), bf16[8,256,128]{2,1,0:T(8,128)(2,1)S(1)}, u32[]{:S(2)}, u32[]{:S(2)}) async-start(bf16[8,256,128]{2,1,0:T(8,128)(2,1)} %bitcast.53), calls=%async_computation.1 | async-start | bytes 1048576 | tf_op jit(solution)/shard_map/all_to_all | solution.py:538
  139.3 15.0 %all-to-all-done.1.gated = bf16[8,256,128]{2,1,0:T(8,128)(2,1)S(1)} async-done(((bf16[8,256,128]{2,1,0:T(8,128)(2,1)}), bf16[8,256,128]{2,1,0:T(8,128)(2,1)S(1)}, u32[]{:S(2)}, u32[]{:S(2)}) %all-to-all-start.1) | async-done | bytes 524320 | tf_op jit(solution)/shard_map/all_to_all | solution.py:538
  154.3 2.2 %copy-done.1 = bf16[16,64,2048]{2,1,0:T(8,128)(2,1)S(1)} copy-done((bf16[16,64,2048]{2,1,0:T(8,128)(2,1)S(1)}, bf16[16,64,2048]{2,1,0:T(8,128)(2,1)}, u32[]{:S(2)}) %copy-start.1) | copy-done | bytes 4194328
  156.5 2.3 %close.1 = bf16[256,2048]{1,0:T(8,128)(2,1)S(1)} custom-call(bf16[8,256,128]{2,1,0:T(8,128)(2,1)S(1)} %all-to-all-done.1.gated, f32[1,1024]{1,0:T(1,128)S(1)} %reshape.98.gain, bf16[1024,2048]{1,0:T(8,128)(2,1)S(1)} %bitcast.92), custom_call_target="tpu_custom_call" | custom-call | flops 1073741824 | bytes 4194304 | tf_op jit(solution)/shard_map/close/pallas_call | solution.py:397
  159.0 1.9 %collective-permute-done.21 = bf16[2,64,2048]{2,1,0:T(8,128)(2,1)S(1)} collective-permute-done((bf16[2,64,2048]{2,1,0:T(8,128)(2,1)S(1)}, bf16[2,64,2048]{2,1,0:T(8,128)(2,1)S(1)}, u32[]{:S(2)}, u32[]{:S(2)}) %collective-permute-start.21) | collective-permute-done | bytes 524320 | tf_op jit(solution)/shard_map/ppermute | solution.py:548
  161.0 1.6 collective-permute-start.22
  162.6 6.8 %collective-permute-done.22 = bf16[64,2048]{1,0:T(8,128)(2,1)S(1)} collective-permute-done((bf16[64,2048]{1,0:T(8,128)(2,1)S(1)}, bf16[64,2048]{1,0:T(8,128)(2,1)S(1)}, u32[]{:S(2)}, u32[]{:S(2)}) %collective-permute-start.22) | collective-permute-done | bytes 262176 | tf_op jit(solution)/shard_map/ppermute | solution.py:552
  169.4 0.8 fusion.1
  (89 shorter events, 2.8 us)
Async XLA Ops:
  0.0 32.1 %copy-start = (f32[4,16]{1,0:T(4,128)S(1)}, f32[4,16]{1,0:T(4,128)}, u32[]{:S(2)}) copy-start(f32[4,16]{1,0:T(4,128)} %param.37) | copy-start | bytes 772
  2.7 7.2 %copy-start.3 = (bf16[256,16,64]{0,2,1:T(8,128)(2,1)S(1)}, bf16[256,16,64]{0,2,1:T(8,128)(2,1)}, u32[]{:S(2)}) copy-start(bf16[256,16,64]{0,2,1:T(8,128)(2,1)} %param.32) | copy-start | bytes 1572868
  2.7 7.2 %copy-start.4 = (bf16[256,16,64]{0,2,1:T(8,128)(2,1)S(1)}, bf16[256,16,64]{0,2,1:T(8,128)(2,1)}, u32[]{:S(2)}) copy-start(bf16[256,16,64]{0,2,1:T(8,128)(2,1)} %param.33) | copy-start | bytes 1572868
  3.4 44.4 %collective-permute-start.5 = (bf16[288,256]{1,0:T(8,128)(2,1)}, bf16[288,256]{1,0:T(8,128)(2,1)}, u32[]{:S(2)}, u32[]{:S(2)}) collective-permute-start(bf16[288,256]{1,0:T(8,128)(2,1)} %maximum_maximum_fusion), channel_id=1, source_target_pairs={{0,8},{8,16},{16,24},{24,28},{28,20},{20,12},{12,4},{4,0},{1,9},{9... | collective-permute-start | bytes 442376 | tf_op jit(solution)/shard_map/ppermute | solution.py:482
  6.5 43.4 %collective-permute-start.6 = (bf16[288,256]{1,0:T(8,128)(2,1)}, bf16[288,256]{1,0:T(8,128)(2,1)S(1)}, u32[]{:S(2)}, u32[]{:S(2)}) collective-permute-start(bf16[288,256]{1,0:T(8,128)(2,1)} %maximum_maximum_fusion), channel_id=1, source_target_pairs={{8,0},{16,8},{24,16},{28,24},{20,28},{12,20},{4,12},{0,4},{9,1},{1... | collective-permute-start | bytes 442376 | tf_op jit(solution)/shard_map/ppermute | solution.py:485
  7.7 42.3 %collective-permute-start = (bf16[128,2048]{1,0:T(8,128)(2,1)S(1)}, bf16[128,2048]{1,0:T(8,128)(2,1)S(1)}, u32[]{:S(2)}, u32[]{:S(2)}) collective-permute-start(bf16[128,2048]{1,0:T(8,128)(2,1)S(1)} %get-tuple-element.38.first), channel_id=1, source_target_pairs={{0,8},{8,16},{16,24},{24,28},{28,20},{20,12},{12,4},{4,0},{1,9},{9... | collective-permute-start | bytes 1572872 | tf_op jit(solution)/shard_map/ppermute | solution.py:506
  9.8 47.8 %collective-permute-start.12 = (bf16[128,2048]{1,0:T(8,128)(2,1)S(1)}, bf16[128,2048]{1,0:T(8,128)(2,1)S(1)}, u32[]{:S(2)}, u32[]{:S(2)}) collective-permute-start(bf16[128,2048]{1,0:T(8,128)(2,1)S(1)} %get-tuple-element.38.first), channel_id=1, source_target_pairs={{8,0},{16,8},{24,16},{28,24},{20,28},{12,20},{4,12},{0,4},{9,1},{1... | collective-permute-start | bytes 1572872 | tf_op jit(solution)/shard_map/ppermute | solution.py:510
  14.9 6.4 %copy-start.13 = (s32[8]{0:T(128)S(1)}, s32[8]{0:T(128)}, u32[]{:S(2)}) copy-start(s32[8]{0:T(128)} %constant.157.clone) | copy-start | bytes 100
  14.9 11.6 %copy-start.6 = (s32[8]{0:T(128)S(1)}, s32[8]{0:T(128)}, u32[]{:S(2)}) copy-start(s32[8]{0:T(128)} %constant.158.clone) | copy-start | bytes 100
  14.9 16.6 %copy-start.7 = (f32[16,64]{1,0:T(8,128)S(1)}, f32[16,64]{1,0:T(8,128)}, u32[]{:S(2)}) copy-start(f32[16,64]{1,0:T(8,128)} %param.41) | copy-start | bytes 12292
  14.9 82.5 %all-to-all-start = ((bf16[256,8,256]{2,0,1:T(8,128)(2,1)}), bf16[256,8,256]{2,0,1:T(8,128)(2,1)}, u32[]{:S(2)}, u32[]{:S(2)}) async-start(bf16[256,8,256]{2,0,1:T(8,128)(2,1)} %reshape.84), calls=%async_computation | async-start | bytes 2097152 | tf_op jit(solution)/shard_map/all_to_all | solution.py:459
  21.3 21.5 %copy-start.10 = (f32[16]{0:T(128)S(1)}, f32[16]{0:T(128)}, u32[]{:S(2)}) copy-start(f32[16]{0:T(128)} %param.39) | copy-start | bytes 196
  21.3 21.7 %copy-start.11 = (f32[16]{0:T(128)S(1)}, f32[16]{0:T(128)}, u32[]{:S(2)}) copy-start(f32[16]{0:T(128)} %param.44) | copy-start | bytes 196
  21.3 22.0 %copy-start.12 = (f32[16]{0:T(128)S(1)}, f32[16]{0:T(128)}, u32[]{:S(2)}) copy-start(f32[16]{0:T(128)} %param.36) | copy-start | bytes 196
  21.3 22.2 %copy-start.5 = (f32[4,16,64]{2,1,0:T(8,128)S(1)}, f32[4,16,64]{2,1,0:T(8,128)}, u32[]{:S(2)}) copy-start(f32[4,16,64]{2,1,0:T(8,128)} %param.40) | copy-start | bytes 49156
  21.3 22.3 %copy-start.9 = (f32[4,1,2,128]{3,2,1,0:T(2,128)S(1)}, f32[4,1,2,128]{3,2,1,0:T(2,128)}, u32[]{:S(2)}) copy-start(f32[4,1,2,128]{3,2,1,0:T(2,128)} %param.42) | copy-start | bytes 12292
  47.9 7.1 %collective-permute-start.7 = (bf16[288,256]{1,0:T(8,128)(2,1)}, bf16[288,256]{1,0:T(8,128)(2,1)S(1)}, u32[]{:S(2)}, u32[]{:S(2)}) collective-permute-start(bf16[288,256]{1,0:T(8,128)(2,1)} %collective-permute-done.5), channel_id=1, source_target_pairs={{0,8},{8,16},{16,24},{24,28},{28,20},{20,12},{12,4},{4,0},{1,9},{9... | collective-permute-start | bytes 442376 | tf_op jit(solution)/shard_map/ppermute | solution.py:482
  49.9 7.0 %collective-permute-start.8 = (bf16[288,256]{1,0:T(8,128)(2,1)S(1)}, bf16[288,256]{1,0:T(8,128)(2,1)S(1)}, u32[]{:S(2)}, u32[]{:S(2)}) collective-permute-start(bf16[288,256]{1,0:T(8,128)(2,1)S(1)} %collective-permute-done.6), channel_id=1, source_target_pairs={{8,0},{16,8},{24,16},{28,24},{20,28},{12,20},{4,12},{0,4},{9,1},{1... | collective-permute-start | bytes 442376 | tf_op jit(solution)/shard_map/ppermute | solution.py:485
  50.0 16.2 %collective-permute-start.1 = (bf16[128,2048]{1,0:T(8,128)(2,1)S(1)}, bf16[128,2048]{1,0:T(8,128)(2,1)S(1)}, u32[]{:S(2)}, u32[]{:S(2)}) collective-permute-start(bf16[128,2048]{1,0:T(8,128)(2,1)S(1)} %collective-permute-done.first), channel_id=1, source_target_pairs={{0,8},{8,16},{16,24},{24,28},{28,20},{20,12},{12,4},{4,0},{1,9},{9... | collective-permute-start | bytes 1572872 | tf_op jit(solution)/shard_map/ppermute | solution.py:506
  54.9 14.4 %collective-permute-start.9 = (bf16[288,256]{1,0:T(8,128)(2,1)S(1)}, bf16[288,256]{1,0:T(8,128)(2,1)S(1)}, u32[]{:S(2)}, u32[]{:S(2)}) collective-permute-start(bf16[288,256]{1,0:T(8,128)(2,1)S(1)} %collective-permute-done.7), channel_id=1, source_target_pairs={{0,8},{8,16},{16,24},{24,28},{28,20},{20,12},{12,4},{4,0},{1,9},{9... | collective-permute-start | bytes 442376 | tf_op jit(solution)/shard_map/ppermute | solution.py:482
  56.9 15.1 %collective-permute-start.10 = (bf16[288,256]{1,0:T(8,128)(2,1)S(1)}, bf16[288,256]{1,0:T(8,128)(2,1)S(1)}, u32[]{:S(2)}, u32[]{:S(2)}) collective-permute-start(bf16[288,256]{1,0:T(8,128)(2,1)S(1)} %collective-permute-done.8), channel_id=1, source_target_pairs={{8,0},{16,8},{24,16},{28,24},{20,28},{12,20},{4,12},{0,4},{9,1},{1... | collective-permute-start | bytes 442376 | tf_op jit(solution)/shard_map/ppermute | solution.py:485
  57.6 15.5 %collective-permute-start.13 = (bf16[128,2048]{1,0:T(8,128)(2,1)S(1)}, bf16[128,2048]{1,0:T(8,128)(2,1)}, u32[]{:S(2)}, u32[]{:S(2)}) collective-permute-start(bf16[128,2048]{1,0:T(8,128)(2,1)S(1)} %collective-permute-done.12.first), channel_id=1, source_target_pairs={{8,0},{16,8},{24,16},{28,24},{20,28},{12,20},{4,12},{0,4},{9,1},{1... | collective-permute-start | bytes 1572872 | tf_op jit(solution)/shard_map/ppermute | solution.py:510
  66.1 14.9 %collective-permute-start.2 = (bf16[128,2048]{1,0:T(8,128)(2,1)S(1)}, bf16[128,2048]{1,0:T(8,128)(2,1)S(1)}, u32[]{:S(2)}, u32[]{:S(2)}) collective-permute-start(bf16[128,2048]{1,0:T(8,128)(2,1)S(1)} %collective-permute-done.1.first), channel_id=1, source_target_pairs={{0,8},{8,16},{16,24},{24,28},{28,20},{20,12},{12,4},{4,0},{1,9},{9... | collective-permute-start | bytes 1572872 | tf_op jit(solution)/shard_map/ppermute | solution.py:506
  69.3 14.9 %collective-permute-start.11 = (bf16[288,256]{1,0:T(8,128)(2,1)S(1)}, bf16[288,256]{1,0:T(8,128)(2,1)S(1)}, u32[]{:S(2)}, u32[]{:S(2)}) collective-permute-start(bf16[288,256]{1,0:T(8,128)(2,1)S(1)} %collective-permute-done.9), channel_id=1, source_target_pairs={{0,8},{8,16},{16,24},{24,28},{28,20},{20,12},{12,4},{4,0},{1,9},{9... | collective-permute-start | bytes 442376 | tf_op jit(solution)/shard_map/ppermute | solution.py:482
  72.6 23.6 %collective-permute-start.20 = (bf16[128,2048]{1,0:T(8,128)(2,1)S(1)}, bf16[128,2048]{1,0:T(8,128)(2,1)}, u32[]{:S(2)}, u32[]{:S(2)}) collective-permute-start(bf16[128,2048]{1,0:T(8,128)(2,1)S(1)} %collective-permute-done.first), channel_id=1, source_target_pairs={{0,1},{1,0},{2,3},{3,2},{4,5},{5,4},{6,7},{7,6},{8,9},{9,8},{10,11... | collective-permute-start | bytes 1572872 | tf_op jit(solution)/shard_map/ppermute | solution.py:507
  72.6 24.1 %collective-permute-start.19 = (bf16[128,2048]{1,0:T(8,128)(2,1)S(1)}, bf16[128,2048]{1,0:T(8,128)(2,1)}, u32[]{:S(2)}, u32[]{:S(2)}) collective-permute-start(bf16[128,2048]{1,0:T(8,128)(2,1)S(1)} %collective-permute-done.12.first), channel_id=1, source_target_pairs={{0,1},{1,0},{2,3},{3,2},{4,5},{5,4},{6,7},{7,6},{8,9},{9,8},{10,11... | collective-permute-start | bytes 1572872 | tf_op jit(solution)/shard_map/ppermute | solution.py:511
  73.1 23.7 %collective-permute-start.14 = (bf16[128,2048]{1,0:T(8,128)(2,1)}, bf16[128,2048]{1,0:T(8,128)(2,1)}, u32[]{:S(2)}, u32[]{:S(2)}) collective-permute-start(bf16[128,2048]{1,0:T(8,128)(2,1)} %collective-permute-done.13.first), channel_id=1, source_target_pairs={{8,0},{16,8},{24,16},{28,24},{20,28},{12,20},{4,12},{0,4},{9,1},{1... | collective-permute-start | bytes 1572872 | tf_op jit(solution)/shard_map/ppermute | solution.py:510
  81.0 16.3 %collective-permute-start.3 = (bf16[128,2048]{1,0:T(8,128)(2,1)S(1)}, bf16[128,2048]{1,0:T(8,128)(2,1)}, u32[]{:S(2)}, u32[]{:S(2)}) collective-permute-start(bf16[128,2048]{1,0:T(8,128)(2,1)S(1)} %collective-permute-done.2.first), channel_id=1, source_target_pairs={{0,8},{8,16},{16,24},{24,28},{28,20},{20,12},{12,4},{4,0},{1,9},{9... | collective-permute-start | bytes 1572872 | tf_op jit(solution)/shard_map/ppermute | solution.py:506
  89.0 17.9 %collective-permute-start.18 = (bf16[128,2048]{1,0:T(8,128)(2,1)S(1)}, bf16[128,2048]{1,0:T(8,128)(2,1)}, u32[]{:S(2)}, u32[]{:S(2)}) collective-permute-start(bf16[128,2048]{1,0:T(8,128)(2,1)S(1)} %collective-permute-done.1.first), channel_id=1, source_target_pairs={{0,1},{1,0},{2,3},{3,2},{4,5},{5,4},{6,7},{7,6},{8,9},{9,8},{10,11... | collective-permute-start | bytes 1572872 | tf_op jit(solution)/shard_map/ppermute | solution.py:507
  96.2 13.5 %collective-permute-start.17 = (bf16[128,2048]{1,0:T(8,128)(2,1)}, bf16[128,2048]{1,0:T(8,128)(2,1)}, u32[]{:S(2)}, u32[]{:S(2)}) collective-permute-start(bf16[128,2048]{1,0:T(8,128)(2,1)} %collective-permute-done.13.first), channel_id=1, source_target_pairs={{0,1},{1,0},{2,3},{3,2},{4,5},{5,4},{6,7},{7,6},{8,9},{9,8},{10,11... | collective-permute-start | bytes 1572872 | tf_op jit(solution)/shard_map/ppermute | solution.py:511
  96.7 16.0 %collective-permute-start.16 = (bf16[128,2048]{1,0:T(8,128)(2,1)S(1)}, bf16[128,2048]{1,0:T(8,128)(2,1)}, u32[]{:S(2)}, u32[]{:S(2)}) collective-permute-start(bf16[128,2048]{1,0:T(8,128)(2,1)S(1)} %collective-permute-done.2.first), channel_id=1, source_target_pairs={{0,1},{1,0},{2,3},{3,2},{4,5},{5,4},{6,7},{7,6},{8,9},{9,8},{10,11... | collective-permute-start | bytes 1572872 | tf_op jit(solution)/shard_map/ppermute | solution.py:507
  96.8 18.7 %collective-permute-start.15 = (bf16[128,2048]{1,0:T(8,128)(2,1)}, bf16[128,2048]{1,0:T(8,128)(2,1)}, u32[]{:S(2)}, u32[]{:S(2)}) collective-permute-start(bf16[128,2048]{1,0:T(8,128)(2,1)} %collective-permute-done.14.first), channel_id=1, source_target_pairs={{0,1},{1,0},{2,3},{3,2},{4,5},{5,4},{6,7},{7,6},{8,9},{9,8},{10,11... | collective-permute-start | bytes 1572872 | tf_op jit(solution)/shard_map/ppermute | solution.py:511
  97.3 21.3 %collective-permute-start.4 = (bf16[128,2048]{1,0:T(8,128)(2,1)}, bf16[128,2048]{1,0:T(8,128)(2,1)}, u32[]{:S(2)}, u32[]{:S(2)}) collective-permute-start(bf16[128,2048]{1,0:T(8,128)(2,1)} %collective-permute-done.3.first), channel_id=1, source_target_pairs={{0,1},{1,0},{2,3},{3,2},{4,5},{5,4},{6,7},{7,6},{8,9},{9,8},{10,11... | collective-permute-start | bytes 1572872 | tf_op jit(solution)/shard_map/ppermute | solution.py:507
  118.6 3.0 %copy-start.2 = (f32[1,2,128]{2,1,0:T(2,128)S(1)}, f32[1,2,128]{2,1,0:T(2,128)}, u32[]{:S(2)}) copy-start(f32[1,2,128]{2,1,0:T(2,128)} %param.43) | copy-start | bytes 3076
  121.6 17.7 %copy-start.8 = (f32[16,64]{1,0:T(8,128)S(1)}, f32[16,64]{1,0:T(8,128)}, u32[]{:S(2)}) copy-start(f32[16,64]{1,0:T(8,128)} %param.45) | copy-start | bytes 12292
  133.3 21.1 %all-to-all-start.1 = ((bf16[8,256,128]{2,1,0:T(8,128)(2,1)}), bf16[8,256,128]{2,1,0:T(8,128)(2,1)S(1)}, u32[]{:S(2)}, u32[]{:S(2)}) async-start(bf16[8,256,128]{2,1,0:T(8,128)(2,1)} %bitcast.53), calls=%async_computation.1 | async-start | bytes 1048576 | tf_op jit(solution)/shard_map/all_to_all | solution.py:538
  154.3 2.2 %copy-start.1 = (bf16[16,64,2048]{2,1,0:T(8,128)(2,1)S(1)}, bf16[16,64,2048]{2,1,0:T(8,128)(2,1)}, u32[]{:S(2)}) copy-start(bf16[16,64,2048]{2,1,0:T(8,128)(2,1)} %param.46) | copy-start | bytes 12582916
  158.9 2.0 %collective-permute-start.21 = (bf16[2,64,2048]{2,1,0:T(8,128)(2,1)S(1)}, bf16[2,64,2048]{2,1,0:T(8,128)(2,1)S(1)}, u32[]{:S(2)}, u32[]{:S(2)}) collective-permute-start(bf16[2,64,2048]{2,1,0:T(8,128)(2,1)S(1)} %dynamic-slice_bitcast_fusion), channel_id=1, source_target_pairs={{0,1},{1,0},{2,3},{3,2},{4,5},{5,4},{6,7},{7,6},{8,9},{9,8},{10,11... | collective-permute-start | bytes 1572872 | tf_op jit(solution)/shard_map/ppermute | solution.py:548
  161.0 8.4 %collective-permute-start.22 = (bf16[64,2048]{1,0:T(8,128)(2,1)S(1)}, bf16[64,2048]{1,0:T(8,128)(2,1)S(1)}, u32[]{:S(2)}, u32[]{:S(2)}) collective-permute-start(bf16[64,2048]{1,0:T(8,128)(2,1)S(1)} %dynamic-slice_bitcast_fusion.1), channel_id=1, source_target_pairs={{0,2},{1,3},{2,0},{3,1},{4,6},{5,7},{6,4},{7,5},{8,10},{9,11},{10,... | collective-permute-start | bytes 786440 | tf_op jit(solution)/shard_map/ppermute | solution.py:552

commit v2 on v0

--- a/solution.py
+++ b/solution.py
@@ -1,6 +1,10 @@
+import functools
+
 import jax
 import jax.numpy as jnp
 from jax import lax
+from jax.experimental import pallas as pl
+from jax.experimental.pallas import tpu as pltpu
 from jax.sharding import PartitionSpec as P
 
 SPAN = 256
@@ -71,7 +75,7 @@
     return (final_state, outputs.reshape((row_total,) + outputs.shape[2:]))
 
 
-def on_device(
+def weights_travel(
     tokens,
     gate_weight,
     input_weight,
@@ -194,6 +198,456 @@
     return layer_out
 
 
+bf16 = jnp.bfloat16
+f32 = jnp.float32
+ROW_PAD = 16
+
+
+def matmul(left, right, dims=((1,), (0,))):
+    return lax.dot_general(left, right, (dims, ((), ())), preferred_element_type=f32)
+
+
+def softplus(value):
+    return jnp.maximum(value, 0.0) + jnp.log1p(jnp.exp(-jnp.abs(value)))
+
+
+def silu(value):
+    return 0.5 * value * (1.0 + jnp.tanh(0.5 * value))
+
+
+def parts_of(value, count):
+    parts = []
+    for _ in range(count):
+        part = value.astype(bf16).astype(f32)
+        parts.append(part)
+        value = value - part
+    return parts
+
+
+def pack_kernel(at, tokens, groups, steps, ids, own, payload):
+    seats, height, part = own.shape
+    rows = tokens.shape[0] // seats
+    for seat in range(seats):
+        for panel in range(height // rows):
+            own[seat, panel * rows : (panel + 1) * rows] = tokens[
+                seat * rows : (seat + 1) * rows, panel * part : (panel + 1) * part
+            ]
+    payload[:height] = own[at[0]]
+    low = height
+    payload[low : low + groups.shape[0]] = groups[...]
+    low += groups.shape[0]
+    payload[low : low + steps.shape[0]] = steps[...]
+    low += steps.shape[0]
+    payload[low:] = jnp.broadcast_to(ids[...].astype(f32), (ROW_PAD, part)).astype(bf16)
+
+
+def pack(at, seats, tokens, groups, steps, ids):
+    rows, depth = tokens.shape
+    part = groups.shape[1]
+    height = rows * depth // (seats * part)
+    full = height + groups.shape[0] + steps.shape[0] + ROW_PAD
+    vmem = pl.BlockSpec(memory_space=pltpu.VMEM)
+    return pl.pallas_call(
+        pack_kernel,
+        in_specs=[pl.BlockSpec(memory_space=pltpu.SMEM)] + [vmem] * 4,
+        out_specs=[vmem, vmem],
+        out_shape=[
+            jax.ShapeDtypeStruct((seats, height, part), bf16),
+            jax.ShapeDtypeStruct((full, part), bf16),
+        ],
+        name="pack",
+    )(at, tokens, groups, steps, ids)
+
+
+def layer_kernel(
+    head_size, counts, table, pair, own, *refs
+):
+    ring = pair.shape[0]
+    payloads, refs = refs[: ring], refs[ring:]
+    pieces, refs = refs[: 4 * len(counts)], refs[4 * len(counts) :]
+    per_head, params, g_taps, g_shift, out = refs[:5]
+    tok, w_pair, w_group, st_rows, id_rows, w_x, w_step, x_all, g_all, gate_all, step_all, state, sems = refs[5:]
+    seats = own.shape[0]
+    height, part = own.shape[1:]
+    channels = out.shape[2]
+    rows = out.shape[1]
+    quarter = rows // seats
+    panels = height // quarter
+    states = part // 2
+    heads = channels // head_size
+    step_heads = st_rows.shape[1]
+    lines = w_step.shape[1]
+    tap_count = g_taps.shape[0]
+    rim = x_all.shape[0] - ring * rows
+
+    pair_copy = pltpu.make_async_copy(pair, w_pair, sems.at[0])
+    pair_copy.start()
+    shared = []
+    for order in range(ring):
+        source = table[order]
+        low = height
+        for kind, target in enumerate((w_group, st_rows, id_rows)):
+            size = target.shape[1]
+            copy = pltpu.make_async_copy(
+                payloads[order].at[pl.ds(low, size)],
+                target.at[source],
+                sems.at[1 + ring + kind * ring + order],
+            )
+            copy.start()
+            shared.append(copy)
+            low += size
+    pltpu.make_async_copy(own, tok.at[table[0]], sems.at[1 + table[0]]).start()
+    order = 1
+    for group, count in enumerate(counts):
+        for at in range(count):
+            source = table[order]
+            for hop in range(seats):
+                pltpu.make_async_copy(
+                    pieces[4 * group + hop].at[at],
+                    tok.at[source, table[ring + hop]],
+                    sems.at[1 + source],
+                ).start()
+            order += 1
+
+    x_all[:rim] = jnp.zeros((rim, channels), f32)
+    g_all[:rim] = jnp.zeros((rim, part), f32)
+    state[...] = jnp.zeros_like(state)
+    one = lambda flag: flag.astype(f32).astype(bf16)
+    iota = lambda shape, dim: lax.broadcasted_iota(jnp.int32, shape, dim)
+    same = one(iota((2 * channels, 2 * channels), 0) == iota((2 * channels, 2 * channels), 1))
+    pick = one(
+        (iota((lines, step_heads), 0) + table[0] * heads == iota((lines, step_heads), 1))
+        & (iota((lines, step_heads), 0) < heads)
+    )
+    pair_copy.wait()
+    for copy in shared:
+        copy.wait()
+    for panel in range(ring):
+        w_x[panel] = matmul(w_pair[panel], same, ((0,), (0,))).astype(bf16)
+        w_step[panel] = matmul(pick, st_rows[panel]).astype(bf16)
+
+    upper = one(iota((rows, rows), 0) <= iota((rows, rows), 1))
+    widen = one(iota((lines, channels), 1) // head_size == iota((lines, channels), 0))
+    half = rows // 2
+    causal = iota((half, half), 0) >= iota((half, half), 1)
+    lane_head = iota((rows, channels), 1) // head_size
+    bias, decay = per_head[:, 0:1], per_head[:, 1:2]
+    skip = params[tap_count + 1 : tap_count + 2]
+
+    def tok_wait(block):
+        pltpu.make_async_copy(own, tok.at[block], sems.at[1 + block]).wait()
+
+    def project(block):
+        total_x = total_g = total_s = None
+        for panel in range(panels):
+            at = panel * quarter
+            piece = jnp.concatenate(
+                [tok[block, seat, at : at + quarter] for seat in range(seats)], axis=0
+            )
+            term_x = matmul(piece, w_x[panel])
+            term_g = matmul(piece, w_group[panel])
+            term_s = matmul(w_step[panel], piece, ((1,), (1,)))
+            total_x = term_x if total_x is None else total_x + term_x
+            total_g = term_g if total_g is None else total_g + term_g
+            total_s = term_s if total_s is None else total_s + term_s
+        base = pl.multiple_of(block * rows, rows)
+        x_all[pl.ds(base + rim, rows)] = total_x[:, :channels].astype(bf16).astype(f32)
+        gate_all[block] = total_x[:, channels:].astype(bf16).astype(f32)
+        g_all[pl.ds(base + rim, rows)] = total_g.astype(bf16).astype(f32)
+        step_all[block] = total_s
+
+    def conv(ref, base, taps, shift):
+        window = ref[pl.ds(base, rows + rim)]
+        first = rim - tap_count + 1
+        running = shift
+        for tap in range(tap_count):
+            running = running + taps[tap : tap + 1] * window[first + tap : first + tap + rows]
+        return silu(running).astype(bf16)
+
+    def stretch(value, count):
+        low = jnp.concatenate(parts_of(value, count), axis=0).astype(bf16)
+        return matmul(low, jnp.concatenate([widen] * count, axis=0), ((0,), (0,)))
+
+    def scan(block):
+        base = pl.multiple_of(block * rows, rows)
+        values = conv(x_all, base, params[:tap_count], params[tap_count : tap_count + 1])
+        values = values.astype(f32)
+        groups = conv(g_all, base, g_taps[...], g_shift[...])
+        b_rows, c_rows = groups[:, :states], groups[:, states:]
+        bucket = id_rows[block].astype(f32)[:1]
+        raw_step = step_all[block] + bias
+        for entry in range(PLACE_BINS):
+            raw_step = raw_step + jnp.where(
+                bucket == float(entry), per_head[:, 2 + entry : 3 + entry], 0.0
+            )
+        sizes = softplus(raw_step).astype(bf16).astype(f32)
+        rates = jnp.concatenate(parts_of(-decay * sizes, 3), axis=0).astype(bf16)
+        sums = matmul(rates, upper)
+        cumulative = sums[:lines] + (sums[lines : 2 * lines] + sums[2 * lines :])
+        last = cumulative[:, rows - 1 : rows]
+        grown = stretch(jnp.exp(cumulative), 3)
+        left = stretch(sizes * jnp.exp(last - cumulative), 3)
+        driven = (stretch(sizes, 1) * values).astype(f32)
+        scores = matmul(c_rows, b_rows, ((1,), (1,)))
+        cum_parts = parts_of(cumulative, 3)
+        ones = jnp.ones((3, rows), f32)
+        pad = jnp.zeros((2, rows), f32)
+        top, low_left, low_right, inputs = [], [], [], []
+        for head in range(heads):
+            mine = jnp.concatenate([p[head : head + 1] for p in cum_parts], axis=0)
+            spread = matmul(
+                jnp.concatenate([mine, ones, pad], axis=0).astype(bf16),
+                jnp.concatenate([ones, -mine, pad], axis=0).astype(bf16),
+                ((0,), (0,)),
+            )
+            decays = lambda part: jnp.exp(jnp.where(causal, part, -1e30))
+            top.append((scores[:half, :half] * decays(spread[:half, :half])).astype(bf16))
+            low_left.append((scores[half:, :half] * jnp.exp(spread[half:, :half])).astype(bf16))
+            low_right.append((scores[half:, half:] * decays(spread[half:, half:])).astype(bf16))
+            inputs.append(jnp.where(lane_head == head, driven, 0.0).astype(bf16))
+        upper_in = jnp.concatenate([d[:half] for d in inputs], axis=0)
+        lower_in = jnp.concatenate([d[half:] for d in inputs], axis=0)
+        upper_out = matmul(jnp.concatenate(top, axis=1), upper_in)
+        lower_out = matmul(
+            jnp.concatenate(low_left + low_right, axis=1),
+            jnp.concatenate([upper_in, lower_in], axis=0),
+        )
+        within = jnp.concatenate([upper_out, lower_out], axis=0)
+        held = state[...]
+        scanned = within + grown * matmul(c_rows, held.astype(bf16)) + skip * values
+        scanned = scanned.astype(bf16).astype(f32)
+        out[block] = (scanned * silu(gate_all[block])).astype(bf16)
+        injected = matmul(b_rows, (left * values).astype(bf16), ((0,), (0,)))
+        state[...] = grown[rows - 1 : rows] * held + injected
+
+    tok_wait(0)
+    project(0)
+
+    def advance(block, carry):
+        tok_wait(block + 1)
+        scan(block)
+        project(block + 1)
+        return carry
+
+    lax.fori_loop(0, ring - 1, advance, 0)
+    scan(ring - 1)
+
+
+def layer(head_size, table, pair, own, payloads, groups, per_head, params, g_taps, g_shift):
+    ring, wide, slab = pair.shape
+    channels = wide // 2
+    seats, height, part = own.shape
+    rows = seats * height * part // (ring * slab)
+    step_heads = payloads[0].shape[0] - height - slab - ROW_PAD
+    lines = per_head.shape[0]
+    rim = 8
+    total = ring * rows
+    counts = [group[0].shape[0] for group in groups]
+    pieces = [piece for group in groups for piece in group]
+    vmem = pl.BlockSpec(memory_space=pltpu.VMEM)
+    anywhere = pl.BlockSpec(memory_space=pl.ANY)
+    return pl.pallas_call(
+        functools.partial(layer_kernel, head_size, counts),
+        in_specs=[pl.BlockSpec(memory_space=pltpu.SMEM)]
+        + [anywhere] * (2 + len(payloads) + len(pieces))
+        + [vmem] * 4,
+        out_specs=vmem,
+        out_shape=jax.ShapeDtypeStruct((ring, rows, channels), bf16),
+        scratch_shapes=[
+            pltpu.VMEM((ring, seats, height, part), bf16),
+            pltpu.VMEM(pair.shape, bf16),
+            pltpu.VMEM((ring, slab, part), bf16),
+            pltpu.VMEM((ring, step_heads, part), bf16),
+            pltpu.VMEM((ring, ROW_PAD, part), bf16),
+            pltpu.VMEM((ring, slab, wide), bf16),
+            pltpu.VMEM((ring, lines, slab), bf16),
+            pltpu.VMEM((rim + total, channels), f32),
+            pltpu.VMEM((rim + total, part), f32),
+            pltpu.VMEM((ring, rows, channels), f32),
+            pltpu.VMEM((ring, lines, rows), f32),
+            pltpu.VMEM((part // 2, channels), f32),
+            pltpu.SemaphoreType.DMA((1 + 4 * ring,)),
+        ],
+        compiler_params=pltpu.CompilerParams(vmem_limit_bytes=48 * 1024 * 1024),
+        cost_estimate=pl.CostEstimate(
+            flops=2 * total * ring * slab * (wide + part),
+            bytes_accessed=2 * total * ring * slab,
+            transcendentals=0,
+        ),
+        name="layer",
+    )(table, pair, own, *payloads, *pieces, per_head, params, g_taps, g_shift)
+
+
+def close_kernel(gated, gain, weight, out):
+    pieces, _, width = gated.shape
+    square = jnp.zeros(gated.shape[1:], f32)
+    total = jnp.zeros(out.shape, f32)
+    parts = []
+    for piece in range(pieces):
+        part = gated[piece].astype(f32)
+        square = square + part * part
+        parts.append((part * gain[:, piece * width : (piece + 1) * width]).astype(bf16))
+    total = matmul(jnp.concatenate(parts, axis=1), weight[...])
+    mean = jnp.sum(square, axis=1, keepdims=True) * (1.0 / (pieces * width))
+    out[...] = (total * lax.rsqrt(mean + norm_epsilon)).astype(bf16)
+
+
+def close(gated, gain, weight):
+    pieces, rows, width = gated.shape
+    columns = 512
+    return pl.pallas_call(
+        close_kernel,
+        grid=(weight.shape[1] // columns,),
+        in_specs=[
+            pl.BlockSpec(gated.shape, lambda i: (0, 0, 0)),
+            pl.BlockSpec(gain.shape, lambda i: (0, 0)),
+            pl.BlockSpec((weight.shape[0], columns), lambda i: (0, i)),
+        ],
+        out_specs=pl.BlockSpec((rows, columns), lambda i: (0, i)),
+        out_shape=jax.ShapeDtypeStruct((rows, weight.shape[1]), bf16),
+        compiler_params=pltpu.CompilerParams(vmem_limit_bytes=32 * 1024 * 1024),
+        cost_estimate=pl.CostEstimate(
+            flops=2 * rows * weight.size, bytes_accessed=2 * weight.size, transcendentals=0
+        ),
+        name="close",
+    )(gated, gain, weight)
+
+
+def tokens_travel(
+    tokens,
+    gate_weight,
+    input_weight,
+    group_weight,
+    step_weight,
+    step_bias,
+    bucket_table,
+    bucket_ids,
+    decay_rate,
+    conv_input,
+    conv_input_bias,
+    conv_group,
+    conv_group_bias,
+    skip_gain,
+    norm_gain,
+    out_weight,
+):
+    rows, depth = tokens.shape
+    slab = gate_weight.shape[0]
+    heads_here = step_bias.shape[0]
+    head_size = gate_weight.shape[2]
+    state_size = group_weight.shape[3]
+    tap_count = conv_input.shape[0]
+    ring = lax.axis_size("seq")
+    seats = lax.axis_size("mp")
+    me = lax.axis_index("seq")
+    seat = lax.axis_index("mp")
+    core = seat % 2
+    channels = heads_here * head_size // ring
+    heads = channels // head_size
+    line = ring // 2
+    swap = lambda size, bit: [(i, i ^ bit) for i in range(size)]
+    column = lambda pairs: [(2 * a + w, 2 * b + w) for a, b in pairs for w in range(2)]
+    others = [[1, 2, 3], [0, 2, 3], [3, 1, 0], [2, 1, 0]]
+    lists = []
+    for seq_at in range(ring):
+        z, x = seq_at // 2, seq_at % 2
+        sources = [seq_at, seq_at ^ 1]
+        for other in others[z]:
+            sources += [2 * other + x, 2 * other + 1 - x]
+        for seat_at in range(seats):
+            lists.append(sources + [seat_at ^ q for q in range(seats)])
+    table = lax.dynamic_index_in_dim(
+        jnp.asarray(lists, jnp.int32), lax.axis_index(("seq", "mp")), 0, False
+    )
+
+    by_channel = lambda w: jnp.transpose(w, (1, 2, 0)).reshape(ring, channels, slab)
+    pair = jnp.concatenate([by_channel(input_weight), by_channel(gate_weight)], axis=1)
+    pair = lax.all_to_all(pair, "seq", split_axis=0, concat_axis=0, tiled=True)
+
+    own, payload = pack(
+        table[ring : ring + 1],
+        seats,
+        tokens,
+        group_weight.reshape(slab, 2 * state_size),
+        jnp.transpose(step_weight),
+        bucket_ids.reshape(1, rows),
+    )
+    inner = (me >= 2) & (me < 6)
+    outward = column([(1, 0), (2, 3)])
+    middle = column([(1, 2), (2, 1)])
+    near = lax.ppermute(payload, "seq", swap(ring, 2))
+    mid = lax.ppermute(payload, "seq", middle)
+    mid_far = lax.ppermute(near, "seq", middle)
+    out_near = lax.ppermute(mid, "seq", outward)
+    out_far = lax.ppermute(mid_far, "seq", outward)
+    arrived = [near, jnp.where(inner, mid, out_near), jnp.where(inner, mid_far, out_far)]
+    payloads = [payload, lax.ppermute(payload, "seq", swap(ring, 1))]
+    for item in arrived:
+        payloads += [item, lax.ppermute(item, "seq", swap(ring, 1))]
+    height = own.shape[1]
+    groups = []
+    for first in range(1, ring, 2):
+        quarter = jnp.stack([item[:height] for item in payloads[first : first + 2]])
+        beside = lax.ppermute(quarter, "mp", swap(seats, 1))
+        across = lax.ppermute(quarter, "mp", swap(seats, 2))
+        groups.append((quarter, beside, across, lax.ppermute(across, "mp", swap(seats, 1))))
+
+    per_head = jnp.concatenate([jnp.stack([step_bias, decay_rate]), bucket_table], axis=0)
+    per_head = lax.dynamic_slice_in_dim(jnp.transpose(per_head), me * heads, heads, 0)
+    per_head = jnp.pad(per_head, ((0, 8 - heads), (0, 0)))
+    params = jnp.concatenate(
+        [
+            conv_input,
+            conv_input_bias[None],
+            jnp.broadcast_to(skip_gain[None, :, None], (1, heads_here, head_size)),
+        ],
+        axis=0,
+    )
+    params = params.reshape(params.shape[0], ring, channels)
+    params = lax.dynamic_index_in_dim(params, me, 1, False)
+    gated = layer(
+        head_size,
+        table,
+        pair,
+        own,
+        payloads,
+        groups,
+        per_head,
+        params,
+        conv_group.reshape(tap_count, 2 * state_size),
+        conv_group_bias.reshape(1, 2 * state_size),
+    )
+    gated = lax.all_to_all(gated, "seq", split_axis=0, concat_axis=0, tiled=True)
+    partial = close(
+        gated, norm_gain.reshape(1, -1), out_weight.reshape(-1, out_weight.shape[2])
+    )
+    quarters = partial.reshape(seats // 2, 2, rows // seats, -1)
+    keep = lax.dynamic_index_in_dim(quarters, core, 1, False)
+    give = lax.dynamic_index_in_dim(quarters, 1 - core, 1, False)
+    both = (keep.astype(f32) + lax.ppermute(give, "mp", swap(seats, 1)).astype(f32)).astype(bf16)
+    chip = seat // 2
+    keep = lax.dynamic_index_in_dim(both, chip, 0, False)
+    give = lax.dynamic_index_in_dim(both, 1 - chip, 0, False)
+    return (keep.astype(f32) + lax.ppermute(give, "mp", swap(seats, 2)).astype(f32)).astype(bf16)
+
+
+def on_device(*arrays):
+    tokens, gate_weight, group_weight = arrays[0], arrays[1], arrays[3]
+    ring = lax.axis_size("seq")
+    channels = gate_weight.shape[1] * gate_weight.shape[2] // ring
+    weights = 2 * gate_weight.size + group_weight.size + arrays[4].size
+    fits = (
+        tokens.size <= weights
+        and channels % 128 == 0
+        and gate_weight.shape[0] == 2 * group_weight.shape[3] == tokens.shape[0]
+        and channels % gate_weight.shape[2] == 0
+        and group_weight.shape[1] == 1
+        and lax.axis_size("mp") == 4
+        and ring == 8
+    )
+    return (tokens_travel if fits else weights_travel)(*arrays)
+
+
 def solution(mesh):
     placed = (
         P("seq", None),

time: 397 us -> 160 us (0.40)
  matrix products: 68.8 us -> 0 us
  blocking collectives: 62.5 us -> 0 us
  waiting for transfers between devices: 131 us -> 76.8 us
  local copies, waits for them, and re-layouts: 53.5 us -> 14.6 us
  Pallas kernels: 0 us -> 24.1 us
  loops' own time: 22.3 us -> 0 us
  other arithmetic: 27.4 us -> 5.6 us
  starting transfers between devices: 16 us -> 37.5 us
  between operations: 13.4 us -> 0.42 us
    dot_general x70 -> x0, matrix products: 68.8 us -> none  [the longest x16 19.5 us: ssd_block(): jnp.einsum('srp,sn->rpn', driven * remaining[:, :, None], block_b.astype(...]
    all_gather x3 -> x0, waiting for transfers between devices: 64.5 us -> none  [the longest x1 44.4 us: on_device(): lax.all_gather(group_weight, 'seq', axis=0, tiled=True)]
    all_gather x1 -> x0, blocking collectives: 62.5 us -> none  [on_device(): lax.all_gather(step_weight, 'seq', axis=0, tiled=True)]
    ppermute x0 -> x23, waiting for transfers between devices: none -> 61.8 us  [the longest x1 13.9 us: tokens_travel(): out_near = lax.ppermute(mid, 'seq', outward)]
    slice x50 -> x1, local copies, waits for them, and re-layouts: 27.1 us -> 0.61 us  [tokens_travel(): table[ring:ring + 1]]
    ppermute x0 -> x23, starting transfers between devices: none -> 26 us  [the longest x3 6.72 us: tokens_travel(): payloads += [item, lax.ppermute(item, 'seq', swap(ring, 1))]]
    all_to_all x4 -> x2, waiting for transfers between devices: 40.7 us -> 15.1 us  [the longest x1 15.1 us: tokens_travel(): lax.all_to_all(gated, 'seq', split_axis=0, concat_axis=0, tiled=True)]
    pallas_call x0 -> x3, Pallas kernels: none -> 24.1 us  [the longest x1 18.7 us: layer(): pl.pallas_call(functools.partial(layer_kernel, head_size, counts), in_spe...]
  transfers between devices with their start and end apart: 8 -> 25, of which waited for: 6 -> 11; matrix products, arithmetic and copies ran while one was open for 36% -> 6% of each run, Pallas kernels for 0% -> 0%
where the time goes in v2:
time: 160 us; the launch traced here: 159 us
  waiting for transfers between devices  76.8 us (48%)
  starting transfers between devices  37.5 us (23%)
  Pallas kernels  24.1 us (15%)
  local copies, waits for them, and re-layouts  14.6 us (9%)
  other arithmetic  5.6 us (4%)
    pallas_call x1, Pallas kernels, layer(): pl.pallas_call(functools.partial(layer_kernel, head_size, counts), in_spe...  18.7 us
    all_to_all x1, waiting for transfers between devices, tokens_travel(): lax.all_to_all(gated, 'seq', split_axis=0, concat_axis=0, tiled=True)  15.1 us
    ppermute x1, waiting for transfers between devices, tokens_travel(): out_near = lax.ppermute(mid, 'seq', outward)  13.9 us
    ppermute x1, waiting for transfers between devices, tokens_travel(): out_far = lax.ppermute(mid_far, 'seq', outward)  13.1 us
    ppermute x4, waiting for transfers between devices, tokens_travel(): across = lax.ppermute(quarter, 'mp', swap(seats, 2))  13 us
    unnamed x33, local copies, waits for them, and re-layouts  8.52 us
    all_to_all x1, starting transfers between devices, tokens_travel(): lax.all_to_all(gated, 'seq', split_axis=0, concat_axis=0, tiled=True)  7.19 us
    ppermute x1, waiting for transfers between devices, tokens_travel(): lax.ppermute(give, 'mp', swap(seats, 2)).astype(f32)  6.83 us
  transfers between devices with their start and end apart: 25, of which 11 were waited for; matrix products, arithmetic and copies ran while one was open for 6% of the time, Pallas kernels for 0%

profile of v2, /device:TPU:0, one launch (start us, length us, event | category | flops | bytes accessed | tf_op | source)
XLA Modules:
  0.0 159.0 jit_solution(935028539325654723)
XLA Ops:
  0.0 0.7 constant_dynamic-slice_fusion
  0.7 0.6 slice.27
  1.3 1.6 copy.35
  2.9 3.1 %pack.1 = (bf16[4,512,256]{2,1,0:T(8,128)(2,1)}, bf16[800,256]{1,0:T(8,128)(2,1)}) custom-call(s32[1]{0:T(128)} %bitcast.5.at, bf16[256,2048]{1,0:T(8,128)(2,1)} %tokens.1, bf16[256,256]{1,0:T(8,128)(2,1)} %bitcast.62, bf16[16,256]{1,0:T(8,128)(2,1)} %bitcast.67, s32[1,256]{1,0:T(1,128)} %bitcast.69), custom_call_target="tpu_custom_call" | custom-call | tf_op jit(solution)/shard_map/pack/pallas_call | solution.py:250
  6.0 0.7 collective-permute-start.3
  6.7 5.9 %collective-permute-start.1 = (bf16[800,256]{1,0:T(8,128)(2,1)}, bf16[800,256]{1,0:T(8,128)(2,1)S(1)}, u32[]{:S(2)}, u32[]{:S(2)}) collective-permute-start(bf16[800,256]{1,0:T(8,128)(2,1)} %get-tuple-element.8.refs_0_), channel_id=1, source_target_pairs={{0,8},{4,12},{8,0},{12,4},{16,24},{20,28},{24,16},{28,20},{1,9},{5... | collective-permute-start | bytes 1228808 | tf_op jit(solution)/shard_map/ppermute | solution.py:578
  12.5 1.5 collective-permute-start
  14.0 2.3 %pad_maximum_fusion = bf16[8,256,256]{2,1,0:T(8,128)(2,1)} fusion(bf16[8,128,256]{2,1,0:T(8,128)(2,1)} %bitcast.63, bf16[8,128,256]{2,1,0:T(8,128)(2,1)} %bitcast.64), kind=kLoop, calls=%fused_computation | loop fusion | flops 2097152 | bytes 2097152 | tf_op jit(solution)/shard_map/concatenate | solution.py:564
  16.3 4.3 %all-to-all-start = ((bf16[8,256,256]{2,1,0:T(8,128)(2,1)}), bf16[8,256,256]{2,1,0:T(8,128)(2,1)}, u32[]{:S(2)}, u32[]{:S(2)}) async-start(bf16[8,256,256]{2,1,0:T(8,128)(2,1)} %pad_maximum_fusion), calls=%async_computation | async-start | bytes 2097152 | tf_op jit(solution)/shard_map/all_to_all | solution.py:565
  20.6 1.3 collective-permute-start.4
  21.9 0.5 collective-permute-done.1.refs_2_
  22.4 0.7 collective-permute-start.6
  23.1 6.3 %collective-permute-done.refs_1_ = bf16[800,256]{1,0:T(8,128)(2,1)S(1)} collective-permute-done((bf16[800,256]{1,0:T(8,128)(2,1)}, bf16[800,256]{1,0:T(8,128)(2,1)S(1)}, u32[]{:S(2)}, u32[]{:S(2)}) %collective-permute-start) | collective-permute-done | bytes 409632 | tf_op jit(solution)/shard_map/ppermute | solution.py:584
  29.4 0.1 pad_maximum_fusion.1.refs_8_
  29.5 0.1 collective-permute-start.9
  29.6 1.6 collective-permute-start.10
  31.2 2.9 %collective-permute-start.2 = (bf16[800,256]{1,0:T(8,128)(2,1)S(1)}, bf16[800,256]{1,0:T(8,128)(2,1)S(1)}, u32[]{:S(2)}, u32[]{:S(2)}) collective-permute-start(bf16[800,256]{1,0:T(8,128)(2,1)S(1)} %collective-permute-done.1.refs_2_), channel_id=1, source_target_pairs={{0,4},{4,0},{8,12},{12,8},{16,20},{20,16},{24,28},{28,24},{1,5},{5... | collective-permute-start | bytes 1228808 | tf_op jit(solution)/shard_map/ppermute | solution.py:586
  34.0 13.9 %collective-permute-done.4 = bf16[800,256]{1,0:T(8,128)(2,1)S(1)} collective-permute-done((bf16[800,256]{1,0:T(8,128)(2,1)S(1)}, bf16[800,256]{1,0:T(8,128)(2,1)S(1)}, u32[]{:S(2)}, u32[]{:S(2)}) %collective-permute-start.4) | collective-permute-done | bytes 409632 | tf_op jit(solution)/shard_map/ppermute | solution.py:581
  48.0 1.5 collective-permute-start.5
  49.4 1.3 collective-permute-start.7
  50.8 0.1 pad_maximum_fusion.2.refs_12_
  50.9 0.0 copy-start.9
  50.9 0.0 copy-start.11
  50.9 0.1 collective-permute-start.12
  51.0 13.1 %collective-permute-done.7 = bf16[800,256]{1,0:T(8,128)(2,1)S(1)} collective-permute-done((bf16[800,256]{1,0:T(8,128)(2,1)S(1)}, bf16[800,256]{1,0:T(8,128)(2,1)S(1)}, u32[]{:S(2)}, u32[]{:S(2)}) %collective-permute-start.7) | collective-permute-done | bytes 409632 | tf_op jit(solution)/shard_map/ppermute | solution.py:582
  64.1 1.5 collective-permute-start.13
  65.7 2.4 %collective-permute-start.8 = (bf16[800,256]{1,0:T(8,128)(2,1)S(1)}, bf16[800,256]{1,0:T(8,128)(2,1)S(1)}, u32[]{:S(2)}, u32[]{:S(2)}) collective-permute-start(bf16[800,256]{1,0:T(8,128)(2,1)S(1)} %broadcast_select_fusion.refs_6_), channel_id=1, source_target_pairs={{0,4},{4,0},{8,12},{12,8},{16,20},{20,16},{24,28},{28,24},{1,5},{5... | collective-permute-start | bytes 1228808 | tf_op jit(solution)/shard_map/ppermute | solution.py:586
  68.0 0.9 pad_maximum_fusion.3.refs_16_
  68.9 0.5 collective-permute-start.16
  69.4 6.3 %collective-permute-done.8.refs_7_ = bf16[800,256]{1,0:T(8,128)(2,1)S(1)} collective-permute-done((bf16[800,256]{1,0:T(8,128)(2,1)S(1)}, bf16[800,256]{1,0:T(8,128)(2,1)S(1)}, u32[]{:S(2)}, u32[]{:S(2)}) %collective-permute-start.8) | collective-permute-done | bytes 409632 | tf_op jit(solution)/shard_map/ppermute | solution.py:586
  75.8 0.9 copy-done.3
  76.7 0.4 collective-permute-start.15
  77.1 1.9 %collective-permute-done.13.refs_14_ = bf16[2,512,256]{2,1,0:T(8,128)(2,1)} collective-permute-done((bf16[2,512,256]{2,1,0:T(8,128)(2,1)S(1)}, bf16[2,512,256]{2,1,0:T(8,128)(2,1)}, u32[]{:S(2)}, u32[]{:S(2)}) %collective-permute-start.13) | collective-permute-done | bytes 524320 | tf_op jit(solution)/shard_map/ppermute | solution.py:592
  79.0 1.6 collective-permute-start.19
  80.6 8.9 %collective-permute-done.16.refs_18_ = bf16[2,512,256]{2,1,0:T(8,128)(2,1)} collective-permute-done((bf16[2,512,256]{2,1,0:T(8,128)(2,1)}, bf16[2,512,256]{2,1,0:T(8,128)(2,1)}, u32[]{:S(2)}, u32[]{:S(2)}) %collective-permute-start.16) | collective-permute-done | bytes 524320 | tf_op jit(solution)/shard_map/ppermute | solution.py:592
  89.5 0.5 collective-permute-start.18
  90.0 2.2 %collective-permute-done.19.refs_22_ = bf16[1,512,256]{2,1,0:T(8,128)(2,1)S(1)} collective-permute-done((bf16[1,512,256]{2,1,0:T(8,128)(2,1)S(1)}, bf16[1,512,256]{2,1,0:T(8,128)(2,1)S(1)}, u32[]{:S(2)}, u32[]{:S(2)}) %collective-permute-start.19) | collective-permute-done | bytes 262176 | tf_op jit(solution)/shard_map/ppermute | solution.py:592
  92.2 0.1 collective-permute-start.20
  92.3 0.1 copy.26
  92.4 0.7 copy.25
  93.1 0.7 copy.24
  93.8 0.8 concatenate.16
  94.6 0.8 concatenate.17
  95.4 0.7 broadcast_in_dim.11
  96.1 0.1 broadcast_in_dim.12
  96.2 0.7 broadcast_in_dim.13
  96.9 0.7 copy.36
  97.6 0.8 fusion.7
  98.3 0.6 fusion.4.refs_25_
  99.0 1.0 copy-done.2
  100.0 1.0 copy-done.4
  101.1 1.0 copy-done.5
  102.1 18.7 %layer.1 = bf16[8,256,128]{2,1,0:T(8,128)(2,1)} custom-call(s32[12]{0:T(128)S(1)} %get-tuple-element.10.table, bf16[8,256,256]{2,1,0:T(8,128)(2,1)} %all-to-all-done.pair, bf16[4,512,256]{2,1,0:T(8,128)(2,1)} %get-tuple-element.7.own, bf16[800,256]{1,0:T(8,128)(2,1)S(1)} %copy-done.5, bf16[800,256]{1,0:T(8,128)(2,1)S(1)} %collective-permute-done.refs_1_, ...), custom_call_target="tpu_custom_call" | custom-call | flops 4294967296 | bytes 8388608 | tf_op jit(solution)/shard_map/layer/pallas_call | solution.py:449
  120.8 7.2 %all-to-all-start.1 = ((bf16[8,256,128]{2,1,0:T(8,128)(2,1)}), bf16[8,256,128]{2,1,0:T(8,128)(2,1)S(1)}, u32[]{:S(2)}, u32[]{:S(2)}) async-start(bf16[8,256,128]{2,1,0:T(8,128)(2,1)} %layer.1), calls=%async_computation.1 | async-start | bytes 1048576 | tf_op jit(solution)/shard_map/all_to_all | solution.py:620
  128.0 0.1 reshape.56.gain
  128.1 15.1 %all-to-all-done.1.gated = bf16[8,256,128]{2,1,0:T(8,128)(2,1)S(1)} async-done(((bf16[8,256,128]{2,1,0:T(8,128)(2,1)}), bf16[8,256,128]{2,1,0:T(8,128)(2,1)S(1)}, u32[]{:S(2)}, u32[]{:S(2)}) %all-to-all-start.1) | async-done | bytes 524320 | tf_op jit(solution)/shard_map/all_to_all | solution.py:620
  143.1 2.2 %copy-done = bf16[16,64,2048]{2,1,0:T(8,128)(2,1)S(1)} copy-done((bf16[16,64,2048]{2,1,0:T(8,128)(2,1)S(1)}, bf16[16,64,2048]{2,1,0:T(8,128)(2,1)}, u32[]{:S(2)}) %copy-start) | copy-done | bytes 4194328
  145.3 2.3 %close.1 = bf16[256,2048]{1,0:T(8,128)(2,1)S(1)} custom-call(bf16[8,256,128]{2,1,0:T(8,128)(2,1)S(1)} %all-to-all-done.1.gated, f32[1,1024]{1,0:T(1,128)S(1)} %reshape.56.gain, bf16[1024,2048]{1,0:T(8,128)(2,1)S(1)} %bitcast.59), custom_call_target="tpu_custom_call" | custom-call | flops 1073741824 | bytes 4194304 | tf_op jit(solution)/shard_map/close/pallas_call | solution.py:498
  147.7 0.1 collective-permute-start.21
  147.8 1.9 %collective-permute-done.21 = bf16[2,64,2048]{2,1,0:T(8,128)(2,1)S(1)} collective-permute-done((bf16[2,64,2048]{2,1,0:T(8,128)(2,1)S(1)}, bf16[2,64,2048]{2,1,0:T(8,128)(2,1)S(1)}, u32[]{:S(2)}, u32[]{:S(2)}) %collective-permute-start.21) | collective-permute-done | bytes 524320 | tf_op jit(solution)/shard_map/ppermute | solution.py:627
  149.6 0.1 fusion
  149.8 1.6 collective-permute-start.22
  151.4 6.8 %collective-permute-done.22 = bf16[64,2048]{1,0:T(8,128)(2,1)S(1)} collective-permute-done((bf16[64,2048]{1,0:T(8,128)(2,1)S(1)}, bf16[64,2048]{1,0:T(8,128)(2,1)S(1)}, u32[]{:S(2)}, u32[]{:S(2)}) %collective-permute-start.22) | collective-permute-done | bytes 262176 | tf_op jit(solution)/shard_map/ppermute | solution.py:631
  158.2 0.8 fusion.1
  (53 shorter events, 0.4 us)
Async XLA Ops:
  6.0 14.6 %collective-permute-start.3 = (bf16[800,256]{1,0:T(8,128)(2,1)}, bf16[800,256]{1,0:T(8,128)(2,1)S(1)}, u32[]{:S(2)}, u32[]{:S(2)}) collective-permute-start(bf16[800,256]{1,0:T(8,128)(2,1)} %get-tuple-element.8.refs_0_), channel_id=1, source_target_pairs={{8,16},{12,20},{16,8},{20,12},{9,17},{13,21},{17,9},{21,13},{10,18... | collective-permute-start | bytes 1228808 | tf_op jit(solution)/shard_map/ppermute | solution.py:579
  6.7 15.7 %collective-permute-start.1 = (bf16[800,256]{1,0:T(8,128)(2,1)}, bf16[800,256]{1,0:T(8,128)(2,1)S(1)}, u32[]{:S(2)}, u32[]{:S(2)}) collective-permute-start(bf16[800,256]{1,0:T(8,128)(2,1)} %get-tuple-element.8.refs_0_), channel_id=1, source_target_pairs={{0,8},{4,12},{8,0},{12,4},{16,24},{20,28},{24,16},{28,20},{1,9},{5... | collective-permute-start | bytes 1228808 | tf_op jit(solution)/shard_map/ppermute | solution.py:578
  12.5 16.9 %collective-permute-start = (bf16[800,256]{1,0:T(8,128)(2,1)}, bf16[800,256]{1,0:T(8,128)(2,1)S(1)}, u32[]{:S(2)}, u32[]{:S(2)}) collective-permute-start(bf16[800,256]{1,0:T(8,128)(2,1)} %get-tuple-element.8.refs_0_), channel_id=1, source_target_pairs={{0,4},{4,0},{8,12},{12,8},{16,20},{20,16},{24,28},{28,24},{1,5},{5... | collective-permute-start | bytes 1228808 | tf_op jit(solution)/shard_map/ppermute | solution.py:584
  16.3 82.7 %all-to-all-start = ((bf16[8,256,256]{2,1,0:T(8,128)(2,1)}), bf16[8,256,256]{2,1,0:T(8,128)(2,1)}, u32[]{:S(2)}, u32[]{:S(2)}) async-start(bf16[8,256,256]{2,1,0:T(8,128)(2,1)} %pad_maximum_fusion), calls=%async_computation | async-start | bytes 2097152 | tf_op jit(solution)/shard_map/all_to_all | solution.py:565
  20.6 27.3 %collective-permute-start.4 = (bf16[800,256]{1,0:T(8,128)(2,1)S(1)}, bf16[800,256]{1,0:T(8,128)(2,1)S(1)}, u32[]{:S(2)}, u32[]{:S(2)}) collective-permute-start(bf16[800,256]{1,0:T(8,128)(2,1)S(1)} %collective-permute-done.3), channel_id=1, source_target_pairs={{8,0},{12,4},{16,24},{20,28},{9,1},{13,5},{17,25},{21,29},{10,2},{... | collective-permute-start | bytes 1228808 | tf_op jit(solution)/shard_map/ppermute | solution.py:581
  22.4 27.1 %collective-permute-start.6 = (bf16[800,256]{1,0:T(8,128)(2,1)S(1)}, bf16[800,256]{1,0:T(8,128)(2,1)S(1)}, u32[]{:S(2)}, u32[]{:S(2)}) collective-permute-start(bf16[800,256]{1,0:T(8,128)(2,1)S(1)} %collective-permute-done.1.refs_2_), channel_id=1, source_target_pairs={{8,16},{12,20},{16,8},{20,12},{9,17},{13,21},{17,9},{21,13},{10,18... | collective-permute-start | bytes 1228808 | tf_op jit(solution)/shard_map/ppermute | solution.py:580
  29.5 46.3 %collective-permute-start.9 = (bf16[2,512,256]{2,1,0:T(8,128)(2,1)S(1)}, bf16[2,512,256]{2,1,0:T(8,128)(2,1)S(1)}, u32[]{:S(2)}, u32[]{:S(2)}) collective-permute-start(bf16[2,512,256]{2,1,0:T(8,128)(2,1)S(1)} %pad_maximum_fusion.1.refs_8_), channel_id=1, source_target_pairs={{0,1},{1,0},{2,3},{3,2},{4,5},{5,4},{6,7},{7,6},{8,9},{9,8},{10,11... | collective-permute-start | bytes 1572872 | tf_op jit(solution)/shard_map/ppermute | solution.py:591
  29.6 39.3 %collective-permute-start.10 = (bf16[2,512,256]{2,1,0:T(8,128)(2,1)S(1)}, bf16[2,512,256]{2,1,0:T(8,128)(2,1)S(1)}, u32[]{:S(2)}, u32[]{:S(2)}) collective-permute-start(bf16[2,512,256]{2,1,0:T(8,128)(2,1)S(1)} %pad_maximum_fusion.1.refs_8_), channel_id=1, source_target_pairs={{0,2},{1,3},{2,0},{3,1},{4,6},{5,7},{6,4},{7,5},{8,10},{9,11},{10,... | collective-permute-start | bytes 1572872 | tf_op jit(solution)/shard_map/ppermute | solution.py:592
  31.2 19.6 %collective-permute-start.2 = (bf16[800,256]{1,0:T(8,128)(2,1)S(1)}, bf16[800,256]{1,0:T(8,128)(2,1)S(1)}, u32[]{:S(2)}, u32[]{:S(2)}) collective-permute-start(bf16[800,256]{1,0:T(8,128)(2,1)S(1)} %collective-permute-done.1.refs_2_), channel_id=1, source_target_pairs={{0,4},{4,0},{8,12},{12,8},{16,20},{20,16},{24,28},{28,24},{1,5},{5... | collective-permute-start | bytes 1228808 | tf_op jit(solution)/shard_map/ppermute | solution.py:586
  48.0 17.7 %collective-permute-start.5 = (bf16[800,256]{1,0:T(8,128)(2,1)S(1)}, bf16[800,256]{1,0:T(8,128)(2,1)S(1)}, u32[]{:S(2)}, u32[]{:S(2)}) collective-permute-start(bf16[800,256]{1,0:T(8,128)(2,1)S(1)} %broadcast_select_fusion.1.refs_4_), channel_id=1, source_target_pairs={{0,4},{4,0},{8,12},{12,8},{16,20},{20,16},{24,28},{28,24},{1,5},{5... | collective-permute-start | bytes 1228808 | tf_op jit(solution)/shard_map/ppermute | solution.py:586
  49.4 14.6 %collective-permute-start.7 = (bf16[800,256]{1,0:T(8,128)(2,1)S(1)}, bf16[800,256]{1,0:T(8,128)(2,1)S(1)}, u32[]{:S(2)}, u32[]{:S(2)}) collective-permute-start(bf16[800,256]{1,0:T(8,128)(2,1)S(1)} %collective-permute-done.6), channel_id=1, source_target_pairs={{8,0},{12,4},{16,24},{20,28},{9,1},{13,5},{17,25},{21,29},{10,2},{... | collective-permute-start | bytes 1228808 | tf_op jit(solution)/shard_map/ppermute | solution.py:582
  50.9 41.4 %copy-start.7 = (bf16[2,512,256]{2,1,0:T(8,128)(2,1)}, bf16[2,512,256]{2,1,0:T(8,128)(2,1)S(1)}, u32[]{:S(2)}) copy-start(bf16[2,512,256]{2,1,0:T(8,128)(2,1)S(1)} %pad_maximum_fusion.2.refs_12_) | copy-start | bytes 1572868
  50.9 41.5 %copy-start.9 = (f32[4,16]{1,0:T(4,128)S(1)}, f32[4,16]{1,0:T(4,128)}, u32[]{:S(2)}) copy-start(f32[4,16]{1,0:T(4,128)} %param.23) | copy-start | bytes 772
  50.9 41.5 %copy-start.10 = (f32[16]{0:T(128)S(1)}, f32[16]{0:T(128)}, u32[]{:S(2)}) copy-start(f32[16]{0:T(128)} %param.25) | copy-start | bytes 196
  50.9 42.2 %copy-start.11 = (f32[16]{0:T(128)S(1)}, f32[16]{0:T(128)}, u32[]{:S(2)}) copy-start(f32[16]{0:T(128)} %param.22) | copy-start | bytes 196
  50.9 48.1 %copy-start.6 = (f32[1,2,128]{2,1,0:T(2,128)S(1)}, f32[1,2,128]{2,1,0:T(2,128)}, u32[]{:S(2)}) copy-start(f32[1,2,128]{2,1,0:T(2,128)} %param.29) | copy-start | bytes 3076
  50.9 28.1 %collective-permute-start.12 = (bf16[2,512,256]{2,1,0:T(8,128)(2,1)S(1)}, bf16[2,512,256]{2,1,0:T(8,128)(2,1)S(1)}, u32[]{:S(2)}, u32[]{:S(2)}) collective-permute-start(bf16[2,512,256]{2,1,0:T(8,128)(2,1)S(1)} %pad_maximum_fusion.2.refs_12_), channel_id=1, source_target_pairs={{0,1},{1,0},{2,3},{3,2},{4,5},{5,4},{6,7},{7,6},{8,9},{9,8},{10,11... | collective-permute-start | bytes 1572872 | tf_op jit(solution)/shard_map/ppermute | solution.py:591
  64.1 15.0 %collective-permute-start.13 = (bf16[2,512,256]{2,1,0:T(8,128)(2,1)S(1)}, bf16[2,512,256]{2,1,0:T(8,128)(2,1)}, u32[]{:S(2)}, u32[]{:S(2)}) collective-permute-start(bf16[2,512,256]{2,1,0:T(8,128)(2,1)S(1)} %pad_maximum_fusion.2.refs_12_), channel_id=1, source_target_pairs={{0,2},{1,3},{2,0},{3,1},{4,6},{5,7},{6,4},{7,5},{8,10},{9,11},{10,... | collective-permute-start | bytes 1572872 | tf_op jit(solution)/shard_map/ppermute | solution.py:592
  65.7 10.1 %collective-permute-start.8 = (bf16[800,256]{1,0:T(8,128)(2,1)S(1)}, bf16[800,256]{1,0:T(8,128)(2,1)S(1)}, u32[]{:S(2)}, u32[]{:S(2)}) collective-permute-start(bf16[800,256]{1,0:T(8,128)(2,1)S(1)} %broadcast_select_fusion.refs_6_), channel_id=1, source_target_pairs={{0,4},{4,0},{8,12},{12,8},{16,20},{20,16},{24,28},{28,24},{1,5},{5... | collective-permute-start | bytes 1228808 | tf_op jit(solution)/shard_map/ppermute | solution.py:586
  68.9 23.3 %copy-start.12 = (bf16[2,512,256]{2,1,0:T(8,128)(2,1)}, bf16[2,512,256]{2,1,0:T(8,128)(2,1)S(1)}, u32[]{:S(2)}) copy-start(bf16[2,512,256]{2,1,0:T(8,128)(2,1)S(1)} %collective-permute-done.10.refs_10_) | copy-start | bytes 1572868
  68.9 20.6 %collective-permute-start.16 = (bf16[2,512,256]{2,1,0:T(8,128)(2,1)}, bf16[2,512,256]{2,1,0:T(8,128)(2,1)}, u32[]{:S(2)}, u32[]{:S(2)}) collective-permute-start(bf16[2,512,256]{2,1,0:T(8,128)(2,1)} %pad_maximum_fusion.3.refs_16_), channel_id=1, source_target_pairs={{0,2},{1,3},{2,0},{3,1},{4,6},{5,7},{6,4},{7,5},{8,10},{9,11},{10,... | collective-permute-start | bytes 1572872 | tf_op jit(solution)/shard_map/ppermute | solution.py:592
  75.8 16.5 %copy-start.1 = (bf16[800,256]{1,0:T(8,128)(2,1)}, bf16[800,256]{1,0:T(8,128)(2,1)S(1)}, u32[]{:S(2)}) copy-start(bf16[800,256]{1,0:T(8,128)(2,1)S(1)} %collective-permute-done.8.refs_7_) | copy-start | bytes 1228804
  75.8 13.8 %collective-permute-start.11 = (bf16[2,512,256]{2,1,0:T(8,128)(2,1)S(1)}, bf16[2,512,256]{2,1,0:T(8,128)(2,1)S(1)}, u32[]{:S(2)}, u32[]{:S(2)}) collective-permute-start(bf16[2,512,256]{2,1,0:T(8,128)(2,1)S(1)} %collective-permute-done.10.refs_10_), channel_id=1, source_target_pairs={{0,1},{1,0},{2,3},{3,2},{4,5},{5,4},{6,7},{7,6},{8,9},{9,8},{10,11... | collective-permute-start | bytes 1572872 | tf_op jit(solution)/shard_map/ppermute | solution.py:593
  75.8 0.9 copy-start.3
  76.7 22.3 %collective-permute-start.15 = (bf16[2,512,256]{2,1,0:T(8,128)(2,1)}, bf16[2,512,256]{2,1,0:T(8,128)(2,1)}, u32[]{:S(2)}, u32[]{:S(2)}) collective-permute-start(bf16[2,512,256]{2,1,0:T(8,128)(2,1)} %pad_maximum_fusion.3.refs_16_), channel_id=1, source_target_pairs={{0,1},{1,0},{2,3},{3,2},{4,5},{5,4},{6,7},{7,6},{8,9},{9,8},{10,11... | collective-permute-start | bytes 1572872 | tf_op jit(solution)/shard_map/ppermute | solution.py:591
  79.0 19.9 %collective-permute-start.14 = (bf16[2,512,256]{2,1,0:T(8,128)(2,1)}, bf16[2,512,256]{2,1,0:T(8,128)(2,1)}, u32[]{:S(2)}, u32[]{:S(2)}) collective-permute-start(bf16[2,512,256]{2,1,0:T(8,128)(2,1)} %collective-permute-done.13.refs_14_), channel_id=1, source_target_pairs={{0,1},{1,0},{2,3},{3,2},{4,5},{5,4},{6,7},{7,6},{8,9},{9,8},{10,11... | collective-permute-start | bytes 1572872 | tf_op jit(solution)/shard_map/ppermute | solution.py:593
  79.0 13.2 %copy-start.13 = (bf16[2,512,256]{2,1,0:T(8,128)(2,1)}, bf16[2,512,256]{2,1,0:T(8,128)(2,1)S(1)}, u32[]{:S(2)}) copy-start(bf16[2,512,256]{2,1,0:T(8,128)(2,1)S(1)} %collective-permute-done.12.refs_13_) | copy-start | bytes 1572868
  79.0 13.2 %collective-permute-start.19 = (bf16[1,512,256]{2,1,0:T(8,128)(2,1)S(1)}, bf16[1,512,256]{2,1,0:T(8,128)(2,1)S(1)}, u32[]{:S(2)}, u32[]{:S(2)}) collective-permute-start(bf16[1,512,256]{2,1,0:T(8,128)(2,1)S(1)} %slice_bitcast_fusion.refs_20_), channel_id=1, source_target_pairs={{0,2},{1,3},{2,0},{3,1},{4,6},{5,7},{6,4},{7,5},{8,10},{9,11},{10,... | collective-permute-start | bytes 786440 | tf_op jit(solution)/shard_map/ppermute | solution.py:592
  89.5 9.5 %collective-permute-start.17 = (bf16[2,512,256]{2,1,0:T(8,128)(2,1)}, bf16[2,512,256]{2,1,0:T(8,128)(2,1)}, u32[]{:S(2)}, u32[]{:S(2)}) collective-permute-start(bf16[2,512,256]{2,1,0:T(8,128)(2,1)} %collective-permute-done.16.refs_18_), channel_id=1, source_target_pairs={{0,1},{1,0},{2,3},{3,2},{4,5},{5,4},{6,7},{7,6},{8,9},{9,8},{10,11... | collective-permute-start | bytes 1572872 | tf_op jit(solution)/shard_map/ppermute | solution.py:593
  89.5 2.7 %copy-start.14 = (bf16[2,512,256]{2,1,0:T(8,128)(2,1)}, bf16[2,512,256]{2,1,0:T(8,128)(2,1)S(1)}, u32[]{:S(2)}) copy-start(bf16[2,512,256]{2,1,0:T(8,128)(2,1)S(1)} %collective-permute-done.11.refs_11_) | copy-start | bytes 1572868
  89.5 9.5 %collective-permute-start.18 = (bf16[1,512,256]{2,1,0:T(8,128)(2,1)S(1)}, bf16[1,512,256]{2,1,0:T(8,128)(2,1)}, u32[]{:S(2)}, u32[]{:S(2)}) collective-permute-start(bf16[1,512,256]{2,1,0:T(8,128)(2,1)S(1)} %slice_bitcast_fusion.refs_20_), channel_id=1, source_target_pairs={{0,1},{1,0},{2,3},{3,2},{4,5},{5,4},{6,7},{7,6},{8,9},{9,8},{10,11... | collective-permute-start | bytes 786440 | tf_op jit(solution)/shard_map/ppermute | solution.py:591
  92.2 6.7 %collective-permute-start.20 = (bf16[1,512,256]{2,1,0:T(8,128)(2,1)S(1)}, bf16[1,512,256]{2,1,0:T(8,128)(2,1)}, u32[]{:S(2)}, u32[]{:S(2)}) collective-permute-start(bf16[1,512,256]{2,1,0:T(8,128)(2,1)S(1)} %collective-permute-done.19.refs_22_), channel_id=1, source_target_pairs={{0,1},{1,0},{2,3},{3,2},{4,5},{5,4},{6,7},{7,6},{8,9},{9,8},{10,11... | collective-permute-start | bytes 786440 | tf_op jit(solution)/shard_map/ppermute | solution.py:593
  99.0 1.0 copy-start.2
  100.0 1.0 copy-start.4
  101.1 1.0 copy-start.5
  102.1 25.9 %copy-start.8 = (f32[16,64]{1,0:T(8,128)S(1)}, f32[16,64]{1,0:T(8,128)}, u32[]{:S(2)}) copy-start(f32[16,64]{1,0:T(8,128)} %param.31) | copy-start | bytes 12292
  120.8 22.3 %all-to-all-start.1 = ((bf16[8,256,128]{2,1,0:T(8,128)(2,1)}), bf16[8,256,128]{2,1,0:T(8,128)(2,1)S(1)}, u32[]{:S(2)}, u32[]{:S(2)}) async-start(bf16[8,256,128]{2,1,0:T(8,128)(2,1)} %layer.1), calls=%async_computation.1 | async-start | bytes 1048576 | tf_op jit(solution)/shard_map/all_to_all | solution.py:620
  143.1 2.2 %copy-start = (bf16[16,64,2048]{2,1,0:T(8,128)(2,1)S(1)}, bf16[16,64,2048]{2,1,0:T(8,128)(2,1)}, u32[]{:S(2)}) copy-start(bf16[16,64,2048]{2,1,0:T(8,128)(2,1)} %param.32) | copy-start | bytes 12582916
  147.7 2.0 %collective-permute-start.21 = (bf16[2,64,2048]{2,1,0:T(8,128)(2,1)S(1)}, bf16[2,64,2048]{2,1,0:T(8,128)(2,1)S(1)}, u32[]{:S(2)}, u32[]{:S(2)}) collective-permute-start(bf16[2,64,2048]{2,1,0:T(8,128)(2,1)S(1)} %dynamic-slice_bitcast_fusion), channel_id=1, source_target_pairs={{0,1},{1,0},{2,3},{3,2},{4,5},{5,4},{6,7},{7,6},{8,9},{9,8},{10,11... | collective-permute-start | bytes 1572872 | tf_op jit(solution)/shard_map/ppermute | solution.py:627
  149.8 8.4 %collective-permute-start.22 = (bf16[64,2048]{1,0:T(8,128)(2,1)S(1)}, bf16[64,2048]{1,0:T(8,128)(2,1)S(1)}, u32[]{:S(2)}, u32[]{:S(2)}) collective-permute-start(bf16[64,2048]{1,0:T(8,128)(2,1)S(1)} %dynamic-slice_bitcast_fusion.1), channel_id=1, source_target_pairs={{0,2},{1,3},{2,0},{3,1},{4,6},{5,7},{6,4},{7,5},{8,10},{9,11},{10,... | collective-permute-start | bytes 786440 | tf_op jit(solution)/shard_map/ppermute | solution.py:631

commit v3 on v2

--- a/solution.py
+++ b/solution.py
@@ -201,6 +201,7 @@
 bf16 = jnp.bfloat16
 f32 = jnp.float32
 ROW_PAD = 16
+LANES = 128
 
 
 def matmul(left, right, dims=((1,), (0,))):
@@ -224,87 +225,109 @@
     return parts
 
 
-def pack_kernel(at, tokens, groups, steps, ids, own, payload):
-    seats, height, part = own.shape
-    rows = tokens.shape[0] // seats
-    for seat in range(seats):
-        for panel in range(height // rows):
-            own[seat, panel * rows : (panel + 1) * rows] = tokens[
-                seat * rows : (seat + 1) * rows, panel * part : (panel + 1) * part
-            ]
-    payload[:height] = own[at[0]]
-    low = height
+HBM = pl.BlockSpec(memory_space=pl.ANY)
+VMEM = pl.BlockSpec(memory_space=pltpu.VMEM)
+
+
+def pack_kernel(tokens, groups, steps, ids, payload, mine, sem):
+    rows, depth = mine.shape
+    seat = lax.axis_index("mp")
+    copy = pltpu.make_async_copy(
+        tokens.at[pl.ds(pl.multiple_of(seat * rows, rows), rows)], mine, sem
+    )
+    copy.start()
+    panels = depth // LANES
+    low = panels * rows
     payload[low : low + groups.shape[0]] = groups[...]
     low += groups.shape[0]
-    payload[low : low + steps.shape[0]] = steps[...]
-    low += steps.shape[0]
-    payload[low:] = jnp.broadcast_to(ids[...].astype(f32), (ROW_PAD, part)).astype(bf16)
-
-
-def pack(at, seats, tokens, groups, steps, ids):
+    high = steps.shape[0]
+    for part in range(steps.shape[1] // LANES):
+        payload[low : low + high] = steps[:, part * LANES : (part + 1) * LANES]
+        low += high
+    marks = ids[...].astype(f32)
+    rest = jnp.zeros((ROW_PAD - marks.shape[0], LANES), f32)
+    payload[low:] = jnp.concatenate([marks, rest], axis=0).astype(bf16)
+    copy.wait()
+    for panel in range(panels):
+        payload[panel * rows : (panel + 1) * rows] = mine[:, panel * LANES : (panel + 1) * LANES]
+
+
+def payload_rows(tokens):
+    return tokens.shape[0] // 4
+
+
+def pack(tokens, groups, steps, ids):
     rows, depth = tokens.shape
-    part = groups.shape[1]
-    height = rows * depth // (seats * part)
-    full = height + groups.shape[0] + steps.shape[0] + ROW_PAD
-    vmem = pl.BlockSpec(memory_space=pltpu.VMEM)
+    extra = steps.size // LANES + ROW_PAD
+    full = payload_rows(tokens) * depth // LANES + groups.shape[0] + extra
     return pl.pallas_call(
         pack_kernel,
-        in_specs=[pl.BlockSpec(memory_space=pltpu.SMEM)] + [vmem] * 4,
-        out_specs=[vmem, vmem],
-        out_shape=[
-            jax.ShapeDtypeStruct((seats, height, part), bf16),
-            jax.ShapeDtypeStruct((full, part), bf16),
+        in_specs=[HBM, VMEM, VMEM, VMEM],
+        out_specs=VMEM,
+        out_shape=jax.ShapeDtypeStruct((full, LANES), bf16),
+        scratch_shapes=[
+            pltpu.VMEM((payload_rows(tokens), depth), bf16),
+            pltpu.SemaphoreType.DMA,
         ],
         name="pack",
-    )(at, tokens, groups, steps, ids)
-
-
-def layer_kernel(
-    head_size, counts, table, pair, own, *refs
-):
-    ring = pair.shape[0]
-    payloads, refs = refs[: ring], refs[ring:]
+    )(tokens, groups, steps, ids)
+
+
+def layer_kernel(head_size, counts, tokens, *refs):
+    columns, refs = refs[:2], refs[2:]
+    ring, channels, slab = columns[0].shape
+    payloads, refs = refs[:ring], refs[ring:]
     pieces, refs = refs[: 4 * len(counts)], refs[4 * len(counts) :]
-    per_head, params, g_taps, g_shift, out = refs[:5]
-    tok, w_pair, w_group, st_rows, id_rows, w_x, w_step, x_all, g_all, gate_all, step_all, state, sems = refs[5:]
-    seats = own.shape[0]
-    height, part = own.shape[1:]
-    channels = out.shape[2]
+    per_head_all, params_all, g_taps, g_shift, out = refs[:5]
+    tok, w_pair, shared, w_x, w_group, w_step, x_all, g_all, gate_all, step_all, state, sems = refs[5:]
+    seats = 4
     rows = out.shape[1]
     quarter = rows // seats
-    panels = height // quarter
+    panels = tok.shape[1]
+    height = panels * quarter
+    part = 2 * g_shift.shape[1] // 2
     states = part // 2
     heads = channels // head_size
-    step_heads = st_rows.shape[1]
     lines = w_step.shape[1]
     tap_count = g_taps.shape[0]
     rim = x_all.shape[0] - ring * rows
-
-    pair_copy = pltpu.make_async_copy(pair, w_pair, sems.at[0])
-    pair_copy.start()
-    shared = []
+    step_rows = shared.shape[1] - 2 * slab - ROW_PAD
+    step_heads = step_rows * LANES // slab
+    me = lax.axis_index("seq")
+    seat = lax.axis_index("mp")
+    beside = me & 1
+    upper_half = me >> 2
+    sources = [me, me ^ 1]
+    for other in ((me >> 1) ^ 1, 2 - upper_half, 3 - 3 * upper_half):
+        sources += [2 * other + beside, 2 * other + 1 - beside]
+
+    arrivals = [2, 1, 4, 3, 6, 5, 7]
+    shared_copies = []
     for order in range(ring):
-        source = table[order]
-        low = height
-        for kind, target in enumerate((w_group, st_rows, id_rows)):
-            size = target.shape[1]
-            copy = pltpu.make_async_copy(
-                payloads[order].at[pl.ds(low, size)],
-                target.at[source],
-                sems.at[1 + ring + kind * ring + order],
-            )
-            copy.start()
-            shared.append(copy)
-            low += size
-    pltpu.make_async_copy(own, tok.at[table[0]], sems.at[1 + table[0]]).start()
-    order = 1
+        copy = pltpu.make_async_copy(
+            payloads[order].at[pl.ds(height, shared.shape[1])],
+            shared.at[sources[order]],
+            sems.at[1 + ring + order],
+        )
+        copy.start()
+        shared_copies.append(copy)
+    for kind in range(2):
+        pltpu.make_async_copy(
+            columns[kind], w_pair.at[:, pl.ds(kind * channels, channels)], sems.at[0]
+        ).start()
+    for panel in range(panels):
+        pltpu.make_async_copy(
+            tokens.at[:, pl.ds(panel * LANES, LANES)], tok.at[me, panel], sems.at[1 + me]
+        ).start()
+    order = 0
     for group, count in enumerate(counts):
         for at in range(count):
-            source = table[order]
+            source = sources[arrivals[order]]
             for hop in range(seats):
+                first = pl.multiple_of((seat ^ hop) * quarter, quarter)
                 pltpu.make_async_copy(
                     pieces[4 * group + hop].at[at],
-                    tok.at[source, table[ring + hop]],
+                    tok.at[source, :, pl.ds(first, quarter)],
                     sems.at[1 + source],
                 ).start()
             order += 1
@@ -316,33 +339,51 @@
     iota = lambda shape, dim: lax.broadcasted_iota(jnp.int32, shape, dim)
     same = one(iota((2 * channels, 2 * channels), 0) == iota((2 * channels, 2 * channels), 1))
     pick = one(
-        (iota((lines, step_heads), 0) + table[0] * heads == iota((lines, step_heads), 1))
+        (iota((lines, step_heads), 0) + me * heads == iota((lines, step_heads), 1))
         & (iota((lines, step_heads), 0) < heads)
     )
-    pair_copy.wait()
-    for copy in shared:
+    unpick = [
+        one(2 * iota((slab, 2 * slab), 0) + kind == iota((slab, 2 * slab), 1)) for kind in range(2)
+    ]
+    for copy in shared_copies:
         copy.wait()
     for panel in range(ring):
+        slab_rows = shared[panel, : 2 * slab]
+        for kind in range(2):
+            w_group[panel, :, kind * states : (kind + 1) * states] = matmul(
+                unpick[kind], slab_rows
+            ).astype(bf16)
+        step_panel = jnp.concatenate(
+            [
+                shared[panel, 2 * slab + low : 2 * slab + low + step_heads]
+                for low in range(0, step_rows, step_heads)
+            ],
+            axis=1,
+        )
+        w_step[panel] = matmul(pick, step_panel).astype(bf16)
+    pltpu.make_async_copy(w_pair, w_pair, sems.at[0]).wait()
+    for panel in range(ring):
         w_x[panel] = matmul(w_pair[panel], same, ((0,), (0,))).astype(bf16)
-        w_step[panel] = matmul(pick, st_rows[panel]).astype(bf16)
 
     upper = one(iota((rows, rows), 0) <= iota((rows, rows), 1))
     widen = one(iota((lines, channels), 1) // head_size == iota((lines, channels), 0))
     half = rows // 2
     causal = iota((half, half), 0) >= iota((half, half), 1)
     lane_head = iota((rows, channels), 1) // head_size
+    per_head = per_head_all[me]
+    params = params_all[me]
     bias, decay = per_head[:, 0:1], per_head[:, 1:2]
     skip = params[tap_count + 1 : tap_count + 2]
 
     def tok_wait(block):
-        pltpu.make_async_copy(own, tok.at[block], sems.at[1 + block]).wait()
+        pltpu.make_async_copy(tok.at[block], tok.at[block], sems.at[1 + block]).wait()
 
     def project(block):
         total_x = total_g = total_s = None
-        for panel in range(panels):
-            at = panel * quarter
+        each = panels // ring
+        for panel in range(ring):
             piece = jnp.concatenate(
-                [tok[block, seat, at : at + quarter] for seat in range(seats)], axis=0
+                [tok[block, panel * each + low] for low in range(each)], axis=1
             )
             term_x = matmul(piece, w_x[panel])
             term_g = matmul(piece, w_group[panel])
@@ -374,7 +415,10 @@
         values = values.astype(f32)
         groups = conv(g_all, base, g_taps[...], g_shift[...])
         b_rows, c_rows = groups[:, :states], groups[:, states:]
-        bucket = id_rows[block].astype(f32)[:1]
+        marks = shared[block, 2 * slab + step_rows :].astype(f32)
+        bucket = jnp.concatenate(
+            [marks[low : low + 1] for low in range(rows // LANES)], axis=1
+        )
         raw_step = step_all[block] + bias
         for entry in range(PLACE_BINS):
             raw_step = raw_step + jnp.where(
@@ -433,79 +477,98 @@
     scan(ring - 1)
 
 
-def layer(head_size, table, pair, own, payloads, groups, per_head, params, g_taps, g_shift):
-    ring, wide, slab = pair.shape
-    channels = wide // 2
-    seats, height, part = own.shape
-    rows = seats * height * part // (ring * slab)
-    step_heads = payloads[0].shape[0] - height - slab - ROW_PAD
-    lines = per_head.shape[0]
+def layer(head_size, tokens, columns, payloads, groups, per_head, params, g_taps, g_shift):
+    ring, channels, slab = columns[0].shape
+    wide = 2 * channels
+    rows, depth = tokens.shape
+    part = g_shift.shape[1]
+    lines = per_head.shape[1]
     rim = 8
     total = ring * rows
     counts = [group[0].shape[0] for group in groups]
     pieces = [piece for group in groups for piece in group]
-    vmem = pl.BlockSpec(memory_space=pltpu.VMEM)
-    anywhere = pl.BlockSpec(memory_space=pl.ANY)
+    shared_rows = payloads[0].shape[0] - payload_rows(tokens) * depth // LANES
     return pl.pallas_call(
         functools.partial(layer_kernel, head_size, counts),
-        in_specs=[pl.BlockSpec(memory_space=pltpu.SMEM)]
-        + [anywhere] * (2 + len(payloads) + len(pieces))
-        + [vmem] * 4,
-        out_specs=vmem,
+        in_specs=[HBM] * (3 + len(payloads) + len(pieces)) + [VMEM] * 4,
+        out_specs=VMEM,
         out_shape=jax.ShapeDtypeStruct((ring, rows, channels), bf16),
         scratch_shapes=[
-            pltpu.VMEM((ring, seats, height, part), bf16),
-            pltpu.VMEM(pair.shape, bf16),
+            pltpu.VMEM((ring, depth // LANES, rows, LANES), bf16),
+            pltpu.VMEM((ring, wide, slab), bf16),
+            pltpu.VMEM((ring, shared_rows, LANES), bf16),
+            pltpu.VMEM((ring, slab, wide), bf16),
             pltpu.VMEM((ring, slab, part), bf16),
-            pltpu.VMEM((ring, step_heads, part), bf16),
-            pltpu.VMEM((ring, ROW_PAD, part), bf16),
-            pltpu.VMEM((ring, slab, wide), bf16),
             pltpu.VMEM((ring, lines, slab), bf16),
             pltpu.VMEM((rim + total, channels), f32),
             pltpu.VMEM((rim + total, part), f32),
             pltpu.VMEM((ring, rows, channels), f32),
             pltpu.VMEM((ring, lines, rows), f32),
             pltpu.VMEM((part // 2, channels), f32),
-            pltpu.SemaphoreType.DMA((1 + 4 * ring,)),
+            pltpu.SemaphoreType.DMA((1 + 2 * ring,)),
         ],
-        compiler_params=pltpu.CompilerParams(vmem_limit_bytes=48 * 1024 * 1024),
+        compiler_params=pltpu.CompilerParams(vmem_limit_bytes=60 * 1024 * 1024),
         cost_estimate=pl.CostEstimate(
             flops=2 * total * ring * slab * (wide + part),
             bytes_accessed=2 * total * ring * slab,
             transcendentals=0,
         ),
         name="layer",
-    )(table, pair, own, *payloads, *pieces, per_head, params, g_taps, g_shift)
-
-
-def close_kernel(gated, gain, weight, out):
-    pieces, _, width = gated.shape
-    square = jnp.zeros(gated.shape[1:], f32)
-    total = jnp.zeros(out.shape, f32)
+    )(tokens, *columns, *payloads, *pieces, per_head, params, g_taps, g_shift)
+
+
+def close_kernel(gated, gain, weight, keep, give, landing, sems):
+    pieces, rows, width = gated.shape
+    steps, _, columns = landing.shape
+    seats = 4
+    quarter = rows // seats
+    copies = [
+        pltpu.make_async_copy(
+            weight.at[:, pl.ds(step * columns, columns)], landing.at[step], sems.at[step]
+        )
+        for step in range(steps)
+    ]
+    for copy in copies:
+        copy.start()
+    seat = lax.axis_index("mp")
+    square = jnp.zeros((rows, width), f32)
     parts = []
     for piece in range(pieces):
         part = gated[piece].astype(f32)
         square = square + part * part
         parts.append((part * gain[:, piece * width : (piece + 1) * width]).astype(bf16))
-    total = matmul(jnp.concatenate(parts, axis=1), weight[...])
+    inputs = jnp.concatenate(parts, axis=1)
     mean = jnp.sum(square, axis=1, keepdims=True) * (1.0 / (pieces * width))
-    out[...] = (total * lax.rsqrt(mean + norm_epsilon)).astype(bf16)
+    scale = lax.rsqrt(mean + norm_epsilon)
+    for step, copy in enumerate(copies):
+        copy.wait()
+        total = (matmul(inputs, landing[step]) * scale).astype(bf16)
+        at = pl.ds(step * columns, columns)
+        for core in range(2):
+
+            @pl.when((seat & 1) == core)
+            def _(core=core):
+                for owner in range(seats):
+                    block = total[owner * quarter : (owner + 1) * quarter]
+                    target = keep if owner % 2 == core else give
+                    target[(owner // 2) ^ (seat >> 1), :, at] = block
 
 
 def close(gated, gain, weight):
     pieces, rows, width = gated.shape
-    columns = 512
+    steps = 4
+    depth, columns = weight.shape
+    shape = jax.ShapeDtypeStruct((2, rows // 4, columns), bf16)
     return pl.pallas_call(
         close_kernel,
-        grid=(weight.shape[1] // columns,),
-        in_specs=[
-            pl.BlockSpec(gated.shape, lambda i: (0, 0, 0)),
-            pl.BlockSpec(gain.shape, lambda i: (0, 0)),
-            pl.BlockSpec((weight.shape[0], columns), lambda i: (0, i)),
+        in_specs=[VMEM, VMEM, HBM],
+        out_specs=[VMEM, VMEM],
+        out_shape=[shape, shape],
+        scratch_shapes=[
+            pltpu.VMEM((steps, depth, columns // steps), bf16),
+            pltpu.SemaphoreType.DMA((steps,)),
         ],
-        out_specs=pl.BlockSpec((rows, columns), lambda i: (0, i)),
-        out_shape=jax.ShapeDtypeStruct((rows, weight.shape[1]), bf16),
-        compiler_params=pltpu.CompilerParams(vmem_limit_bytes=32 * 1024 * 1024),
+        compiler_params=pltpu.CompilerParams(vmem_limit_bytes=60 * 1024 * 1024),
         cost_estimate=pl.CostEstimate(
             flops=2 * rows * weight.size, bytes_accessed=2 * weight.size, transcendentals=0
         ),
@@ -540,61 +603,31 @@
     ring = lax.axis_size("seq")
     seats = lax.axis_size("mp")
     me = lax.axis_index("seq")
-    seat = lax.axis_index("mp")
-    core = seat % 2
     channels = heads_here * head_size // ring
     heads = channels // head_size
-    line = ring // 2
     swap = lambda size, bit: [(i, i ^ bit) for i in range(size)]
     column = lambda pairs: [(2 * a + w, 2 * b + w) for a, b in pairs for w in range(2)]
-    others = [[1, 2, 3], [0, 2, 3], [3, 1, 0], [2, 1, 0]]
-    lists = []
-    for seq_at in range(ring):
-        z, x = seq_at // 2, seq_at % 2
-        sources = [seq_at, seq_at ^ 1]
-        for other in others[z]:
-            sources += [2 * other + x, 2 * other + 1 - x]
-        for seat_at in range(seats):
-            lists.append(sources + [seat_at ^ q for q in range(seats)])
-    table = lax.dynamic_index_in_dim(
-        jnp.asarray(lists, jnp.int32), lax.axis_index(("seq", "mp")), 0, False
-    )
-
-    by_channel = lambda w: jnp.transpose(w, (1, 2, 0)).reshape(ring, channels, slab)
-    pair = jnp.concatenate([by_channel(input_weight), by_channel(gate_weight)], axis=1)
-    pair = lax.all_to_all(pair, "seq", split_axis=0, concat_axis=0, tiled=True)
-
-    own, payload = pack(
-        table[ring : ring + 1],
-        seats,
+
+    payload = pack(
         tokens,
-        group_weight.reshape(slab, 2 * state_size),
+        group_weight.reshape(2 * slab, state_size),
         jnp.transpose(step_weight),
-        bucket_ids.reshape(1, rows),
+        bucket_ids.reshape(rows // LANES, LANES),
     )
     inner = (me >= 2) & (me < 6)
     outward = column([(1, 0), (2, 3)])
     middle = column([(1, 2), (2, 1)])
     near = lax.ppermute(payload, "seq", swap(ring, 2))
     mid = lax.ppermute(payload, "seq", middle)
-    mid_far = lax.ppermute(near, "seq", middle)
-    out_near = lax.ppermute(mid, "seq", outward)
-    out_far = lax.ppermute(mid_far, "seq", outward)
-    arrived = [near, jnp.where(inner, mid, out_near), jnp.where(inner, mid_far, out_far)]
-    payloads = [payload, lax.ppermute(payload, "seq", swap(ring, 1))]
-    for item in arrived:
-        payloads += [item, lax.ppermute(item, "seq", swap(ring, 1))]
-    height = own.shape[1]
-    groups = []
-    for first in range(1, ring, 2):
-        quarter = jnp.stack([item[:height] for item in payloads[first : first + 2]])
-        beside = lax.ppermute(quarter, "mp", swap(seats, 1))
-        across = lax.ppermute(quarter, "mp", swap(seats, 2))
-        groups.append((quarter, beside, across, lax.ppermute(across, "mp", swap(seats, 1))))
-
+    across_own = lax.ppermute(payload, "seq", swap(ring, 1))
+
+    by_channel = lambda w: jnp.transpose(w, (1, 2, 0)).reshape(ring, channels, slab)
+    trade = lambda w: lax.all_to_all(w, "seq", split_axis=0, concat_axis=0, tiled=True)
+    cross = lambda item: lax.ppermute(item, "seq", swap(ring, 1))
+    x_weight, gate = by_channel(input_weight), by_channel(gate_weight)
     per_head = jnp.concatenate([jnp.stack([step_bias, decay_rate]), bucket_table], axis=0)
-    per_head = lax.dynamic_slice_in_dim(jnp.transpose(per_head), me * heads, heads, 0)
-    per_head = jnp.pad(per_head, ((0, 8 - heads), (0, 0)))
+    per_head = jnp.transpose(per_head).reshape(ring, heads, -1)
+    per_head = jnp.pad(per_head, ((0, 0), (0, 8 - heads), (0, 0)))
     params = jnp.concatenate(
         [
             conv_input,
@@ -603,32 +636,51 @@
         ],
         axis=0,
     )
-    params = params.reshape(params.shape[0], ring, channels)
-    params = lax.dynamic_index_in_dim(params, me, 1, False)
-    gated = layer(
-        head_size,
-        table,
-        pair,
-        own,
-        payloads,
-        groups,
-        per_head,
-        params,
-        conv_group.reshape(tap_count, 2 * state_size),
-        conv_group_bias.reshape(1, 2 * state_size),
-    )
+    params = jnp.moveaxis(params.reshape(params.shape[0], ring, channels), 1, 0)
+    g_taps = conv_group.reshape(tap_count, 2 * state_size)
+    g_shift = conv_group_bias.reshape(1, 2 * state_size)
+    after = lambda value, *others: lax.optimization_barrier((value,) + others)[0]
+    quarter = payload_rows(tokens)
+    panels = depth // LANES
+
+    def spread(*items):
+        own = jnp.stack(
+            [item[: panels * quarter].reshape(panels, quarter, LANES) for item in items]
+        )
+        beside = lax.ppermute(own, "mp", swap(seats, 1))
+        across = lax.ppermute(own, "mp", swap(seats, 2))
+        return own, beside, across, lax.ppermute(across, "mp", swap(seats, 1))
+
+    near, mid, across_own, x_weight, per_head, params, g_taps, g_shift = lax.optimization_barrier(
+        (near, mid, across_own, x_weight, per_head, params, g_taps, g_shift)
+    )
+    mid_far = lax.ppermute(near, "seq", middle)
+    out_near = lax.ppermute(mid, "seq", outward)
+    across_near = cross(near)
+    x_weight = trade(x_weight)
+    groups = [spread(near, across_own)]
+
+    out_far = lax.ppermute(mid_far, "seq", outward)
+    second = jnp.where(inner, mid, out_near)
+    groups.append(spread(second, across_near))
+    gate = trade(after(gate, mid_far, x_weight))
+    third = jnp.where(inner, mid_far, out_far)
+    across_second = cross(after(second, across_near))
+    third = after(third, groups[0][1], groups[0][3], groups[1][2], across_second)
+    across_third = cross(third)
+    groups.append(spread(third, across_second))
+    across_third = after(across_third, groups[1][1], groups[1][3], groups[2][2])
+    groups.append(spread(across_third))
+    columns = [x_weight, gate]
+    payloads = [payload, across_own, near, across_near, second, across_second, third, across_third]
+
+    gated = layer(head_size, tokens, columns, payloads, groups, per_head, params, g_taps, g_shift)
     gated = lax.all_to_all(gated, "seq", split_axis=0, concat_axis=0, tiled=True)
-    partial = close(
-        gated, norm_gain.reshape(1, -1), out_weight.reshape(-1, out_weight.shape[2])
-    )
-    quarters = partial.reshape(seats // 2, 2, rows // seats, -1)
-    keep = lax.dynamic_index_in_dim(quarters, core, 1, False)
-    give = lax.dynamic_index_in_dim(quarters, 1 - core, 1, False)
-    both = (keep.astype(f32) + lax.ppermute(give, "mp", swap(seats, 1)).astype(f32)).astype(bf16)
-    chip = seat // 2
-    keep = lax.dynamic_index_in_dim(both, chip, 0, False)
-    give = lax.dynamic_index_in_dim(both, 1 - chip, 0, False)
-    return (keep.astype(f32) + lax.ppermute(give, "mp", swap(seats, 2)).astype(f32)).astype(bf16)
+    keep, give = close(gated, norm_gain.reshape(1, -1), out_weight.reshape(-1, depth))
+    took = lax.ppermute(give, "mp", swap(seats, 1))
+    send = (keep[1].astype(f32) + took[1].astype(f32)).astype(bf16)
+    took_far = lax.ppermute(send, "mp", swap(seats, 2))
+    return (keep[0].astype(f32) + took[0].astype(f32) + took_far.astype(f32)).astype(bf16)
 
 
 def on_device(*arrays):

time: 160 us -> 139 us (0.87)
  waiting for transfers between devices: 76.8 us -> 58.4 us
  local copies, waits for them, and re-layouts: 14.6 us -> 9.78 us
  Pallas kernels: 24.1 us -> 27.2 us
    ppermute x18, waiting for transfers between devices: 34.4 us -> 26.5 us  [the longest x3 9.06 us: tokens_travel(): cross = lambda item: lax.ppermute(item, 'seq', swap(ring, 1))]
    ppermute x1, waiting for transfers between devices: 13.9 us -> 8 us  [tokens_travel(): out_near = lax.ppermute(mid, 'seq', outward)]
    unnamed x33, local copies, waits for them, and re-layouts: 8.52 us -> 2.93 us
    all_to_all x1 -> x2, starting transfers between devices: 4.25 us -> 9.19 us  [tokens_travel(): lax.all_to_all(w, 'seq', split_axis=0, concat_axis=0, tiled=True)]
    ppermute x1, waiting for transfers between devices: 13.1 us -> 8.24 us  [tokens_travel(): out_far = lax.ppermute(mid_far, 'seq', outward)]
    ppermute x1, starting transfers between devices: 5.89 us -> 3.09 us  [tokens_travel(): near = lax.ppermute(payload, 'seq', swap(ring, 2))]
    pallas_call x2, Pallas kernels: 5.39 us -> 7.84 us  [the longest x1 5.14 us: close(): pl.pallas_call(close_kernel, in_specs=[VMEM, VMEM, HBM], out_specs=[VMEM,...]
    slice x1 -> x7, local copies, waits for them, and re-layouts: 0.61 us -> 2.98 us  [spread(): item[:panels * quarter].reshape(panels, quarter, LANES)]
  transfers between devices with their start and end apart: 25 -> 26, of which waited for: 11 -> 10; matrix products, arithmetic and copies ran while one was open for 6% -> 7% of each run, Pallas kernels for 0% -> 0%
where the time goes in v3:
time: 139 us; the launch traced here: 138 us
  waiting for transfers between devices  58.4 us (42%)
  starting transfers between devices  38 us (27%)
  Pallas kernels  27.2 us (20%)
  local copies, waits for them, and re-layouts  9.78 us (7%)
  other arithmetic  4.35 us (3%)
    pallas_call x1, Pallas kernels, layer(): pl.pallas_call(functools.partial(layer_kernel, head_size, counts), in_spe...  19.3 us
    all_to_all x1, waiting for transfers between devices, tokens_travel(): lax.all_to_all(gated, 'seq', split_axis=0, concat_axis=0, tiled=True)  14.1 us
    all_to_all x2, starting transfers between devices, tokens_travel(): lax.all_to_all(w, 'seq', split_axis=0, concat_axis=0, tiled=True)  9.19 us
    ppermute x3, waiting for transfers between devices, tokens_travel(): cross = lambda item: lax.ppermute(item, 'seq', swap(ring, 1))  9.06 us
    ppermute x1, waiting for transfers between devices, tokens_travel(): out_far = lax.ppermute(mid_far, 'seq', outward)  8.24 us
    ppermute x1, waiting for transfers between devices, tokens_travel(): out_near = lax.ppermute(mid, 'seq', outward)  8 us
    all_to_all x1, starting transfers between devices, tokens_travel(): lax.all_to_all(gated, 'seq', split_axis=0, concat_axis=0, tiled=True)  7.24 us
    ppermute x1, waiting for transfers between devices, tokens_travel(): took_far = lax.ppermute(send, 'mp', swap(seats, 2))  6.75 us
  transfers between devices with their start and end apart: 26, of which 10 were waited for; matrix products, arithmetic and copies ran while one was open for 7% of the time, Pallas kernels for 0%

profile of v3, /device:TPU:0, one launch (start us, length us, event | category | flops | bytes accessed | tf_op | source)
XLA Modules:
  0.0 138.1 jit_solution(7236298980683049115)
XLA Ops:
  0.0 2.7 %pack.1.refs_2_ = bf16[1584,128]{1,0:T(8,128)(2,1)} custom-call(bf16[256,2048]{1,0:T(8,128)(2,1)} %tokens.3, bf16[512,128]{1,0:T(8,128)(2,1)} %bitcast.46, bf16[16,256]{1,0:T(8,128)(2,1)} %bitcast.48, s32[2,128]{1,0:T(2,128)} %bitcast.51), custom_call_target="tpu_custom_call" | custom-call | tf_op jit(solution)/shard_map/pack/pallas_call | solution.py:263
  2.7 3.1 %collective-permute-start = (bf16[1584,128]{1,0:T(8,128)(2,1)}, bf16[1584,128]{1,0:T(8,128)(2,1)S(1)}, u32[]{:S(2)}, u32[]{:S(2)}) collective-permute-start(bf16[1584,128]{1,0:T(8,128)(2,1)} %pack.1.refs_2_), channel_id=1, source_target_pairs={{0,8},{4,12},{8,0},{12,4},{16,24},{20,28},{24,16},{28,20},{1,9},{5... | collective-permute-start | bytes 1216520 | tf_op jit(solution)/shard_map/ppermute | solution.py:620
  5.8 0.7 collective-permute-start.1
  6.5 1.6 %collective-permute-start.2 = (bf16[1584,128]{1,0:T(8,128)(2,1)}, bf16[1584,128]{1,0:T(8,128)(2,1)S(1)}, u32[]{:S(2)}, u32[]{:S(2)}) collective-permute-start(bf16[1584,128]{1,0:T(8,128)(2,1)} %pack.1.refs_2_), channel_id=1, source_target_pairs={{0,4},{4,0},{8,12},{12,8},{16,20},{20,16},{24,28},{28,24},{1,5},{5... | collective-permute-start | bytes 1216520 | tf_op jit(solution)/shard_map/ppermute | solution.py:622
  8.0 0.8 concatenate.12
  8.9 0.7 broadcast_in_dim.11
  9.6 0.1 broadcast_in_dim.12
  9.7 0.1 broadcast_in_dim.13
  9.8 0.8 concatenate.13
  10.5 0.7 maximum_bitcast_fusion.1
  11.3 0.1 copy.18
  11.3 1.3 copy.22
  12.6 0.6 pad.4.refs_26_
  13.2 0.6 maximum_bitcast_fusion.refs_27_
  13.8 1.5 %collective-permute-done.refs_4_ = bf16[1584,128]{1,0:T(8,128)(2,1)S(1)} collective-permute-done((bf16[1584,128]{1,0:T(8,128)(2,1)}, bf16[1584,128]{1,0:T(8,128)(2,1)S(1)}, u32[]{:S(2)}, u32[]{:S(2)}) %collective-permute-start) | collective-permute-done | bytes 405536 | tf_op jit(solution)/shard_map/ppermute | solution.py:620
  15.4 2.2 %collective-permute-done.2.refs_3_ = bf16[1584,128]{1,0:T(8,128)(2,1)S(1)} collective-permute-done((bf16[1584,128]{1,0:T(8,128)(2,1)}, bf16[1584,128]{1,0:T(8,128)(2,1)S(1)}, u32[]{:S(2)}, u32[]{:S(2)}) %collective-permute-start.2) | collective-permute-done | bytes 405536 | tf_op jit(solution)/shard_map/ppermute | solution.py:622
  17.6 1.3 collective-permute-start.5
  18.9 1.6 %collective-permute-start.4 = (bf16[1584,128]{1,0:T(8,128)(2,1)S(1)}, bf16[1584,128]{1,0:T(8,128)(2,1)S(1)}, u32[]{:S(2)}, u32[]{:S(2)}) collective-permute-start(bf16[1584,128]{1,0:T(8,128)(2,1)S(1)} %collective-permute-done.refs_4_), channel_id=1, source_target_pairs={{0,4},{4,0},{8,12},{12,8},{16,20},{20,16},{24,28},{28,24},{1,5},{5... | collective-permute-start | bytes 1216520 | tf_op jit(solution)/shard_map/ppermute | solution.py:626
  20.4 0.7 collective-permute-start.3
  21.2 0.1 pad_maximum_fusion.refs_10_
  21.3 1.6 %collective-permute-start.9 = (bf16[2,16,64,128]{3,2,1,0:T(8,128)(2,1)S(1)}, bf16[2,16,64,128]{3,2,1,0:T(8,128)(2,1)}, u32[]{:S(2)}, u32[]{:S(2)}) collective-permute-start(bf16[2,16,64,128]{3,2,1,0:T(8,128)(2,1)S(1)} %pad_maximum_fusion.refs_10_), channel_id=1, source_target_pairs={{0,2},{1,3},{2,0},{3,1},{4,6},{5,7},{6,4},{7,5},{8,10},{9,11},{10,... | collective-permute-start | bytes 1572872 | tf_op jit(solution)/shard_map/ppermute | solution.py:651
  22.8 8.0 %collective-permute-done.5 = bf16[1584,128]{1,0:T(8,128)(2,1)S(1)} collective-permute-done((bf16[1584,128]{1,0:T(8,128)(2,1)S(1)}, bf16[1584,128]{1,0:T(8,128)(2,1)S(1)}, u32[]{:S(2)}, u32[]{:S(2)}) %collective-permute-start.5) | collective-permute-done | bytes 405536 | tf_op jit(solution)/shard_map/ppermute | solution.py:658
  30.8 0.1 broadcast_select_fusion.1.refs_6_
  30.9 1.6 %collective-permute-start.6 = (bf16[1584,128]{1,0:T(8,128)(2,1)S(1)}, bf16[1584,128]{1,0:T(8,128)(2,1)}, u32[]{:S(2)}, u32[]{:S(2)}) collective-permute-start(bf16[1584,128]{1,0:T(8,128)(2,1)S(1)} %broadcast_select_fusion.1.refs_6_), channel_id=1, source_target_pairs={{0,4},{4,0},{8,12},{12,8},{16,20},{20,16},{24,28},{28,24},{1,5},{5... | collective-permute-start | bytes 1216520 | tf_op jit(solution)/shard_map/ppermute | solution.py:626
  32.5 0.0 collective-permute-done.3
  32.5 1.3 collective-permute-start.7
  33.8 4.6 %all-to-all-start = ((bf16[8,128,256]{2,1,0:T(8,128)(2,1)}), bf16[8,128,256]{2,1,0:T(8,128)(2,1)S(1)}, u32[]{:S(2)}, u32[]{:S(2)}) async-start(bf16[8,128,256]{2,1,0:T(8,128)(2,1)} %bitcast.4), calls=%async_computation | async-start | bytes 1048576 | tf_op jit(solution)/shard_map/all_to_all | solution.py:625
  38.5 1.0 slice.45
  39.4 0.1 pad_maximum_fusion.1.refs_14_
  39.5 1.6 %collective-permute-start.11 = (bf16[2,16,64,128]{3,2,1,0:T(8,128)(2,1)S(1)}, bf16[2,16,64,128]{3,2,1,0:T(8,128)(2,1)}, u32[]{:S(2)}, u32[]{:S(2)}) collective-permute-start(bf16[2,16,64,128]{3,2,1,0:T(8,128)(2,1)S(1)} %pad_maximum_fusion.1.refs_14_), channel_id=1, source_target_pairs={{0,2},{1,3},{2,0},{3,1},{4,6},{5,7},{6,4},{7,5},{8,10},{9,11},{10,... | collective-permute-start | bytes 1572872 | tf_op jit(solution)/shard_map/ppermute | solution.py:651
  41.1 0.0 collective-permute-start.8
  41.1 0.0 collective-permute-done.9.refs_12_
  41.1 0.5 collective-permute-start.10
  41.6 0.0 collective-permute-done.6.refs_7_
  41.6 0.1 collective-permute-start.13
  41.7 1.0 slice.46
  42.6 8.2 %collective-permute-done.7 = bf16[1584,128]{1,0:T(8,128)(2,1)S(1)} collective-permute-done((bf16[1584,128]{1,0:T(8,128)(2,1)S(1)}, bf16[1584,128]{1,0:T(8,128)(2,1)S(1)}, u32[]{:S(2)}, u32[]{:S(2)}) %collective-permute-start.7) | collective-permute-done | bytes 405536 | tf_op jit(solution)/shard_map/ppermute | solution.py:663
  51.0 0.1 collective-permute-start.14
  51.1 0.0 collective-permute-done.10.refs_13_
  51.1 0.1 pad_maximum_fusion.2.refs_18_
  51.2 1.6 %collective-permute-start.15 = (bf16[2,16,64,128]{3,2,1,0:T(8,128)(2,1)S(1)}, bf16[2,16,64,128]{3,2,1,0:T(8,128)(2,1)}, u32[]{:S(2)}, u32[]{:S(2)}) collective-permute-start(bf16[2,16,64,128]{3,2,1,0:T(8,128)(2,1)S(1)} %pad_maximum_fusion.2.refs_18_), channel_id=1, source_target_pairs={{0,2},{1,3},{2,0},{3,1},{4,6},{5,7},{6,4},{7,5},{8,10},{9,11},{10,... | collective-permute-start | bytes 1572872 | tf_op jit(solution)/shard_map/ppermute | solution.py:651
  52.8 1.5 %collective-permute-start.12 = (bf16[1584,128]{1,0:T(8,128)(2,1)S(1)}, bf16[1584,128]{1,0:T(8,128)(2,1)}, u32[]{:S(2)}, u32[]{:S(2)}) collective-permute-start(bf16[1584,128]{1,0:T(8,128)(2,1)S(1)} %broadcast_select_fusion.refs_8_), channel_id=1, source_target_pairs={{0,4},{4,0},{8,12},{12,8},{16,20},{20,16},{24,28},{28,24},{1,5},{5... | collective-permute-start | bytes 1216520 | tf_op jit(solution)/shard_map/ppermute | solution.py:626
  54.2 4.5 %all-to-all-start.1 = ((bf16[8,128,256]{2,1,0:T(8,128)(2,1)}), bf16[8,128,256]{2,1,0:T(8,128)(2,1)S(1)}, u32[]{:S(2)}, u32[]{:S(2)}) async-start(bf16[8,128,256]{2,1,0:T(8,128)(2,1)} %bitcast.12), calls=%async_computation.1 | async-start | bytes 1048576 | tf_op jit(solution)/shard_map/all_to_all | solution.py:625
  58.8 9.1 %collective-permute-done.12.refs_9_ = bf16[1584,128]{1,0:T(8,128)(2,1)} collective-permute-done((bf16[1584,128]{1,0:T(8,128)(2,1)S(1)}, bf16[1584,128]{1,0:T(8,128)(2,1)}, u32[]{:S(2)}, u32[]{:S(2)}) %collective-permute-start.12) | collective-permute-done | bytes 405536 | tf_op jit(solution)/shard_map/ppermute | solution.py:626
  67.9 1.0 slice.39
  68.8 0.0 copy-start.8
  68.8 0.0 copy-start.12
  68.9 0.8 collective-permute-start.19
  69.6 0.5 collective-permute-start.18
  70.1 5.3 %collective-permute-done.19.refs_24_ = bf16[1,16,64,128]{3,2,1,0:T(8,128)(2,1)} collective-permute-done((bf16[1,16,64,128]{3,2,1,0:T(8,128)(2,1)S(1)}, bf16[1,16,64,128]{3,2,1,0:T(8,128)(2,1)}, u32[]{:S(2)}, u32[]{:S(2)}) %collective-permute-start.19) | collective-permute-done | bytes 262176 | tf_op jit(solution)/shard_map/ppermute | solution.py:651
  75.4 0.8 copy-done.15
  76.2 1.1 collective-permute-done.20.refs_25_
  77.3 19.3 %layer.1 = bf16[8,256,128]{2,1,0:T(8,128)(2,1)} custom-call(bf16[256,2048]{1,0:T(8,128)(2,1)} %tokens.3, bf16[8,128,256]{2,1,0:T(8,128)(2,1)} %copy-done.4, bf16[8,128,256]{2,1,0:T(8,128)(2,1)} %copy-done.7, bf16[1584,128]{1,0:T(8,128)(2,1)} %pack.1.refs_2_, bf16[1584,128]{1,0:T(8,128)(2,1)} %copy-done.10, bf16[1584,128]{1,0:T(8,128)(2,1)} %copy-done.9, ...), custom_call_target="tpu_custom_call" | custom-call | flops 4294967296 | bytes 8388608 | tf_op jit(solution)/shard_map/layer/pallas_call | solution.py:491
  96.7 7.2 %all-to-all-start.2 = ((bf16[8,256,128]{2,1,0:T(8,128)(2,1)}), bf16[8,256,128]{2,1,0:T(8,128)(2,1)S(1)}, u32[]{:S(2)}, u32[]{:S(2)}) async-start(bf16[8,256,128]{2,1,0:T(8,128)(2,1)} %layer.1), calls=%async_computation.2 | async-start | bytes 1048576 | tf_op jit(solution)/shard_map/all_to_all | solution.py:678
  103.9 0.7 reshape.59.gain
  104.6 14.1 %all-to-all-done.2.gated = bf16[8,256,128]{2,1,0:T(8,128)(2,1)S(1)} async-done(((bf16[8,256,128]{2,1,0:T(8,128)(2,1)}), bf16[8,256,128]{2,1,0:T(8,128)(2,1)S(1)}, u32[]{:S(2)}, u32[]{:S(2)}) %all-to-all-start.2) | async-done | bytes 524320 | tf_op jit(solution)/shard_map/all_to_all | solution.py:678
  118.7 0.8 copy-done
  119.5 5.1 %close.1 = (bf16[2,64,2048]{2,1,0:T(8,128)(2,1)}, bf16[2,64,2048]{2,1,0:T(8,128)(2,1)}) custom-call(bf16[8,256,128]{2,1,0:T(8,128)(2,1)} %copy-done, f32[1,1024]{1,0:T(1,128)} %reshape.59.gain, bf16[1024,2048]{1,0:T(8,128)(2,1)} %bitcast.36), custom_call_target="tpu_custom_call" | custom-call | flops 1073741824 | bytes 4194304 | tf_op jit(solution)/shard_map/close/pallas_call | solution.py:562
  124.7 0.1 collective-permute-start.21
  124.8 2.1 %collective-permute-done.21 = bf16[2,64,2048]{2,1,0:T(8,128)(2,1)S(1)} collective-permute-done((bf16[2,64,2048]{2,1,0:T(8,128)(2,1)}, bf16[2,64,2048]{2,1,0:T(8,128)(2,1)S(1)}, u32[]{:S(2)}, u32[]{:S(2)}) %collective-permute-start.21) | collective-permute-done | bytes 524320 | tf_op jit(solution)/shard_map/ppermute | solution.py:680
  126.9 1.0 fusion.1
  127.9 1.7 %collective-permute-start.22 = (bf16[64,2048]{1,0:T(8,128)(2,1)S(1)}, bf16[64,2048]{1,0:T(8,128)(2,1)S(1)}, u32[]{:S(2)}, u32[]{:S(2)}) collective-permute-start(bf16[64,2048]{1,0:T(8,128)(2,1)S(1)} %fusion.1), channel_id=1, source_target_pairs={{0,2},{1,3},{2,0},{3,1},{4,6},{5,7},{6,4},{7,5},{8,10},{9,11},{10,... | collective-permute-start | bytes 786440 | tf_op jit(solution)/shard_map/ppermute | solution.py:682
  129.6 6.7 %collective-permute-done.22 = bf16[64,2048]{1,0:T(8,128)(2,1)S(1)} collective-permute-done((bf16[64,2048]{1,0:T(8,128)(2,1)S(1)}, bf16[64,2048]{1,0:T(8,128)(2,1)S(1)}, u32[]{:S(2)}, u32[]{:S(2)}) %collective-permute-start.22) | collective-permute-done | bytes 262176 | tf_op jit(solution)/shard_map/ppermute | solution.py:682
  136.3 1.8 %fusion = bf16[64,2048]{1,0:T(8,128)(2,1)} fusion(bf16[64,2048]{1,0:T(8,128)(2,1)S(1)} %collective-permute-done.22, bf16[2,64,2048]{2,1,0:T(8,128)(2,1)S(1)} %collective-permute-done.21, bf16[2,64,2048]{2,1,0:T(8,128)(2,1)} %get-tuple-element.31), kind=kLoop, calls=%fused_computation.4 | loop fusion | flops 786432 | bytes 1048576 | tf_op jit(solution)/shard_map/convert_element_type | solution.py:683
  (49 shorter events, 0.2 us)
Async XLA Ops:
  2.7 12.7 %collective-permute-start = (bf16[1584,128]{1,0:T(8,128)(2,1)}, bf16[1584,128]{1,0:T(8,128)(2,1)S(1)}, u32[]{:S(2)}, u32[]{:S(2)}) collective-permute-start(bf16[1584,128]{1,0:T(8,128)(2,1)} %pack.1.refs_2_), channel_id=1, source_target_pairs={{0,8},{4,12},{8,0},{12,4},{16,24},{20,28},{24,16},{28,20},{1,9},{5... | collective-permute-start | bytes 1216520 | tf_op jit(solution)/shard_map/ppermute | solution.py:620
  5.8 9.6 %collective-permute-start.1 = (bf16[1584,128]{1,0:T(8,128)(2,1)}, bf16[1584,128]{1,0:T(8,128)(2,1)S(1)}, u32[]{:S(2)}, u32[]{:S(2)}) collective-permute-start(bf16[1584,128]{1,0:T(8,128)(2,1)} %pack.1.refs_2_), channel_id=1, source_target_pairs={{8,16},{12,20},{16,8},{20,12},{9,17},{13,21},{17,9},{21,13},{10,18... | collective-permute-start | bytes 1216520 | tf_op jit(solution)/shard_map/ppermute | solution.py:621
  6.5 11.1 %collective-permute-start.2 = (bf16[1584,128]{1,0:T(8,128)(2,1)}, bf16[1584,128]{1,0:T(8,128)(2,1)S(1)}, u32[]{:S(2)}, u32[]{:S(2)}) collective-permute-start(bf16[1584,128]{1,0:T(8,128)(2,1)} %pack.1.refs_2_), channel_id=1, source_target_pairs={{0,4},{4,0},{8,12},{12,8},{16,20},{20,16},{24,28},{28,24},{1,5},{5... | collective-permute-start | bytes 1216520 | tf_op jit(solution)/shard_map/ppermute | solution.py:622
  15.4 18.4 %copy-start.9 = (bf16[1584,128]{1,0:T(8,128)(2,1)}, bf16[1584,128]{1,0:T(8,128)(2,1)S(1)}, u32[]{:S(2)}) copy-start(bf16[1584,128]{1,0:T(8,128)(2,1)S(1)} %collective-permute-done.refs_4_) | copy-start | bytes 1216516
  17.6 5.2 %copy-start.10 = (bf16[1584,128]{1,0:T(8,128)(2,1)}, bf16[1584,128]{1,0:T(8,128)(2,1)S(1)}, u32[]{:S(2)}) copy-start(bf16[1584,128]{1,0:T(8,128)(2,1)S(1)} %collective-permute-done.2.refs_3_) | copy-start | bytes 1216516
  17.6 13.2 %collective-permute-start.5 = (bf16[1584,128]{1,0:T(8,128)(2,1)S(1)}, bf16[1584,128]{1,0:T(8,128)(2,1)S(1)}, u32[]{:S(2)}, u32[]{:S(2)}) collective-permute-start(bf16[1584,128]{1,0:T(8,128)(2,1)S(1)} %collective-permute-done.1), channel_id=1, source_target_pairs={{8,0},{12,4},{16,24},{20,28},{9,1},{13,5},{17,25},{21,29},{10,2},{... | collective-permute-start | bytes 1216520 | tf_op jit(solution)/shard_map/ppermute | solution.py:658
  18.9 12.0 %collective-permute-start.4 = (bf16[1584,128]{1,0:T(8,128)(2,1)S(1)}, bf16[1584,128]{1,0:T(8,128)(2,1)S(1)}, u32[]{:S(2)}, u32[]{:S(2)}) collective-permute-start(bf16[1584,128]{1,0:T(8,128)(2,1)S(1)} %collective-permute-done.refs_4_), channel_id=1, source_target_pairs={{0,4},{4,0},{8,12},{12,8},{16,20},{20,16},{24,28},{28,24},{1,5},{5... | collective-permute-start | bytes 1216520 | tf_op jit(solution)/shard_map/ppermute | solution.py:626
  20.4 12.0 %collective-permute-start.3 = (bf16[1584,128]{1,0:T(8,128)(2,1)S(1)}, bf16[1584,128]{1,0:T(8,128)(2,1)S(1)}, u32[]{:S(2)}, u32[]{:S(2)}) collective-permute-start(bf16[1584,128]{1,0:T(8,128)(2,1)S(1)} %collective-permute-done.refs_4_), channel_id=1, source_target_pairs={{8,16},{12,20},{16,8},{20,12},{9,17},{13,21},{17,9},{21,13},{10,18... | collective-permute-start | bytes 1216520 | tf_op jit(solution)/shard_map/ppermute | solution.py:657
  21.2 33.0 %copy-start.3 = (bf16[2,16,64,128]{3,2,1,0:T(8,128)(2,1)}, bf16[2,16,64,128]{3,2,1,0:T(8,128)(2,1)S(1)}, u32[]{:S(2)}) copy-start(bf16[2,16,64,128]{3,2,1,0:T(8,128)(2,1)S(1)} %pad_maximum_fusion.refs_10_) | copy-start | bytes 1572868
  21.3 19.8 %collective-permute-start.9 = (bf16[2,16,64,128]{3,2,1,0:T(8,128)(2,1)S(1)}, bf16[2,16,64,128]{3,2,1,0:T(8,128)(2,1)}, u32[]{:S(2)}, u32[]{:S(2)}) collective-permute-start(bf16[2,16,64,128]{3,2,1,0:T(8,128)(2,1)S(1)} %pad_maximum_fusion.refs_10_), channel_id=1, source_target_pairs={{0,2},{1,3},{2,0},{3,1},{4,6},{5,7},{6,4},{7,5},{8,10},{9,11},{10,... | collective-permute-start | bytes 1572872 | tf_op jit(solution)/shard_map/ppermute | solution.py:651
  30.9 46.4 %copy-start.1 = (bf16[1584,128]{1,0:T(8,128)(2,1)}, bf16[1584,128]{1,0:T(8,128)(2,1)S(1)}, u32[]{:S(2)}) copy-start(bf16[1584,128]{1,0:T(8,128)(2,1)S(1)} %broadcast_select_fusion.1.refs_6_) | copy-start | bytes 1216516
  30.9 1.6 %copy-start.11 = (bf16[1584,128]{1,0:T(8,128)(2,1)}, bf16[1584,128]{1,0:T(8,128)(2,1)S(1)}, u32[]{:S(2)}) copy-start(bf16[1584,128]{1,0:T(8,128)(2,1)S(1)} %collective-permute-done.4.refs_5_) | copy-start | bytes 1216516
  30.9 10.7 %collective-permute-start.6 = (bf16[1584,128]{1,0:T(8,128)(2,1)S(1)}, bf16[1584,128]{1,0:T(8,128)(2,1)}, u32[]{:S(2)}, u32[]{:S(2)}) collective-permute-start(bf16[1584,128]{1,0:T(8,128)(2,1)S(1)} %broadcast_select_fusion.1.refs_6_), channel_id=1, source_target_pairs={{0,4},{4,0},{8,12},{12,8},{16,20},{20,16},{24,28},{28,24},{1,5},{5... | collective-permute-start | bytes 1216520 | tf_op jit(solution)/shard_map/ppermute | solution.py:626
  32.5 18.4 %collective-permute-start.7 = (bf16[1584,128]{1,0:T(8,128)(2,1)S(1)}, bf16[1584,128]{1,0:T(8,128)(2,1)S(1)}, u32[]{:S(2)}, u32[]{:S(2)}) collective-permute-start(bf16[1584,128]{1,0:T(8,128)(2,1)S(1)} %collective-permute-done.3), channel_id=1, source_target_pairs={{8,0},{12,4},{16,24},{20,28},{9,1},{13,5},{17,25},{21,29},{10,2},{... | collective-permute-start | bytes 1216520 | tf_op jit(solution)/shard_map/ppermute | solution.py:663
  33.8 20.4 %all-to-all-start = ((bf16[8,128,256]{2,1,0:T(8,128)(2,1)}), bf16[8,128,256]{2,1,0:T(8,128)(2,1)S(1)}, u32[]{:S(2)}, u32[]{:S(2)}) async-start(bf16[8,128,256]{2,1,0:T(8,128)(2,1)} %bitcast.4), calls=%async_computation | async-start | bytes 1048576 | tf_op jit(solution)/shard_map/all_to_all | solution.py:625
  39.5 37.8 %copy-start.5 = (bf16[2,16,64,128]{3,2,1,0:T(8,128)(2,1)}, bf16[2,16,64,128]{3,2,1,0:T(8,128)(2,1)S(1)}, u32[]{:S(2)}) copy-start(bf16[2,16,64,128]{3,2,1,0:T(8,128)(2,1)S(1)} %pad_maximum_fusion.1.refs_14_) | copy-start | bytes 1572868
  39.5 11.4 %collective-permute-start.11 = (bf16[2,16,64,128]{3,2,1,0:T(8,128)(2,1)S(1)}, bf16[2,16,64,128]{3,2,1,0:T(8,128)(2,1)}, u32[]{:S(2)}, u32[]{:S(2)}) collective-permute-start(bf16[2,16,64,128]{3,2,1,0:T(8,128)(2,1)S(1)} %pad_maximum_fusion.1.refs_14_), channel_id=1, source_target_pairs={{0,2},{1,3},{2,0},{3,1},{4,6},{5,7},{6,4},{7,5},{8,10},{9,11},{10,... | collective-permute-start | bytes 1572872 | tf_op jit(solution)/shard_map/ppermute | solution.py:651
  41.1 9.9 %collective-permute-start.8 = (bf16[2,16,64,128]{3,2,1,0:T(8,128)(2,1)S(1)}, bf16[2,16,64,128]{3,2,1,0:T(8,128)(2,1)S(1)}, u32[]{:S(2)}, u32[]{:S(2)}) collective-permute-start(bf16[2,16,64,128]{3,2,1,0:T(8,128)(2,1)S(1)} %pad_maximum_fusion.refs_10_), channel_id=1, source_target_pairs={{0,1},{1,0},{2,3},{3,2},{4,5},{5,4},{6,7},{7,6},{8,9},{9,8},{10,11... | collective-permute-start | bytes 1572872 | tf_op jit(solution)/shard_map/ppermute | solution.py:650
  41.1 10.0 %collective-permute-start.10 = (bf16[2,16,64,128]{3,2,1,0:T(8,128)(2,1)}, bf16[2,16,64,128]{3,2,1,0:T(8,128)(2,1)S(1)}, u32[]{:S(2)}, u32[]{:S(2)}) collective-permute-start(bf16[2,16,64,128]{3,2,1,0:T(8,128)(2,1)} %collective-permute-done.9.refs_12_), channel_id=1, source_target_pairs={{0,1},{1,0},{2,3},{3,2},{4,5},{5,4},{6,7},{7,6},{8,9},{9,8},{10,11... | collective-permute-start | bytes 1572872 | tf_op jit(solution)/shard_map/ppermute | solution.py:652
  41.6 17.2 %collective-permute-start.13 = (bf16[2,16,64,128]{3,2,1,0:T(8,128)(2,1)S(1)}, bf16[2,16,64,128]{3,2,1,0:T(8,128)(2,1)}, u32[]{:S(2)}, u32[]{:S(2)}) collective-permute-start(bf16[2,16,64,128]{3,2,1,0:T(8,128)(2,1)S(1)} %pad_maximum_fusion.1.refs_14_), channel_id=1, source_target_pairs={{0,1},{1,0},{2,3},{3,2},{4,5},{5,4},{6,7},{7,6},{8,9},{9,8},{10,11... | collective-permute-start | bytes 1572872 | tf_op jit(solution)/shard_map/ppermute | solution.py:650
  50.9 26.4 %copy-start.2 = (bf16[1584,128]{1,0:T(8,128)(2,1)}, bf16[1584,128]{1,0:T(8,128)(2,1)S(1)}, u32[]{:S(2)}) copy-start(bf16[1584,128]{1,0:T(8,128)(2,1)S(1)} %broadcast_select_fusion.refs_8_) | copy-start | bytes 1216516
  51.0 16.9 %collective-permute-start.14 = (bf16[2,16,64,128]{3,2,1,0:T(8,128)(2,1)}, bf16[2,16,64,128]{3,2,1,0:T(8,128)(2,1)}, u32[]{:S(2)}, u32[]{:S(2)}) collective-permute-start(bf16[2,16,64,128]{3,2,1,0:T(8,128)(2,1)} %collective-permute-done.11.refs_16_), channel_id=1, source_target_pairs={{0,1},{1,0},{2,3},{3,2},{4,5},{5,4},{6,7},{7,6},{8,9},{9,8},{10,11... | collective-permute-start | bytes 1572872 | tf_op jit(solution)/shard_map/ppermute | solution.py:652
  51.0 1.7 %copy-start.13 = (bf16[2,16,64,128]{3,2,1,0:T(8,128)(2,1)}, bf16[2,16,64,128]{3,2,1,0:T(8,128)(2,1)S(1)}, u32[]{:S(2)}) copy-start(bf16[2,16,64,128]{3,2,1,0:T(8,128)(2,1)S(1)} %collective-permute-done.8.refs_11_) | copy-start | bytes 1572868
  51.1 1.7 %copy-start.14 = (bf16[2,16,64,128]{3,2,1,0:T(8,128)(2,1)}, bf16[2,16,64,128]{3,2,1,0:T(8,128)(2,1)S(1)}, u32[]{:S(2)}) copy-start(bf16[2,16,64,128]{3,2,1,0:T(8,128)(2,1)S(1)} %collective-permute-done.10.refs_13_) | copy-start | bytes 1572868
  51.2 26.1 %copy-start.6 = (bf16[2,16,64,128]{3,2,1,0:T(8,128)(2,1)}, bf16[2,16,64,128]{3,2,1,0:T(8,128)(2,1)S(1)}, u32[]{:S(2)}) copy-start(bf16[2,16,64,128]{3,2,1,0:T(8,128)(2,1)S(1)} %pad_maximum_fusion.2.refs_18_) | copy-start | bytes 1572868
  51.2 16.7 %collective-permute-start.15 = (bf16[2,16,64,128]{3,2,1,0:T(8,128)(2,1)S(1)}, bf16[2,16,64,128]{3,2,1,0:T(8,128)(2,1)}, u32[]{:S(2)}, u32[]{:S(2)}) collective-permute-start(bf16[2,16,64,128]{3,2,1,0:T(8,128)(2,1)S(1)} %pad_maximum_fusion.2.refs_18_), channel_id=1, source_target_pairs={{0,2},{1,3},{2,0},{3,1},{4,6},{5,7},{6,4},{7,5},{8,10},{9,11},{10,... | collective-permute-start | bytes 1572872 | tf_op jit(solution)/shard_map/ppermute | solution.py:651
  52.8 15.1 %collective-permute-start.12 = (bf16[1584,128]{1,0:T(8,128)(2,1)S(1)}, bf16[1584,128]{1,0:T(8,128)(2,1)}, u32[]{:S(2)}, u32[]{:S(2)}) collective-permute-start(bf16[1584,128]{1,0:T(8,128)(2,1)S(1)} %broadcast_select_fusion.refs_8_), channel_id=1, source_target_pairs={{0,4},{4,0},{8,12},{12,8},{16,20},{20,16},{24,28},{28,24},{1,5},{5... | collective-permute-start | bytes 1216520 | tf_op jit(solution)/shard_map/ppermute | solution.py:626
  54.2 23.1 %copy-start.4 = (bf16[8,128,256]{2,1,0:T(8,128)(2,1)}, bf16[8,128,256]{2,1,0:T(8,128)(2,1)S(1)}, u32[]{:S(2)}) copy-start(bf16[8,128,256]{2,1,0:T(8,128)(2,1)S(1)} %all-to-all-done.refs_0_) | copy-start | bytes 1572868
  54.2 22.0 %all-to-all-start.1 = ((bf16[8,128,256]{2,1,0:T(8,128)(2,1)}), bf16[8,128,256]{2,1,0:T(8,128)(2,1)S(1)}, u32[]{:S(2)}, u32[]{:S(2)}) async-start(bf16[8,128,256]{2,1,0:T(8,128)(2,1)} %bitcast.12), calls=%async_computation.1 | async-start | bytes 1048576 | tf_op jit(solution)/shard_map/all_to_all | solution.py:625
  58.8 16.6 %collective-permute-start.16 = (bf16[2,16,64,128]{3,2,1,0:T(8,128)(2,1)S(1)}, bf16[2,16,64,128]{3,2,1,0:T(8,128)(2,1)S(1)}, u32[]{:S(2)}, u32[]{:S(2)}) collective-permute-start(bf16[2,16,64,128]{3,2,1,0:T(8,128)(2,1)S(1)} %pad_maximum_fusion.2.refs_18_), channel_id=1, source_target_pairs={{0,1},{1,0},{2,3},{3,2},{4,5},{5,4},{6,7},{7,6},{8,9},{9,8},{10,11... | collective-permute-start | bytes 1572872 | tf_op jit(solution)/shard_map/ppermute | solution.py:650
  68.8 8.5 %copy-start.8 = (bf16[1024,128]{1,0:T(8,128)(2,1)}, bf16[1024,128]{1,0:T(8,128)(2,1)S(1)}, u32[]{:S(2)}) copy-start(bf16[1024,128]{1,0:T(8,128)(2,1)S(1)} %slice.39) | copy-start | bytes 786436
  68.8 35.1 %copy-start.12 = (f32[16,64]{1,0:T(8,128)S(1)}, f32[16,64]{1,0:T(8,128)}, u32[]{:S(2)}) copy-start(f32[16,64]{1,0:T(8,128)} %param.30) | copy-start | bytes 12292
  68.9 6.5 %collective-permute-start.19 = (bf16[1,16,64,128]{3,2,1,0:T(8,128)(2,1)S(1)}, bf16[1,16,64,128]{3,2,1,0:T(8,128)(2,1)}, u32[]{:S(2)}, u32[]{:S(2)}) collective-permute-start(bf16[1,16,64,128]{3,2,1,0:T(8,128)(2,1)S(1)} %bitcast.43), channel_id=1, source_target_pairs={{0,2},{1,3},{2,0},{3,1},{4,6},{5,7},{6,4},{7,5},{8,10},{9,11},{10,... | collective-permute-start | bytes 786440 | tf_op jit(solution)/shard_map/ppermute | solution.py:651
  69.6 7.7 %collective-permute-start.17 = (bf16[2,16,64,128]{3,2,1,0:T(8,128)(2,1)}, bf16[2,16,64,128]{3,2,1,0:T(8,128)(2,1)}, u32[]{:S(2)}, u32[]{:S(2)}) collective-permute-start(bf16[2,16,64,128]{3,2,1,0:T(8,128)(2,1)} %collective-permute-done.15.refs_20_), channel_id=1, source_target_pairs={{0,1},{1,0},{2,3},{3,2},{4,5},{5,4},{6,7},{7,6},{8,9},{9,8},{10,11... | collective-permute-start | bytes 1572872 | tf_op jit(solution)/shard_map/ppermute | solution.py:652
  69.6 6.6 %collective-permute-start.18 = (bf16[1,16,64,128]{3,2,1,0:T(8,128)(2,1)S(1)}, bf16[1,16,64,128]{3,2,1,0:T(8,128)(2,1)}, u32[]{:S(2)}, u32[]{:S(2)}) collective-permute-start(bf16[1,16,64,128]{3,2,1,0:T(8,128)(2,1)S(1)} %bitcast.44), channel_id=1, source_target_pairs={{0,1},{1,0},{2,3},{3,2},{4,5},{5,4},{6,7},{7,6},{8,9},{9,8},{10,11... | collective-permute-start | bytes 786440 | tf_op jit(solution)/shard_map/ppermute | solution.py:650
  75.4 1.9 %collective-permute-start.20 = (bf16[1,16,64,128]{3,2,1,0:T(8,128)(2,1)}, bf16[1,16,64,128]{3,2,1,0:T(8,128)(2,1)}, u32[]{:S(2)}, u32[]{:S(2)}) collective-permute-start(bf16[1,16,64,128]{3,2,1,0:T(8,128)(2,1)} %collective-permute-done.19.refs_24_), channel_id=1, source_target_pairs={{0,1},{1,0},{2,3},{3,2},{4,5},{5,4},{6,7},{7,6},{8,9},{9,8},{10,11... | collective-permute-start | bytes 786440 | tf_op jit(solution)/shard_map/ppermute | solution.py:652
  75.4 0.8 copy-start.15
  76.2 1.1 copy-start.7
  96.7 22.1 %all-to-all-start.2 = ((bf16[8,256,128]{2,1,0:T(8,128)(2,1)}), bf16[8,256,128]{2,1,0:T(8,128)(2,1)S(1)}, u32[]{:S(2)}, u32[]{:S(2)}) async-start(bf16[8,256,128]{2,1,0:T(8,128)(2,1)} %layer.1), calls=%async_computation.2 | async-start | bytes 1048576 | tf_op jit(solution)/shard_map/all_to_all | solution.py:678
  118.7 0.8 copy-start
  124.7 2.2 %collective-permute-start.21 = (bf16[2,64,2048]{2,1,0:T(8,128)(2,1)}, bf16[2,64,2048]{2,1,0:T(8,128)(2,1)S(1)}, u32[]{:S(2)}, u32[]{:S(2)}) collective-permute-start(bf16[2,64,2048]{2,1,0:T(8,128)(2,1)} %get-tuple-element.32), channel_id=1, source_target_pairs={{0,1},{1,0},{2,3},{3,2},{4,5},{5,4},{6,7},{7,6},{8,9},{9,8},{10,11... | collective-permute-start | bytes 1572872 | tf_op jit(solution)/shard_map/ppermute | solution.py:680
  127.9 8.4 %collective-permute-start.22 = (bf16[64,2048]{1,0:T(8,128)(2,1)S(1)}, bf16[64,2048]{1,0:T(8,128)(2,1)S(1)}, u32[]{:S(2)}, u32[]{:S(2)}) collective-permute-start(bf16[64,2048]{1,0:T(8,128)(2,1)S(1)} %fusion.1), channel_id=1, source_target_pairs={{0,2},{1,3},{2,0},{3,1},{4,6},{5,7},{6,4},{7,5},{8,10},{9,11},{10,... | collective-permute-start | bytes 786440 | tf_op jit(solution)/shard_map/ppermute | solution.py:682

commit v4 on v3

--- a/solution.py
+++ b/solution.py
@@ -279,7 +279,7 @@
     payloads, refs = refs[:ring], refs[ring:]
     pieces, refs = refs[: 4 * len(counts)], refs[4 * len(counts) :]
     per_head_all, params_all, g_taps, g_shift, out = refs[:5]
-    tok, w_pair, shared, w_x, w_group, w_step, x_all, g_all, gate_all, step_all, state, sems = refs[5:]
+    tok, shared, w_x, w_group, w_step, x_all, g_all, gate_all, step_all, state, sems = refs[5:]
     seats = 4
     rows = out.shape[1]
     quarter = rows // seats
@@ -313,7 +313,7 @@
         shared_copies.append(copy)
     for kind in range(2):
         pltpu.make_async_copy(
-            columns[kind], w_pair.at[:, pl.ds(kind * channels, channels)], sems.at[0]
+            columns[kind], w_x.at[:, pl.ds(kind * channels, channels)], sems.at[0]
         ).start()
     for panel in range(panels):
         pltpu.make_async_copy(
@@ -337,7 +337,6 @@
     state[...] = jnp.zeros_like(state)
     one = lambda flag: flag.astype(f32).astype(bf16)
     iota = lambda shape, dim: lax.broadcasted_iota(jnp.int32, shape, dim)
-    same = one(iota((2 * channels, 2 * channels), 0) == iota((2 * channels, 2 * channels), 1))
     pick = one(
         (iota((lines, step_heads), 0) + me * heads == iota((lines, step_heads), 1))
         & (iota((lines, step_heads), 0) < heads)
@@ -361,9 +360,7 @@
             axis=1,
         )
         w_step[panel] = matmul(pick, step_panel).astype(bf16)
-    pltpu.make_async_copy(w_pair, w_pair, sems.at[0]).wait()
-    for panel in range(ring):
-        w_x[panel] = matmul(w_pair[panel], same, ((0,), (0,))).astype(bf16)
+    pltpu.make_async_copy(w_x, w_x, sems.at[0]).wait()
 
     upper = one(iota((rows, rows), 0) <= iota((rows, rows), 1))
     widen = one(iota((lines, channels), 1) // head_size == iota((lines, channels), 0))
@@ -385,7 +382,7 @@
             piece = jnp.concatenate(
                 [tok[block, panel * each + low] for low in range(each)], axis=1
             )
-            term_x = matmul(piece, w_x[panel])
+            term_x = matmul(piece, w_x[panel], ((1,), (1,)))
             term_g = matmul(piece, w_group[panel])
             term_s = matmul(w_step[panel], piece, ((1,), (1,)))
             total_x = term_x if total_x is None else total_x + term_x
@@ -460,21 +457,24 @@
         held = state[...]
         scanned = within + grown * matmul(c_rows, held.astype(bf16)) + skip * values
         scanned = scanned.astype(bf16).astype(f32)
-        out[block] = (scanned * silu(gate_all[block])).astype(bf16)
+        out[me ^ block] = (scanned * silu(gate_all[block])).astype(bf16)
         injected = matmul(b_rows, (left * values).astype(bf16), ((0,), (0,)))
         state[...] = grown[rows - 1 : rows] * held + injected
 
-    tok_wait(0)
-    project(0)
-
-    def advance(block, carry):
-        tok_wait(block + 1)
-        scan(block)
-        project(block + 1)
+    def project_step(step, carry):
+        for low in range(1):
+            tok_wait(1 * step + low)
+            project(1 * step + low)
         return carry
 
-    lax.fori_loop(0, ring - 1, advance, 0)
-    scan(ring - 1)
+    lax.fori_loop(0, ring // 1, project_step, 0)
+
+    def advance(step, carry):
+        for low in range(8):
+            scan(8 * step + low)
+        return carry
+
+    lax.fori_loop(0, ring // 8, advance, 0)
 
 
 def layer(head_size, tokens, columns, payloads, groups, per_head, params, g_taps, g_shift):
@@ -495,9 +495,8 @@
         out_shape=jax.ShapeDtypeStruct((ring, rows, channels), bf16),
         scratch_shapes=[
             pltpu.VMEM((ring, depth // LANES, rows, LANES), bf16),
+            pltpu.VMEM((ring, shared_rows, LANES), bf16),
             pltpu.VMEM((ring, wide, slab), bf16),
-            pltpu.VMEM((ring, shared_rows, LANES), bf16),
-            pltpu.VMEM((ring, slab, wide), bf16),
             pltpu.VMEM((ring, slab, part), bf16),
             pltpu.VMEM((ring, lines, slab), bf16),
             pltpu.VMEM((rim + total, channels), f32),
@@ -517,33 +516,25 @@
     )(tokens, *columns, *payloads, *pieces, per_head, params, g_taps, g_shift)
 
 
-def close_kernel(gated, gain, weight, keep, give, landing, sems):
-    pieces, rows, width = gated.shape
-    steps, _, columns = landing.shape
+def close_kernel(offsets, gain, weight, *refs):
+    parts, (keep, give, inputs) = refs[:-3], refs[-3:]
+    rows, width = parts[0].shape
     seats = 4
     quarter = rows // seats
-    copies = [
-        pltpu.make_async_copy(
-            weight.at[:, pl.ds(step * columns, columns)], landing.at[step], sems.at[step]
-        )
-        for step in range(steps)
-    ]
-    for copy in copies:
-        copy.start()
+    columns = weight.shape[1] // 4
+    me = lax.axis_index("seq")
     seat = lax.axis_index("mp")
     square = jnp.zeros((rows, width), f32)
-    parts = []
-    for piece in range(pieces):
-        part = gated[piece].astype(f32)
-        square = square + part * part
-        parts.append((part * gain[:, piece * width : (piece + 1) * width]).astype(bf16))
-    inputs = jnp.concatenate(parts, axis=1)
-    mean = jnp.sum(square, axis=1, keepdims=True) * (1.0 / (pieces * width))
+    for offset, part in zip(offsets, parts):
+        value = part[...].astype(f32)
+        square = square + value * value
+        at = pl.multiple_of((me ^ offset) * width, width)
+        inputs[:, pl.ds(at, width)] = (value * gain[:, pl.ds(at, width)]).astype(bf16)
+    mean = jnp.sum(square, axis=1, keepdims=True) * (1.0 / (len(parts) * width))
     scale = lax.rsqrt(mean + norm_epsilon)
-    for step, copy in enumerate(copies):
-        copy.wait()
-        total = (matmul(inputs, landing[step]) * scale).astype(bf16)
+    for step in range(4):
         at = pl.ds(step * columns, columns)
+        total = (matmul(inputs[...], weight[:, at]) * scale).astype(bf16)
         for core in range(2):
 
             @pl.when((seat & 1) == core)
@@ -554,26 +545,21 @@
                     target[(owner // 2) ^ (seat >> 1), :, at] = block
 
 
-def close(gated, gain, weight):
-    pieces, rows, width = gated.shape
-    steps = 4
-    depth, columns = weight.shape
-    shape = jax.ShapeDtypeStruct((2, rows // 4, columns), bf16)
+def close(offsets, gain, weight, parts):
+    rows, width = parts[0].shape
+    shape = jax.ShapeDtypeStruct((2, rows // 4, weight.shape[1]), bf16)
     return pl.pallas_call(
-        close_kernel,
-        in_specs=[VMEM, VMEM, HBM],
-        out_specs=[VMEM, VMEM],
+        functools.partial(close_kernel, offsets),
+        in_specs=[VMEM] * (2 + len(parts)),
+        out_specs=[VMEM] * 2,
         out_shape=[shape, shape],
-        scratch_shapes=[
-            pltpu.VMEM((steps, depth, columns // steps), bf16),
-            pltpu.SemaphoreType.DMA((steps,)),
-        ],
-        compiler_params=pltpu.CompilerParams(vmem_limit_bytes=60 * 1024 * 1024),
+        scratch_shapes=[pltpu.VMEM((rows, len(parts) * width), bf16)],
+        compiler_params=pltpu.CompilerParams(vmem_limit_bytes=16 * 1024 * 1024),
         cost_estimate=pl.CostEstimate(
             flops=2 * rows * weight.size, bytes_accessed=2 * weight.size, transcendentals=0
         ),
         name="close",
-    )(gated, gain, weight)
+    )(gain, weight, *parts)
 
 
 def tokens_travel(
@@ -675,8 +661,10 @@
     payloads = [payload, across_own, near, across_near, second, across_second, third, across_third]
 
     gated = layer(head_size, tokens, columns, payloads, groups, per_head, params, g_taps, g_shift)
-    gated = lax.all_to_all(gated, "seq", split_axis=0, concat_axis=0, tiled=True)
-    keep, give = close(gated, norm_gain.reshape(1, -1), out_weight.reshape(-1, depth))
+    offsets = (6, 7, 5, 4, 3, 2, 1)
+    parts = [lax.ppermute(gated[at], "seq", swap(ring, at)) for at in offsets] + [gated[0]]
+    gain, weight = norm_gain.reshape(1, -1), out_weight.reshape(-1, depth)
+    keep, give = close(offsets + (0,), gain, weight, parts)
     took = lax.ppermute(give, "mp", swap(seats, 1))
     send = (keep[1].astype(f32) + took[1].astype(f32)).astype(bf16)
     took_far = lax.ppermute(send, "mp", swap(seats, 2))

time: 139 us -> 131 us (0.942)
  waiting for transfers between devices: 58.4 us -> 47.2 us
  starting transfers between devices: 38 us -> 45.5 us
  Pallas kernels: 27.2 us -> 22.2 us
  local copies, waits for them, and re-layouts: 9.78 us -> 11.7 us
  other arithmetic: 4.35 us -> 2.43 us
    ppermute x0 -> x7, starting transfers between devices: none -> 15 us  [tokens_travel(): lax.ppermute(gated[at], 'seq', swap(ring, at))]
    all_to_all x1 -> x0, waiting for transfers between devices: 14.1 us -> none  [tokens_travel(): lax.all_to_all(gated, 'seq', split_axis=0, concat_axis=0, tiled=True)]
    all_to_all x1 -> x0, starting transfers between devices: 7.24 us -> none  [tokens_travel(): lax.all_to_all(gated, 'seq', split_axis=0, concat_axis=0, tiled=True)]
    pallas_call x1, Pallas kernels: 5.14 us -> 2.03 us  [close(): pl.pallas_call(functools.partial(close_kernel, offsets), in_specs=[VMEM]...]
    ppermute x0 -> x7, waiting for transfers between devices: none -> 2.97 us  [tokens_travel(): lax.ppermute(gated[at], 'seq', swap(ring, at))]
    pallas_call x1, Pallas kernels: 19.3 us -> 17.5 us  [layer(): pl.pallas_call(functools.partial(layer_kernel, head_size, counts), in_spe...]
    unnamed x33, local copies, waits for them, and re-layouts: 2.93 us -> 4.33 us
  transfers between devices with their start and end apart: 26 -> 32, of which waited for: 10 -> 13; matrix products, arithmetic and copies ran while one was open for 7% -> 7% of each run, Pallas kernels for 0% -> 0%
where the time goes in v4:
time: 131 us; the launch traced here: 129 us
  waiting for transfers between devices  47.2 us (36%)
  starting transfers between devices  45.5 us (35%)
  Pallas kernels  22.2 us (17%)
  local copies, waits for them, and re-layouts  11.7 us (9%)
  other arithmetic  2.43 us (2%)
    pallas_call x1, Pallas kernels, layer(): pl.pallas_call(functools.partial(layer_kernel, head_size, counts), in_spe...  17.5 us
    ppermute x7, starting transfers between devices, tokens_travel(): lax.ppermute(gated[at], 'seq', swap(ring, at))  15 us
    all_to_all x2, starting transfers between devices, tokens_travel(): lax.all_to_all(w, 'seq', split_axis=0, concat_axis=0, tiled=True)  9.2 us
    ppermute x3, waiting for transfers between devices, tokens_travel(): cross = lambda item: lax.ppermute(item, 'seq', swap(ring, 1))  9.06 us
    ppermute x1, waiting for transfers between devices, tokens_travel(): out_far = lax.ppermute(mid_far, 'seq', outward)  8.24 us
    ppermute x1, waiting for transfers between devices, tokens_travel(): out_near = lax.ppermute(mid, 'seq', outward)  7.99 us
    ppermute x1, waiting for transfers between devices, tokens_travel(): took_far = lax.ppermute(send, 'mp', swap(seats, 2))  7 us
    ppermute x4, starting transfers between devices, spread(): across = lax.ppermute(own, 'mp', swap(seats, 2))  5.52 us
  transfers between devices with their start and end apart: 32, of which 13 were waited for; matrix products, arithmetic and copies ran while one was open for 7% of the time, Pallas kernels for 0%

profile of v4, /device:TPU:0, one launch (start us, length us, event | category | flops | bytes accessed | tf_op | source)
XLA Modules:
  0.0 129.5 jit_solution(9579338383334832217)
XLA Ops:
  0.0 2.7 %pack.1.refs_2_ = bf16[1584,128]{1,0:T(8,128)(2,1)} custom-call(bf16[256,2048]{1,0:T(8,128)(2,1)} %tokens.3, bf16[512,128]{1,0:T(8,128)(2,1)} %bitcast.62, bf16[16,256]{1,0:T(8,128)(2,1)} %bitcast.64, s32[2,128]{1,0:T(2,128)} %bitcast.67), custom_call_target="tpu_custom_call" | custom-call | tf_op jit(solution)/shard_map/pack/pallas_call | solution.py:263
  2.7 3.1 %collective-permute-start = (bf16[1584,128]{1,0:T(8,128)(2,1)}, bf16[1584,128]{1,0:T(8,128)(2,1)S(1)}, u32[]{:S(2)}, u32[]{:S(2)}) collective-permute-start(bf16[1584,128]{1,0:T(8,128)(2,1)} %pack.1.refs_2_), channel_id=1, source_target_pairs={{0,8},{4,12},{8,0},{12,4},{16,24},{20,28},{24,16},{28,20},{1,9},{5... | collective-permute-start | bytes 1216520 | tf_op jit(solution)/shard_map/ppermute | solution.py:606
  5.8 0.7 collective-permute-start.1
  6.5 1.6 %collective-permute-start.2 = (bf16[1584,128]{1,0:T(8,128)(2,1)}, bf16[1584,128]{1,0:T(8,128)(2,1)S(1)}, u32[]{:S(2)}, u32[]{:S(2)}) collective-permute-start(bf16[1584,128]{1,0:T(8,128)(2,1)} %pack.1.refs_2_), channel_id=1, source_target_pairs={{0,4},{4,0},{8,12},{12,8},{16,20},{20,16},{24,28},{28,24},{1,5},{5... | collective-permute-start | bytes 1216520 | tf_op jit(solution)/shard_map/ppermute | solution.py:608
  8.1 0.8 concatenate.12
  8.9 0.7 broadcast_in_dim.11
  9.6 0.1 broadcast_in_dim.12
  9.7 0.1 broadcast_in_dim.13
  9.8 0.8 concatenate.13
  10.6 0.7 maximum_bitcast_fusion.1
  11.3 0.1 copy.18
  11.4 1.3 copy.22
  12.6 0.6 pad.4.refs_26_
  13.3 0.6 maximum_bitcast_fusion.refs_27_
  13.9 1.5 %collective-permute-done.refs_4_ = bf16[1584,128]{1,0:T(8,128)(2,1)S(1)} collective-permute-done((bf16[1584,128]{1,0:T(8,128)(2,1)}, bf16[1584,128]{1,0:T(8,128)(2,1)S(1)}, u32[]{:S(2)}, u32[]{:S(2)}) %collective-permute-start) | collective-permute-done | bytes 405536 | tf_op jit(solution)/shard_map/ppermute | solution.py:606
  15.4 2.2 %collective-permute-done.2.refs_3_ = bf16[1584,128]{1,0:T(8,128)(2,1)S(1)} collective-permute-done((bf16[1584,128]{1,0:T(8,128)(2,1)}, bf16[1584,128]{1,0:T(8,128)(2,1)S(1)}, u32[]{:S(2)}, u32[]{:S(2)}) %collective-permute-start.2) | collective-permute-done | bytes 405536 | tf_op jit(solution)/shard_map/ppermute | solution.py:608
  17.6 1.3 collective-permute-start.5
  18.9 1.6 %collective-permute-start.4 = (bf16[1584,128]{1,0:T(8,128)(2,1)S(1)}, bf16[1584,128]{1,0:T(8,128)(2,1)S(1)}, u32[]{:S(2)}, u32[]{:S(2)}) collective-permute-start(bf16[1584,128]{1,0:T(8,128)(2,1)S(1)} %collective-permute-done.refs_4_), channel_id=1, source_target_pairs={{0,4},{4,0},{8,12},{12,8},{16,20},{20,16},{24,28},{28,24},{1,5},{5... | collective-permute-start | bytes 1216520 | tf_op jit(solution)/shard_map/ppermute | solution.py:612
  20.5 0.7 collective-permute-start.3
  21.2 0.1 pad_maximum_fusion.refs_10_
  21.3 1.6 %collective-permute-start.9 = (bf16[2,16,64,128]{3,2,1,0:T(8,128)(2,1)S(1)}, bf16[2,16,64,128]{3,2,1,0:T(8,128)(2,1)}, u32[]{:S(2)}, u32[]{:S(2)}) collective-permute-start(bf16[2,16,64,128]{3,2,1,0:T(8,128)(2,1)S(1)} %pad_maximum_fusion.refs_10_), channel_id=1, source_target_pairs={{0,2},{1,3},{2,0},{3,1},{4,6},{5,7},{6,4},{7,5},{8,10},{9,11},{10,... | collective-permute-start | bytes 1572872 | tf_op jit(solution)/shard_map/ppermute | solution.py:637
  22.9 8.0 %collective-permute-done.5 = bf16[1584,128]{1,0:T(8,128)(2,1)S(1)} collective-permute-done((bf16[1584,128]{1,0:T(8,128)(2,1)S(1)}, bf16[1584,128]{1,0:T(8,128)(2,1)S(1)}, u32[]{:S(2)}, u32[]{:S(2)}) %collective-permute-start.5) | collective-permute-done | bytes 405536 | tf_op jit(solution)/shard_map/ppermute | solution.py:644
  30.9 1.6 %collective-permute-start.6 = (bf16[1584,128]{1,0:T(8,128)(2,1)S(1)}, bf16[1584,128]{1,0:T(8,128)(2,1)}, u32[]{:S(2)}, u32[]{:S(2)}) collective-permute-start(bf16[1584,128]{1,0:T(8,128)(2,1)S(1)} %broadcast_select_fusion.1.refs_6_), channel_id=1, source_target_pairs={{0,4},{4,0},{8,12},{12,8},{16,20},{20,16},{24,28},{28,24},{1,5},{5... | collective-permute-start | bytes 1216520 | tf_op jit(solution)/shard_map/ppermute | solution.py:612
  32.5 1.3 collective-permute-start.7
  33.8 4.7 %all-to-all-start = ((bf16[8,128,256]{2,1,0:T(8,128)(2,1)}), bf16[8,128,256]{2,1,0:T(8,128)(2,1)S(1)}, u32[]{:S(2)}, u32[]{:S(2)}) async-start(bf16[8,128,256]{2,1,0:T(8,128)(2,1)} %bitcast.5), calls=%async_computation | async-start | bytes 1048576 | tf_op jit(solution)/shard_map/all_to_all | solution.py:611
  38.5 1.0 slice.77
  39.5 0.1 pad_maximum_fusion.1.refs_14_
  39.5 1.6 %collective-permute-start.11 = (bf16[2,16,64,128]{3,2,1,0:T(8,128)(2,1)S(1)}, bf16[2,16,64,128]{3,2,1,0:T(8,128)(2,1)}, u32[]{:S(2)}, u32[]{:S(2)}) collective-permute-start(bf16[2,16,64,128]{3,2,1,0:T(8,128)(2,1)S(1)} %pad_maximum_fusion.1.refs_14_), channel_id=1, source_target_pairs={{0,2},{1,3},{2,0},{3,1},{4,6},{5,7},{6,4},{7,5},{8,10},{9,11},{10,... | collective-permute-start | bytes 1572872 | tf_op jit(solution)/shard_map/ppermute | solution.py:637
  41.1 0.5 collective-permute-start.10
  41.6 0.1 collective-permute-start.13
  41.7 1.0 slice.78
  42.7 8.2 %collective-permute-done.7 = bf16[1584,128]{1,0:T(8,128)(2,1)S(1)} collective-permute-done((bf16[1584,128]{1,0:T(8,128)(2,1)S(1)}, bf16[1584,128]{1,0:T(8,128)(2,1)S(1)}, u32[]{:S(2)}, u32[]{:S(2)}) %collective-permute-start.7) | collective-permute-done | bytes 405536 | tf_op jit(solution)/shard_map/ppermute | solution.py:649
  51.0 0.1 collective-permute-start.14
  51.2 1.6 %collective-permute-start.15 = (bf16[2,16,64,128]{3,2,1,0:T(8,128)(2,1)S(1)}, bf16[2,16,64,128]{3,2,1,0:T(8,128)(2,1)}, u32[]{:S(2)}, u32[]{:S(2)}) collective-permute-start(bf16[2,16,64,128]{3,2,1,0:T(8,128)(2,1)S(1)} %pad_maximum_fusion.2.refs_18_), channel_id=1, source_target_pairs={{0,2},{1,3},{2,0},{3,1},{4,6},{5,7},{6,4},{7,5},{8,10},{9,11},{10,... | collective-permute-start | bytes 1572872 | tf_op jit(solution)/shard_map/ppermute | solution.py:637
  52.8 1.5 %collective-permute-start.12 = (bf16[1584,128]{1,0:T(8,128)(2,1)S(1)}, bf16[1584,128]{1,0:T(8,128)(2,1)}, u32[]{:S(2)}, u32[]{:S(2)}) collective-permute-start(bf16[1584,128]{1,0:T(8,128)(2,1)S(1)} %broadcast_select_fusion.refs_8_), channel_id=1, source_target_pairs={{0,4},{4,0},{8,12},{12,8},{16,20},{20,16},{24,28},{28,24},{1,5},{5... | collective-permute-start | bytes 1216520 | tf_op jit(solution)/shard_map/ppermute | solution.py:612
  54.3 4.5 %all-to-all-start.1 = ((bf16[8,128,256]{2,1,0:T(8,128)(2,1)}), bf16[8,128,256]{2,1,0:T(8,128)(2,1)S(1)}, u32[]{:S(2)}, u32[]{:S(2)}) async-start(bf16[8,128,256]{2,1,0:T(8,128)(2,1)} %bitcast.13), calls=%async_computation.1 | async-start | bytes 1048576 | tf_op jit(solution)/shard_map/all_to_all | solution.py:611
  58.8 9.1 %collective-permute-done.12.refs_9_ = bf16[1584,128]{1,0:T(8,128)(2,1)} collective-permute-done((bf16[1584,128]{1,0:T(8,128)(2,1)S(1)}, bf16[1584,128]{1,0:T(8,128)(2,1)}, u32[]{:S(2)}, u32[]{:S(2)}) %collective-permute-start.12) | collective-permute-done | bytes 405536 | tf_op jit(solution)/shard_map/ppermute | solution.py:612
  67.9 1.0 slice.63
  68.9 0.8 collective-permute-start.19
  69.7 0.5 collective-permute-start.18
  70.2 5.3 %collective-permute-done.19.refs_24_ = bf16[1,16,64,128]{3,2,1,0:T(8,128)(2,1)} collective-permute-done((bf16[1,16,64,128]{3,2,1,0:T(8,128)(2,1)S(1)}, bf16[1,16,64,128]{3,2,1,0:T(8,128)(2,1)}, u32[]{:S(2)}, u32[]{:S(2)}) %collective-permute-start.19) | collective-permute-done | bytes 262176 | tf_op jit(solution)/shard_map/ppermute | solution.py:637
  75.4 0.8 copy-done.15
  76.2 1.1 collective-permute-done.20.refs_25_
  77.4 17.5 %layer.1 = bf16[8,256,128]{2,1,0:T(8,128)(2,1)} custom-call(bf16[256,2048]{1,0:T(8,128)(2,1)} %tokens.3, bf16[8,128,256]{2,1,0:T(8,128)(2,1)} %copy-done.4, bf16[8,128,256]{2,1,0:T(8,128)(2,1)} %copy-done.7, bf16[1584,128]{1,0:T(8,128)(2,1)} %pack.1.refs_2_, bf16[1584,128]{1,0:T(8,128)(2,1)} %copy-done.10, bf16[1584,128]{1,0:T(8,128)(2,1)} %copy-done.9, ...), custom_call_target="tpu_custom_call" | custom-call | flops 4294967296 | bytes 8388608 | tf_op jit(solution)/shard_map/layer/pallas_call | solution.py:491
  94.8 1.1 slice_bitcast_fusion
  96.0 5.6 %collective-permute-start.21 = (bf16[256,128]{1,0:T(8,128)(2,1)S(1)}, bf16[256,128]{1,0:T(8,128)(2,1)S(1)}, u32[]{:S(2)}, u32[]{:S(2)}) collective-permute-start(bf16[256,128]{1,0:T(8,128)(2,1)S(1)} %get-tuple-element.40), channel_id=1, source_target_pairs={{0,24},{4,28},{8,16},{12,20},{16,8},{20,12},{24,0},{28,4},{1,25},{... | collective-permute-start | bytes 196616 | tf_op jit(solution)/shard_map/ppermute | solution.py:665
  101.6 1.0 collective-permute-start.22
  102.6 2.9 %collective-permute-start.24 = (bf16[256,128]{1,0:T(8,128)(2,1)S(1)}, bf16[256,128]{1,0:T(8,128)(2,1)S(1)}, u32[]{:S(2)}, u32[]{:S(2)}) collective-permute-start(bf16[256,128]{1,0:T(8,128)(2,1)S(1)} %get-tuple-element.37), channel_id=1, source_target_pairs={{0,16},{4,20},{8,24},{12,28},{16,0},{20,4},{24,8},{28,12},{1,17},{... | collective-permute-start | bytes 196616 | tf_op jit(solution)/shard_map/ppermute | solution.py:665
  105.5 2.3 %collective-permute-start.25 = (bf16[256,128]{1,0:T(8,128)(2,1)S(1)}, bf16[256,128]{1,0:T(8,128)(2,1)S(1)}, u32[]{:S(2)}, u32[]{:S(2)}) collective-permute-start(bf16[256,128]{1,0:T(8,128)(2,1)S(1)} %get-tuple-element.36), channel_id=1, source_target_pairs={{0,12},{4,8},{8,4},{12,0},{16,28},{20,24},{24,20},{28,16},{1,13},{... | collective-permute-start | bytes 196616 | tf_op jit(solution)/shard_map/ppermute | solution.py:665
  107.8 0.6 collective-permute-start.26
  108.5 0.6 collective-permute-done.22.refs_1_
  109.0 2.5 %collective-permute-start.27 = (bf16[256,128]{1,0:T(8,128)(2,1)S(1)}, bf16[256,128]{1,0:T(8,128)(2,1)S(1)}, u32[]{:S(2)}, u32[]{:S(2)}) collective-permute-start(bf16[256,128]{1,0:T(8,128)(2,1)S(1)} %get-tuple-element.34), channel_id=1, source_target_pairs={{0,4},{4,0},{8,12},{12,8},{16,20},{20,16},{24,28},{28,24},{1,5},{5... | collective-permute-start | bytes 196616 | tf_op jit(solution)/shard_map/ppermute | solution.py:665
  111.5 0.1 reshape.52.gain
  111.6 1.9 %collective-permute-done.23.refs_2_ = bf16[256,128]{1,0:T(8,128)(2,1)S(1)} collective-permute-done((bf16[256,128]{1,0:T(8,128)(2,1)S(1)}, bf16[256,128]{1,0:T(8,128)(2,1)S(1)}, u32[]{:S(2)}, u32[]{:S(2)}) %collective-permute-start.23) | collective-permute-done | bytes 65568 | tf_op jit(solution)/shard_map/ppermute | solution.py:665
  113.5 0.2 collective-permute-done.24.refs_3_
  113.7 0.3 collective-permute-done.26.refs_5_
  114.0 2.2 %copy-done = bf16[16,64,2048]{2,1,0:T(8,128)(2,1)S(1)} copy-done((bf16[16,64,2048]{2,1,0:T(8,128)(2,1)S(1)}, bf16[16,64,2048]{2,1,0:T(8,128)(2,1)}, u32[]{:S(2)}) %copy-start) | copy-done | bytes 4194328
  116.2 2.0 %close.1 = (bf16[2,64,2048]{2,1,0:T(8,128)(2,1)S(1)}, bf16[2,64,2048]{2,1,0:T(8,128)(2,1)S(1)}) custom-call(f32[1,1024]{1,0:T(1,128)S(1)} %reshape.52.gain, bf16[1024,2048]{1,0:T(8,128)(2,1)S(1)} %bitcast.52, bf16[256,128]{1,0:T(8,128)(2,1)S(1)} %collective-permute-done.21.refs_0_, bf16[256,128]{1,0:T(8,128)(2,1)S(1)} %collective-permute-done.22.refs_1_, ...), custom_call_target="tpu_custom_call" | custom-call | flops 1073741824 | bytes 4194304 | tf_op jit(solution)/shard_map/close/pallas_call | solution.py:551
  118.2 0.1 collective-permute-start.28
  118.3 1.9 %collective-permute-done.28 = bf16[2,64,2048]{2,1,0:T(8,128)(2,1)S(1)} collective-permute-done((bf16[2,64,2048]{2,1,0:T(8,128)(2,1)S(1)}, bf16[2,64,2048]{2,1,0:T(8,128)(2,1)S(1)}, u32[]{:S(2)}, u32[]{:S(2)}) %collective-permute-start.28) | collective-permute-done | bytes 524320 | tf_op jit(solution)/shard_map/ppermute | solution.py:668
  120.2 0.1 fusion.1
  120.3 1.4 %collective-permute-start.29 = (bf16[64,2048]{1,0:T(8,128)(2,1)S(1)}, bf16[64,2048]{1,0:T(8,128)(2,1)S(1)}, u32[]{:S(2)}, u32[]{:S(2)}) collective-permute-start(bf16[64,2048]{1,0:T(8,128)(2,1)S(1)} %fusion.1), channel_id=1, source_target_pairs={{0,2},{1,3},{2,0},{3,1},{4,6},{5,7},{6,4},{7,5},{8,10},{9,11},{10,... | collective-permute-start | bytes 786440 | tf_op jit(solution)/shard_map/ppermute | solution.py:670
  121.7 7.0 %collective-permute-done.29 = bf16[64,2048]{1,0:T(8,128)(2,1)S(1)} collective-permute-done((bf16[64,2048]{1,0:T(8,128)(2,1)S(1)}, bf16[64,2048]{1,0:T(8,128)(2,1)S(1)}, u32[]{:S(2)}, u32[]{:S(2)}) %collective-permute-start.29) | collective-permute-done | bytes 262176 | tf_op jit(solution)/shard_map/ppermute | solution.py:670
  128.7 0.8 fusion
  (62 shorter events, 0.3 us)
Async XLA Ops:
  2.7 12.7 %collective-permute-start = (bf16[1584,128]{1,0:T(8,128)(2,1)}, bf16[1584,128]{1,0:T(8,128)(2,1)S(1)}, u32[]{:S(2)}, u32[]{:S(2)}) collective-permute-start(bf16[1584,128]{1,0:T(8,128)(2,1)} %pack.1.refs_2_), channel_id=1, source_target_pairs={{0,8},{4,12},{8,0},{12,4},{16,24},{20,28},{24,16},{28,20},{1,9},{5... | collective-permute-start | bytes 1216520 | tf_op jit(solution)/shard_map/ppermute | solution.py:606
  5.8 9.6 %collective-permute-start.1 = (bf16[1584,128]{1,0:T(8,128)(2,1)}, bf16[1584,128]{1,0:T(8,128)(2,1)S(1)}, u32[]{:S(2)}, u32[]{:S(2)}) collective-permute-start(bf16[1584,128]{1,0:T(8,128)(2,1)} %pack.1.refs_2_), channel_id=1, source_target_pairs={{8,16},{12,20},{16,8},{20,12},{9,17},{13,21},{17,9},{21,13},{10,18... | collective-permute-start | bytes 1216520 | tf_op jit(solution)/shard_map/ppermute | solution.py:607
  6.5 11.1 %collective-permute-start.2 = (bf16[1584,128]{1,0:T(8,128)(2,1)}, bf16[1584,128]{1,0:T(8,128)(2,1)S(1)}, u32[]{:S(2)}, u32[]{:S(2)}) collective-permute-start(bf16[1584,128]{1,0:T(8,128)(2,1)} %pack.1.refs_2_), channel_id=1, source_target_pairs={{0,4},{4,0},{8,12},{12,8},{16,20},{20,16},{24,28},{28,24},{1,5},{5... | collective-permute-start | bytes 1216520 | tf_op jit(solution)/shard_map/ppermute | solution.py:608
  15.4 24.0 %copy-start.9 = (bf16[1584,128]{1,0:T(8,128)(2,1)}, bf16[1584,128]{1,0:T(8,128)(2,1)S(1)}, u32[]{:S(2)}) copy-start(bf16[1584,128]{1,0:T(8,128)(2,1)S(1)} %collective-permute-done.refs_4_) | copy-start | bytes 1216516
  17.6 3.6 %copy-start.10 = (bf16[1584,128]{1,0:T(8,128)(2,1)}, bf16[1584,128]{1,0:T(8,128)(2,1)S(1)}, u32[]{:S(2)}) copy-start(bf16[1584,128]{1,0:T(8,128)(2,1)S(1)} %collective-permute-done.2.refs_3_) | copy-start | bytes 1216516
  17.6 13.2 %collective-permute-start.5 = (bf16[1584,128]{1,0:T(8,128)(2,1)S(1)}, bf16[1584,128]{1,0:T(8,128)(2,1)S(1)}, u32[]{:S(2)}, u32[]{:S(2)}) collective-permute-start(bf16[1584,128]{1,0:T(8,128)(2,1)S(1)} %collective-permute-done.1), channel_id=1, source_target_pairs={{8,0},{12,4},{16,24},{20,28},{9,1},{13,5},{17,25},{21,29},{10,2},{... | collective-permute-start | bytes 1216520 | tf_op jit(solution)/shard_map/ppermute | solution.py:644
  18.9 12.0 %collective-permute-start.4 = (bf16[1584,128]{1,0:T(8,128)(2,1)S(1)}, bf16[1584,128]{1,0:T(8,128)(2,1)S(1)}, u32[]{:S(2)}, u32[]{:S(2)}) collective-permute-start(bf16[1584,128]{1,0:T(8,128)(2,1)S(1)} %collective-permute-done.refs_4_), channel_id=1, source_target_pairs={{0,4},{4,0},{8,12},{12,8},{16,20},{20,16},{24,28},{28,24},{1,5},{5... | collective-permute-start | bytes 1216520 | tf_op jit(solution)/shard_map/ppermute | solution.py:612
  20.5 12.0 %collective-permute-start.3 = (bf16[1584,128]{1,0:T(8,128)(2,1)S(1)}, bf16[1584,128]{1,0:T(8,128)(2,1)S(1)}, u32[]{:S(2)}, u32[]{:S(2)}) collective-permute-start(bf16[1584,128]{1,0:T(8,128)(2,1)S(1)} %collective-permute-done.refs_4_), channel_id=1, source_target_pairs={{8,16},{12,20},{16,8},{20,12},{9,17},{13,21},{17,9},{21,13},{10,18... | collective-permute-start | bytes 1216520 | tf_op jit(solution)/shard_map/ppermute | solution.py:643
  21.3 33.0 %copy-start.3 = (bf16[2,16,64,128]{3,2,1,0:T(8,128)(2,1)}, bf16[2,16,64,128]{3,2,1,0:T(8,128)(2,1)S(1)}, u32[]{:S(2)}) copy-start(bf16[2,16,64,128]{3,2,1,0:T(8,128)(2,1)S(1)} %pad_maximum_fusion.refs_10_) | copy-start | bytes 1572868
  21.3 19.8 %collective-permute-start.9 = (bf16[2,16,64,128]{3,2,1,0:T(8,128)(2,1)S(1)}, bf16[2,16,64,128]{3,2,1,0:T(8,128)(2,1)}, u32[]{:S(2)}, u32[]{:S(2)}) collective-permute-start(bf16[2,16,64,128]{3,2,1,0:T(8,128)(2,1)S(1)} %pad_maximum_fusion.refs_10_), channel_id=1, source_target_pairs={{0,2},{1,3},{2,0},{3,1},{4,6},{5,7},{6,4},{7,5},{8,10},{9,11},{10,... | collective-permute-start | bytes 1572872 | tf_op jit(solution)/shard_map/ppermute | solution.py:637
  30.9 46.4 %copy-start.1 = (bf16[1584,128]{1,0:T(8,128)(2,1)}, bf16[1584,128]{1,0:T(8,128)(2,1)S(1)}, u32[]{:S(2)}) copy-start(bf16[1584,128]{1,0:T(8,128)(2,1)S(1)} %broadcast_select_fusion.1.refs_6_) | copy-start | bytes 1216516
  30.9 1.6 %copy-start.11 = (bf16[1584,128]{1,0:T(8,128)(2,1)}, bf16[1584,128]{1,0:T(8,128)(2,1)S(1)}, u32[]{:S(2)}) copy-start(bf16[1584,128]{1,0:T(8,128)(2,1)S(1)} %collective-permute-done.4.refs_5_) | copy-start | bytes 1216516
  30.9 10.7 %collective-permute-start.6 = (bf16[1584,128]{1,0:T(8,128)(2,1)S(1)}, bf16[1584,128]{1,0:T(8,128)(2,1)}, u32[]{:S(2)}, u32[]{:S(2)}) collective-permute-start(bf16[1584,128]{1,0:T(8,128)(2,1)S(1)} %broadcast_select_fusion.1.refs_6_), channel_id=1, source_target_pairs={{0,4},{4,0},{8,12},{12,8},{16,20},{20,16},{24,28},{28,24},{1,5},{5... | collective-permute-start | bytes 1216520 | tf_op jit(solution)/shard_map/ppermute | solution.py:612
  32.5 18.4 %collective-permute-start.7 = (bf16[1584,128]{1,0:T(8,128)(2,1)S(1)}, bf16[1584,128]{1,0:T(8,128)(2,1)S(1)}, u32[]{:S(2)}, u32[]{:S(2)}) collective-permute-start(bf16[1584,128]{1,0:T(8,128)(2,1)S(1)} %collective-permute-done.3), channel_id=1, source_target_pairs={{8,0},{12,4},{16,24},{20,28},{9,1},{13,5},{17,25},{21,29},{10,2},{... | collective-permute-start | bytes 1216520 | tf_op jit(solution)/shard_map/ppermute | solution.py:649
  33.8 20.5 %all-to-all-start = ((bf16[8,128,256]{2,1,0:T(8,128)(2,1)}), bf16[8,128,256]{2,1,0:T(8,128)(2,1)S(1)}, u32[]{:S(2)}, u32[]{:S(2)}) async-start(bf16[8,128,256]{2,1,0:T(8,128)(2,1)} %bitcast.5), calls=%async_computation | async-start | bytes 1048576 | tf_op jit(solution)/shard_map/all_to_all | solution.py:611
  39.5 37.8 %copy-start.5 = (bf16[2,16,64,128]{3,2,1,0:T(8,128)(2,1)}, bf16[2,16,64,128]{3,2,1,0:T(8,128)(2,1)S(1)}, u32[]{:S(2)}) copy-start(bf16[2,16,64,128]{3,2,1,0:T(8,128)(2,1)S(1)} %pad_maximum_fusion.1.refs_14_) | copy-start | bytes 1572868
  39.5 11.4 %collective-permute-start.11 = (bf16[2,16,64,128]{3,2,1,0:T(8,128)(2,1)S(1)}, bf16[2,16,64,128]{3,2,1,0:T(8,128)(2,1)}, u32[]{:S(2)}, u32[]{:S(2)}) collective-permute-start(bf16[2,16,64,128]{3,2,1,0:T(8,128)(2,1)S(1)} %pad_maximum_fusion.1.refs_14_), channel_id=1, source_target_pairs={{0,2},{1,3},{2,0},{3,1},{4,6},{5,7},{6,4},{7,5},{8,10},{9,11},{10,... | collective-permute-start | bytes 1572872 | tf_op jit(solution)/shard_map/ppermute | solution.py:637
  41.1 9.9 %collective-permute-start.8 = (bf16[2,16,64,128]{3,2,1,0:T(8,128)(2,1)S(1)}, bf16[2,16,64,128]{3,2,1,0:T(8,128)(2,1)S(1)}, u32[]{:S(2)}, u32[]{:S(2)}) collective-permute-start(bf16[2,16,64,128]{3,2,1,0:T(8,128)(2,1)S(1)} %pad_maximum_fusion.refs_10_), channel_id=1, source_target_pairs={{0,1},{1,0},{2,3},{3,2},{4,5},{5,4},{6,7},{7,6},{8,9},{9,8},{10,11... | collective-permute-start | bytes 1572872 | tf_op jit(solution)/shard_map/ppermute | solution.py:636
  41.1 10.0 %collective-permute-start.10 = (bf16[2,16,64,128]{3,2,1,0:T(8,128)(2,1)}, bf16[2,16,64,128]{3,2,1,0:T(8,128)(2,1)S(1)}, u32[]{:S(2)}, u32[]{:S(2)}) collective-permute-start(bf16[2,16,64,128]{3,2,1,0:T(8,128)(2,1)} %collective-permute-done.9.refs_12_), channel_id=1, source_target_pairs={{0,1},{1,0},{2,3},{3,2},{4,5},{5,4},{6,7},{7,6},{8,9},{9,8},{10,11... | collective-permute-start | bytes 1572872 | tf_op jit(solution)/shard_map/ppermute | solution.py:638
  41.6 17.2 %collective-permute-start.13 = (bf16[2,16,64,128]{3,2,1,0:T(8,128)(2,1)S(1)}, bf16[2,16,64,128]{3,2,1,0:T(8,128)(2,1)}, u32[]{:S(2)}, u32[]{:S(2)}) collective-permute-start(bf16[2,16,64,128]{3,2,1,0:T(8,128)(2,1)S(1)} %pad_maximum_fusion.1.refs_14_), channel_id=1, source_target_pairs={{0,1},{1,0},{2,3},{3,2},{4,5},{5,4},{6,7},{7,6},{8,9},{9,8},{10,11... | collective-permute-start | bytes 1572872 | tf_op jit(solution)/shard_map/ppermute | solution.py:636
  51.0 26.4 %copy-start.2 = (bf16[1584,128]{1,0:T(8,128)(2,1)}, bf16[1584,128]{1,0:T(8,128)(2,1)S(1)}, u32[]{:S(2)}) copy-start(bf16[1584,128]{1,0:T(8,128)(2,1)S(1)} %broadcast_select_fusion.refs_8_) | copy-start | bytes 1216516
  51.0 16.9 %collective-permute-start.14 = (bf16[2,16,64,128]{3,2,1,0:T(8,128)(2,1)}, bf16[2,16,64,128]{3,2,1,0:T(8,128)(2,1)}, u32[]{:S(2)}, u32[]{:S(2)}) collective-permute-start(bf16[2,16,64,128]{3,2,1,0:T(8,128)(2,1)} %collective-permute-done.11.refs_16_), channel_id=1, source_target_pairs={{0,1},{1,0},{2,3},{3,2},{4,5},{5,4},{6,7},{7,6},{8,9},{9,8},{10,11... | collective-permute-start | bytes 1572872 | tf_op jit(solution)/shard_map/ppermute | solution.py:638
  51.1 1.7 %copy-start.13 = (bf16[2,16,64,128]{3,2,1,0:T(8,128)(2,1)}, bf16[2,16,64,128]{3,2,1,0:T(8,128)(2,1)S(1)}, u32[]{:S(2)}) copy-start(bf16[2,16,64,128]{3,2,1,0:T(8,128)(2,1)S(1)} %collective-permute-done.8.refs_11_) | copy-start | bytes 1572868
  51.1 1.7 %copy-start.14 = (bf16[2,16,64,128]{3,2,1,0:T(8,128)(2,1)}, bf16[2,16,64,128]{3,2,1,0:T(8,128)(2,1)S(1)}, u32[]{:S(2)}) copy-start(bf16[2,16,64,128]{3,2,1,0:T(8,128)(2,1)S(1)} %collective-permute-done.10.refs_13_) | copy-start | bytes 1572868
  51.2 26.1 %copy-start.6 = (bf16[2,16,64,128]{3,2,1,0:T(8,128)(2,1)}, bf16[2,16,64,128]{3,2,1,0:T(8,128)(2,1)S(1)}, u32[]{:S(2)}) copy-start(bf16[2,16,64,128]{3,2,1,0:T(8,128)(2,1)S(1)} %pad_maximum_fusion.2.refs_18_) | copy-start | bytes 1572868
  51.2 16.7 %collective-permute-start.15 = (bf16[2,16,64,128]{3,2,1,0:T(8,128)(2,1)S(1)}, bf16[2,16,64,128]{3,2,1,0:T(8,128)(2,1)}, u32[]{:S(2)}, u32[]{:S(2)}) collective-permute-start(bf16[2,16,64,128]{3,2,1,0:T(8,128)(2,1)S(1)} %pad_maximum_fusion.2.refs_18_), channel_id=1, source_target_pairs={{0,2},{1,3},{2,0},{3,1},{4,6},{5,7},{6,4},{7,5},{8,10},{9,11},{10,... | collective-permute-start | bytes 1572872 | tf_op jit(solution)/shard_map/ppermute | solution.py:637
  52.8 15.1 %collective-permute-start.12 = (bf16[1584,128]{1,0:T(8,128)(2,1)S(1)}, bf16[1584,128]{1,0:T(8,128)(2,1)}, u32[]{:S(2)}, u32[]{:S(2)}) collective-permute-start(bf16[1584,128]{1,0:T(8,128)(2,1)S(1)} %broadcast_select_fusion.refs_8_), channel_id=1, source_target_pairs={{0,4},{4,0},{8,12},{12,8},{16,20},{20,16},{24,28},{28,24},{1,5},{5... | collective-permute-start | bytes 1216520 | tf_op jit(solution)/shard_map/ppermute | solution.py:612
  54.3 23.1 %copy-start.4 = (bf16[8,128,256]{2,1,0:T(8,128)(2,1)}, bf16[8,128,256]{2,1,0:T(8,128)(2,1)S(1)}, u32[]{:S(2)}) copy-start(bf16[8,128,256]{2,1,0:T(8,128)(2,1)S(1)} %all-to-all-done.refs_0_) | copy-start | bytes 1572868
  54.3 22.0 %all-to-all-start.1 = ((bf16[8,128,256]{2,1,0:T(8,128)(2,1)}), bf16[8,128,256]{2,1,0:T(8,128)(2,1)S(1)}, u32[]{:S(2)}, u32[]{:S(2)}) async-start(bf16[8,128,256]{2,1,0:T(8,128)(2,1)} %bitcast.13), calls=%async_computation.1 | async-start | bytes 1048576 | tf_op jit(solution)/shard_map/all_to_all | solution.py:611
  58.8 16.6 %collective-permute-start.16 = (bf16[2,16,64,128]{3,2,1,0:T(8,128)(2,1)S(1)}, bf16[2,16,64,128]{3,2,1,0:T(8,128)(2,1)S(1)}, u32[]{:S(2)}, u32[]{:S(2)}) collective-permute-start(bf16[2,16,64,128]{3,2,1,0:T(8,128)(2,1)S(1)} %pad_maximum_fusion.2.refs_18_), channel_id=1, source_target_pairs={{0,1},{1,0},{2,3},{3,2},{4,5},{5,4},{6,7},{7,6},{8,9},{9,8},{10,11... | collective-permute-start | bytes 1572872 | tf_op jit(solution)/shard_map/ppermute | solution.py:636
  68.9 8.5 %copy-start.8 = (bf16[1024,128]{1,0:T(8,128)(2,1)}, bf16[1024,128]{1,0:T(8,128)(2,1)S(1)}, u32[]{:S(2)}) copy-start(bf16[1024,128]{1,0:T(8,128)(2,1)S(1)} %slice.63) | copy-start | bytes 786436
  68.9 42.6 %copy-start.12 = (f32[16,64]{1,0:T(8,128)S(1)}, f32[16,64]{1,0:T(8,128)}, u32[]{:S(2)}) copy-start(f32[16,64]{1,0:T(8,128)} %param.30) | copy-start | bytes 12292
  68.9 6.5 %collective-permute-start.19 = (bf16[1,16,64,128]{3,2,1,0:T(8,128)(2,1)S(1)}, bf16[1,16,64,128]{3,2,1,0:T(8,128)(2,1)}, u32[]{:S(2)}, u32[]{:S(2)}) collective-permute-start(bf16[1,16,64,128]{3,2,1,0:T(8,128)(2,1)S(1)} %bitcast.59), channel_id=1, source_target_pairs={{0,2},{1,3},{2,0},{3,1},{4,6},{5,7},{6,4},{7,5},{8,10},{9,11},{10,... | collective-permute-start | bytes 786440 | tf_op jit(solution)/shard_map/ppermute | solution.py:637
  69.7 7.7 %collective-permute-start.17 = (bf16[2,16,64,128]{3,2,1,0:T(8,128)(2,1)}, bf16[2,16,64,128]{3,2,1,0:T(8,128)(2,1)}, u32[]{:S(2)}, u32[]{:S(2)}) collective-permute-start(bf16[2,16,64,128]{3,2,1,0:T(8,128)(2,1)} %collective-permute-done.15.refs_20_), channel_id=1, source_target_pairs={{0,1},{1,0},{2,3},{3,2},{4,5},{5,4},{6,7},{7,6},{8,9},{9,8},{10,11... | collective-permute-start | bytes 1572872 | tf_op jit(solution)/shard_map/ppermute | solution.py:638
  69.7 6.6 %collective-permute-start.18 = (bf16[1,16,64,128]{3,2,1,0:T(8,128)(2,1)S(1)}, bf16[1,16,64,128]{3,2,1,0:T(8,128)(2,1)}, u32[]{:S(2)}, u32[]{:S(2)}) collective-permute-start(bf16[1,16,64,128]{3,2,1,0:T(8,128)(2,1)S(1)} %bitcast.60), channel_id=1, source_target_pairs={{0,1},{1,0},{2,3},{3,2},{4,5},{5,4},{6,7},{7,6},{8,9},{9,8},{10,11... | collective-permute-start | bytes 786440 | tf_op jit(solution)/shard_map/ppermute | solution.py:636
  75.4 1.9 %collective-permute-start.20 = (bf16[1,16,64,128]{3,2,1,0:T(8,128)(2,1)}, bf16[1,16,64,128]{3,2,1,0:T(8,128)(2,1)}, u32[]{:S(2)}, u32[]{:S(2)}) collective-permute-start(bf16[1,16,64,128]{3,2,1,0:T(8,128)(2,1)} %collective-permute-done.19.refs_24_), channel_id=1, source_target_pairs={{0,1},{1,0},{2,3},{3,2},{4,5},{5,4},{6,7},{7,6},{8,9},{9,8},{10,11... | collective-permute-start | bytes 786440 | tf_op jit(solution)/shard_map/ppermute | solution.py:638
  75.4 0.8 copy-start.15
  76.2 1.1 copy-start.7
  96.0 11.9 %collective-permute-start.21 = (bf16[256,128]{1,0:T(8,128)(2,1)S(1)}, bf16[256,128]{1,0:T(8,128)(2,1)S(1)}, u32[]{:S(2)}, u32[]{:S(2)}) collective-permute-start(bf16[256,128]{1,0:T(8,128)(2,1)S(1)} %get-tuple-element.40), channel_id=1, source_target_pairs={{0,24},{4,28},{8,16},{12,20},{16,8},{20,12},{24,0},{28,4},{1,25},{... | collective-permute-start | bytes 196616 | tf_op jit(solution)/shard_map/ppermute | solution.py:665
  101.6 7.5 %collective-permute-start.22 = (bf16[256,128]{1,0:T(8,128)(2,1)S(1)}, bf16[256,128]{1,0:T(8,128)(2,1)S(1)}, u32[]{:S(2)}, u32[]{:S(2)}) collective-permute-start(bf16[256,128]{1,0:T(8,128)(2,1)S(1)} %get-tuple-element.39), channel_id=1, source_target_pairs={{0,28},{4,24},{8,20},{12,16},{16,12},{20,8},{24,4},{28,0},{1,29},{... | collective-permute-start | bytes 196616 | tf_op jit(solution)/shard_map/ppermute | solution.py:665
  102.6 10.9 %collective-permute-start.23 = (bf16[256,128]{1,0:T(8,128)(2,1)S(1)}, bf16[256,128]{1,0:T(8,128)(2,1)S(1)}, u32[]{:S(2)}, u32[]{:S(2)}) collective-permute-start(bf16[256,128]{1,0:T(8,128)(2,1)S(1)} %get-tuple-element.38), channel_id=1, source_target_pairs={{0,20},{4,16},{8,28},{12,24},{16,4},{20,0},{24,12},{28,8},{1,21},{... | collective-permute-start | bytes 196616 | tf_op jit(solution)/shard_map/ppermute | solution.py:665
  102.6 11.1 %collective-permute-start.24 = (bf16[256,128]{1,0:T(8,128)(2,1)S(1)}, bf16[256,128]{1,0:T(8,128)(2,1)S(1)}, u32[]{:S(2)}, u32[]{:S(2)}) collective-permute-start(bf16[256,128]{1,0:T(8,128)(2,1)S(1)} %get-tuple-element.37), channel_id=1, source_target_pairs={{0,16},{4,20},{8,24},{12,28},{16,0},{20,4},{24,8},{28,12},{1,17},{... | collective-permute-start | bytes 196616 | tf_op jit(solution)/shard_map/ppermute | solution.py:665
  105.5 8.2 %collective-permute-start.25 = (bf16[256,128]{1,0:T(8,128)(2,1)S(1)}, bf16[256,128]{1,0:T(8,128)(2,1)S(1)}, u32[]{:S(2)}, u32[]{:S(2)}) collective-permute-start(bf16[256,128]{1,0:T(8,128)(2,1)S(1)} %get-tuple-element.36), channel_id=1, source_target_pairs={{0,12},{4,8},{8,4},{12,0},{16,28},{20,24},{24,20},{28,16},{1,13},{... | collective-permute-start | bytes 196616 | tf_op jit(solution)/shard_map/ppermute | solution.py:665
  107.8 6.2 %collective-permute-start.26 = (bf16[256,128]{1,0:T(8,128)(2,1)S(1)}, bf16[256,128]{1,0:T(8,128)(2,1)S(1)}, u32[]{:S(2)}, u32[]{:S(2)}) collective-permute-start(bf16[256,128]{1,0:T(8,128)(2,1)S(1)} %get-tuple-element.35), channel_id=1, source_target_pairs={{0,8},{4,12},{8,0},{12,4},{16,24},{20,28},{24,16},{28,20},{1,9},{5... | collective-permute-start | bytes 196616 | tf_op jit(solution)/shard_map/ppermute | solution.py:665
  109.0 4.9 %collective-permute-start.27 = (bf16[256,128]{1,0:T(8,128)(2,1)S(1)}, bf16[256,128]{1,0:T(8,128)(2,1)S(1)}, u32[]{:S(2)}, u32[]{:S(2)}) collective-permute-start(bf16[256,128]{1,0:T(8,128)(2,1)S(1)} %get-tuple-element.34), channel_id=1, source_target_pairs={{0,4},{4,0},{8,12},{12,8},{16,20},{20,16},{24,28},{28,24},{1,5},{5... | collective-permute-start | bytes 196616 | tf_op jit(solution)/shard_map/ppermute | solution.py:665
  114.0 2.2 %copy-start = (bf16[16,64,2048]{2,1,0:T(8,128)(2,1)S(1)}, bf16[16,64,2048]{2,1,0:T(8,128)(2,1)}, u32[]{:S(2)}) copy-start(bf16[16,64,2048]{2,1,0:T(8,128)(2,1)} %param.31) | copy-start | bytes 12582916
  118.2 2.0 %collective-permute-start.28 = (bf16[2,64,2048]{2,1,0:T(8,128)(2,1)S(1)}, bf16[2,64,2048]{2,1,0:T(8,128)(2,1)S(1)}, u32[]{:S(2)}, u32[]{:S(2)}) collective-permute-start(bf16[2,64,2048]{2,1,0:T(8,128)(2,1)S(1)} %get-tuple-element.32), channel_id=1, source_target_pairs={{0,1},{1,0},{2,3},{3,2},{4,5},{5,4},{6,7},{7,6},{8,9},{9,8},{10,11... | collective-permute-start | bytes 1572872 | tf_op jit(solution)/shard_map/ppermute | solution.py:668
  120.3 8.4 %collective-permute-start.29 = (bf16[64,2048]{1,0:T(8,128)(2,1)S(1)}, bf16[64,2048]{1,0:T(8,128)(2,1)S(1)}, u32[]{:S(2)}, u32[]{:S(2)}) collective-permute-start(bf16[64,2048]{1,0:T(8,128)(2,1)S(1)} %fusion.1), channel_id=1, source_target_pairs={{0,2},{1,3},{2,0},{3,1},{4,6},{5,7},{6,4},{7,5},{8,10},{9,11},{10,... | collective-permute-start | bytes 786440 | tf_op jit(solution)/shard_map/ppermute | solution.py:670

commit v5 on v4

--- a/solution.py
+++ b/solution.py
@@ -516,6 +516,28 @@
     )(tokens, *columns, *payloads, *pieces, per_head, params, g_taps, g_shift)
 
 
+def hold_kernel(gated, weight, held, sem):
+    del gated
+    copy = pltpu.make_async_copy(weight, held, sem)
+    copy.start()
+    copy.wait()
+
+
+def hold(gated, weight):
+    return pl.pallas_call(
+        hold_kernel,
+        in_specs=[HBM, HBM],
+        out_specs=VMEM,
+        out_shape=pltpu.VMEM(weight.shape, weight.dtype),
+        scratch_shapes=[pltpu.SemaphoreType.DMA],
+        compiler_params=pltpu.CompilerParams(vmem_limit_bytes=48 * 1024 * 1024),
+        cost_estimate=pl.CostEstimate(
+            flops=0, bytes_accessed=4 * weight.size, transcendentals=0
+        ),
+        name="hold",
+    )(gated, weight)
+
+
 def close_kernel(offsets, gain, weight, *refs):
     parts, (keep, give, inputs) = refs[:-3], refs[-3:]
     rows, width = parts[0].shape
@@ -559,7 +581,7 @@
             flops=2 * rows * weight.size, bytes_accessed=2 * weight.size, transcendentals=0
         ),
         name="close",
-    )(gain, weight, *parts)
+    )(gain, pltpu.with_memory_space_constraint(weight, pltpu.VMEM), *parts)
 
 
 def tokens_travel(
@@ -664,7 +686,7 @@
     offsets = (6, 7, 5, 4, 3, 2, 1)
     parts = [lax.ppermute(gated[at], "seq", swap(ring, at)) for at in offsets] + [gated[0]]
     gain, weight = norm_gain.reshape(1, -1), out_weight.reshape(-1, depth)
-    keep, give = close(offsets + (0,), gain, weight, parts)
+    keep, give = close(offsets + (0,), gain, hold(gated[0, :ROW_PAD], weight), parts)
     took = lax.ppermute(give, "mp", swap(seats, 1))
     send = (keep[1].astype(f32) + took[1].astype(f32)).astype(bf16)
     took_far = lax.ppermute(send, "mp", swap(seats, 2))

time: 131 us -> 129 us (0.985)
  waiting for transfers between devices: 47.2 us -> 44.7 us
  Pallas kernels: 22.2 us -> 24.3 us
  local copies, waits for them, and re-layouts: 11.7 us -> 10.2 us
    ppermute x7, waiting for transfers between devices: 2.97 us -> 0.53 us  [tokens_travel(): lax.ppermute(gated[at], 'seq', swap(ring, at))]
    unnamed x33 -> x31, local copies, waits for them, and re-layouts: 4.33 us -> 2.13 us
    pallas_call x0 -> x1, Pallas kernels: none -> 2.2 us  [hold(): pl.pallas_call(hold_kernel, in_specs=[HBM, HBM], out_specs=VMEM, out_shap...]
  transfers between devices with their start and end apart: 32 -> 32, of which waited for: 13 -> 10; matrix products, arithmetic and copies ran while one was open for 7% -> 8% of each run, Pallas kernels for 0% -> 2%
where the time goes in v5:
time: 129 us; the launch traced here: 128 us
  starting transfers between devices  45.6 us (35%)
  waiting for transfers between devices  44.7 us (35%)
  Pallas kernels  24.3 us (19%)
  local copies, waits for them, and re-layouts  10.2 us (8%)
  other arithmetic  2.46 us (2%)
    pallas_call x1, Pallas kernels, layer(): pl.pallas_call(functools.partial(layer_kernel, head_size, counts), in_spe...  17.4 us
    ppermute x7, starting transfers between devices, tokens_travel(): lax.ppermute(gated[at], 'seq', swap(ring, at))  14.9 us
    all_to_all x2, starting transfers between devices, tokens_travel(): lax.all_to_all(w, 'seq', split_axis=0, concat_axis=0, tiled=True)  9.19 us
    ppermute x3, waiting for transfers between devices, tokens_travel(): cross = lambda item: lax.ppermute(item, 'seq', swap(ring, 1))  9.06 us
    ppermute x1, waiting for transfers between devices, tokens_travel(): out_far = lax.ppermute(mid_far, 'seq', outward)  8.24 us
    ppermute x1, waiting for transfers between devices, tokens_travel(): out_near = lax.ppermute(mid, 'seq', outward)  8 us
    ppermute x1, waiting for transfers between devices, tokens_travel(): took_far = lax.ppermute(send, 'mp', swap(seats, 2))  6.84 us
    ppermute x4, starting transfers between devices, spread(): across = lax.ppermute(own, 'mp', swap(seats, 2))  5.52 us
  transfers between devices with their start and end apart: 32, of which 10 were waited for; matrix products, arithmetic and copies ran while one was open for 8% of the time, Pallas kernels for 2%

profile of v5, /device:TPU:0, one launch (start us, length us, event | category | flops | bytes accessed | tf_op | source)
XLA Modules:
  0.0 127.6 jit_solution(13776384528754977059)
XLA Ops:
  0.0 2.7 %pack.1.refs_2_ = bf16[1584,128]{1,0:T(8,128)(2,1)} custom-call(bf16[256,2048]{1,0:T(8,128)(2,1)} %tokens.3, bf16[512,128]{1,0:T(8,128)(2,1)} %bitcast.64, bf16[16,256]{1,0:T(8,128)(2,1)} %bitcast.66, s32[2,128]{1,0:T(2,128)} %bitcast.69), custom_call_target="tpu_custom_call" | custom-call | tf_op jit(solution)/shard_map/pack/pallas_call | solution.py:263
  2.7 3.1 %collective-permute-start = (bf16[1584,128]{1,0:T(8,128)(2,1)}, bf16[1584,128]{1,0:T(8,128)(2,1)S(1)}, u32[]{:S(2)}, u32[]{:S(2)}) collective-permute-start(bf16[1584,128]{1,0:T(8,128)(2,1)} %pack.1.refs_2_), channel_id=1, source_target_pairs={{0,8},{4,12},{8,0},{12,4},{16,24},{20,28},{24,16},{28,20},{1,9},{5... | collective-permute-start | bytes 1216520 | tf_op jit(solution)/shard_map/ppermute | solution.py:628
  5.8 0.7 collective-permute-start.1
  6.5 1.6 %collective-permute-start.2 = (bf16[1584,128]{1,0:T(8,128)(2,1)}, bf16[1584,128]{1,0:T(8,128)(2,1)S(1)}, u32[]{:S(2)}, u32[]{:S(2)}) collective-permute-start(bf16[1584,128]{1,0:T(8,128)(2,1)} %pack.1.refs_2_), channel_id=1, source_target_pairs={{0,4},{4,0},{8,12},{12,8},{16,20},{20,16},{24,28},{28,24},{1,5},{5... | collective-permute-start | bytes 1216520 | tf_op jit(solution)/shard_map/ppermute | solution.py:630
  8.0 0.8 concatenate.12
  8.9 0.7 broadcast_in_dim.11
  9.6 0.1 broadcast_in_dim.12
  9.7 0.1 broadcast_in_dim.13
  9.8 0.8 concatenate.13
  10.6 0.7 maximum_bitcast_fusion.1
  11.3 0.1 copy.18
  11.4 1.3 copy.22
  12.6 0.6 pad.4.refs_26_
  13.2 0.6 maximum_bitcast_fusion.refs_27_
  13.9 1.5 %collective-permute-done.refs_4_ = bf16[1584,128]{1,0:T(8,128)(2,1)S(1)} collective-permute-done((bf16[1584,128]{1,0:T(8,128)(2,1)}, bf16[1584,128]{1,0:T(8,128)(2,1)S(1)}, u32[]{:S(2)}, u32[]{:S(2)}) %collective-permute-start) | collective-permute-done | bytes 405536 | tf_op jit(solution)/shard_map/ppermute | solution.py:628
  15.4 2.2 %collective-permute-done.2.refs_3_ = bf16[1584,128]{1,0:T(8,128)(2,1)S(1)} collective-permute-done((bf16[1584,128]{1,0:T(8,128)(2,1)}, bf16[1584,128]{1,0:T(8,128)(2,1)S(1)}, u32[]{:S(2)}, u32[]{:S(2)}) %collective-permute-start.2) | collective-permute-done | bytes 405536 | tf_op jit(solution)/shard_map/ppermute | solution.py:630
  17.6 1.3 %collective-permute-start.5 = (bf16[1584,128]{1,0:T(8,128)(2,1)S(1)}, bf16[1584,128]{1,0:T(8,128)(2,1)S(1)}, u32[]{:S(2)}, u32[]{:S(2)}) collective-permute-start(bf16[1584,128]{1,0:T(8,128)(2,1)S(1)} %collective-permute-done.1), channel_id=1, source_target_pairs={{8,0},{12,4},{16,24},{20,28},{9,1},{13,5},{17,25},{21,29},{10,2},{... | collective-permute-start | bytes 1216520 | tf_op jit(solution)/shard_map/ppermute | solution.py:666
  18.9 1.6 %collective-permute-start.4 = (bf16[1584,128]{1,0:T(8,128)(2,1)S(1)}, bf16[1584,128]{1,0:T(8,128)(2,1)S(1)}, u32[]{:S(2)}, u32[]{:S(2)}) collective-permute-start(bf16[1584,128]{1,0:T(8,128)(2,1)S(1)} %collective-permute-done.refs_4_), channel_id=1, source_target_pairs={{0,4},{4,0},{8,12},{12,8},{16,20},{20,16},{24,28},{28,24},{1,5},{5... | collective-permute-start | bytes 1216520 | tf_op jit(solution)/shard_map/ppermute | solution.py:634
  20.5 0.7 collective-permute-start.3
  21.2 0.1 pad_maximum_fusion.refs_10_
  21.3 1.6 %collective-permute-start.9 = (bf16[2,16,64,128]{3,2,1,0:T(8,128)(2,1)S(1)}, bf16[2,16,64,128]{3,2,1,0:T(8,128)(2,1)}, u32[]{:S(2)}, u32[]{:S(2)}) collective-permute-start(bf16[2,16,64,128]{3,2,1,0:T(8,128)(2,1)S(1)} %pad_maximum_fusion.refs_10_), channel_id=1, source_target_pairs={{0,2},{1,3},{2,0},{3,1},{4,6},{5,7},{6,4},{7,5},{8,10},{9,11},{10,... | collective-permute-start | bytes 1572872 | tf_op jit(solution)/shard_map/ppermute | solution.py:659
  22.9 8.0 %collective-permute-done.5 = bf16[1584,128]{1,0:T(8,128)(2,1)S(1)} collective-permute-done((bf16[1584,128]{1,0:T(8,128)(2,1)S(1)}, bf16[1584,128]{1,0:T(8,128)(2,1)S(1)}, u32[]{:S(2)}, u32[]{:S(2)}) %collective-permute-start.5) | collective-permute-done | bytes 405536 | tf_op jit(solution)/shard_map/ppermute | solution.py:666
  30.9 0.1 broadcast_select_fusion.1.refs_6_
  30.9 1.6 %collective-permute-start.6 = (bf16[1584,128]{1,0:T(8,128)(2,1)S(1)}, bf16[1584,128]{1,0:T(8,128)(2,1)}, u32[]{:S(2)}, u32[]{:S(2)}) collective-permute-start(bf16[1584,128]{1,0:T(8,128)(2,1)S(1)} %broadcast_select_fusion.1.refs_6_), channel_id=1, source_target_pairs={{0,4},{4,0},{8,12},{12,8},{16,20},{20,16},{24,28},{28,24},{1,5},{5... | collective-permute-start | bytes 1216520 | tf_op jit(solution)/shard_map/ppermute | solution.py:634
  32.5 1.3 %collective-permute-start.7 = (bf16[1584,128]{1,0:T(8,128)(2,1)S(1)}, bf16[1584,128]{1,0:T(8,128)(2,1)S(1)}, u32[]{:S(2)}, u32[]{:S(2)}) collective-permute-start(bf16[1584,128]{1,0:T(8,128)(2,1)S(1)} %collective-permute-done.3), channel_id=1, source_target_pairs={{8,0},{12,4},{16,24},{20,28},{9,1},{13,5},{17,25},{21,29},{10,2},{... | collective-permute-start | bytes 1216520 | tf_op jit(solution)/shard_map/ppermute | solution.py:671
  33.8 4.6 %all-to-all-start = ((bf16[8,128,256]{2,1,0:T(8,128)(2,1)}), bf16[8,128,256]{2,1,0:T(8,128)(2,1)S(1)}, u32[]{:S(2)}, u32[]{:S(2)}) async-start(bf16[8,128,256]{2,1,0:T(8,128)(2,1)} %bitcast.4), calls=%async_computation | async-start | bytes 1048576 | tf_op jit(solution)/shard_map/all_to_all | solution.py:633
  38.5 1.0 slice.81
  39.4 0.1 pad_maximum_fusion.1.refs_14_
  39.5 1.6 %collective-permute-start.11 = (bf16[2,16,64,128]{3,2,1,0:T(8,128)(2,1)S(1)}, bf16[2,16,64,128]{3,2,1,0:T(8,128)(2,1)}, u32[]{:S(2)}, u32[]{:S(2)}) collective-permute-start(bf16[2,16,64,128]{3,2,1,0:T(8,128)(2,1)S(1)} %pad_maximum_fusion.1.refs_14_), channel_id=1, source_target_pairs={{0,2},{1,3},{2,0},{3,1},{4,6},{5,7},{6,4},{7,5},{8,10},{9,11},{10,... | collective-permute-start | bytes 1572872 | tf_op jit(solution)/shard_map/ppermute | solution.py:659
  41.1 0.5 collective-permute-start.10
  41.6 0.1 collective-permute-start.13
  41.7 1.0 slice.82
  42.7 8.2 %collective-permute-done.7 = bf16[1584,128]{1,0:T(8,128)(2,1)S(1)} collective-permute-done((bf16[1584,128]{1,0:T(8,128)(2,1)S(1)}, bf16[1584,128]{1,0:T(8,128)(2,1)S(1)}, u32[]{:S(2)}, u32[]{:S(2)}) %collective-permute-start.7) | collective-permute-done | bytes 405536 | tf_op jit(solution)/shard_map/ppermute | solution.py:671
  51.0 0.1 collective-permute-start.14
  51.1 0.1 pad_maximum_fusion.2.refs_18_
  51.2 1.6 %collective-permute-start.15 = (bf16[2,16,64,128]{3,2,1,0:T(8,128)(2,1)S(1)}, bf16[2,16,64,128]{3,2,1,0:T(8,128)(2,1)}, u32[]{:S(2)}, u32[]{:S(2)}) collective-permute-start(bf16[2,16,64,128]{3,2,1,0:T(8,128)(2,1)S(1)} %pad_maximum_fusion.2.refs_18_), channel_id=1, source_target_pairs={{0,2},{1,3},{2,0},{3,1},{4,6},{5,7},{6,4},{7,5},{8,10},{9,11},{10,... | collective-permute-start | bytes 1572872 | tf_op jit(solution)/shard_map/ppermute | solution.py:659
  52.8 1.5 %collective-permute-start.12 = (bf16[1584,128]{1,0:T(8,128)(2,1)S(1)}, bf16[1584,128]{1,0:T(8,128)(2,1)}, u32[]{:S(2)}, u32[]{:S(2)}) collective-permute-start(bf16[1584,128]{1,0:T(8,128)(2,1)S(1)} %broadcast_select_fusion.refs_8_), channel_id=1, source_target_pairs={{0,4},{4,0},{8,12},{12,8},{16,20},{20,16},{24,28},{28,24},{1,5},{5... | collective-permute-start | bytes 1216520 | tf_op jit(solution)/shard_map/ppermute | solution.py:634
  54.2 4.5 %all-to-all-start.1 = ((bf16[8,128,256]{2,1,0:T(8,128)(2,1)}), bf16[8,128,256]{2,1,0:T(8,128)(2,1)S(1)}, u32[]{:S(2)}, u32[]{:S(2)}) async-start(bf16[8,128,256]{2,1,0:T(8,128)(2,1)} %bitcast.12), calls=%async_computation.1 | async-start | bytes 1048576 | tf_op jit(solution)/shard_map/all_to_all | solution.py:633
  58.8 9.1 %collective-permute-done.12.refs_9_ = bf16[1584,128]{1,0:T(8,128)(2,1)} collective-permute-done((bf16[1584,128]{1,0:T(8,128)(2,1)S(1)}, bf16[1584,128]{1,0:T(8,128)(2,1)}, u32[]{:S(2)}, u32[]{:S(2)}) %collective-permute-start.12) | collective-permute-done | bytes 405536 | tf_op jit(solution)/shard_map/ppermute | solution.py:634
  67.9 1.0 slice.66
  68.9 0.8 collective-permute-start.19
  69.6 0.5 collective-permute-start.18
  70.1 5.3 %collective-permute-done.19.refs_24_ = bf16[1,16,64,128]{3,2,1,0:T(8,128)(2,1)} collective-permute-done((bf16[1,16,64,128]{3,2,1,0:T(8,128)(2,1)S(1)}, bf16[1,16,64,128]{3,2,1,0:T(8,128)(2,1)}, u32[]{:S(2)}, u32[]{:S(2)}) %collective-permute-start.19) | collective-permute-done | bytes 262176 | tf_op jit(solution)/shard_map/ppermute | solution.py:659
  75.4 0.8 copy-done.14
  76.2 1.1 collective-permute-done.20.refs_25_
  77.4 17.4 %layer.1 = bf16[8,256,128]{2,1,0:T(8,128)(2,1)} custom-call(bf16[256,2048]{1,0:T(8,128)(2,1)} %tokens.3, bf16[8,128,256]{2,1,0:T(8,128)(2,1)} %copy-done.3, bf16[8,128,256]{2,1,0:T(8,128)(2,1)} %copy-done.6, bf16[1584,128]{1,0:T(8,128)(2,1)} %pack.1.refs_2_, bf16[1584,128]{1,0:T(8,128)(2,1)} %copy-done.9, bf16[1584,128]{1,0:T(8,128)(2,1)} %copy-done.8, ...), custom_call_target="tpu_custom_call" | custom-call | flops 4294967296 | bytes 8388608 | tf_op jit(solution)/shard_map/layer/pallas_call | solution.py:491
  94.8 1.1 slice_bitcast_fusion
  95.9 5.6 %collective-permute-start.21 = (bf16[256,128]{1,0:T(8,128)(2,1)S(1)}, bf16[256,128]{1,0:T(8,128)(2,1)S(1)}, u32[]{:S(2)}, u32[]{:S(2)}) collective-permute-start(bf16[256,128]{1,0:T(8,128)(2,1)S(1)} %get-tuple-element.40), channel_id=1, source_target_pairs={{0,24},{4,28},{8,16},{12,20},{16,8},{20,12},{24,0},{28,4},{1,25},{... | collective-permute-start | bytes 196616 | tf_op jit(solution)/shard_map/ppermute | solution.py:687
  101.5 1.0 collective-permute-start.22
  102.5 0.1 reshape.52.gain
  102.6 2.9 %collective-permute-start.24 = (bf16[256,128]{1,0:T(8,128)(2,1)S(1)}, bf16[256,128]{1,0:T(8,128)(2,1)S(1)}, u32[]{:S(2)}, u32[]{:S(2)}) collective-permute-start(bf16[256,128]{1,0:T(8,128)(2,1)S(1)} %get-tuple-element.37), channel_id=1, source_target_pairs={{0,16},{4,20},{8,24},{12,28},{16,0},{20,4},{24,8},{28,12},{1,17},{... | collective-permute-start | bytes 196616 | tf_op jit(solution)/shard_map/ppermute | solution.py:687
  105.5 2.3 %collective-permute-start.25 = (bf16[256,128]{1,0:T(8,128)(2,1)S(1)}, bf16[256,128]{1,0:T(8,128)(2,1)S(1)}, u32[]{:S(2)}, u32[]{:S(2)}) collective-permute-start(bf16[256,128]{1,0:T(8,128)(2,1)S(1)} %get-tuple-element.36), channel_id=1, source_target_pairs={{0,12},{4,8},{8,4},{12,0},{16,28},{20,24},{24,20},{28,16},{1,13},{... | collective-permute-start | bytes 196616 | tf_op jit(solution)/shard_map/ppermute | solution.py:687
  107.8 0.6 collective-permute-start.26
  108.4 0.5 collective-permute-done.22.refs_1_
  109.0 2.4 %collective-permute-start.27 = (bf16[256,128]{1,0:T(8,128)(2,1)S(1)}, bf16[256,128]{1,0:T(8,128)(2,1)S(1)}, u32[]{:S(2)}, u32[]{:S(2)}) collective-permute-start(bf16[256,128]{1,0:T(8,128)(2,1)S(1)} %get-tuple-element.34), channel_id=1, source_target_pairs={{0,4},{4,0},{8,12},{12,8},{16,20},{20,16},{24,28},{28,24},{1,5},{5... | collective-permute-start | bytes 196616 | tf_op jit(solution)/shard_map/ppermute | solution.py:687
  111.4 0.7 slice_bitcast_fusion.8.gated
  112.1 2.2 %hold.1.weight = bf16[1024,2048]{1,0:T(8,128)(2,1)S(1)} custom-call(bf16[16,128]{1,0:T(8,128)(2,1)S(1)} %slice_bitcast_fusion.8.gated, bf16[1024,2048]{1,0:T(8,128)(2,1)} %bitcast.54), custom_call_target="tpu_custom_call" | custom-call | bytes 8388608 | tf_op jit(solution)/shard_map/hold/pallas_call | solution.py:527
  114.3 2.0 %close.1 = (bf16[2,64,2048]{2,1,0:T(8,128)(2,1)S(1)}, bf16[2,64,2048]{2,1,0:T(8,128)(2,1)S(1)}) custom-call(f32[1,1024]{1,0:T(1,128)S(1)} %reshape.52.gain, bf16[1024,2048]{1,0:T(8,128)(2,1)S(1)} %hold.1.weight, bf16[256,128]{1,0:T(8,128)(2,1)S(1)} %collective-permute-done.21.refs_0_, bf16[256,128]{1,0:T(8,128)(2,1)S(1)} %collective-permute-done.22.refs_1_, ...), custom_call_target="tpu_custom_call" | custom-call | flops 1073741824 | bytes 4194304 | tf_op jit(solution)/shard_map/close/pallas_call | solution.py:573
  116.4 0.1 collective-permute-start.28
  116.4 1.9 %collective-permute-done.28 = bf16[2,64,2048]{2,1,0:T(8,128)(2,1)S(1)} collective-permute-done((bf16[2,64,2048]{2,1,0:T(8,128)(2,1)S(1)}, bf16[2,64,2048]{2,1,0:T(8,128)(2,1)S(1)}, u32[]{:S(2)}, u32[]{:S(2)}) %collective-permute-start.28) | collective-permute-done | bytes 524320 | tf_op jit(solution)/shard_map/ppermute | solution.py:690
  118.3 0.1 fusion.1
  118.4 1.6 %collective-permute-start.29 = (bf16[64,2048]{1,0:T(8,128)(2,1)S(1)}, bf16[64,2048]{1,0:T(8,128)(2,1)S(1)}, u32[]{:S(2)}, u32[]{:S(2)}) collective-permute-start(bf16[64,2048]{1,0:T(8,128)(2,1)S(1)} %fusion.1), channel_id=1, source_target_pairs={{0,2},{1,3},{2,0},{3,1},{4,6},{5,7},{6,4},{7,5},{8,10},{9,11},{10,... | collective-permute-start | bytes 786440 | tf_op jit(solution)/shard_map/ppermute | solution.py:692
  120.0 6.8 %collective-permute-done.29 = bf16[64,2048]{1,0:T(8,128)(2,1)S(1)} collective-permute-done((bf16[64,2048]{1,0:T(8,128)(2,1)S(1)}, bf16[64,2048]{1,0:T(8,128)(2,1)S(1)}, u32[]{:S(2)}, u32[]{:S(2)}) %collective-permute-start.29) | collective-permute-done | bytes 262176 | tf_op jit(solution)/shard_map/ppermute | solution.py:692
  126.8 0.8 fusion
  (62 shorter events, 0.3 us)
Async XLA Ops:
  2.7 12.7 %collective-permute-start = (bf16[1584,128]{1,0:T(8,128)(2,1)}, bf16[1584,128]{1,0:T(8,128)(2,1)S(1)}, u32[]{:S(2)}, u32[]{:S(2)}) collective-permute-start(bf16[1584,128]{1,0:T(8,128)(2,1)} %pack.1.refs_2_), channel_id=1, source_target_pairs={{0,8},{4,12},{8,0},{12,4},{16,24},{20,28},{24,16},{28,20},{1,9},{5... | collective-permute-start | bytes 1216520 | tf_op jit(solution)/shard_map/ppermute | solution.py:628
  5.8 9.6 %collective-permute-start.1 = (bf16[1584,128]{1,0:T(8,128)(2,1)}, bf16[1584,128]{1,0:T(8,128)(2,1)S(1)}, u32[]{:S(2)}, u32[]{:S(2)}) collective-permute-start(bf16[1584,128]{1,0:T(8,128)(2,1)} %pack.1.refs_2_), channel_id=1, source_target_pairs={{8,16},{12,20},{16,8},{20,12},{9,17},{13,21},{17,9},{21,13},{10,18... | collective-permute-start | bytes 1216520 | tf_op jit(solution)/shard_map/ppermute | solution.py:629
  6.5 11.1 %collective-permute-start.2 = (bf16[1584,128]{1,0:T(8,128)(2,1)}, bf16[1584,128]{1,0:T(8,128)(2,1)S(1)}, u32[]{:S(2)}, u32[]{:S(2)}) collective-permute-start(bf16[1584,128]{1,0:T(8,128)(2,1)} %pack.1.refs_2_), channel_id=1, source_target_pairs={{0,4},{4,0},{8,12},{12,8},{16,20},{20,16},{24,28},{28,24},{1,5},{5... | collective-permute-start | bytes 1216520 | tf_op jit(solution)/shard_map/ppermute | solution.py:630
  15.4 18.4 %copy-start.8 = (bf16[1584,128]{1,0:T(8,128)(2,1)}, bf16[1584,128]{1,0:T(8,128)(2,1)S(1)}, u32[]{:S(2)}) copy-start(bf16[1584,128]{1,0:T(8,128)(2,1)S(1)} %collective-permute-done.refs_4_) | copy-start | bytes 1216516
  17.6 5.2 %copy-start.9 = (bf16[1584,128]{1,0:T(8,128)(2,1)}, bf16[1584,128]{1,0:T(8,128)(2,1)S(1)}, u32[]{:S(2)}) copy-start(bf16[1584,128]{1,0:T(8,128)(2,1)S(1)} %collective-permute-done.2.refs_3_) | copy-start | bytes 1216516
  17.6 13.2 %collective-permute-start.5 = (bf16[1584,128]{1,0:T(8,128)(2,1)S(1)}, bf16[1584,128]{1,0:T(8,128)(2,1)S(1)}, u32[]{:S(2)}, u32[]{:S(2)}) collective-permute-start(bf16[1584,128]{1,0:T(8,128)(2,1)S(1)} %collective-permute-done.1), channel_id=1, source_target_pairs={{8,0},{12,4},{16,24},{20,28},{9,1},{13,5},{17,25},{21,29},{10,2},{... | collective-permute-start | bytes 1216520 | tf_op jit(solution)/shard_map/ppermute | solution.py:666
  18.9 12.0 %collective-permute-start.4 = (bf16[1584,128]{1,0:T(8,128)(2,1)S(1)}, bf16[1584,128]{1,0:T(8,128)(2,1)S(1)}, u32[]{:S(2)}, u32[]{:S(2)}) collective-permute-start(bf16[1584,128]{1,0:T(8,128)(2,1)S(1)} %collective-permute-done.refs_4_), channel_id=1, source_target_pairs={{0,4},{4,0},{8,12},{12,8},{16,20},{20,16},{24,28},{28,24},{1,5},{5... | collective-permute-start | bytes 1216520 | tf_op jit(solution)/shard_map/ppermute | solution.py:634
  20.5 12.0 %collective-permute-start.3 = (bf16[1584,128]{1,0:T(8,128)(2,1)S(1)}, bf16[1584,128]{1,0:T(8,128)(2,1)S(1)}, u32[]{:S(2)}, u32[]{:S(2)}) collective-permute-start(bf16[1584,128]{1,0:T(8,128)(2,1)S(1)} %collective-permute-done.refs_4_), channel_id=1, source_target_pairs={{8,16},{12,20},{16,8},{20,12},{9,17},{13,21},{17,9},{21,13},{10,18... | collective-permute-start | bytes 1216520 | tf_op jit(solution)/shard_map/ppermute | solution.py:665
  21.3 33.0 %copy-start.2 = (bf16[2,16,64,128]{3,2,1,0:T(8,128)(2,1)}, bf16[2,16,64,128]{3,2,1,0:T(8,128)(2,1)S(1)}, u32[]{:S(2)}) copy-start(bf16[2,16,64,128]{3,2,1,0:T(8,128)(2,1)S(1)} %pad_maximum_fusion.refs_10_) | copy-start | bytes 1572868
  21.3 19.8 %collective-permute-start.9 = (bf16[2,16,64,128]{3,2,1,0:T(8,128)(2,1)S(1)}, bf16[2,16,64,128]{3,2,1,0:T(8,128)(2,1)}, u32[]{:S(2)}, u32[]{:S(2)}) collective-permute-start(bf16[2,16,64,128]{3,2,1,0:T(8,128)(2,1)S(1)} %pad_maximum_fusion.refs_10_), channel_id=1, source_target_pairs={{0,2},{1,3},{2,0},{3,1},{4,6},{5,7},{6,4},{7,5},{8,10},{9,11},{10,... | collective-permute-start | bytes 1572872 | tf_op jit(solution)/shard_map/ppermute | solution.py:659
  30.9 46.4 %copy-start = (bf16[1584,128]{1,0:T(8,128)(2,1)}, bf16[1584,128]{1,0:T(8,128)(2,1)S(1)}, u32[]{:S(2)}) copy-start(bf16[1584,128]{1,0:T(8,128)(2,1)S(1)} %broadcast_select_fusion.1.refs_6_) | copy-start | bytes 1216516
  30.9 1.6 %copy-start.10 = (bf16[1584,128]{1,0:T(8,128)(2,1)}, bf16[1584,128]{1,0:T(8,128)(2,1)S(1)}, u32[]{:S(2)}) copy-start(bf16[1584,128]{1,0:T(8,128)(2,1)S(1)} %collective-permute-done.4.refs_5_) | copy-start | bytes 1216516
  30.9 10.7 %collective-permute-start.6 = (bf16[1584,128]{1,0:T(8,128)(2,1)S(1)}, bf16[1584,128]{1,0:T(8,128)(2,1)}, u32[]{:S(2)}, u32[]{:S(2)}) collective-permute-start(bf16[1584,128]{1,0:T(8,128)(2,1)S(1)} %broadcast_select_fusion.1.refs_6_), channel_id=1, source_target_pairs={{0,4},{4,0},{8,12},{12,8},{16,20},{20,16},{24,28},{28,24},{1,5},{5... | collective-permute-start | bytes 1216520 | tf_op jit(solution)/shard_map/ppermute | solution.py:634
  32.5 18.4 %collective-permute-start.7 = (bf16[1584,128]{1,0:T(8,128)(2,1)S(1)}, bf16[1584,128]{1,0:T(8,128)(2,1)S(1)}, u32[]{:S(2)}, u32[]{:S(2)}) collective-permute-start(bf16[1584,128]{1,0:T(8,128)(2,1)S(1)} %collective-permute-done.3), channel_id=1, source_target_pairs={{8,0},{12,4},{16,24},{20,28},{9,1},{13,5},{17,25},{21,29},{10,2},{... | collective-permute-start | bytes 1216520 | tf_op jit(solution)/shard_map/ppermute | solution.py:671
  33.8 20.4 %all-to-all-start = ((bf16[8,128,256]{2,1,0:T(8,128)(2,1)}), bf16[8,128,256]{2,1,0:T(8,128)(2,1)S(1)}, u32[]{:S(2)}, u32[]{:S(2)}) async-start(bf16[8,128,256]{2,1,0:T(8,128)(2,1)} %bitcast.4), calls=%async_computation | async-start | bytes 1048576 | tf_op jit(solution)/shard_map/all_to_all | solution.py:633
  39.5 37.8 %copy-start.4 = (bf16[2,16,64,128]{3,2,1,0:T(8,128)(2,1)}, bf16[2,16,64,128]{3,2,1,0:T(8,128)(2,1)S(1)}, u32[]{:S(2)}) copy-start(bf16[2,16,64,128]{3,2,1,0:T(8,128)(2,1)S(1)} %pad_maximum_fusion.1.refs_14_) | copy-start | bytes 1572868
  39.5 11.4 %collective-permute-start.11 = (bf16[2,16,64,128]{3,2,1,0:T(8,128)(2,1)S(1)}, bf16[2,16,64,128]{3,2,1,0:T(8,128)(2,1)}, u32[]{:S(2)}, u32[]{:S(2)}) collective-permute-start(bf16[2,16,64,128]{3,2,1,0:T(8,128)(2,1)S(1)} %pad_maximum_fusion.1.refs_14_), channel_id=1, source_target_pairs={{0,2},{1,3},{2,0},{3,1},{4,6},{5,7},{6,4},{7,5},{8,10},{9,11},{10,... | collective-permute-start | bytes 1572872 | tf_op jit(solution)/shard_map/ppermute | solution.py:659
  41.1 9.9 %collective-permute-start.8 = (bf16[2,16,64,128]{3,2,1,0:T(8,128)(2,1)S(1)}, bf16[2,16,64,128]{3,2,1,0:T(8,128)(2,1)S(1)}, u32[]{:S(2)}, u32[]{:S(2)}) collective-permute-start(bf16[2,16,64,128]{3,2,1,0:T(8,128)(2,1)S(1)} %pad_maximum_fusion.refs_10_), channel_id=1, source_target_pairs={{0,1},{1,0},{2,3},{3,2},{4,5},{5,4},{6,7},{7,6},{8,9},{9,8},{10,11... | collective-permute-start | bytes 1572872 | tf_op jit(solution)/shard_map/ppermute | solution.py:658
  41.1 10.0 %collective-permute-start.10 = (bf16[2,16,64,128]{3,2,1,0:T(8,128)(2,1)}, bf16[2,16,64,128]{3,2,1,0:T(8,128)(2,1)S(1)}, u32[]{:S(2)}, u32[]{:S(2)}) collective-permute-start(bf16[2,16,64,128]{3,2,1,0:T(8,128)(2,1)} %collective-permute-done.9.refs_12_), channel_id=1, source_target_pairs={{0,1},{1,0},{2,3},{3,2},{4,5},{5,4},{6,7},{7,6},{8,9},{9,8},{10,11... | collective-permute-start | bytes 1572872 | tf_op jit(solution)/shard_map/ppermute | solution.py:660
  41.6 17.2 %collective-permute-start.13 = (bf16[2,16,64,128]{3,2,1,0:T(8,128)(2,1)S(1)}, bf16[2,16,64,128]{3,2,1,0:T(8,128)(2,1)}, u32[]{:S(2)}, u32[]{:S(2)}) collective-permute-start(bf16[2,16,64,128]{3,2,1,0:T(8,128)(2,1)S(1)} %pad_maximum_fusion.1.refs_14_), channel_id=1, source_target_pairs={{0,1},{1,0},{2,3},{3,2},{4,5},{5,4},{6,7},{7,6},{8,9},{9,8},{10,11... | collective-permute-start | bytes 1572872 | tf_op jit(solution)/shard_map/ppermute | solution.py:658
  50.9 26.4 %copy-start.1 = (bf16[1584,128]{1,0:T(8,128)(2,1)}, bf16[1584,128]{1,0:T(8,128)(2,1)S(1)}, u32[]{:S(2)}) copy-start(bf16[1584,128]{1,0:T(8,128)(2,1)S(1)} %broadcast_select_fusion.refs_8_) | copy-start | bytes 1216516
  51.0 16.9 %collective-permute-start.14 = (bf16[2,16,64,128]{3,2,1,0:T(8,128)(2,1)}, bf16[2,16,64,128]{3,2,1,0:T(8,128)(2,1)}, u32[]{:S(2)}, u32[]{:S(2)}) collective-permute-start(bf16[2,16,64,128]{3,2,1,0:T(8,128)(2,1)} %collective-permute-done.11.refs_16_), channel_id=1, source_target_pairs={{0,1},{1,0},{2,3},{3,2},{4,5},{5,4},{6,7},{7,6},{8,9},{9,8},{10,11... | collective-permute-start | bytes 1572872 | tf_op jit(solution)/shard_map/ppermute | solution.py:660
  51.1 1.7 %copy-start.12 = (bf16[2,16,64,128]{3,2,1,0:T(8,128)(2,1)}, bf16[2,16,64,128]{3,2,1,0:T(8,128)(2,1)S(1)}, u32[]{:S(2)}) copy-start(bf16[2,16,64,128]{3,2,1,0:T(8,128)(2,1)S(1)} %collective-permute-done.8.refs_11_) | copy-start | bytes 1572868
  51.1 1.7 %copy-start.13 = (bf16[2,16,64,128]{3,2,1,0:T(8,128)(2,1)}, bf16[2,16,64,128]{3,2,1,0:T(8,128)(2,1)S(1)}, u32[]{:S(2)}) copy-start(bf16[2,16,64,128]{3,2,1,0:T(8,128)(2,1)S(1)} %collective-permute-done.10.refs_13_) | copy-start | bytes 1572868
  51.2 26.1 %copy-start.5 = (bf16[2,16,64,128]{3,2,1,0:T(8,128)(2,1)}, bf16[2,16,64,128]{3,2,1,0:T(8,128)(2,1)S(1)}, u32[]{:S(2)}) copy-start(bf16[2,16,64,128]{3,2,1,0:T(8,128)(2,1)S(1)} %pad_maximum_fusion.2.refs_18_) | copy-start | bytes 1572868
  51.2 16.7 %collective-permute-start.15 = (bf16[2,16,64,128]{3,2,1,0:T(8,128)(2,1)S(1)}, bf16[2,16,64,128]{3,2,1,0:T(8,128)(2,1)}, u32[]{:S(2)}, u32[]{:S(2)}) collective-permute-start(bf16[2,16,64,128]{3,2,1,0:T(8,128)(2,1)S(1)} %pad_maximum_fusion.2.refs_18_), channel_id=1, source_target_pairs={{0,2},{1,3},{2,0},{3,1},{4,6},{5,7},{6,4},{7,5},{8,10},{9,11},{10,... | collective-permute-start | bytes 1572872 | tf_op jit(solution)/shard_map/ppermute | solution.py:659
  52.8 15.1 %collective-permute-start.12 = (bf16[1584,128]{1,0:T(8,128)(2,1)S(1)}, bf16[1584,128]{1,0:T(8,128)(2,1)}, u32[]{:S(2)}, u32[]{:S(2)}) collective-permute-start(bf16[1584,128]{1,0:T(8,128)(2,1)S(1)} %broadcast_select_fusion.refs_8_), channel_id=1, source_target_pairs={{0,4},{4,0},{8,12},{12,8},{16,20},{20,16},{24,28},{28,24},{1,5},{5... | collective-permute-start | bytes 1216520 | tf_op jit(solution)/shard_map/ppermute | solution.py:634
  54.2 23.1 %copy-start.3 = (bf16[8,128,256]{2,1,0:T(8,128)(2,1)}, bf16[8,128,256]{2,1,0:T(8,128)(2,1)S(1)}, u32[]{:S(2)}) copy-start(bf16[8,128,256]{2,1,0:T(8,128)(2,1)S(1)} %all-to-all-done.refs_0_) | copy-start | bytes 1572868
  54.2 22.0 %all-to-all-start.1 = ((bf16[8,128,256]{2,1,0:T(8,128)(2,1)}), bf16[8,128,256]{2,1,0:T(8,128)(2,1)S(1)}, u32[]{:S(2)}, u32[]{:S(2)}) async-start(bf16[8,128,256]{2,1,0:T(8,128)(2,1)} %bitcast.12), calls=%async_computation.1 | async-start | bytes 1048576 | tf_op jit(solution)/shard_map/all_to_all | solution.py:633
  58.8 16.6 %collective-permute-start.16 = (bf16[2,16,64,128]{3,2,1,0:T(8,128)(2,1)S(1)}, bf16[2,16,64,128]{3,2,1,0:T(8,128)(2,1)S(1)}, u32[]{:S(2)}, u32[]{:S(2)}) collective-permute-start(bf16[2,16,64,128]{3,2,1,0:T(8,128)(2,1)S(1)} %pad_maximum_fusion.2.refs_18_), channel_id=1, source_target_pairs={{0,1},{1,0},{2,3},{3,2},{4,5},{5,4},{6,7},{7,6},{8,9},{9,8},{10,11... | collective-permute-start | bytes 1572872 | tf_op jit(solution)/shard_map/ppermute | solution.py:658
  68.8 8.5 %copy-start.7 = (bf16[1024,128]{1,0:T(8,128)(2,1)}, bf16[1024,128]{1,0:T(8,128)(2,1)S(1)}, u32[]{:S(2)}) copy-start(bf16[1024,128]{1,0:T(8,128)(2,1)S(1)} %slice.66) | copy-start | bytes 786436
  68.9 33.7 %copy-start.11 = (f32[16,64]{1,0:T(8,128)S(1)}, f32[16,64]{1,0:T(8,128)}, u32[]{:S(2)}) copy-start(f32[16,64]{1,0:T(8,128)} %param.30) | copy-start | bytes 12292
  68.9 6.5 %collective-permute-start.19 = (bf16[1,16,64,128]{3,2,1,0:T(8,128)(2,1)S(1)}, bf16[1,16,64,128]{3,2,1,0:T(8,128)(2,1)}, u32[]{:S(2)}, u32[]{:S(2)}) collective-permute-start(bf16[1,16,64,128]{3,2,1,0:T(8,128)(2,1)S(1)} %bitcast.61), channel_id=1, source_target_pairs={{0,2},{1,3},{2,0},{3,1},{4,6},{5,7},{6,4},{7,5},{8,10},{9,11},{10,... | collective-permute-start | bytes 786440 | tf_op jit(solution)/shard_map/ppermute | solution.py:659
  69.6 7.7 %collective-permute-start.17 = (bf16[2,16,64,128]{3,2,1,0:T(8,128)(2,1)}, bf16[2,16,64,128]{3,2,1,0:T(8,128)(2,1)}, u32[]{:S(2)}, u32[]{:S(2)}) collective-permute-start(bf16[2,16,64,128]{3,2,1,0:T(8,128)(2,1)} %collective-permute-done.15.refs_20_), channel_id=1, source_target_pairs={{0,1},{1,0},{2,3},{3,2},{4,5},{5,4},{6,7},{7,6},{8,9},{9,8},{10,11... | collective-permute-start | bytes 1572872 | tf_op jit(solution)/shard_map/ppermute | solution.py:660
  69.6 6.6 %collective-permute-start.18 = (bf16[1,16,64,128]{3,2,1,0:T(8,128)(2,1)S(1)}, bf16[1,16,64,128]{3,2,1,0:T(8,128)(2,1)}, u32[]{:S(2)}, u32[]{:S(2)}) collective-permute-start(bf16[1,16,64,128]{3,2,1,0:T(8,128)(2,1)S(1)} %bitcast.62), channel_id=1, source_target_pairs={{0,1},{1,0},{2,3},{3,2},{4,5},{5,4},{6,7},{7,6},{8,9},{9,8},{10,11... | collective-permute-start | bytes 786440 | tf_op jit(solution)/shard_map/ppermute | solution.py:658
  75.4 1.9 %collective-permute-start.20 = (bf16[1,16,64,128]{3,2,1,0:T(8,128)(2,1)}, bf16[1,16,64,128]{3,2,1,0:T(8,128)(2,1)}, u32[]{:S(2)}, u32[]{:S(2)}) collective-permute-start(bf16[1,16,64,128]{3,2,1,0:T(8,128)(2,1)} %collective-permute-done.19.refs_24_), channel_id=1, source_target_pairs={{0,1},{1,0},{2,3},{3,2},{4,5},{5,4},{6,7},{7,6},{8,9},{9,8},{10,11... | collective-permute-start | bytes 786440 | tf_op jit(solution)/shard_map/ppermute | solution.py:660
  75.4 0.8 copy-start.14
  76.2 1.1 copy-start.6
  95.9 11.9 %collective-permute-start.21 = (bf16[256,128]{1,0:T(8,128)(2,1)S(1)}, bf16[256,128]{1,0:T(8,128)(2,1)S(1)}, u32[]{:S(2)}, u32[]{:S(2)}) collective-permute-start(bf16[256,128]{1,0:T(8,128)(2,1)S(1)} %get-tuple-element.40), channel_id=1, source_target_pairs={{0,24},{4,28},{8,16},{12,20},{16,8},{20,12},{24,0},{28,4},{1,25},{... | collective-permute-start | bytes 196616 | tf_op jit(solution)/shard_map/ppermute | solution.py:687
  101.5 7.5 %collective-permute-start.22 = (bf16[256,128]{1,0:T(8,128)(2,1)S(1)}, bf16[256,128]{1,0:T(8,128)(2,1)S(1)}, u32[]{:S(2)}, u32[]{:S(2)}) collective-permute-start(bf16[256,128]{1,0:T(8,128)(2,1)S(1)} %get-tuple-element.39), channel_id=1, source_target_pairs={{0,28},{4,24},{8,20},{12,16},{16,12},{20,8},{24,4},{28,0},{1,29},{... | collective-permute-start | bytes 196616 | tf_op jit(solution)/shard_map/ppermute | solution.py:687
  102.6 11.7 %collective-permute-start.23 = (bf16[256,128]{1,0:T(8,128)(2,1)S(1)}, bf16[256,128]{1,0:T(8,128)(2,1)S(1)}, u32[]{:S(2)}, u32[]{:S(2)}) collective-permute-start(bf16[256,128]{1,0:T(8,128)(2,1)S(1)} %get-tuple-element.38), channel_id=1, source_target_pairs={{0,20},{4,16},{8,28},{12,24},{16,4},{20,0},{24,12},{28,8},{1,21},{... | collective-permute-start | bytes 196616 | tf_op jit(solution)/shard_map/ppermute | solution.py:687
  102.6 11.7 %collective-permute-start.24 = (bf16[256,128]{1,0:T(8,128)(2,1)S(1)}, bf16[256,128]{1,0:T(8,128)(2,1)S(1)}, u32[]{:S(2)}, u32[]{:S(2)}) collective-permute-start(bf16[256,128]{1,0:T(8,128)(2,1)S(1)} %get-tuple-element.37), channel_id=1, source_target_pairs={{0,16},{4,20},{8,24},{12,28},{16,0},{20,4},{24,8},{28,12},{1,17},{... | collective-permute-start | bytes 196616 | tf_op jit(solution)/shard_map/ppermute | solution.py:687
  105.5 8.8 %collective-permute-start.25 = (bf16[256,128]{1,0:T(8,128)(2,1)S(1)}, bf16[256,128]{1,0:T(8,128)(2,1)S(1)}, u32[]{:S(2)}, u32[]{:S(2)}) collective-permute-start(bf16[256,128]{1,0:T(8,128)(2,1)S(1)} %get-tuple-element.36), channel_id=1, source_target_pairs={{0,12},{4,8},{8,4},{12,0},{16,28},{20,24},{24,20},{28,16},{1,13},{... | collective-permute-start | bytes 196616 | tf_op jit(solution)/shard_map/ppermute | solution.py:687
  107.8 6.5 %collective-permute-start.26 = (bf16[256,128]{1,0:T(8,128)(2,1)S(1)}, bf16[256,128]{1,0:T(8,128)(2,1)S(1)}, u32[]{:S(2)}, u32[]{:S(2)}) collective-permute-start(bf16[256,128]{1,0:T(8,128)(2,1)S(1)} %get-tuple-element.35), channel_id=1, source_target_pairs={{0,8},{4,12},{8,0},{12,4},{16,24},{20,28},{24,16},{28,20},{1,9},{5... | collective-permute-start | bytes 196616 | tf_op jit(solution)/shard_map/ppermute | solution.py:687
  109.0 5.4 %collective-permute-start.27 = (bf16[256,128]{1,0:T(8,128)(2,1)S(1)}, bf16[256,128]{1,0:T(8,128)(2,1)S(1)}, u32[]{:S(2)}, u32[]{:S(2)}) collective-permute-start(bf16[256,128]{1,0:T(8,128)(2,1)S(1)} %get-tuple-element.34), channel_id=1, source_target_pairs={{0,4},{4,0},{8,12},{12,8},{16,20},{20,16},{24,28},{28,24},{1,5},{5... | collective-permute-start | bytes 196616 | tf_op jit(solution)/shard_map/ppermute | solution.py:687
  116.4 2.0 %collective-permute-start.28 = (bf16[2,64,2048]{2,1,0:T(8,128)(2,1)S(1)}, bf16[2,64,2048]{2,1,0:T(8,128)(2,1)S(1)}, u32[]{:S(2)}, u32[]{:S(2)}) collective-permute-start(bf16[2,64,2048]{2,1,0:T(8,128)(2,1)S(1)} %get-tuple-element.32), channel_id=1, source_target_pairs={{0,1},{1,0},{2,3},{3,2},{4,5},{5,4},{6,7},{7,6},{8,9},{9,8},{10,11... | collective-permute-start | bytes 1572872 | tf_op jit(solution)/shard_map/ppermute | solution.py:690
  118.4 8.4 %collective-permute-start.29 = (bf16[64,2048]{1,0:T(8,128)(2,1)S(1)}, bf16[64,2048]{1,0:T(8,128)(2,1)S(1)}, u32[]{:S(2)}, u32[]{:S(2)}) collective-permute-start(bf16[64,2048]{1,0:T(8,128)(2,1)S(1)} %fusion.1), channel_id=1, source_target_pairs={{0,2},{1,3},{2,0},{3,1},{4,6},{5,7},{6,4},{7,5},{8,10},{9,11},{10,... | collective-permute-start | bytes 786440 | tf_op jit(solution)/shard_map/ppermute | solution.py:692

commit v6 on v5

--- a/solution.py
+++ b/solution.py
@@ -278,10 +278,11 @@
     ring, channels, slab = columns[0].shape
     payloads, refs = refs[:ring], refs[ring:]
     pieces, refs = refs[: 4 * len(counts)], refs[4 * len(counts) :]
-    per_head_all, params_all, g_taps, g_shift, out = refs[:5]
-    tok, shared, w_x, w_group, w_step, x_all, g_all, gate_all, step_all, state, sems = refs[5:]
+    per_head_all, params_all, g_taps, g_shift = refs[:4]
+    parts, refs = refs[4 : 4 + ring], refs[4 + ring :]
+    tok, shared, w_x, w_group, w_step, x_all, g_all, gate_all, step_all, state, out, sems = refs
     seats = 4
-    rows = out.shape[1]
+    rows = parts[0].shape[0]
     quarter = rows // seats
     panels = tok.shape[1]
     height = panels * quarter
@@ -457,7 +458,7 @@
         held = state[...]
         scanned = within + grown * matmul(c_rows, held.astype(bf16)) + skip * values
         scanned = scanned.astype(bf16).astype(f32)
-        out[me ^ block] = (scanned * silu(gate_all[block])).astype(bf16)
+        out[block] = (scanned * silu(gate_all[block])).astype(bf16)
         injected = matmul(b_rows, (left * values).astype(bf16), ((0,), (0,)))
         state[...] = grown[rows - 1 : rows] * held + injected
 
@@ -475,6 +476,8 @@
         return carry
 
     lax.fori_loop(0, ring // 8, advance, 0)
+    for offset, part_out in enumerate(parts):
+        part_out[...] = out[me ^ offset]
 
 
 def layer(head_size, tokens, columns, payloads, groups, per_head, params, g_taps, g_shift):
@@ -491,8 +494,8 @@
     return pl.pallas_call(
         functools.partial(layer_kernel, head_size, counts),
         in_specs=[HBM] * (3 + len(payloads) + len(pieces)) + [VMEM] * 4,
-        out_specs=VMEM,
-        out_shape=jax.ShapeDtypeStruct((ring, rows, channels), bf16),
+        out_specs=[VMEM] * ring,
+        out_shape=[jax.ShapeDtypeStruct((rows, channels), bf16)] * ring,
         scratch_shapes=[
             pltpu.VMEM((ring, depth // LANES, rows, LANES), bf16),
             pltpu.VMEM((ring, shared_rows, LANES), bf16),
@@ -504,6 +507,7 @@
             pltpu.VMEM((ring, rows, channels), f32),
             pltpu.VMEM((ring, lines, rows), f32),
             pltpu.VMEM((part // 2, channels), f32),
+            pltpu.VMEM((ring, rows, channels), bf16),
             pltpu.SemaphoreType.DMA((1 + 2 * ring,)),
         ],
         compiler_params=pltpu.CompilerParams(vmem_limit_bytes=60 * 1024 * 1024),
@@ -538,17 +542,18 @@
     )(gated, weight)
 
 
-def close_kernel(offsets, gain, weight, *refs):
+def close_kernel(offsets, other, gain, weight, *refs):
     parts, (keep, give, inputs) = refs[:-3], refs[-3:]
     rows, width = parts[0].shape
-    seats = 4
-    quarter = rows // seats
+    rows = rows // 2
+    quarter = rows // 2
     columns = weight.shape[1] // 4
     me = lax.axis_index("seq")
     seat = lax.axis_index("mp")
+    first = pl.multiple_of(((seat >> 1) ^ other) * rows, rows)
     square = jnp.zeros((rows, width), f32)
     for offset, part in zip(offsets, parts):
-        value = part[...].astype(f32)
+        value = part[pl.ds(first, rows)].astype(f32)
         square = square + value * value
         at = pl.multiple_of((me ^ offset) * width, width)
         inputs[:, pl.ds(at, width)] = (value * gain[:, pl.ds(at, width)]).astype(bf16)
@@ -561,24 +566,23 @@
 
             @pl.when((seat & 1) == core)
             def _(core=core):
-                for owner in range(seats):
-                    block = total[owner * quarter : (owner + 1) * quarter]
-                    target = keep if owner % 2 == core else give
-                    target[(owner // 2) ^ (seat >> 1), :, at] = block
-
-
-def close(offsets, gain, weight, parts):
+                for owner in range(2):
+                    target = keep if owner == core else give
+                    target[:, at] = total[owner * quarter : (owner + 1) * quarter]
+
+
+def close(offsets, other, gain, weight, parts):
     rows, width = parts[0].shape
-    shape = jax.ShapeDtypeStruct((2, rows // 4, weight.shape[1]), bf16)
+    shape = jax.ShapeDtypeStruct((rows // 4, weight.shape[1]), bf16)
     return pl.pallas_call(
-        functools.partial(close_kernel, offsets),
+        functools.partial(close_kernel, offsets, other),
         in_specs=[VMEM] * (2 + len(parts)),
         out_specs=[VMEM] * 2,
         out_shape=[shape, shape],
-        scratch_shapes=[pltpu.VMEM((rows, len(parts) * width), bf16)],
+        scratch_shapes=[pltpu.VMEM((rows // 2, len(parts) * width), bf16)],
         compiler_params=pltpu.CompilerParams(vmem_limit_bytes=16 * 1024 * 1024),
         cost_estimate=pl.CostEstimate(
-            flops=2 * rows * weight.size, bytes_accessed=2 * weight.size, transcendentals=0
+            flops=rows * weight.size, bytes_accessed=2 * weight.size, transcendentals=0
         ),
         name="close",
     )(gain, pltpu.with_memory_space_constraint(weight, pltpu.VMEM), *parts)
@@ -686,11 +690,14 @@
     offsets = (6, 7, 5, 4, 3, 2, 1)
     parts = [lax.ppermute(gated[at], "seq", swap(ring, at)) for at in offsets] + [gated[0]]
     gain, weight = norm_gain.reshape(1, -1), out_weight.reshape(-1, depth)
-    keep, give = close(offsets + (0,), gain, hold(gated[0, :ROW_PAD], weight), parts)
+    held = hold(gated[0][:ROW_PAD], weight)
+    keep, give = close(offsets + (0,), 1, gain, held, parts)
     took = lax.ppermute(give, "mp", swap(seats, 1))
-    send = (keep[1].astype(f32) + took[1].astype(f32)).astype(bf16)
+    send = (keep.astype(f32) + took.astype(f32)).astype(bf16)
+    keep, give = close(offsets + (0,), 0, gain, held, parts)
+    took = lax.ppermute(give, "mp", swap(seats, 1))
     took_far = lax.ppermute(send, "mp", swap(seats, 2))
-    return (keep[0].astype(f32) + took[0].astype(f32) + took_far.astype(f32)).astype(bf16)
+    return (keep.astype(f32) + took.astype(f32) + took_far.astype(f32)).astype(bf16)
 
 
 def on_device(*arrays):

time: 129 us -> 127 us (0.984)
  waiting for transfers between devices: 44.7 us -> 43.1 us
    ppermute x1 -> x2, waiting for transfers between devices: 1.9 us -> 0.01 us  [tokens_travel(): took = lax.ppermute(give, 'mp', swap(seats, 1))]
    squeeze x2 -> x0, local copies, waits for them, and re-layouts: 1.78 us -> none  [the longest x1 1.1 us: tokens_travel(): gated[0]]
    pallas_call x1 -> x2, Pallas kernels: 2.01 us -> 2.74 us  [close(): pl.pallas_call(functools.partial(close_kernel, offsets, other), in_specs=...]
  transfers between devices with their start and end apart: 32 -> 33, of which waited for: 10 -> 9; matrix products, arithmetic and copies ran while one was open for 8% -> 8% of each run, Pallas kernels for 2% -> 3%
where the time goes in v6:
time: 127 us; the launch traced here: 126 us
  starting transfers between devices  46.2 us (36%)
  waiting for transfers between devices  43.1 us (34%)
  Pallas kernels  25.1 us (20%)
  local copies, waits for them, and re-layouts  9.07 us (7%)
  other arithmetic  2.45 us (2%)
    pallas_call x1, Pallas kernels, layer(): pl.pallas_call(functools.partial(layer_kernel, head_size, counts), in_spe...  17.4 us
    ppermute x7, starting transfers between devices, tokens_travel(): lax.ppermute(gated[at], 'seq', swap(ring, at))  15.1 us
    all_to_all x2, starting transfers between devices, tokens_travel(): lax.all_to_all(w, 'seq', split_axis=0, concat_axis=0, tiled=True)  9.19 us
    ppermute x3, waiting for transfers between devices, tokens_travel(): cross = lambda item: lax.ppermute(item, 'seq', swap(ring, 1))  9.06 us
    ppermute x1, waiting for transfers between devices, tokens_travel(): out_far = lax.ppermute(mid_far, 'seq', outward)  8.24 us
    ppermute x1, waiting for transfers between devices, tokens_travel(): out_near = lax.ppermute(mid, 'seq', outward)  8 us
    ppermute x1, waiting for transfers between devices, tokens_travel(): took_far = lax.ppermute(send, 'mp', swap(seats, 2))  6.91 us
    ppermute x4, starting transfers between devices, spread(): across = lax.ppermute(own, 'mp', swap(seats, 2))  5.58 us
  transfers between devices with their start and end apart: 33, of which 9 were waited for; matrix products, arithmetic and copies ran while one was open for 8% of the time, Pallas kernels for 3%

profile of v6, /device:TPU:0, one launch (start us, length us, event | category | flops | bytes accessed | tf_op | source)
XLA Modules:
  0.0 126.3 jit_solution(8368850687564173235)
XLA Ops:
  0.0 2.7 %pack.1.refs_2_ = bf16[1584,128]{1,0:T(8,128)(2,1)} custom-call(bf16[256,2048]{1,0:T(8,128)(2,1)} %tokens.3, bf16[512,128]{1,0:T(8,128)(2,1)} %bitcast.40, bf16[16,256]{1,0:T(8,128)(2,1)} %bitcast.42, s32[2,128]{1,0:T(2,128)} %bitcast.45), custom_call_target="tpu_custom_call" | custom-call | tf_op jit(solution)/shard_map/pack/pallas_call | solution.py:263
  2.7 3.1 %collective-permute-start = (bf16[1584,128]{1,0:T(8,128)(2,1)}, bf16[1584,128]{1,0:T(8,128)(2,1)S(1)}, u32[]{:S(2)}, u32[]{:S(2)}) collective-permute-start(bf16[1584,128]{1,0:T(8,128)(2,1)} %pack.1.refs_2_), channel_id=1, source_target_pairs={{0,8},{4,12},{8,0},{12,4},{16,24},{20,28},{24,16},{28,20},{1,9},{5... | collective-permute-start | bytes 1216520 | tf_op jit(solution)/shard_map/ppermute | solution.py:632
  5.8 0.7 collective-permute-start.1
  6.5 1.6 %collective-permute-start.2 = (bf16[1584,128]{1,0:T(8,128)(2,1)}, bf16[1584,128]{1,0:T(8,128)(2,1)S(1)}, u32[]{:S(2)}, u32[]{:S(2)}) collective-permute-start(bf16[1584,128]{1,0:T(8,128)(2,1)} %pack.1.refs_2_), channel_id=1, source_target_pairs={{0,4},{4,0},{8,12},{12,8},{16,20},{20,16},{24,28},{28,24},{1,5},{5... | collective-permute-start | bytes 1216520 | tf_op jit(solution)/shard_map/ppermute | solution.py:634
  8.1 0.8 concatenate.12
  8.9 0.7 broadcast_in_dim.11
  9.6 0.1 broadcast_in_dim.12
  9.7 0.1 broadcast_in_dim.13
  9.8 0.8 concatenate.13
  10.6 0.7 maximum_bitcast_fusion.1
  11.3 0.1 copy.18
  11.4 1.3 %copy.22 = f32[1,4,2,128]{3,1,2,0:T(4,128)} copy(f32[1,4,2,128]{3,2,1,0:T(2,128)} %bitcast.43) | data formatting | bytes 8192
  12.6 0.6 pad.4.refs_26_
  13.3 0.6 maximum_bitcast_fusion.refs_27_
  13.9 1.5 %collective-permute-done.refs_4_ = bf16[1584,128]{1,0:T(8,128)(2,1)S(1)} collective-permute-done((bf16[1584,128]{1,0:T(8,128)(2,1)}, bf16[1584,128]{1,0:T(8,128)(2,1)S(1)}, u32[]{:S(2)}, u32[]{:S(2)}) %collective-permute-start) | collective-permute-done | bytes 405536 | tf_op jit(solution)/shard_map/ppermute | solution.py:632
  15.4 2.2 %collective-permute-done.2.refs_3_ = bf16[1584,128]{1,0:T(8,128)(2,1)S(1)} collective-permute-done((bf16[1584,128]{1,0:T(8,128)(2,1)}, bf16[1584,128]{1,0:T(8,128)(2,1)S(1)}, u32[]{:S(2)}, u32[]{:S(2)}) %collective-permute-start.2) | collective-permute-done | bytes 405536 | tf_op jit(solution)/shard_map/ppermute | solution.py:634
  17.6 1.3 %collective-permute-start.5 = (bf16[1584,128]{1,0:T(8,128)(2,1)S(1)}, bf16[1584,128]{1,0:T(8,128)(2,1)S(1)}, u32[]{:S(2)}, u32[]{:S(2)}) collective-permute-start(bf16[1584,128]{1,0:T(8,128)(2,1)S(1)} %collective-permute-done.1), channel_id=1, source_target_pairs={{8,0},{12,4},{16,24},{20,28},{9,1},{13,5},{17,25},{21,29},{10,2},{... | collective-permute-start | bytes 1216520 | tf_op jit(solution)/shard_map/ppermute | solution.py:670
  18.9 1.6 %collective-permute-start.4 = (bf16[1584,128]{1,0:T(8,128)(2,1)S(1)}, bf16[1584,128]{1,0:T(8,128)(2,1)S(1)}, u32[]{:S(2)}, u32[]{:S(2)}) collective-permute-start(bf16[1584,128]{1,0:T(8,128)(2,1)S(1)} %collective-permute-done.refs_4_), channel_id=1, source_target_pairs={{0,4},{4,0},{8,12},{12,8},{16,20},{20,16},{24,28},{28,24},{1,5},{5... | collective-permute-start | bytes 1216520 | tf_op jit(solution)/shard_map/ppermute | solution.py:638
  20.5 0.7 collective-permute-start.3
  21.2 0.1 pad_maximum_fusion.refs_10_
  21.3 1.6 %collective-permute-start.9 = (bf16[2,16,64,128]{3,2,1,0:T(8,128)(2,1)S(1)}, bf16[2,16,64,128]{3,2,1,0:T(8,128)(2,1)}, u32[]{:S(2)}, u32[]{:S(2)}) collective-permute-start(bf16[2,16,64,128]{3,2,1,0:T(8,128)(2,1)S(1)} %pad_maximum_fusion.refs_10_), channel_id=1, source_target_pairs={{0,2},{1,3},{2,0},{3,1},{4,6},{5,7},{6,4},{7,5},{8,10},{9,11},{10,... | collective-permute-start | bytes 1572872 | tf_op jit(solution)/shard_map/ppermute | solution.py:663
  22.9 8.0 %collective-permute-done.5 = bf16[1584,128]{1,0:T(8,128)(2,1)S(1)} collective-permute-done((bf16[1584,128]{1,0:T(8,128)(2,1)S(1)}, bf16[1584,128]{1,0:T(8,128)(2,1)S(1)}, u32[]{:S(2)}, u32[]{:S(2)}) %collective-permute-start.5) | collective-permute-done | bytes 405536 | tf_op jit(solution)/shard_map/ppermute | solution.py:670
  30.9 0.1 broadcast_select_fusion.1.refs_6_
  31.0 1.6 %collective-permute-start.6 = (bf16[1584,128]{1,0:T(8,128)(2,1)S(1)}, bf16[1584,128]{1,0:T(8,128)(2,1)}, u32[]{:S(2)}, u32[]{:S(2)}) collective-permute-start(bf16[1584,128]{1,0:T(8,128)(2,1)S(1)} %broadcast_select_fusion.1.refs_6_), channel_id=1, source_target_pairs={{0,4},{4,0},{8,12},{12,8},{16,20},{20,16},{24,28},{28,24},{1,5},{5... | collective-permute-start | bytes 1216520 | tf_op jit(solution)/shard_map/ppermute | solution.py:638
  32.5 1.3 %collective-permute-start.7 = (bf16[1584,128]{1,0:T(8,128)(2,1)S(1)}, bf16[1584,128]{1,0:T(8,128)(2,1)S(1)}, u32[]{:S(2)}, u32[]{:S(2)}) collective-permute-start(bf16[1584,128]{1,0:T(8,128)(2,1)S(1)} %collective-permute-done.3), channel_id=1, source_target_pairs={{8,0},{12,4},{16,24},{20,28},{9,1},{13,5},{17,25},{21,29},{10,2},{... | collective-permute-start | bytes 1216520 | tf_op jit(solution)/shard_map/ppermute | solution.py:675
  33.8 4.6 %all-to-all-start = ((bf16[8,128,256]{2,1,0:T(8,128)(2,1)}), bf16[8,128,256]{2,1,0:T(8,128)(2,1)S(1)}, u32[]{:S(2)}, u32[]{:S(2)}) async-start(bf16[8,128,256]{2,1,0:T(8,128)(2,1)} %bitcast.4), calls=%async_computation | async-start | bytes 1048576 | tf_op jit(solution)/shard_map/all_to_all | solution.py:637
  38.5 1.0 slice.33
  39.5 0.1 pad_maximum_fusion.1.refs_14_
  39.5 1.6 %collective-permute-start.11 = (bf16[2,16,64,128]{3,2,1,0:T(8,128)(2,1)S(1)}, bf16[2,16,64,128]{3,2,1,0:T(8,128)(2,1)}, u32[]{:S(2)}, u32[]{:S(2)}) collective-permute-start(bf16[2,16,64,128]{3,2,1,0:T(8,128)(2,1)S(1)} %pad_maximum_fusion.1.refs_14_), channel_id=1, source_target_pairs={{0,2},{1,3},{2,0},{3,1},{4,6},{5,7},{6,4},{7,5},{8,10},{9,11},{10,... | collective-permute-start | bytes 1572872 | tf_op jit(solution)/shard_map/ppermute | solution.py:663
  41.1 0.5 collective-permute-start.10
  41.6 0.1 collective-permute-start.13
  41.7 1.0 slice.34
  42.7 8.2 %collective-permute-done.7 = bf16[1584,128]{1,0:T(8,128)(2,1)S(1)} collective-permute-done((bf16[1584,128]{1,0:T(8,128)(2,1)S(1)}, bf16[1584,128]{1,0:T(8,128)(2,1)S(1)}, u32[]{:S(2)}, u32[]{:S(2)}) %collective-permute-start.7) | collective-permute-done | bytes 405536 | tf_op jit(solution)/shard_map/ppermute | solution.py:675
  51.0 0.1 collective-permute-start.14
  51.1 0.1 pad_maximum_fusion.2.refs_18_
  51.2 1.6 %collective-permute-start.15 = (bf16[2,16,64,128]{3,2,1,0:T(8,128)(2,1)S(1)}, bf16[2,16,64,128]{3,2,1,0:T(8,128)(2,1)}, u32[]{:S(2)}, u32[]{:S(2)}) collective-permute-start(bf16[2,16,64,128]{3,2,1,0:T(8,128)(2,1)S(1)} %pad_maximum_fusion.2.refs_18_), channel_id=1, source_target_pairs={{0,2},{1,3},{2,0},{3,1},{4,6},{5,7},{6,4},{7,5},{8,10},{9,11},{10,... | collective-permute-start | bytes 1572872 | tf_op jit(solution)/shard_map/ppermute | solution.py:663
  52.8 1.5 %collective-permute-start.12 = (bf16[1584,128]{1,0:T(8,128)(2,1)S(1)}, bf16[1584,128]{1,0:T(8,128)(2,1)}, u32[]{:S(2)}, u32[]{:S(2)}) collective-permute-start(bf16[1584,128]{1,0:T(8,128)(2,1)S(1)} %broadcast_select_fusion.refs_8_), channel_id=1, source_target_pairs={{0,4},{4,0},{8,12},{12,8},{16,20},{20,16},{24,28},{28,24},{1,5},{5... | collective-permute-start | bytes 1216520 | tf_op jit(solution)/shard_map/ppermute | solution.py:638
  54.3 4.5 %all-to-all-start.1 = ((bf16[8,128,256]{2,1,0:T(8,128)(2,1)}), bf16[8,128,256]{2,1,0:T(8,128)(2,1)S(1)}, u32[]{:S(2)}, u32[]{:S(2)}) async-start(bf16[8,128,256]{2,1,0:T(8,128)(2,1)} %bitcast.12), calls=%async_computation.1 | async-start | bytes 1048576 | tf_op jit(solution)/shard_map/all_to_all | solution.py:637
  58.8 9.1 %collective-permute-done.12.refs_9_ = bf16[1584,128]{1,0:T(8,128)(2,1)} collective-permute-done((bf16[1584,128]{1,0:T(8,128)(2,1)S(1)}, bf16[1584,128]{1,0:T(8,128)(2,1)}, u32[]{:S(2)}, u32[]{:S(2)}) %collective-permute-start.12) | collective-permute-done | bytes 405536 | tf_op jit(solution)/shard_map/ppermute | solution.py:638
  67.9 1.0 slice.30
  68.9 0.8 collective-permute-start.19
  69.7 0.5 collective-permute-start.18
  70.2 5.2 %collective-permute-done.19.refs_24_ = bf16[1,16,64,128]{3,2,1,0:T(8,128)(2,1)} collective-permute-done((bf16[1,16,64,128]{3,2,1,0:T(8,128)(2,1)S(1)}, bf16[1,16,64,128]{3,2,1,0:T(8,128)(2,1)}, u32[]{:S(2)}, u32[]{:S(2)}) %collective-permute-start.19) | collective-permute-done | bytes 262176 | tf_op jit(solution)/shard_map/ppermute | solution.py:663
  75.4 0.8 copy-done.15
  76.2 1.1 collective-permute-done.20.refs_25_
  77.4 17.4 %layer.1 = (bf16[256,128]{1,0:T(8,128)(2,1)}, bf16[256,128]{1,0:T(8,128)(2,1)}, bf16[256,128]{1,0:T(8,128)(2,1)}, bf16[256,128]{1,0:T(8,128)(2,1)}, bf16[256,128...) custom-call(bf16[256,2048]{1,0:T(8,128)(2,1)} %tokens.3, ...), custom_call_target="tpu_custom_call" | custom-call | flops 4294967296 | bytes 8388608 | tf_op jit(solution)/shard_map/layer/pallas_call | solution.py:494
  94.8 5.6 %collective-permute-start.21 = (bf16[256,128]{1,0:T(8,128)(2,1)}, bf16[256,128]{1,0:T(8,128)(2,1)S(1)}, u32[]{:S(2)}, u32[]{:S(2)}) collective-permute-start(bf16[256,128]{1,0:T(8,128)(2,1)} %get-tuple-element.42), channel_id=1, source_target_pairs={{0,24},{4,28},{8,16},{12,20},{16,8},{20,12},{24,0},{28,4},{1,25},{... | collective-permute-start | bytes 196616 | tf_op jit(solution)/shard_map/ppermute | solution.py:691
  100.4 1.0 collective-permute-start.22
  101.4 2.9 %collective-permute-start.24 = (bf16[256,128]{1,0:T(8,128)(2,1)}, bf16[256,128]{1,0:T(8,128)(2,1)S(1)}, u32[]{:S(2)}, u32[]{:S(2)}) collective-permute-start(bf16[256,128]{1,0:T(8,128)(2,1)} %get-tuple-element.45), channel_id=1, source_target_pairs={{0,16},{4,20},{8,24},{12,28},{16,0},{20,4},{24,8},{28,12},{1,17},{... | collective-permute-start | bytes 196616 | tf_op jit(solution)/shard_map/ppermute | solution.py:691
  104.3 2.3 %collective-permute-start.25 = (bf16[256,128]{1,0:T(8,128)(2,1)}, bf16[256,128]{1,0:T(8,128)(2,1)S(1)}, u32[]{:S(2)}, u32[]{:S(2)}) collective-permute-start(bf16[256,128]{1,0:T(8,128)(2,1)} %get-tuple-element.46), channel_id=1, source_target_pairs={{0,12},{4,8},{8,4},{12,0},{16,28},{20,24},{24,20},{28,16},{1,13},{... | collective-permute-start | bytes 196616 | tf_op jit(solution)/shard_map/ppermute | solution.py:691
  106.6 0.6 collective-permute-start.26
  107.3 0.8 collective-permute-done.22.refs_1_
  108.1 2.6 %collective-permute-start.27 = (bf16[256,128]{1,0:T(8,128)(2,1)}, bf16[256,128]{1,0:T(8,128)(2,1)S(1)}, u32[]{:S(2)}, u32[]{:S(2)}) collective-permute-start(bf16[256,128]{1,0:T(8,128)(2,1)} %get-tuple-element.48), channel_id=1, source_target_pairs={{0,4},{4,0},{8,12},{12,8},{16,20},{20,16},{24,28},{28,24},{1,5},{5... | collective-permute-start | bytes 196616 | tf_op jit(solution)/shard_map/ppermute | solution.py:691
  110.6 0.1 reshape.45.gain
  110.7 0.7 slice.31.gated
  111.4 2.2 %hold.1.weight = bf16[1024,2048]{1,0:T(8,128)(2,1)S(1)} custom-call(bf16[16,128]{1,0:T(8,128)(2,1)S(1)} %slice.31.gated, bf16[1024,2048]{1,0:T(8,128)(2,1)} %bitcast.30), custom_call_target="tpu_custom_call" | custom-call | bytes 8388608 | tf_op jit(solution)/shard_map/hold/pallas_call | solution.py:531
  113.7 1.4 %close.3 = (bf16[64,2048]{1,0:T(8,128)(2,1)S(1)}, bf16[64,2048]{1,0:T(8,128)(2,1)S(1)}) custom-call(f32[1,1024]{1,0:T(1,128)S(1)} %reshape.45.gain, bf16[1024,2048]{1,0:T(8,128)(2,1)S(1)} %hold.1.weight, bf16[256,128]{1,0:T(8,128)(2,1)S(1)} %collective-permute-done.21.refs_0_, bf16[256,128]{1,0:T(8,128)(2,1)S(1)} %collective-permute-done.22.refs_1_, ...), custom_call_target="tpu_custom_call" | custom-call | flops 536870912 | bytes 4194304 | tf_op jit(solution)/shard_map/close/pallas_call | solution.py:577
  115.1 0.1 collective-permute-start.29
  115.1 1.4 %close.2 = (bf16[64,2048]{1,0:T(8,128)(2,1)S(1)}, bf16[64,2048]{1,0:T(8,128)(2,1)S(1)}) custom-call(f32[1,1024]{1,0:T(1,128)S(1)} %reshape.45.gain, bf16[1024,2048]{1,0:T(8,128)(2,1)S(1)} %hold.1.weight, bf16[256,128]{1,0:T(8,128)(2,1)S(1)} %collective-permute-done.21.refs_0_, bf16[256,128]{1,0:T(8,128)(2,1)S(1)} %collective-permute-done.22.refs_1_, ...), custom_call_target="tpu_custom_call" | custom-call | flops 536870912 | bytes 4194304 | tf_op jit(solution)/shard_map/close/pallas_call | solution.py:577
  116.5 0.6 collective-permute-start.28
  117.1 0.1 add_convert_fusion.1
  117.2 1.4 %collective-permute-start.30 = (bf16[64,2048]{1,0:T(8,128)(2,1)S(1)}, bf16[64,2048]{1,0:T(8,128)(2,1)S(1)}, u32[]{:S(2)}, u32[]{:S(2)}) collective-permute-start(bf16[64,2048]{1,0:T(8,128)(2,1)S(1)} %add_convert_fusion.1), channel_id=1, source_target_pairs={{0,2},{1,3},{2,0},{3,1},{4,6},{5,7},{6,4},{7,5},{8,10},{9,11},{10,... | collective-permute-start | bytes 786440 | tf_op jit(solution)/shard_map/ppermute | solution.py:699
  118.6 6.9 %collective-permute-done.30 = bf16[64,2048]{1,0:T(8,128)(2,1)S(1)} collective-permute-done((bf16[64,2048]{1,0:T(8,128)(2,1)S(1)}, bf16[64,2048]{1,0:T(8,128)(2,1)S(1)}, u32[]{:S(2)}, u32[]{:S(2)}) %collective-permute-start.30) | collective-permute-done | bytes 262176 | tf_op jit(solution)/shard_map/ppermute | solution.py:699
  125.5 0.8 add_convert_fusion
  (66 shorter events, 0.3 us)
Async XLA Ops:
  2.7 12.7 %collective-permute-start = (bf16[1584,128]{1,0:T(8,128)(2,1)}, bf16[1584,128]{1,0:T(8,128)(2,1)S(1)}, u32[]{:S(2)}, u32[]{:S(2)}) collective-permute-start(bf16[1584,128]{1,0:T(8,128)(2,1)} %pack.1.refs_2_), channel_id=1, source_target_pairs={{0,8},{4,12},{8,0},{12,4},{16,24},{20,28},{24,16},{28,20},{1,9},{5... | collective-permute-start | bytes 1216520 | tf_op jit(solution)/shard_map/ppermute | solution.py:632
  5.8 9.6 %collective-permute-start.1 = (bf16[1584,128]{1,0:T(8,128)(2,1)}, bf16[1584,128]{1,0:T(8,128)(2,1)S(1)}, u32[]{:S(2)}, u32[]{:S(2)}) collective-permute-start(bf16[1584,128]{1,0:T(8,128)(2,1)} %pack.1.refs_2_), channel_id=1, source_target_pairs={{8,16},{12,20},{16,8},{20,12},{9,17},{13,21},{17,9},{21,13},{10,18... | collective-permute-start | bytes 1216520 | tf_op jit(solution)/shard_map/ppermute | solution.py:633
  6.5 11.1 %collective-permute-start.2 = (bf16[1584,128]{1,0:T(8,128)(2,1)}, bf16[1584,128]{1,0:T(8,128)(2,1)S(1)}, u32[]{:S(2)}, u32[]{:S(2)}) collective-permute-start(bf16[1584,128]{1,0:T(8,128)(2,1)} %pack.1.refs_2_), channel_id=1, source_target_pairs={{0,4},{4,0},{8,12},{12,8},{16,20},{20,16},{24,28},{28,24},{1,5},{5... | collective-permute-start | bytes 1216520 | tf_op jit(solution)/shard_map/ppermute | solution.py:634
  15.4 18.4 %copy-start.9 = (bf16[1584,128]{1,0:T(8,128)(2,1)}, bf16[1584,128]{1,0:T(8,128)(2,1)S(1)}, u32[]{:S(2)}) copy-start(bf16[1584,128]{1,0:T(8,128)(2,1)S(1)} %collective-permute-done.refs_4_) | copy-start | bytes 1216516
  17.6 5.2 %copy-start.10 = (bf16[1584,128]{1,0:T(8,128)(2,1)}, bf16[1584,128]{1,0:T(8,128)(2,1)S(1)}, u32[]{:S(2)}) copy-start(bf16[1584,128]{1,0:T(8,128)(2,1)S(1)} %collective-permute-done.2.refs_3_) | copy-start | bytes 1216516
  17.6 13.2 %collective-permute-start.5 = (bf16[1584,128]{1,0:T(8,128)(2,1)S(1)}, bf16[1584,128]{1,0:T(8,128)(2,1)S(1)}, u32[]{:S(2)}, u32[]{:S(2)}) collective-permute-start(bf16[1584,128]{1,0:T(8,128)(2,1)S(1)} %collective-permute-done.1), channel_id=1, source_target_pairs={{8,0},{12,4},{16,24},{20,28},{9,1},{13,5},{17,25},{21,29},{10,2},{... | collective-permute-start | bytes 1216520 | tf_op jit(solution)/shard_map/ppermute | solution.py:670
  18.9 12.0 %collective-permute-start.4 = (bf16[1584,128]{1,0:T(8,128)(2,1)S(1)}, bf16[1584,128]{1,0:T(8,128)(2,1)S(1)}, u32[]{:S(2)}, u32[]{:S(2)}) collective-permute-start(bf16[1584,128]{1,0:T(8,128)(2,1)S(1)} %collective-permute-done.refs_4_), channel_id=1, source_target_pairs={{0,4},{4,0},{8,12},{12,8},{16,20},{20,16},{24,28},{28,24},{1,5},{5... | collective-permute-start | bytes 1216520 | tf_op jit(solution)/shard_map/ppermute | solution.py:638
  20.5 12.0 %collective-permute-start.3 = (bf16[1584,128]{1,0:T(8,128)(2,1)S(1)}, bf16[1584,128]{1,0:T(8,128)(2,1)S(1)}, u32[]{:S(2)}, u32[]{:S(2)}) collective-permute-start(bf16[1584,128]{1,0:T(8,128)(2,1)S(1)} %collective-permute-done.refs_4_), channel_id=1, source_target_pairs={{8,16},{12,20},{16,8},{20,12},{9,17},{13,21},{17,9},{21,13},{10,18... | collective-permute-start | bytes 1216520 | tf_op jit(solution)/shard_map/ppermute | solution.py:669
  21.3 33.0 %copy-start.3 = (bf16[2,16,64,128]{3,2,1,0:T(8,128)(2,1)}, bf16[2,16,64,128]{3,2,1,0:T(8,128)(2,1)S(1)}, u32[]{:S(2)}) copy-start(bf16[2,16,64,128]{3,2,1,0:T(8,128)(2,1)S(1)} %pad_maximum_fusion.refs_10_) | copy-start | bytes 1572868
  21.3 19.8 %collective-permute-start.9 = (bf16[2,16,64,128]{3,2,1,0:T(8,128)(2,1)S(1)}, bf16[2,16,64,128]{3,2,1,0:T(8,128)(2,1)}, u32[]{:S(2)}, u32[]{:S(2)}) collective-permute-start(bf16[2,16,64,128]{3,2,1,0:T(8,128)(2,1)S(1)} %pad_maximum_fusion.refs_10_), channel_id=1, source_target_pairs={{0,2},{1,3},{2,0},{3,1},{4,6},{5,7},{6,4},{7,5},{8,10},{9,11},{10,... | collective-permute-start | bytes 1572872 | tf_op jit(solution)/shard_map/ppermute | solution.py:663
  30.9 46.4 %copy-start.1 = (bf16[1584,128]{1,0:T(8,128)(2,1)}, bf16[1584,128]{1,0:T(8,128)(2,1)S(1)}, u32[]{:S(2)}) copy-start(bf16[1584,128]{1,0:T(8,128)(2,1)S(1)} %broadcast_select_fusion.1.refs_6_) | copy-start | bytes 1216516
  31.0 1.6 %copy-start.11 = (bf16[1584,128]{1,0:T(8,128)(2,1)}, bf16[1584,128]{1,0:T(8,128)(2,1)S(1)}, u32[]{:S(2)}) copy-start(bf16[1584,128]{1,0:T(8,128)(2,1)S(1)} %collective-permute-done.4.refs_5_) | copy-start | bytes 1216516
  31.0 10.7 %collective-permute-start.6 = (bf16[1584,128]{1,0:T(8,128)(2,1)S(1)}, bf16[1584,128]{1,0:T(8,128)(2,1)}, u32[]{:S(2)}, u32[]{:S(2)}) collective-permute-start(bf16[1584,128]{1,0:T(8,128)(2,1)S(1)} %broadcast_select_fusion.1.refs_6_), channel_id=1, source_target_pairs={{0,4},{4,0},{8,12},{12,8},{16,20},{20,16},{24,28},{28,24},{1,5},{5... | collective-permute-start | bytes 1216520 | tf_op jit(solution)/shard_map/ppermute | solution.py:638
  32.5 18.4 %collective-permute-start.7 = (bf16[1584,128]{1,0:T(8,128)(2,1)S(1)}, bf16[1584,128]{1,0:T(8,128)(2,1)S(1)}, u32[]{:S(2)}, u32[]{:S(2)}) collective-permute-start(bf16[1584,128]{1,0:T(8,128)(2,1)S(1)} %collective-permute-done.3), channel_id=1, source_target_pairs={{8,0},{12,4},{16,24},{20,28},{9,1},{13,5},{17,25},{21,29},{10,2},{... | collective-permute-start | bytes 1216520 | tf_op jit(solution)/shard_map/ppermute | solution.py:675
  33.8 20.4 %all-to-all-start = ((bf16[8,128,256]{2,1,0:T(8,128)(2,1)}), bf16[8,128,256]{2,1,0:T(8,128)(2,1)S(1)}, u32[]{:S(2)}, u32[]{:S(2)}) async-start(bf16[8,128,256]{2,1,0:T(8,128)(2,1)} %bitcast.4), calls=%async_computation | async-start | bytes 1048576 | tf_op jit(solution)/shard_map/all_to_all | solution.py:637
  39.5 37.8 %copy-start.5 = (bf16[2,16,64,128]{3,2,1,0:T(8,128)(2,1)}, bf16[2,16,64,128]{3,2,1,0:T(8,128)(2,1)S(1)}, u32[]{:S(2)}) copy-start(bf16[2,16,64,128]{3,2,1,0:T(8,128)(2,1)S(1)} %pad_maximum_fusion.1.refs_14_) | copy-start | bytes 1572868
  39.5 11.4 %collective-permute-start.11 = (bf16[2,16,64,128]{3,2,1,0:T(8,128)(2,1)S(1)}, bf16[2,16,64,128]{3,2,1,0:T(8,128)(2,1)}, u32[]{:S(2)}, u32[]{:S(2)}) collective-permute-start(bf16[2,16,64,128]{3,2,1,0:T(8,128)(2,1)S(1)} %pad_maximum_fusion.1.refs_14_), channel_id=1, source_target_pairs={{0,2},{1,3},{2,0},{3,1},{4,6},{5,7},{6,4},{7,5},{8,10},{9,11},{10,... | collective-permute-start | bytes 1572872 | tf_op jit(solution)/shard_map/ppermute | solution.py:663
  41.1 9.9 %collective-permute-start.8 = (bf16[2,16,64,128]{3,2,1,0:T(8,128)(2,1)S(1)}, bf16[2,16,64,128]{3,2,1,0:T(8,128)(2,1)S(1)}, u32[]{:S(2)}, u32[]{:S(2)}) collective-permute-start(bf16[2,16,64,128]{3,2,1,0:T(8,128)(2,1)S(1)} %pad_maximum_fusion.refs_10_), channel_id=1, source_target_pairs={{0,1},{1,0},{2,3},{3,2},{4,5},{5,4},{6,7},{7,6},{8,9},{9,8},{10,11... | collective-permute-start | bytes 1572872 | tf_op jit(solution)/shard_map/ppermute | solution.py:662
  41.1 10.0 %collective-permute-start.10 = (bf16[2,16,64,128]{3,2,1,0:T(8,128)(2,1)}, bf16[2,16,64,128]{3,2,1,0:T(8,128)(2,1)S(1)}, u32[]{:S(2)}, u32[]{:S(2)}) collective-permute-start(bf16[2,16,64,128]{3,2,1,0:T(8,128)(2,1)} %collective-permute-done.9.refs_12_), channel_id=1, source_target_pairs={{0,1},{1,0},{2,3},{3,2},{4,5},{5,4},{6,7},{7,6},{8,9},{9,8},{10,11... | collective-permute-start | bytes 1572872 | tf_op jit(solution)/shard_map/ppermute | solution.py:664
  41.6 17.2 %collective-permute-start.13 = (bf16[2,16,64,128]{3,2,1,0:T(8,128)(2,1)S(1)}, bf16[2,16,64,128]{3,2,1,0:T(8,128)(2,1)}, u32[]{:S(2)}, u32[]{:S(2)}) collective-permute-start(bf16[2,16,64,128]{3,2,1,0:T(8,128)(2,1)S(1)} %pad_maximum_fusion.1.refs_14_), channel_id=1, source_target_pairs={{0,1},{1,0},{2,3},{3,2},{4,5},{5,4},{6,7},{7,6},{8,9},{9,8},{10,11... | collective-permute-start | bytes 1572872 | tf_op jit(solution)/shard_map/ppermute | solution.py:662
  51.0 26.4 %copy-start.2 = (bf16[1584,128]{1,0:T(8,128)(2,1)}, bf16[1584,128]{1,0:T(8,128)(2,1)S(1)}, u32[]{:S(2)}) copy-start(bf16[1584,128]{1,0:T(8,128)(2,1)S(1)} %broadcast_select_fusion.refs_8_) | copy-start | bytes 1216516
  51.0 16.9 %collective-permute-start.14 = (bf16[2,16,64,128]{3,2,1,0:T(8,128)(2,1)}, bf16[2,16,64,128]{3,2,1,0:T(8,128)(2,1)}, u32[]{:S(2)}, u32[]{:S(2)}) collective-permute-start(bf16[2,16,64,128]{3,2,1,0:T(8,128)(2,1)} %collective-permute-done.11.refs_16_), channel_id=1, source_target_pairs={{0,1},{1,0},{2,3},{3,2},{4,5},{5,4},{6,7},{7,6},{8,9},{9,8},{10,11... | collective-permute-start | bytes 1572872 | tf_op jit(solution)/shard_map/ppermute | solution.py:664
  51.1 1.7 %copy-start.13 = (bf16[2,16,64,128]{3,2,1,0:T(8,128)(2,1)}, bf16[2,16,64,128]{3,2,1,0:T(8,128)(2,1)S(1)}, u32[]{:S(2)}) copy-start(bf16[2,16,64,128]{3,2,1,0:T(8,128)(2,1)S(1)} %collective-permute-done.8.refs_11_) | copy-start | bytes 1572868
  51.1 1.7 %copy-start.14 = (bf16[2,16,64,128]{3,2,1,0:T(8,128)(2,1)}, bf16[2,16,64,128]{3,2,1,0:T(8,128)(2,1)S(1)}, u32[]{:S(2)}) copy-start(bf16[2,16,64,128]{3,2,1,0:T(8,128)(2,1)S(1)} %collective-permute-done.10.refs_13_) | copy-start | bytes 1572868
  51.2 26.1 %copy-start.6 = (bf16[2,16,64,128]{3,2,1,0:T(8,128)(2,1)}, bf16[2,16,64,128]{3,2,1,0:T(8,128)(2,1)S(1)}, u32[]{:S(2)}) copy-start(bf16[2,16,64,128]{3,2,1,0:T(8,128)(2,1)S(1)} %pad_maximum_fusion.2.refs_18_) | copy-start | bytes 1572868
  51.2 16.7 %collective-permute-start.15 = (bf16[2,16,64,128]{3,2,1,0:T(8,128)(2,1)S(1)}, bf16[2,16,64,128]{3,2,1,0:T(8,128)(2,1)}, u32[]{:S(2)}, u32[]{:S(2)}) collective-permute-start(bf16[2,16,64,128]{3,2,1,0:T(8,128)(2,1)S(1)} %pad_maximum_fusion.2.refs_18_), channel_id=1, source_target_pairs={{0,2},{1,3},{2,0},{3,1},{4,6},{5,7},{6,4},{7,5},{8,10},{9,11},{10,... | collective-permute-start | bytes 1572872 | tf_op jit(solution)/shard_map/ppermute | solution.py:663
  52.8 15.1 %collective-permute-start.12 = (bf16[1584,128]{1,0:T(8,128)(2,1)S(1)}, bf16[1584,128]{1,0:T(8,128)(2,1)}, u32[]{:S(2)}, u32[]{:S(2)}) collective-permute-start(bf16[1584,128]{1,0:T(8,128)(2,1)S(1)} %broadcast_select_fusion.refs_8_), channel_id=1, source_target_pairs={{0,4},{4,0},{8,12},{12,8},{16,20},{20,16},{24,28},{28,24},{1,5},{5... | collective-permute-start | bytes 1216520 | tf_op jit(solution)/shard_map/ppermute | solution.py:638
  54.3 23.1 %copy-start.4 = (bf16[8,128,256]{2,1,0:T(8,128)(2,1)}, bf16[8,128,256]{2,1,0:T(8,128)(2,1)S(1)}, u32[]{:S(2)}) copy-start(bf16[8,128,256]{2,1,0:T(8,128)(2,1)S(1)} %all-to-all-done.refs_0_) | copy-start | bytes 1572868
  54.3 22.0 %all-to-all-start.1 = ((bf16[8,128,256]{2,1,0:T(8,128)(2,1)}), bf16[8,128,256]{2,1,0:T(8,128)(2,1)S(1)}, u32[]{:S(2)}, u32[]{:S(2)}) async-start(bf16[8,128,256]{2,1,0:T(8,128)(2,1)} %bitcast.12), calls=%async_computation.1 | async-start | bytes 1048576 | tf_op jit(solution)/shard_map/all_to_all | solution.py:637
  58.8 16.6 %collective-permute-start.16 = (bf16[2,16,64,128]{3,2,1,0:T(8,128)(2,1)S(1)}, bf16[2,16,64,128]{3,2,1,0:T(8,128)(2,1)S(1)}, u32[]{:S(2)}, u32[]{:S(2)}) collective-permute-start(bf16[2,16,64,128]{3,2,1,0:T(8,128)(2,1)S(1)} %pad_maximum_fusion.2.refs_18_), channel_id=1, source_target_pairs={{0,1},{1,0},{2,3},{3,2},{4,5},{5,4},{6,7},{7,6},{8,9},{9,8},{10,11... | collective-permute-start | bytes 1572872 | tf_op jit(solution)/shard_map/ppermute | solution.py:662
  68.9 8.5 %copy-start.8 = (bf16[1024,128]{1,0:T(8,128)(2,1)}, bf16[1024,128]{1,0:T(8,128)(2,1)S(1)}, u32[]{:S(2)}) copy-start(bf16[1024,128]{1,0:T(8,128)(2,1)S(1)} %slice.30) | copy-start | bytes 786436
  68.9 41.8 %copy-start.12 = (f32[16,64]{1,0:T(8,128)S(1)}, f32[16,64]{1,0:T(8,128)}, u32[]{:S(2)}) copy-start(f32[16,64]{1,0:T(8,128)} %param.30) | copy-start | bytes 12292
  68.9 6.5 %collective-permute-start.19 = (bf16[1,16,64,128]{3,2,1,0:T(8,128)(2,1)S(1)}, bf16[1,16,64,128]{3,2,1,0:T(8,128)(2,1)}, u32[]{:S(2)}, u32[]{:S(2)}) collective-permute-start(bf16[1,16,64,128]{3,2,1,0:T(8,128)(2,1)S(1)} %bitcast.37), channel_id=1, source_target_pairs={{0,2},{1,3},{2,0},{3,1},{4,6},{5,7},{6,4},{7,5},{8,10},{9,11},{10,... | collective-permute-start | bytes 786440 | tf_op jit(solution)/shard_map/ppermute | solution.py:663
  69.7 7.6 %collective-permute-start.17 = (bf16[2,16,64,128]{3,2,1,0:T(8,128)(2,1)}, bf16[2,16,64,128]{3,2,1,0:T(8,128)(2,1)}, u32[]{:S(2)}, u32[]{:S(2)}) collective-permute-start(bf16[2,16,64,128]{3,2,1,0:T(8,128)(2,1)} %collective-permute-done.15.refs_20_), channel_id=1, source_target_pairs={{0,1},{1,0},{2,3},{3,2},{4,5},{5,4},{6,7},{7,6},{8,9},{9,8},{10,11... | collective-permute-start | bytes 1572872 | tf_op jit(solution)/shard_map/ppermute | solution.py:664
  69.7 6.5 %collective-permute-start.18 = (bf16[1,16,64,128]{3,2,1,0:T(8,128)(2,1)S(1)}, bf16[1,16,64,128]{3,2,1,0:T(8,128)(2,1)}, u32[]{:S(2)}, u32[]{:S(2)}) collective-permute-start(bf16[1,16,64,128]{3,2,1,0:T(8,128)(2,1)S(1)} %bitcast.38), channel_id=1, source_target_pairs={{0,1},{1,0},{2,3},{3,2},{4,5},{5,4},{6,7},{7,6},{8,9},{9,8},{10,11... | collective-permute-start | bytes 786440 | tf_op jit(solution)/shard_map/ppermute | solution.py:662
  75.4 1.9 %collective-permute-start.20 = (bf16[1,16,64,128]{3,2,1,0:T(8,128)(2,1)}, bf16[1,16,64,128]{3,2,1,0:T(8,128)(2,1)}, u32[]{:S(2)}, u32[]{:S(2)}) collective-permute-start(bf16[1,16,64,128]{3,2,1,0:T(8,128)(2,1)} %collective-permute-done.19.refs_24_), channel_id=1, source_target_pairs={{0,1},{1,0},{2,3},{3,2},{4,5},{5,4},{6,7},{7,6},{8,9},{9,8},{10,11... | collective-permute-start | bytes 786440 | tf_op jit(solution)/shard_map/ppermute | solution.py:664
  75.4 0.8 copy-start.15
  76.2 1.1 copy-start.7
  94.8 11.9 %collective-permute-start.21 = (bf16[256,128]{1,0:T(8,128)(2,1)}, bf16[256,128]{1,0:T(8,128)(2,1)S(1)}, u32[]{:S(2)}, u32[]{:S(2)}) collective-permute-start(bf16[256,128]{1,0:T(8,128)(2,1)} %get-tuple-element.42), channel_id=1, source_target_pairs={{0,24},{4,28},{8,16},{12,20},{16,8},{20,12},{24,0},{28,4},{1,25},{... | collective-permute-start | bytes 196616 | tf_op jit(solution)/shard_map/ppermute | solution.py:691
  100.4 7.7 %collective-permute-start.22 = (bf16[256,128]{1,0:T(8,128)(2,1)}, bf16[256,128]{1,0:T(8,128)(2,1)S(1)}, u32[]{:S(2)}, u32[]{:S(2)}) collective-permute-start(bf16[256,128]{1,0:T(8,128)(2,1)} %get-tuple-element.43), channel_id=1, source_target_pairs={{0,28},{4,24},{8,20},{12,16},{16,12},{20,8},{24,4},{28,0},{1,29},{... | collective-permute-start | bytes 196616 | tf_op jit(solution)/shard_map/ppermute | solution.py:691
  101.4 12.2 %collective-permute-start.23 = (bf16[256,128]{1,0:T(8,128)(2,1)}, bf16[256,128]{1,0:T(8,128)(2,1)S(1)}, u32[]{:S(2)}, u32[]{:S(2)}) collective-permute-start(bf16[256,128]{1,0:T(8,128)(2,1)} %get-tuple-element.44), channel_id=1, source_target_pairs={{0,20},{4,16},{8,28},{12,24},{16,4},{20,0},{24,12},{28,8},{1,21},{... | collective-permute-start | bytes 196616 | tf_op jit(solution)/shard_map/ppermute | solution.py:691
  101.4 12.2 %collective-permute-start.24 = (bf16[256,128]{1,0:T(8,128)(2,1)}, bf16[256,128]{1,0:T(8,128)(2,1)S(1)}, u32[]{:S(2)}, u32[]{:S(2)}) collective-permute-start(bf16[256,128]{1,0:T(8,128)(2,1)} %get-tuple-element.45), channel_id=1, source_target_pairs={{0,16},{4,20},{8,24},{12,28},{16,0},{20,4},{24,8},{28,12},{1,17},{... | collective-permute-start | bytes 196616 | tf_op jit(solution)/shard_map/ppermute | solution.py:691
  104.3 9.4 %collective-permute-start.25 = (bf16[256,128]{1,0:T(8,128)(2,1)}, bf16[256,128]{1,0:T(8,128)(2,1)S(1)}, u32[]{:S(2)}, u32[]{:S(2)}) collective-permute-start(bf16[256,128]{1,0:T(8,128)(2,1)} %get-tuple-element.46), channel_id=1, source_target_pairs={{0,12},{4,8},{8,4},{12,0},{16,28},{20,24},{24,20},{28,16},{1,13},{... | collective-permute-start | bytes 196616 | tf_op jit(solution)/shard_map/ppermute | solution.py:691
  106.6 7.0 %collective-permute-start.26 = (bf16[256,128]{1,0:T(8,128)(2,1)}, bf16[256,128]{1,0:T(8,128)(2,1)S(1)}, u32[]{:S(2)}, u32[]{:S(2)}) collective-permute-start(bf16[256,128]{1,0:T(8,128)(2,1)} %get-tuple-element.47), channel_id=1, source_target_pairs={{0,8},{4,12},{8,0},{12,4},{16,24},{20,28},{24,16},{28,20},{1,9},{5... | collective-permute-start | bytes 196616 | tf_op jit(solution)/shard_map/ppermute | solution.py:691
  108.1 5.6 %collective-permute-start.27 = (bf16[256,128]{1,0:T(8,128)(2,1)}, bf16[256,128]{1,0:T(8,128)(2,1)S(1)}, u32[]{:S(2)}, u32[]{:S(2)}) collective-permute-start(bf16[256,128]{1,0:T(8,128)(2,1)} %get-tuple-element.48), channel_id=1, source_target_pairs={{0,4},{4,0},{8,12},{12,8},{16,20},{20,16},{24,28},{28,24},{1,5},{5... | collective-permute-start | bytes 196616 | tf_op jit(solution)/shard_map/ppermute | solution.py:691
  111.4 2.3 %copy-start = (bf16[256,128]{1,0:T(8,128)(2,1)S(1)}, bf16[256,128]{1,0:T(8,128)(2,1)}, u32[]{:S(2)}) copy-start(bf16[256,128]{1,0:T(8,128)(2,1)} %get-tuple-element.41.refs_7_) | copy-start | bytes 196612
  115.1 2.0 %collective-permute-start.29 = (bf16[64,2048]{1,0:T(8,128)(2,1)S(1)}, bf16[64,2048]{1,0:T(8,128)(2,1)S(1)}, u32[]{:S(2)}, u32[]{:S(2)}) collective-permute-start(bf16[64,2048]{1,0:T(8,128)(2,1)S(1)} %get-tuple-element.52), channel_id=1, source_target_pairs={{0,1},{1,0},{2,3},{3,2},{4,5},{5,4},{6,7},{7,6},{8,9},{9,8},{10,11... | collective-permute-start | bytes 786440 | tf_op jit(solution)/shard_map/ppermute | solution.py:695
  116.5 2.0 %collective-permute-start.28 = (bf16[64,2048]{1,0:T(8,128)(2,1)S(1)}, bf16[64,2048]{1,0:T(8,128)(2,1)S(1)}, u32[]{:S(2)}, u32[]{:S(2)}) collective-permute-start(bf16[64,2048]{1,0:T(8,128)(2,1)S(1)} %get-tuple-element.50), channel_id=1, source_target_pairs={{0,1},{1,0},{2,3},{3,2},{4,5},{5,4},{6,7},{7,6},{8,9},{9,8},{10,11... | collective-permute-start | bytes 786440 | tf_op jit(solution)/shard_map/ppermute | solution.py:698
  117.2 8.3 %collective-permute-start.30 = (bf16[64,2048]{1,0:T(8,128)(2,1)S(1)}, bf16[64,2048]{1,0:T(8,128)(2,1)S(1)}, u32[]{:S(2)}, u32[]{:S(2)}) collective-permute-start(bf16[64,2048]{1,0:T(8,128)(2,1)S(1)} %add_convert_fusion.1), channel_id=1, source_target_pairs={{0,2},{1,3},{2,0},{3,1},{4,6},{5,7},{6,4},{7,5},{8,10},{9,11},{10,... | collective-permute-start | bytes 786440 | tf_op jit(solution)/shard_map/ppermute | solution.py:699

commit v7 on v6

--- a/solution.py
+++ b/solution.py
@@ -672,6 +672,7 @@
     x_weight = trade(x_weight)
     groups = [spread(near, across_own)]
 
+    mid_far = after(mid_far, groups[0][1])
     out_far = lax.ppermute(mid_far, "seq", outward)
     second = jnp.where(inner, mid, out_near)
     groups.append(spread(second, across_near))

time: 127 us -> 125 us (0.984)
  waiting for transfers between devices: 43.1 us -> 40 us
    ppermute x3, waiting for transfers between devices: 9.06 us -> 3.04 us  [tokens_travel(): cross = lambda item: lax.ppermute(item, 'seq', swap(ring, 1))]
    ppermute x4, waiting for transfers between devices: 5.21 us -> 8.22 us  [spread(): across = lax.ppermute(own, 'mp', swap(seats, 2))]
    ppermute x1, waiting for transfers between devices: 8.24 us -> 5.32 us  [tokens_travel(): out_far = lax.ppermute(mid_far, 'seq', outward)]
    all_to_all x2, waiting for transfers between devices: 0.01 us -> 2.82 us  [tokens_travel(): lax.all_to_all(w, 'seq', split_axis=0, concat_axis=0, tiled=True)]
    unnamed x33, local copies, waits for them, and re-layouts: 2.13 us -> 3.8 us
    ppermute x7, waiting for transfers between devices: 0.8 us -> 2.39 us  [tokens_travel(): lax.ppermute(gated[at], 'seq', swap(ring, at))]
  transfers between devices with their start and end apart: 33 -> 33, of which waited for: 9 -> 14; matrix products, arithmetic and copies ran while one was open for 8% -> 7% of each run, Pallas kernels for 3% -> 3%
where the time goes in v7:
time: 125 us; the launch traced here: 124 us
  starting transfers between devices  46.5 us (37%)
  waiting for transfers between devices  40 us (32%)
  Pallas kernels  25 us (20%)
  local copies, waits for them, and re-layouts  9.79 us (8%)
  other arithmetic  2.43 us (2%)
    pallas_call x1, Pallas kernels, layer(): pl.pallas_call(functools.partial(layer_kernel, head_size, counts), in_spe...  17.3 us
    ppermute x7, starting transfers between devices, tokens_travel(): lax.ppermute(gated[at], 'seq', swap(ring, at))  15 us
    all_to_all x2, starting transfers between devices, tokens_travel(): lax.all_to_all(w, 'seq', split_axis=0, concat_axis=0, tiled=True)  10.4 us
    ppermute x4, waiting for transfers between devices, spread(): across = lax.ppermute(own, 'mp', swap(seats, 2))  8.22 us
    ppermute x1, waiting for transfers between devices, tokens_travel(): out_near = lax.ppermute(mid, 'seq', outward)  7.91 us
    ppermute x1, waiting for transfers between devices, tokens_travel(): took_far = lax.ppermute(send, 'mp', swap(seats, 2))  6.5 us
    ppermute x1, waiting for transfers between devices, tokens_travel(): out_far = lax.ppermute(mid_far, 'seq', outward)  5.32 us
    ppermute x4, starting transfers between devices, spread(): across = lax.ppermute(own, 'mp', swap(seats, 2))  4.61 us
  transfers between devices with their start and end apart: 33, of which 14 were waited for; matrix products, arithmetic and copies ran while one was open for 7% of the time, Pallas kernels for 3%

profile of v7, /device:TPU:0, one launch (start us, length us, event | category | flops | bytes accessed | tf_op | source)
XLA Modules:
  0.0 124.1 jit_solution(18013062875768082746)
XLA Ops:
  0.0 2.7 %pack.1.refs_2_ = bf16[1584,128]{1,0:T(8,128)(2,1)} custom-call(bf16[256,2048]{1,0:T(8,128)(2,1)} %tokens.3, bf16[512,128]{1,0:T(8,128)(2,1)} %bitcast.40, bf16[16,256]{1,0:T(8,128)(2,1)} %bitcast.42, s32[2,128]{1,0:T(2,128)} %bitcast.45), custom_call_target="tpu_custom_call" | custom-call | tf_op jit(solution)/shard_map/pack/pallas_call | solution.py:263
  2.7 3.1 %collective-permute-start = (bf16[1584,128]{1,0:T(8,128)(2,1)}, bf16[1584,128]{1,0:T(8,128)(2,1)S(1)}, u32[]{:S(2)}, u32[]{:S(2)}) collective-permute-start(bf16[1584,128]{1,0:T(8,128)(2,1)} %pack.1.refs_2_), channel_id=1, source_target_pairs={{0,8},{4,12},{8,0},{12,4},{16,24},{20,28},{24,16},{28,20},{1,9},{5... | collective-permute-start | bytes 1216520 | tf_op jit(solution)/shard_map/ppermute | solution.py:632
  5.8 0.7 collective-permute-start.1
  6.5 1.6 %collective-permute-start.2 = (bf16[1584,128]{1,0:T(8,128)(2,1)}, bf16[1584,128]{1,0:T(8,128)(2,1)S(1)}, u32[]{:S(2)}, u32[]{:S(2)}) collective-permute-start(bf16[1584,128]{1,0:T(8,128)(2,1)} %pack.1.refs_2_), channel_id=1, source_target_pairs={{0,4},{4,0},{8,12},{12,8},{16,20},{20,16},{24,28},{28,24},{1,5},{5... | collective-permute-start | bytes 1216520 | tf_op jit(solution)/shard_map/ppermute | solution.py:634
  8.1 0.8 concatenate.12
  8.9 0.7 broadcast_in_dim.11
  9.6 0.1 broadcast_in_dim.12
  9.7 0.1 broadcast_in_dim.13
  9.8 0.8 concatenate.13
  10.6 0.7 maximum_bitcast_fusion.1
  11.3 0.1 copy.18
  11.4 1.3 %copy.22 = f32[1,4,2,128]{3,1,2,0:T(4,128)} copy(f32[1,4,2,128]{3,2,1,0:T(2,128)} %bitcast.43) | data formatting | bytes 8192
  12.6 0.6 pad.4.refs_26_
  13.3 0.6 maximum_bitcast_fusion.refs_27_
  13.9 1.5 %collective-permute-done.refs_4_ = bf16[1584,128]{1,0:T(8,128)(2,1)S(1)} collective-permute-done((bf16[1584,128]{1,0:T(8,128)(2,1)}, bf16[1584,128]{1,0:T(8,128)(2,1)S(1)}, u32[]{:S(2)}, u32[]{:S(2)}) %collective-permute-start) | collective-permute-done | bytes 405536 | tf_op jit(solution)/shard_map/ppermute | solution.py:632
  15.4 2.2 %collective-permute-done.2.refs_3_ = bf16[1584,128]{1,0:T(8,128)(2,1)S(1)} collective-permute-done((bf16[1584,128]{1,0:T(8,128)(2,1)}, bf16[1584,128]{1,0:T(8,128)(2,1)S(1)}, u32[]{:S(2)}, u32[]{:S(2)}) %collective-permute-start.2) | collective-permute-done | bytes 405536 | tf_op jit(solution)/shard_map/ppermute | solution.py:634
  17.6 1.3 %collective-permute-start.6 = (bf16[1584,128]{1,0:T(8,128)(2,1)S(1)}, bf16[1584,128]{1,0:T(8,128)(2,1)S(1)}, u32[]{:S(2)}, u32[]{:S(2)}) collective-permute-start(bf16[1584,128]{1,0:T(8,128)(2,1)S(1)} %collective-permute-done.1), channel_id=1, source_target_pairs={{8,0},{12,4},{16,24},{20,28},{9,1},{13,5},{17,25},{21,29},{10,2},{... | collective-permute-start | bytes 1216520 | tf_op jit(solution)/shard_map/ppermute | solution.py:670
  18.9 0.7 collective-permute-start.3
  19.6 1.6 %collective-permute-start.5 = (bf16[1584,128]{1,0:T(8,128)(2,1)S(1)}, bf16[1584,128]{1,0:T(8,128)(2,1)S(1)}, u32[]{:S(2)}, u32[]{:S(2)}) collective-permute-start(bf16[1584,128]{1,0:T(8,128)(2,1)S(1)} %collective-permute-done.refs_4_), channel_id=1, source_target_pairs={{0,4},{4,0},{8,12},{12,8},{16,20},{20,16},{24,28},{28,24},{1,5},{5... | collective-permute-start | bytes 1216520 | tf_op jit(solution)/shard_map/ppermute | solution.py:638
  21.4 1.6 %collective-permute-start.9 = (bf16[2,16,64,128]{3,2,1,0:T(8,128)(2,1)S(1)}, bf16[2,16,64,128]{3,2,1,0:T(8,128)(2,1)}, u32[]{:S(2)}, u32[]{:S(2)}) collective-permute-start(bf16[2,16,64,128]{3,2,1,0:T(8,128)(2,1)S(1)} %pad_maximum_fusion.refs_10_), channel_id=1, source_target_pairs={{0,2},{1,3},{2,0},{3,1},{4,6},{5,7},{6,4},{7,5},{8,10},{9,11},{10,... | collective-permute-start | bytes 1572872 | tf_op jit(solution)/shard_map/ppermute | solution.py:663
  23.0 7.9 %collective-permute-done.6 = bf16[1584,128]{1,0:T(8,128)(2,1)S(1)} collective-permute-done((bf16[1584,128]{1,0:T(8,128)(2,1)S(1)}, bf16[1584,128]{1,0:T(8,128)(2,1)S(1)}, u32[]{:S(2)}, u32[]{:S(2)}) %collective-permute-start.6) | collective-permute-done | bytes 405536 | tf_op jit(solution)/shard_map/ppermute | solution.py:670
  31.1 1.6 %collective-permute-start.11 = (bf16[2,16,64,128]{3,2,1,0:T(8,128)(2,1)S(1)}, bf16[2,16,64,128]{3,2,1,0:T(8,128)(2,1)}, u32[]{:S(2)}, u32[]{:S(2)}) collective-permute-start(bf16[2,16,64,128]{3,2,1,0:T(8,128)(2,1)S(1)} %pad_maximum_fusion.1.refs_14_), channel_id=1, source_target_pairs={{0,2},{1,3},{2,0},{3,1},{4,6},{5,7},{6,4},{7,5},{8,10},{9,11},{10,... | collective-permute-start | bytes 1572872 | tf_op jit(solution)/shard_map/ppermute | solution.py:663
  32.7 1.5 %collective-permute-start.7 = (bf16[1584,128]{1,0:T(8,128)(2,1)S(1)}, bf16[1584,128]{1,0:T(8,128)(2,1)}, u32[]{:S(2)}, u32[]{:S(2)}) collective-permute-start(bf16[1584,128]{1,0:T(8,128)(2,1)S(1)} %broadcast_select_fusion.1.refs_6_), channel_id=1, source_target_pairs={{0,4},{4,0},{8,12},{12,8},{16,20},{20,16},{24,28},{28,24},{1,5},{5... | collective-permute-start | bytes 1216520 | tf_op jit(solution)/shard_map/ppermute | solution.py:638
  34.2 0.8 copy-done.13
  34.9 1.3 %collective-permute-start.8 = (bf16[1584,128]{1,0:T(8,128)(2,1)S(1)}, bf16[1584,128]{1,0:T(8,128)(2,1)S(1)}, u32[]{:S(2)}, u32[]{:S(2)}) collective-permute-start(bf16[1584,128]{1,0:T(8,128)(2,1)S(1)} %collective-permute-done.3), channel_id=1, source_target_pairs={{8,0},{12,4},{16,24},{20,28},{9,1},{13,5},{17,25},{21,29},{10,2},{... | collective-permute-start | bytes 1216520 | tf_op jit(solution)/shard_map/ppermute | solution.py:676
  36.2 6.2 %all-to-all-start = ((bf16[8,128,256]{2,1,0:T(8,128)(2,1)}), bf16[8,128,256]{2,1,0:T(8,128)(2,1)S(1)}, u32[]{:S(2)}, u32[]{:S(2)}) async-start(bf16[8,128,256]{2,1,0:T(8,128)(2,1)} %bitcast.4), calls=%async_computation | async-start | bytes 1048576 | tf_op jit(solution)/shard_map/all_to_all | solution.py:637
  42.5 0.5 collective-permute-start.13
  43.0 1.0 slice.34
  44.0 3.1 %collective-permute-done.11.refs_16_ = bf16[2,16,64,128]{3,2,1,0:T(8,128)(2,1)} collective-permute-done((bf16[2,16,64,128]{3,2,1,0:T(8,128)(2,1)S(1)}, bf16[2,16,64,128]{3,2,1,0:T(8,128)(2,1)}, u32[]{:S(2)}, u32[]{:S(2)}) %collective-permute-start.11) | collective-permute-done | bytes 524320 | tf_op jit(solution)/shard_map/ppermute | solution.py:663
  47.1 5.3 %collective-permute-done.8 = bf16[1584,128]{1,0:T(8,128)(2,1)S(1)} collective-permute-done((bf16[1584,128]{1,0:T(8,128)(2,1)S(1)}, bf16[1584,128]{1,0:T(8,128)(2,1)S(1)}, u32[]{:S(2)}, u32[]{:S(2)}) %collective-permute-start.8) | collective-permute-done | bytes 405536 | tf_op jit(solution)/shard_map/ppermute | solution.py:676
  52.5 0.6 collective-permute-start.15
  53.1 0.2 copy-done.14
  53.3 1.2 collective-permute-start.12
  54.5 0.7 all-to-all-done.refs_0_
  55.3 4.2 %all-to-all-start.1 = ((bf16[8,128,256]{2,1,0:T(8,128)(2,1)}), bf16[8,128,256]{2,1,0:T(8,128)(2,1)S(1)}, u32[]{:S(2)}, u32[]{:S(2)}) async-start(bf16[8,128,256]{2,1,0:T(8,128)(2,1)} %bitcast.12), calls=%async_computation.1 | async-start | bytes 1048576 | tf_op jit(solution)/shard_map/all_to_all | solution.py:637
  59.5 3.0 %collective-permute-done.12.refs_9_ = bf16[1584,128]{1,0:T(8,128)(2,1)} collective-permute-done((bf16[1584,128]{1,0:T(8,128)(2,1)S(1)}, bf16[1584,128]{1,0:T(8,128)(2,1)}, u32[]{:S(2)}, u32[]{:S(2)}) %collective-permute-start.12) | collective-permute-done | bytes 405536 | tf_op jit(solution)/shard_map/ppermute | solution.py:638
  62.5 1.0 slice.30
  63.5 0.9 collective-permute-start.19
  64.4 0.5 collective-permute-start.18
  64.9 5.2 %collective-permute-done.19.refs_24_ = bf16[1,16,64,128]{3,2,1,0:T(8,128)(2,1)} collective-permute-done((bf16[1,16,64,128]{3,2,1,0:T(8,128)(2,1)S(1)}, bf16[1,16,64,128]{3,2,1,0:T(8,128)(2,1)}, u32[]{:S(2)}, u32[]{:S(2)}) %collective-permute-start.19) | collective-permute-done | bytes 262176 | tf_op jit(solution)/shard_map/ppermute | solution.py:663
  70.1 0.8 copy-done.15
  70.9 2.1 %all-to-all-done.1.refs_1_ = bf16[8,128,256]{2,1,0:T(8,128)(2,1)S(1)} async-done(((bf16[8,128,256]{2,1,0:T(8,128)(2,1)}), bf16[8,128,256]{2,1,0:T(8,128)(2,1)S(1)}, u32[]{:S(2)}, u32[]{:S(2)}) %all-to-all-start.1) | async-done | bytes 524320 | tf_op jit(solution)/shard_map/all_to_all | solution.py:637
  73.0 0.7 copy-done.7
  73.8 17.3 %layer.1 = (bf16[256,128]{1,0:T(8,128)(2,1)}, bf16[256,128]{1,0:T(8,128)(2,1)}, bf16[256,128]{1,0:T(8,128)(2,1)}, bf16[256,128]{1,0:T(8,128)(2,1)}, bf16[256,128...) custom-call(bf16[256,2048]{1,0:T(8,128)(2,1)} %tokens.3, ...), custom_call_target="tpu_custom_call" | custom-call | flops 4294967296 | bytes 8388608 | tf_op jit(solution)/shard_map/layer/pallas_call | solution.py:494
  91.1 3.3 %collective-permute-start.21 = (bf16[256,128]{1,0:T(8,128)(2,1)}, bf16[256,128]{1,0:T(8,128)(2,1)S(1)}, u32[]{:S(2)}, u32[]{:S(2)}) collective-permute-start(bf16[256,128]{1,0:T(8,128)(2,1)} %get-tuple-element.44), channel_id=1, source_target_pairs={{0,24},{4,28},{8,16},{12,20},{16,8},{20,12},{24,0},{28,4},{1,25},{... | collective-permute-start | bytes 196616 | tf_op jit(solution)/shard_map/ppermute | solution.py:692
  94.4 1.4 %collective-permute-start.22 = (bf16[256,128]{1,0:T(8,128)(2,1)}, bf16[256,128]{1,0:T(8,128)(2,1)S(1)}, u32[]{:S(2)}, u32[]{:S(2)}) collective-permute-start(bf16[256,128]{1,0:T(8,128)(2,1)} %get-tuple-element.45), channel_id=1, source_target_pairs={{0,28},{4,24},{8,20},{12,16},{16,12},{20,8},{24,4},{28,0},{1,29},{... | collective-permute-start | bytes 196616 | tf_op jit(solution)/shard_map/ppermute | solution.py:692
  95.9 5.4 %collective-permute-start.23 = (bf16[256,128]{1,0:T(8,128)(2,1)}, bf16[256,128]{1,0:T(8,128)(2,1)S(1)}, u32[]{:S(2)}, u32[]{:S(2)}) collective-permute-start(bf16[256,128]{1,0:T(8,128)(2,1)} %get-tuple-element.46), channel_id=1, source_target_pairs={{0,20},{4,16},{8,28},{12,24},{16,4},{20,0},{24,12},{28,8},{1,21},{... | collective-permute-start | bytes 196616 | tf_op jit(solution)/shard_map/ppermute | solution.py:692
  101.3 1.3 %collective-permute-start.24 = (bf16[256,128]{1,0:T(8,128)(2,1)}, bf16[256,128]{1,0:T(8,128)(2,1)S(1)}, u32[]{:S(2)}, u32[]{:S(2)}) collective-permute-start(bf16[256,128]{1,0:T(8,128)(2,1)} %get-tuple-element.47), channel_id=1, source_target_pairs={{0,16},{4,20},{8,24},{12,28},{16,0},{20,4},{24,8},{28,12},{1,17},{... | collective-permute-start | bytes 196616 | tf_op jit(solution)/shard_map/ppermute | solution.py:692
  102.6 2.4 %collective-permute-start.25 = (bf16[256,128]{1,0:T(8,128)(2,1)}, bf16[256,128]{1,0:T(8,128)(2,1)S(1)}, u32[]{:S(2)}, u32[]{:S(2)}) collective-permute-start(bf16[256,128]{1,0:T(8,128)(2,1)} %get-tuple-element.48), channel_id=1, source_target_pairs={{0,12},{4,8},{8,4},{12,0},{16,28},{20,24},{24,20},{28,16},{1,13},{... | collective-permute-start | bytes 196616 | tf_op jit(solution)/shard_map/ppermute | solution.py:692
  105.1 0.5 collective-permute-start.26
  105.6 0.6 collective-permute-start.27
  106.1 0.1 reshape.45.gain
  106.2 0.7 slice.31.gated
  106.9 2.2 %hold.1.weight = bf16[1024,2048]{1,0:T(8,128)(2,1)S(1)} custom-call(bf16[16,128]{1,0:T(8,128)(2,1)S(1)} %slice.31.gated, bf16[1024,2048]{1,0:T(8,128)(2,1)} %bitcast.30), custom_call_target="tpu_custom_call" | custom-call | bytes 8388608 | tf_op jit(solution)/shard_map/hold/pallas_call | solution.py:531
  109.1 0.3 collective-permute-done.23.refs_2_
  109.4 0.9 collective-permute-done.24.refs_3_
  110.3 0.1 collective-permute-done.25.refs_4_
  110.4 1.1 collective-permute-done.26.refs_5_
  111.5 1.4 %close.3 = (bf16[64,2048]{1,0:T(8,128)(2,1)S(1)}, bf16[64,2048]{1,0:T(8,128)(2,1)S(1)}) custom-call(f32[1,1024]{1,0:T(1,128)S(1)} %reshape.45.gain, bf16[1024,2048]{1,0:T(8,128)(2,1)S(1)} %hold.1.weight, bf16[256,128]{1,0:T(8,128)(2,1)S(1)} %collective-permute-done.21.refs_0_, bf16[256,128]{1,0:T(8,128)(2,1)S(1)} %collective-permute-done.22.refs_1_, ...), custom_call_target="tpu_custom_call" | custom-call | flops 536870912 | bytes 4194304 | tf_op jit(solution)/shard_map/close/pallas_call | solution.py:577
  113.0 1.4 %close.2 = (bf16[64,2048]{1,0:T(8,128)(2,1)S(1)}, bf16[64,2048]{1,0:T(8,128)(2,1)S(1)}) custom-call(f32[1,1024]{1,0:T(1,128)S(1)} %reshape.45.gain, bf16[1024,2048]{1,0:T(8,128)(2,1)S(1)} %hold.1.weight, bf16[256,128]{1,0:T(8,128)(2,1)S(1)} %collective-permute-done.21.refs_0_, bf16[256,128]{1,0:T(8,128)(2,1)S(1)} %collective-permute-done.22.refs_1_, ...), custom_call_target="tpu_custom_call" | custom-call | flops 536870912 | bytes 4194304 | tf_op jit(solution)/shard_map/close/pallas_call | solution.py:577
  114.3 0.6 collective-permute-start.28
  115.0 1.8 %collective-permute-start.30 = (bf16[64,2048]{1,0:T(8,128)(2,1)S(1)}, bf16[64,2048]{1,0:T(8,128)(2,1)S(1)}, u32[]{:S(2)}, u32[]{:S(2)}) collective-permute-start(bf16[64,2048]{1,0:T(8,128)(2,1)S(1)} %add_convert_fusion.1), channel_id=1, source_target_pairs={{0,2},{1,3},{2,0},{3,1},{4,6},{5,7},{6,4},{7,5},{8,10},{9,11},{10,... | collective-permute-start | bytes 786440 | tf_op jit(solution)/shard_map/ppermute | solution.py:700
  116.8 6.5 %collective-permute-done.30 = bf16[64,2048]{1,0:T(8,128)(2,1)S(1)} collective-permute-done((bf16[64,2048]{1,0:T(8,128)(2,1)S(1)}, bf16[64,2048]{1,0:T(8,128)(2,1)S(1)}, u32[]{:S(2)}, u32[]{:S(2)}) %collective-permute-start.30) | collective-permute-done | bytes 262176 | tf_op jit(solution)/shard_map/ppermute | solution.py:700
  123.3 0.8 add_convert_fusion
  (66 shorter events, 0.7 us)
Async XLA Ops:
  2.7 12.7 %collective-permute-start = (bf16[1584,128]{1,0:T(8,128)(2,1)}, bf16[1584,128]{1,0:T(8,128)(2,1)S(1)}, u32[]{:S(2)}, u32[]{:S(2)}) collective-permute-start(bf16[1584,128]{1,0:T(8,128)(2,1)} %pack.1.refs_2_), channel_id=1, source_target_pairs={{0,8},{4,12},{8,0},{12,4},{16,24},{20,28},{24,16},{28,20},{1,9},{5... | collective-permute-start | bytes 1216520 | tf_op jit(solution)/shard_map/ppermute | solution.py:632
  5.8 9.6 %collective-permute-start.1 = (bf16[1584,128]{1,0:T(8,128)(2,1)}, bf16[1584,128]{1,0:T(8,128)(2,1)S(1)}, u32[]{:S(2)}, u32[]{:S(2)}) collective-permute-start(bf16[1584,128]{1,0:T(8,128)(2,1)} %pack.1.refs_2_), channel_id=1, source_target_pairs={{8,16},{12,20},{16,8},{20,12},{9,17},{13,21},{17,9},{21,13},{10,18... | collective-permute-start | bytes 1216520 | tf_op jit(solution)/shard_map/ppermute | solution.py:633
  6.5 11.1 %collective-permute-start.2 = (bf16[1584,128]{1,0:T(8,128)(2,1)}, bf16[1584,128]{1,0:T(8,128)(2,1)S(1)}, u32[]{:S(2)}, u32[]{:S(2)}) collective-permute-start(bf16[1584,128]{1,0:T(8,128)(2,1)} %pack.1.refs_2_), channel_id=1, source_target_pairs={{0,4},{4,0},{8,12},{12,8},{16,20},{20,16},{24,28},{28,24},{1,5},{5... | collective-permute-start | bytes 1216520 | tf_op jit(solution)/shard_map/ppermute | solution.py:634
  15.4 20.8 %copy-start.9 = (bf16[1584,128]{1,0:T(8,128)(2,1)}, bf16[1584,128]{1,0:T(8,128)(2,1)S(1)}, u32[]{:S(2)}) copy-start(bf16[1584,128]{1,0:T(8,128)(2,1)S(1)} %collective-permute-done.refs_4_) | copy-start | bytes 1216516
  17.6 5.3 %copy-start.10 = (bf16[1584,128]{1,0:T(8,128)(2,1)}, bf16[1584,128]{1,0:T(8,128)(2,1)S(1)}, u32[]{:S(2)}) copy-start(bf16[1584,128]{1,0:T(8,128)(2,1)S(1)} %collective-permute-done.2.refs_3_) | copy-start | bytes 1216516
  17.6 13.2 %collective-permute-start.6 = (bf16[1584,128]{1,0:T(8,128)(2,1)S(1)}, bf16[1584,128]{1,0:T(8,128)(2,1)S(1)}, u32[]{:S(2)}, u32[]{:S(2)}) collective-permute-start(bf16[1584,128]{1,0:T(8,128)(2,1)S(1)} %collective-permute-done.1), channel_id=1, source_target_pairs={{8,0},{12,4},{16,24},{20,28},{9,1},{13,5},{17,25},{21,29},{10,2},{... | collective-permute-start | bytes 1216520 | tf_op jit(solution)/shard_map/ppermute | solution.py:670
  18.9 15.2 %collective-permute-start.3 = (bf16[1584,128]{1,0:T(8,128)(2,1)S(1)}, bf16[1584,128]{1,0:T(8,128)(2,1)S(1)}, u32[]{:S(2)}, u32[]{:S(2)}) collective-permute-start(bf16[1584,128]{1,0:T(8,128)(2,1)S(1)} %collective-permute-done.refs_4_), channel_id=1, source_target_pairs={{8,16},{12,20},{16,8},{20,12},{9,17},{13,21},{17,9},{21,13},{10,18... | collective-permute-start | bytes 1216520 | tf_op jit(solution)/shard_map/ppermute | solution.py:669
  19.6 11.3 %collective-permute-start.5 = (bf16[1584,128]{1,0:T(8,128)(2,1)S(1)}, bf16[1584,128]{1,0:T(8,128)(2,1)S(1)}, u32[]{:S(2)}, u32[]{:S(2)}) collective-permute-start(bf16[1584,128]{1,0:T(8,128)(2,1)S(1)} %collective-permute-done.refs_4_), channel_id=1, source_target_pairs={{0,4},{4,0},{8,12},{12,8},{16,20},{20,16},{24,28},{28,24},{1,5},{5... | collective-permute-start | bytes 1216520 | tf_op jit(solution)/shard_map/ppermute | solution.py:638
  21.3 34.0 %copy-start.3 = (bf16[2,16,64,128]{3,2,1,0:T(8,128)(2,1)}, bf16[2,16,64,128]{3,2,1,0:T(8,128)(2,1)S(1)}, u32[]{:S(2)}) copy-start(bf16[2,16,64,128]{3,2,1,0:T(8,128)(2,1)S(1)} %pad_maximum_fusion.refs_10_) | copy-start | bytes 1572868
  21.3 12.9 %collective-permute-start.4 = (bf16[2,16,64,128]{3,2,1,0:T(8,128)(2,1)S(1)}, bf16[2,16,64,128]{3,2,1,0:T(8,128)(2,1)S(1)}, u32[]{:S(2)}, u32[]{:S(2)}) collective-permute-start(bf16[2,16,64,128]{3,2,1,0:T(8,128)(2,1)S(1)} %pad_maximum_fusion.refs_10_), channel_id=1, source_target_pairs={{0,1},{1,0},{2,3},{3,2},{4,5},{5,4},{6,7},{7,6},{8,9},{9,8},{10,11... | collective-permute-start | bytes 1572872 | tf_op jit(solution)/shard_map/ppermute | solution.py:662
  21.4 21.1 %collective-permute-start.9 = (bf16[2,16,64,128]{3,2,1,0:T(8,128)(2,1)S(1)}, bf16[2,16,64,128]{3,2,1,0:T(8,128)(2,1)}, u32[]{:S(2)}, u32[]{:S(2)}) collective-permute-start(bf16[2,16,64,128]{3,2,1,0:T(8,128)(2,1)S(1)} %pad_maximum_fusion.refs_10_), channel_id=1, source_target_pairs={{0,2},{1,3},{2,0},{3,1},{4,6},{5,7},{6,4},{7,5},{8,10},{9,11},{10,... | collective-permute-start | bytes 1572872 | tf_op jit(solution)/shard_map/ppermute | solution.py:663
  30.9 42.1 %copy-start.1 = (bf16[1584,128]{1,0:T(8,128)(2,1)}, bf16[1584,128]{1,0:T(8,128)(2,1)S(1)}, u32[]{:S(2)}) copy-start(bf16[1584,128]{1,0:T(8,128)(2,1)S(1)} %broadcast_select_fusion.1.refs_6_) | copy-start | bytes 1216516
  31.0 3.2 %copy-start.11 = (bf16[1584,128]{1,0:T(8,128)(2,1)}, bf16[1584,128]{1,0:T(8,128)(2,1)S(1)}, u32[]{:S(2)}) copy-start(bf16[1584,128]{1,0:T(8,128)(2,1)S(1)} %collective-permute-done.5.refs_5_) | copy-start | bytes 1216516
  31.1 41.9 %copy-start.4 = (bf16[2,16,64,128]{3,2,1,0:T(8,128)(2,1)}, bf16[2,16,64,128]{3,2,1,0:T(8,128)(2,1)S(1)}, u32[]{:S(2)}) copy-start(bf16[2,16,64,128]{3,2,1,0:T(8,128)(2,1)S(1)} %pad_maximum_fusion.1.refs_14_) | copy-start | bytes 1572868
  31.1 16.0 %collective-permute-start.11 = (bf16[2,16,64,128]{3,2,1,0:T(8,128)(2,1)S(1)}, bf16[2,16,64,128]{3,2,1,0:T(8,128)(2,1)}, u32[]{:S(2)}, u32[]{:S(2)}) collective-permute-start(bf16[2,16,64,128]{3,2,1,0:T(8,128)(2,1)S(1)} %pad_maximum_fusion.1.refs_14_), channel_id=1, source_target_pairs={{0,2},{1,3},{2,0},{3,1},{4,6},{5,7},{6,4},{7,5},{8,10},{9,11},{10,... | collective-permute-start | bytes 1572872 | tf_op jit(solution)/shard_map/ppermute | solution.py:663
  32.7 10.4 %collective-permute-start.7 = (bf16[1584,128]{1,0:T(8,128)(2,1)S(1)}, bf16[1584,128]{1,0:T(8,128)(2,1)}, u32[]{:S(2)}, u32[]{:S(2)}) collective-permute-start(bf16[1584,128]{1,0:T(8,128)(2,1)S(1)} %broadcast_select_fusion.1.refs_6_), channel_id=1, source_target_pairs={{0,4},{4,0},{8,12},{12,8},{16,20},{20,16},{24,28},{28,24},{1,5},{5... | collective-permute-start | bytes 1216520 | tf_op jit(solution)/shard_map/ppermute | solution.py:638
  34.2 0.8 copy-start.13
  34.9 17.4 %collective-permute-start.8 = (bf16[1584,128]{1,0:T(8,128)(2,1)S(1)}, bf16[1584,128]{1,0:T(8,128)(2,1)S(1)}, u32[]{:S(2)}, u32[]{:S(2)}) collective-permute-start(bf16[1584,128]{1,0:T(8,128)(2,1)S(1)} %collective-permute-done.3), channel_id=1, source_target_pairs={{8,0},{12,4},{16,24},{20,28},{9,1},{13,5},{17,25},{21,29},{10,2},{... | collective-permute-start | bytes 1216520 | tf_op jit(solution)/shard_map/ppermute | solution.py:676
  36.2 19.0 %all-to-all-start = ((bf16[8,128,256]{2,1,0:T(8,128)(2,1)}), bf16[8,128,256]{2,1,0:T(8,128)(2,1)S(1)}, u32[]{:S(2)}, u32[]{:S(2)}) async-start(bf16[8,128,256]{2,1,0:T(8,128)(2,1)} %bitcast.4), calls=%async_computation | async-start | bytes 1048576 | tf_op jit(solution)/shard_map/all_to_all | solution.py:637
  42.4 10.0 %collective-permute-start.10 = (bf16[2,16,64,128]{3,2,1,0:T(8,128)(2,1)}, bf16[2,16,64,128]{3,2,1,0:T(8,128)(2,1)S(1)}, u32[]{:S(2)}, u32[]{:S(2)}) collective-permute-start(bf16[2,16,64,128]{3,2,1,0:T(8,128)(2,1)} %collective-permute-done.9.refs_12_), channel_id=1, source_target_pairs={{0,1},{1,0},{2,3},{3,2},{4,5},{5,4},{6,7},{7,6},{8,9},{9,8},{10,11... | collective-permute-start | bytes 1572872 | tf_op jit(solution)/shard_map/ppermute | solution.py:664
  42.5 17.0 %collective-permute-start.13 = (bf16[2,16,64,128]{3,2,1,0:T(8,128)(2,1)S(1)}, bf16[2,16,64,128]{3,2,1,0:T(8,128)(2,1)}, u32[]{:S(2)}, u32[]{:S(2)}) collective-permute-start(bf16[2,16,64,128]{3,2,1,0:T(8,128)(2,1)S(1)} %pad_maximum_fusion.1.refs_14_), channel_id=1, source_target_pairs={{0,1},{1,0},{2,3},{3,2},{4,5},{5,4},{6,7},{7,6},{8,9},{9,8},{10,11... | collective-permute-start | bytes 1572872 | tf_op jit(solution)/shard_map/ppermute | solution.py:662
  47.0 15.5 %collective-permute-start.14 = (bf16[2,16,64,128]{3,2,1,0:T(8,128)(2,1)}, bf16[2,16,64,128]{3,2,1,0:T(8,128)(2,1)}, u32[]{:S(2)}, u32[]{:S(2)}) collective-permute-start(bf16[2,16,64,128]{3,2,1,0:T(8,128)(2,1)} %collective-permute-done.11.refs_16_), channel_id=1, source_target_pairs={{0,1},{1,0},{2,3},{3,2},{4,5},{5,4},{6,7},{7,6},{8,9},{9,8},{10,11... | collective-permute-start | bytes 1572872 | tf_op jit(solution)/shard_map/ppermute | solution.py:664
  52.4 20.6 %copy-start.2 = (bf16[1584,128]{1,0:T(8,128)(2,1)}, bf16[1584,128]{1,0:T(8,128)(2,1)S(1)}, u32[]{:S(2)}) copy-start(bf16[1584,128]{1,0:T(8,128)(2,1)S(1)} %broadcast_select_fusion.refs_8_) | copy-start | bytes 1216516
  52.4 0.8 copy-start.14
  52.5 20.5 %copy-start.6 = (bf16[2,16,64,128]{3,2,1,0:T(8,128)(2,1)}, bf16[2,16,64,128]{3,2,1,0:T(8,128)(2,1)S(1)}, u32[]{:S(2)}) copy-start(bf16[2,16,64,128]{3,2,1,0:T(8,128)(2,1)S(1)} %pad_maximum_fusion.2.refs_18_) | copy-start | bytes 1572868
  52.5 10.0 %collective-permute-start.15 = (bf16[2,16,64,128]{3,2,1,0:T(8,128)(2,1)S(1)}, bf16[2,16,64,128]{3,2,1,0:T(8,128)(2,1)}, u32[]{:S(2)}, u32[]{:S(2)}) collective-permute-start(bf16[2,16,64,128]{3,2,1,0:T(8,128)(2,1)S(1)} %pad_maximum_fusion.2.refs_18_), channel_id=1, source_target_pairs={{0,2},{1,3},{2,0},{3,1},{4,6},{5,7},{6,4},{7,5},{8,10},{9,11},{10,... | collective-permute-start | bytes 1572872 | tf_op jit(solution)/shard_map/ppermute | solution.py:663
  53.3 9.3 %collective-permute-start.12 = (bf16[1584,128]{1,0:T(8,128)(2,1)S(1)}, bf16[1584,128]{1,0:T(8,128)(2,1)}, u32[]{:S(2)}, u32[]{:S(2)}) collective-permute-start(bf16[1584,128]{1,0:T(8,128)(2,1)S(1)} %broadcast_select_fusion.refs_8_), channel_id=1, source_target_pairs={{0,4},{4,0},{8,12},{12,8},{16,20},{20,16},{24,28},{28,24},{1,5},{5... | collective-permute-start | bytes 1216520 | tf_op jit(solution)/shard_map/ppermute | solution.py:638
  55.3 17.8 %copy-start.5 = (bf16[8,128,256]{2,1,0:T(8,128)(2,1)}, bf16[8,128,256]{2,1,0:T(8,128)(2,1)S(1)}, u32[]{:S(2)}) copy-start(bf16[8,128,256]{2,1,0:T(8,128)(2,1)S(1)} %all-to-all-done.refs_0_) | copy-start | bytes 1572868
  55.3 17.7 %all-to-all-start.1 = ((bf16[8,128,256]{2,1,0:T(8,128)(2,1)}), bf16[8,128,256]{2,1,0:T(8,128)(2,1)S(1)}, u32[]{:S(2)}, u32[]{:S(2)}) async-start(bf16[8,128,256]{2,1,0:T(8,128)(2,1)} %bitcast.12), calls=%async_computation.1 | async-start | bytes 1048576 | tf_op jit(solution)/shard_map/all_to_all | solution.py:637
  59.5 10.6 %collective-permute-start.16 = (bf16[2,16,64,128]{3,2,1,0:T(8,128)(2,1)S(1)}, bf16[2,16,64,128]{3,2,1,0:T(8,128)(2,1)S(1)}, u32[]{:S(2)}, u32[]{:S(2)}) collective-permute-start(bf16[2,16,64,128]{3,2,1,0:T(8,128)(2,1)S(1)} %pad_maximum_fusion.2.refs_18_), channel_id=1, source_target_pairs={{0,1},{1,0},{2,3},{3,2},{4,5},{5,4},{6,7},{7,6},{8,9},{9,8},{10,11... | collective-permute-start | bytes 1572872 | tf_op jit(solution)/shard_map/ppermute | solution.py:662
  63.5 9.5 %copy-start.8 = (bf16[1024,128]{1,0:T(8,128)(2,1)}, bf16[1024,128]{1,0:T(8,128)(2,1)S(1)}, u32[]{:S(2)}) copy-start(bf16[1024,128]{1,0:T(8,128)(2,1)S(1)} %slice.30) | copy-start | bytes 786436
  63.5 42.6 %copy-start.12 = (f32[16,64]{1,0:T(8,128)S(1)}, f32[16,64]{1,0:T(8,128)}, u32[]{:S(2)}) copy-start(f32[16,64]{1,0:T(8,128)} %param.30) | copy-start | bytes 12292
  63.5 6.5 %collective-permute-start.19 = (bf16[1,16,64,128]{3,2,1,0:T(8,128)(2,1)S(1)}, bf16[1,16,64,128]{3,2,1,0:T(8,128)(2,1)}, u32[]{:S(2)}, u32[]{:S(2)}) collective-permute-start(bf16[1,16,64,128]{3,2,1,0:T(8,128)(2,1)S(1)} %bitcast.37), channel_id=1, source_target_pairs={{0,2},{1,3},{2,0},{3,1},{4,6},{5,7},{6,4},{7,5},{8,10},{9,11},{10,... | collective-permute-start | bytes 786440 | tf_op jit(solution)/shard_map/ppermute | solution.py:663
  64.4 8.6 %collective-permute-start.17 = (bf16[2,16,64,128]{3,2,1,0:T(8,128)(2,1)}, bf16[2,16,64,128]{3,2,1,0:T(8,128)(2,1)}, u32[]{:S(2)}, u32[]{:S(2)}) collective-permute-start(bf16[2,16,64,128]{3,2,1,0:T(8,128)(2,1)} %collective-permute-done.15.refs_20_), channel_id=1, source_target_pairs={{0,1},{1,0},{2,3},{3,2},{4,5},{5,4},{6,7},{7,6},{8,9},{9,8},{10,11... | collective-permute-start | bytes 1572872 | tf_op jit(solution)/shard_map/ppermute | solution.py:664
  64.4 6.5 %collective-permute-start.18 = (bf16[1,16,64,128]{3,2,1,0:T(8,128)(2,1)S(1)}, bf16[1,16,64,128]{3,2,1,0:T(8,128)(2,1)}, u32[]{:S(2)}, u32[]{:S(2)}) collective-permute-start(bf16[1,16,64,128]{3,2,1,0:T(8,128)(2,1)S(1)} %bitcast.38), channel_id=1, source_target_pairs={{0,1},{1,0},{2,3},{3,2},{4,5},{5,4},{6,7},{7,6},{8,9},{9,8},{10,11... | collective-permute-start | bytes 786440 | tf_op jit(solution)/shard_map/ppermute | solution.py:662
  70.1 2.9 %collective-permute-start.20 = (bf16[1,16,64,128]{3,2,1,0:T(8,128)(2,1)}, bf16[1,16,64,128]{3,2,1,0:T(8,128)(2,1)}, u32[]{:S(2)}, u32[]{:S(2)}) collective-permute-start(bf16[1,16,64,128]{3,2,1,0:T(8,128)(2,1)} %collective-permute-done.19.refs_24_), channel_id=1, source_target_pairs={{0,1},{1,0},{2,3},{3,2},{4,5},{5,4},{6,7},{7,6},{8,9},{9,8},{10,11... | collective-permute-start | bytes 786440 | tf_op jit(solution)/shard_map/ppermute | solution.py:664
  70.1 0.8 copy-start.15
  73.0 0.8 copy-start.7
  91.1 14.0 %collective-permute-start.21 = (bf16[256,128]{1,0:T(8,128)(2,1)}, bf16[256,128]{1,0:T(8,128)(2,1)S(1)}, u32[]{:S(2)}, u32[]{:S(2)}) collective-permute-start(bf16[256,128]{1,0:T(8,128)(2,1)} %get-tuple-element.44), channel_id=1, source_target_pairs={{0,24},{4,28},{8,16},{12,20},{16,8},{20,12},{24,0},{28,4},{1,25},{... | collective-permute-start | bytes 196616 | tf_op jit(solution)/shard_map/ppermute | solution.py:692
  94.4 11.1 %collective-permute-start.22 = (bf16[256,128]{1,0:T(8,128)(2,1)}, bf16[256,128]{1,0:T(8,128)(2,1)S(1)}, u32[]{:S(2)}, u32[]{:S(2)}) collective-permute-start(bf16[256,128]{1,0:T(8,128)(2,1)} %get-tuple-element.45), channel_id=1, source_target_pairs={{0,28},{4,24},{8,20},{12,16},{16,12},{20,8},{24,4},{28,0},{1,29},{... | collective-permute-start | bytes 196616 | tf_op jit(solution)/shard_map/ppermute | solution.py:692
  95.9 13.5 %collective-permute-start.23 = (bf16[256,128]{1,0:T(8,128)(2,1)}, bf16[256,128]{1,0:T(8,128)(2,1)S(1)}, u32[]{:S(2)}, u32[]{:S(2)}) collective-permute-start(bf16[256,128]{1,0:T(8,128)(2,1)} %get-tuple-element.46), channel_id=1, source_target_pairs={{0,20},{4,16},{8,28},{12,24},{16,4},{20,0},{24,12},{28,8},{1,21},{... | collective-permute-start | bytes 196616 | tf_op jit(solution)/shard_map/ppermute | solution.py:692
  101.3 9.0 %collective-permute-start.24 = (bf16[256,128]{1,0:T(8,128)(2,1)}, bf16[256,128]{1,0:T(8,128)(2,1)S(1)}, u32[]{:S(2)}, u32[]{:S(2)}) collective-permute-start(bf16[256,128]{1,0:T(8,128)(2,1)} %get-tuple-element.47), channel_id=1, source_target_pairs={{0,16},{4,20},{8,24},{12,28},{16,0},{20,4},{24,8},{28,12},{1,17},{... | collective-permute-start | bytes 196616 | tf_op jit(solution)/shard_map/ppermute | solution.py:692
  102.6 7.8 %collective-permute-start.25 = (bf16[256,128]{1,0:T(8,128)(2,1)}, bf16[256,128]{1,0:T(8,128)(2,1)S(1)}, u32[]{:S(2)}, u32[]{:S(2)}) collective-permute-start(bf16[256,128]{1,0:T(8,128)(2,1)} %get-tuple-element.48), channel_id=1, source_target_pairs={{0,12},{4,8},{8,4},{12,0},{16,28},{20,24},{24,20},{28,16},{1,13},{... | collective-permute-start | bytes 196616 | tf_op jit(solution)/shard_map/ppermute | solution.py:692
  105.1 6.4 %collective-permute-start.26 = (bf16[256,128]{1,0:T(8,128)(2,1)}, bf16[256,128]{1,0:T(8,128)(2,1)S(1)}, u32[]{:S(2)}, u32[]{:S(2)}) collective-permute-start(bf16[256,128]{1,0:T(8,128)(2,1)} %get-tuple-element.49), channel_id=1, source_target_pairs={{0,8},{4,12},{8,0},{12,4},{16,24},{20,28},{24,16},{28,20},{1,9},{5... | collective-permute-start | bytes 196616 | tf_op jit(solution)/shard_map/ppermute | solution.py:692
  105.6 5.9 %collective-permute-start.27 = (bf16[256,128]{1,0:T(8,128)(2,1)}, bf16[256,128]{1,0:T(8,128)(2,1)S(1)}, u32[]{:S(2)}, u32[]{:S(2)}) collective-permute-start(bf16[256,128]{1,0:T(8,128)(2,1)} %get-tuple-element.50), channel_id=1, source_target_pairs={{0,4},{4,0},{8,12},{12,8},{16,20},{20,16},{24,28},{28,24},{1,5},{5... | collective-permute-start | bytes 196616 | tf_op jit(solution)/shard_map/ppermute | solution.py:692
  106.9 4.6 %copy-start = (bf16[256,128]{1,0:T(8,128)(2,1)S(1)}, bf16[256,128]{1,0:T(8,128)(2,1)}, u32[]{:S(2)}) copy-start(bf16[256,128]{1,0:T(8,128)(2,1)} %get-tuple-element.43.refs_7_) | copy-start | bytes 196612
  112.9 2.0 %collective-permute-start.29 = (bf16[64,2048]{1,0:T(8,128)(2,1)S(1)}, bf16[64,2048]{1,0:T(8,128)(2,1)S(1)}, u32[]{:S(2)}, u32[]{:S(2)}) collective-permute-start(bf16[64,2048]{1,0:T(8,128)(2,1)S(1)} %get-tuple-element.54), channel_id=1, source_target_pairs={{0,1},{1,0},{2,3},{3,2},{4,5},{5,4},{6,7},{7,6},{8,9},{9,8},{10,11... | collective-permute-start | bytes 786440 | tf_op jit(solution)/shard_map/ppermute | solution.py:696
  114.3 2.5 %collective-permute-start.28 = (bf16[64,2048]{1,0:T(8,128)(2,1)S(1)}, bf16[64,2048]{1,0:T(8,128)(2,1)S(1)}, u32[]{:S(2)}, u32[]{:S(2)}) collective-permute-start(bf16[64,2048]{1,0:T(8,128)(2,1)S(1)} %get-tuple-element.52), channel_id=1, source_target_pairs={{0,1},{1,0},{2,3},{3,2},{4,5},{5,4},{6,7},{7,6},{8,9},{9,8},{10,11... | collective-permute-start | bytes 786440 | tf_op jit(solution)/shard_map/ppermute | solution.py:699
  115.0 8.3 %collective-permute-start.30 = (bf16[64,2048]{1,0:T(8,128)(2,1)S(1)}, bf16[64,2048]{1,0:T(8,128)(2,1)S(1)}, u32[]{:S(2)}, u32[]{:S(2)}) collective-permute-start(bf16[64,2048]{1,0:T(8,128)(2,1)S(1)} %add_convert_fusion.1), channel_id=1, source_target_pairs={{0,2},{1,3},{2,0},{3,1},{4,6},{5,7},{6,4},{7,5},{8,10},{9,11},{10,... | collective-permute-start | bytes 786440 | tf_op jit(solution)/shard_map/ppermute | solution.py:700
